TPU v7x, 32 devices: a whole 2x2x4 slice. The times are simulated.
32 devices in a mesh: sec: 4 (over y, core), gx: 4 (over z), gy: 2 (over x).
Axes of the slice: x: 2, y: 2, z: 4, core: 2. Of those that a mesh axis runs over, the one named last changes fastest.
Arguments:
- composition_matrix: float32 [22, 32, 32, 512], P(None, 'gx', 'gy', 'sec'), may hold values from 0 to 1
- local_mixing_coefficient: float32 [32, 32, 512], P('gx', 'gy', 'sec'), may hold values from 0.3 to 3
- thermal_field: float32 [32, 32, 512], P('gx', 'gy', 'sec'), may hold values from 0.5 to 2
- component_mixing_weight: float32 [22], replicated, may hold values from 0.05 to 1
- kinetics_jacobian: float32 [22, 22], replicated, may hold values from -1.25 to 1.25
- mixture_classes: int32 [32, 32, 512], P('gx', 'gy', 'sec'), may hold values from 0 to 63, as said below
- streamwise_positions: int32 [32], replicated, may hold values from 0 to 15, as said below
Outputs:
- advanced_composition: float32 [22, 32, 32, 512], P(None, 'gx', 'gy', 'sec')
- cond_means: float32 [22, 16, 64], P(None, 'gx')
Inputs may be any that keep to these rules, and one draw needn't show every extreme that they name: `mixture_classes`: bins of each plane cluster around a plane-dependent range. `streamwise_positions`: plane p has station ((p + h) // 2) mod 16 for one odd h between 1 and 7, so each station holds two axial planes.
All inputs are finite; a program needn't handle non-finite values.
Results may differ from a plain program's by a relative error of at most 0.0003.
Values sent between devices are 32-bit elements; how exact they have to be, the bound alone decides.
No kernel may reach another device: no remote copies, remote signals or barrier semaphores. Data moves between devices by JAX's collectives and lax.ppermute only.
A program may use at most 64 MiB of HBM per device.

v0:
```python
import jax
import jax.numpy as jnp
from jax import lax
from jax.sharding import PartitionSpec as P

NB = 64


def extended(cells, sides, width):
    for axis, dim in sides:
        count = lax.axis_size(axis)
        ends = count - 1
        head = lax.slice_in_dim(cells, 0, width, axis=dim)
        tail = lax.slice_in_dim(cells, cells.shape[dim] - width, cells.shape[dim], axis=dim)
        cells = jnp.concatenate(
            [
                lax.ppermute(tail, axis, [(i, (i + 1) % count) for i in range(ends)]),
                cells,
                lax.ppermute(head, axis, [((i + 1) % count, i) for i in range(ends)]),
            ],
            axis=dim,
        )
    return cells


def shifted(shard, axis, by):
    peers = lax.axis_size(axis)
    return lax.ppermute(shard, axis, [(i, (i + by) % peers) for i in range(peers)])


def neighbour(padded_composition, axis, start):
    index = [slice(None), slice(1, -1), slice(1, -1), slice(1, -1)]
    index[axis] = slice(start, start + padded_composition.shape[axis] - 2)
    return padded_composition[tuple(index)]


def kinetic_source_term(central_voxels, thermal_field, kinetics_jacobian):
    averaged_composition = jnp.einsum(
        "kj,jxyz->kxyz", kinetics_jacobian, central_voxels, precision=lax.Precision.HIGHEST
    )
    return 4.0 * jnp.exp(-2.0 / thermal_field) * averaged_composition


def on_device(
    composition_matrix,
    local_mixing_coefficient,
    thermal_field,
    component_mixing_weight,
    kinetics_jacobian,
    mixture_classes,
    streamwise_positions,
):
    collected_slabs = jnp.concatenate([composition_matrix, local_mixing_coefficient[None]], axis=0)
    padded_composition = extended(collected_slabs, (("sec", 3), ("gx", 1), ("gy", 2)), 1)
    reactive_yield_term = kinetic_source_term(composition_matrix, thermal_field, kinetics_jacobian)
    total = jnp.zeros_like(composition_matrix)
    for axis in (1, 2, 3):
        for start in (0, 2):
            other = neighbour(padded_composition, axis, start)
            total = total + 0.5 * (local_mixing_coefficient + other[-1]) * (
                other[:-1] - composition_matrix
            )
    advanced_composition = composition_matrix + 0.05 * (
        component_mixing_weight[:, None, None, None] * total + reactive_yield_term
    )
    planes = composition_matrix.shape[1]
    cells = composition_matrix.shape[2] * composition_matrix.shape[3]
    values = jnp.concatenate(
        [advanced_composition, jnp.ones_like(advanced_composition[:1])], axis=0
    )
    values = values.reshape(values.shape[0], planes, cells)
    levels = jnp.arange(NB, dtype=jnp.int32)
    onehot = (mixture_classes.reshape(planes, cells)[None] == levels[:, None, None]).astype(
        jnp.float32
    )
    partial_sums = jnp.einsum("kxc,bxc->kxb", values, onehot, precision=lax.Precision.HIGHEST)
    first_plane = lax.axis_index("gx") * planes
    own_stations = lax.dynamic_slice_in_dim(streamwise_positions, first_plane, planes)
    station_count = streamwise_positions.shape[0] // 2
    per_device = station_count // lax.axis_size("gx")
    window_ids = (
        lax.axis_index("gx") * per_device + jnp.arange(2 * per_device, dtype=jnp.int32)
    ) % station_count
    window_owner = (own_stations[:, None] == window_ids[None]).astype(jnp.float32)
    window = jnp.einsum("kxb,xs->ksb", partial_sums, window_owner, precision=lax.Precision.HIGHEST)
    summed = lax.psum(window, ("sec", "gy"))
    passed = shifted(summed[:, per_device:], "gx", 1)
    totals = summed[:, :per_device] + passed
    cond_means = totals[:-1] / jnp.maximum(totals[-1], 1.0)[None]
    return (advanced_composition, cond_means)


def solution(mesh):
    in_specs = (
        P(None, "gx", "gy", "sec"),
        P("gx", "gy", "sec"),
        P("gx", "gy", "sec"),
        P(),
        P(),
        P("gx", "gy", "sec"),
        P(),
    )
    out_specs = (P(None, "gx", "gy", "sec"), P(None, "gx", None))
    return jax.shard_map(
        on_device, mesh=mesh, in_specs=in_specs, out_specs=out_specs, check_vma=False
    )
```

profile of v0, /device:TPU:0, one launch (start us, length us, event | category | flops | bytes accessed | tf_op | source)
XLA Modules:
  0.0 105.6 jit_solution(11558755004724292841)
XLA Ops:
  0.6 0.0 copy-start
  0.6 3.6 %fusion.13 = (f32[23,8,16,1]{3,2,1,0:T(8,128)S(1)}, f32[23,8,16,1]{3,2,1,0:T(8,128)}) fusion(f32[1,8,16,128]{3,2,1,0:T(8,128)} %bitcast.55, f32[22,8,16,128]{3,2,1,0:T(8,128)} %param.7), kind=kLoop, calls=%fused_computation.16 | loop fusion | flops 5888 | bytes 1530880 | tf_op jit(solution)/shard_map/concatenate | solution.py:53
  4.2 2.5 %copy.25 = f32[23,8,16,1]{0,2,3,1:T(8,128)S(1)} copy(f32[23,8,16,1]{3,2,1,0:T(8,128)} %get-tuple-element.18) | data formatting | bytes 23552 | tf_op jit(solution)/shard_map/slice | solution.py:13
  6.7 1.3 %collective-permute-start.1 = (f32[23,8,16,1]{0,2,3,1:T(8,128)S(1)}, f32[23,8,16,1]{0,2,3,1:T(8,128)S(1)}, u32[]{:S(2)}, u32[]{:S(2)}) collective-permute-start(f32[23,8,16,1]{0,2,3,1:T(8,128)S(1)} %copy.25), channel_id=1, source_target_pairs={{8,0},{16,8},{24,16},{9,1},{17,9},{25,17},{10,2},{18,10},{26,18},{... | collective-permute-start | bytes 35336 | tf_op jit(solution)/shard_map/ppermute | solution.py:19
  8.0 1.1 %copy.24 = f32[23,8,16,1]{0,2,3,1:T(8,128)S(1)} copy(f32[23,8,16,1]{3,2,1,0:T(8,128)S(1)} %get-tuple-element.17) | data formatting | bytes 23552 | tf_op jit(solution)/shard_map/slice | solution.py:14
  9.1 3.0 %collective-permute-start = (f32[23,8,16,1]{0,2,3,1:T(8,128)S(1)}, f32[23,8,16,1]{0,2,3,1:T(8,128)S(1)}, u32[]{:S(2)}, u32[]{:S(2)}) collective-permute-start(f32[23,8,16,1]{0,2,3,1:T(8,128)S(1)} %copy.24), channel_id=1, source_target_pairs={{0,8},{8,16},{16,24},{1,9},{9,17},{17,25},{2,10},{10,18},{18,26},{... | collective-permute-start | bytes 35336 | tf_op jit(solution)/shard_map/ppermute | solution.py:17
  12.1 0.0 copy-done.6
  12.2 0.0 copy-done.1
  12.2 0.0 copy-done.5
  12.2 0.1 pad_maximum_fusion
  12.3 0.0 copy-start.7
  12.4 0.0 copy-start.10
  12.4 2.1 %copy.29 = f32[23,8,16,128]{3,0,2,1:T(8,128)} copy(f32[23,8,16,128]{3,2,1,0:T(8,128)S(1)} %pad_maximum_fusion) | data formatting | bytes 3014656 | tf_op jit(solution)/shard_map/concatenate | solution.py:53
  14.4 0.0 copy-done.7
  14.4 0.7 copy.53
  15.1 0.1 dynamic_slice.3
  15.2 0.0 collective-permute-done.1
  15.2 1.5 %copy.27 = f32[23,8,16,1]{3,2,1,0:T(8,128)S(1)} copy(f32[23,8,16,1]{0,2,3,1:T(8,128)S(1)} %collective-permute-done.1) | data formatting | bytes 23552 | tf_op jit(solution)/shard_map/ppermute | solution.py:19
  16.7 0.0 collective-permute-done
  16.7 2.4 %copy.26 = f32[23,8,16,1]{3,2,1,0:T(8,128)} copy(f32[23,8,16,1]{0,2,3,1:T(8,128)S(1)} %collective-permute-done) | data formatting | bytes 23552 | tf_op jit(solution)/shard_map/ppermute | solution.py:17
  19.1 2.3 %pad_maximum_fusion.27 = (f32[23,1,16,130]{3,2,1,0:T(8,128)}, f32[23,1,16,130]{3,2,1,0:T(8,128)}) fusion(f32[23,8,16,1]{3,2,1,0:T(8,128)S(1)} %copy.27, f32[23,8,16,1]{3,2,1,0:T(8,128)} %copy.26, f32[1,8,16,128]{3,2,1,0:T(8,128)S(1)} %bitcast.57, f32[22,8,16,128]{3,2,1,0:T(8,128)S(1)} %copy-done.1), kind=kLoop, calls=%fused_computation.59 | loop fusion | flops 287040 | bytes 1913600 | tf_op jit(solution)/shard_map/slice | solution.py:14
  21.4 4.9 %collective-permute-start.2 = (f32[23,1,16,130]{3,2,1,0:T(8,128)}, f32[23,1,16,130]{3,2,1,0:T(8,128)S(1)}, u32[]{:S(2)}, u32[]{:S(2)}) collective-permute-start(f32[23,1,16,130]{3,2,1,0:T(8,128)} %get-tuple-element.14), channel_id=1, source_target_pairs={{0,2},{2,4},{4,6},{1,3},{3,5},{5,7},{8,10},{10,12},{12,14},{9,11},... | collective-permute-start | bytes 574088 | tf_op jit(solution)/shard_map/ppermute | solution.py:17
  26.3 1.3 %collective-permute-start.3 = (f32[23,1,16,130]{3,2,1,0:T(8,128)}, f32[23,1,16,130]{3,2,1,0:T(8,128)}, u32[]{:S(2)}, u32[]{:S(2)}) collective-permute-start(f32[23,1,16,130]{3,2,1,0:T(8,128)} %get-tuple-element.15), channel_id=1, source_target_pairs={{2,0},{4,2},{6,4},{3,1},{5,3},{7,5},{10,8},{12,10},{14,12},{11,9},... | collective-permute-start | bytes 574088 | tf_op jit(solution)/shard_map/ppermute | solution.py:19
  27.6 2.0 %copy.30 = f32[23,8,16,1]{3,0,2,1:T(8,128)} copy(f32[23,8,16,1]{0,2,3,1:T(8,128)S(1)} %collective-permute-done.1) | data formatting | bytes 23552 | tf_op jit(solution)/shard_map/ppermute | solution.py:19
  29.7 1.7 %pad_maximum_fusion.34 = f32[1,8,16,128]{3,0,2,1:T(1,128)S(1)} fusion(f32[23,8,16,1]{3,0,2,1:T(8,128)} %copy.30, f32[23,8,16,128]{3,0,2,1:T(8,128)} %copy.29), kind=kLoop, calls=%fused_computation.68 | loop fusion | flops 16384 | bytes 1584640 | tf_op jit(solution)/shard_map/slice | solution.py:60
  31.3 4.3 %collective-permute-done.2 = f32[23,1,16,130]{3,2,1,0:T(8,128)S(1)} collective-permute-done((f32[23,1,16,130]{3,2,1,0:T(8,128)}, f32[23,1,16,130]{3,2,1,0:T(8,128)S(1)}, u32[]{:S(2)}, u32[]{:S(2)}) %collective-permute-start.2) | collective-permute-done | bytes 191392 | tf_op jit(solution)/shard_map/ppermute | solution.py:17
  35.6 4.5 %collective-permute-done.3 = f32[23,1,16,130]{3,2,1,0:T(8,128)} collective-permute-done((f32[23,1,16,130]{3,2,1,0:T(8,128)}, f32[23,1,16,130]{3,2,1,0:T(8,128)}, u32[]{:S(2)}, u32[]{:S(2)}) %collective-permute-start.3) | collective-permute-done | bytes 191392 | tf_op jit(solution)/shard_map/ppermute | solution.py:19
  40.1 0.0 copy-done.2
  40.1 2.3 %pad_maximum_fusion.33 = (f32[23,10,1,130]{3,2,1,0:T(1,128)S(1)}, f32[23,10,1,130]{3,2,1,0:T(1,128)S(1)}) fusion(f32[23,1,16,130]{3,2,1,0:T(8,128)} %collective-permute-done.3, f32[23,1,16,130]{3,2,1,0:T(8,128)S(1)} %collective-permute-done.2, f32[23,8,16,1]{3,2,1,0:T(8,128)S(1)} %copy.27, f32[23,8,16,1]{3,2,1,0:T(8,128)S(1)} %copy-done.2, ...), kind=kLoop, calls=%fused_computation.65 | loop fusion | flops 299000 | bytes 2152800 | tf_op jit(solution)/shard_map/slice | solution.py:14
  42.4 3.4 %collective-permute-start.4 = (f32[23,10,1,130]{3,2,1,0:T(1,128)S(1)}, f32[23,10,1,130]{3,2,1,0:T(1,128)S(1)}, u32[]{:S(2)}, u32[]{:S(2)}) collective-permute-start(f32[23,10,1,130]{3,2,1,0:T(1,128)S(1)} %get-tuple-element.10), channel_id=1, source_target_pairs={{0,1},{2,3},{4,5},{6,7},{8,9},{10,11},{12,13},{14,15},{16,17},{18,... | collective-permute-start | bytes 358808 | tf_op jit(solution)/shard_map/ppermute | solution.py:17
  45.8 1.5 %collective-permute-start.5 = (f32[23,10,1,130]{3,2,1,0:T(1,128)S(1)}, f32[23,10,1,130]{3,2,1,0:T(1,128)S(1)}, u32[]{:S(2)}, u32[]{:S(2)}) collective-permute-start(f32[23,10,1,130]{3,2,1,0:T(1,128)S(1)} %get-tuple-element.11), channel_id=1, source_target_pairs={{1,0},{3,2},{5,4},{7,6},{9,8},{11,10},{13,12},{15,14},{17,16},{19,... | collective-permute-start | bytes 358808 | tf_op jit(solution)/shard_map/ppermute | solution.py:19
  47.3 0.8 fusion.40
  48.1 2.8 %collective-permute-done.4 = f32[23,10,1,130]{3,2,1,0:T(1,128)S(1)} collective-permute-done((f32[23,10,1,130]{3,2,1,0:T(1,128)S(1)}, f32[23,10,1,130]{3,2,1,0:T(1,128)S(1)}, u32[]{:S(2)}, u32[]{:S(2)}) %collective-permute-start.4) | collective-permute-done | bytes 119632 | tf_op jit(solution)/shard_map/ppermute | solution.py:17
  50.9 4.1 %collective-permute-done.5 = f32[23,10,1,130]{3,2,1,0:T(1,128)S(1)} collective-permute-done((f32[23,10,1,130]{3,2,1,0:T(1,128)S(1)}, f32[23,10,1,130]{3,2,1,0:T(1,128)S(1)}, u32[]{:S(2)}, u32[]{:S(2)}) %collective-permute-start.5) | collective-permute-done | bytes 119632 | tf_op jit(solution)/shard_map/ppermute | solution.py:19
  55.0 0.1 fusion.36
  55.2 0.0 copy-start.9
  55.2 7.8 %fusion.17 = f32[22,8,16,128]{3,2,1,0:T(8,128)S(1)} fusion(f32[22,8,16,128]{3,2,1,0:T(8,128)S(1)} %copy-done.1, f32[23,8,16,1]{3,2,1,0:T(8,128)S(1)} %copy-done.2, f32[1,8,16,128]{3,2,1,0:T(8,128)S(1)} %bitcast.61, f32[23,10,1,130]{3,2,1,0:T(1,128)S(1)} %collective-permute-done.5, f32[23,1,16,130]{3,2,1,0:T(8,128)} %collective-permute-done.3, ...), kind=kLoop, calls=%fused_computation.21 | loop fusion | flops 12976128 | bytes 3922272 | tf_op jit(solution)/shard_map/add | solution.py:60
  63.0 4.3 %fusion.8 = f32[22,8,16,128]{3,0,2,1:T(8,128)S(1)} fusion(f32[23,8,16,1]{3,0,2,1:T(8,128)S(1)} %copy-done.4, f32[23,8,16,128]{3,0,2,1:T(8,128)S(1)} %copy-done.3, f32[22,8,16,128]{3,2,1,0:T(8,128)S(1)} %fusion.17, f32[22,8,16,128]{3,2,1,0:T(8,128)S(1)} %copy-done.1, f32[8,16,128]{2,1,0:T(8,128)S(1)} %exponential_multiply_fusion, ...), kind=kOutput, calls=%fused_computation.13 | convolution fusion | flops 98402304 | bytes 5977576 | tf_op jit(solution)/shard_map/kj,jxyz->kxyz/dot_general | solution.py:38
  67.3 0.3 copy.42
  67.6 1.3 %concatenate.40.clone = f32[23,8,16,128]{3,2,0,1:T(8,128)} pad(f32[22,8,16,128]{3,2,0,1:T(8,128)S(1)} %copy.42, f32[]{:T(128)} %constant.38.clone.1), padding=0_1x0_0x0_0x0_0 | pad | bytes 2949124 | tf_op jit(solution)/shard_map/concatenate | solution.py:68
  68.8 2.6 %reshape.35 = f32[23,8,2048]{2,0,1:T(8,128)} reshape(f32[23,8,16,128]{3,2,0,1:T(8,128)} %concatenate.40.clone) | data formatting | bytes 3014656 | tf_op jit(solution)/shard_map/reshape | solution.py:71
  71.5 3.6 %fusion.29 = f32[23,8,64]{2,0,1:T(8,128)S(1)} fusion(f32[23,8,2048]{2,0,1:T(8,128)} %reshape.35, s32[8,2048]{1,0:T(8,128)S(1)} %bitcast.64), kind=kOutput, calls=%fused_computation.54 | convolution fusion | flops 290455552 | bytes 1619968 | tf_op jit(solution)/shard_map/kxc,bxc->kxb/dot_general | solution.py:76
  75.0 0.2 convolution_bitcast_fusion
  75.3 23.7 %psum.7 = f32[23,8,64]{2,1,0:T(8,128)S(1)} all-reduce(f32[23,8,64]{2,1,0:T(8,128)S(1)} %convolution_bitcast_fusion), channel_id=1, replica_groups=mesh['sec'=4,'gx'=4,'gy'=2] {'sec','gy'}, use_global_device_ids=true, to_apply=%region_0.1 | all-reduce | flops 11776 | bytes 94208 | tf_op jit(solution)/shard_map/psum | solution.py:86
  99.0 1.6 %collective-permute-start.6 = (f32[23,4,64]{2,1,0:T(4,128)S(1)}, f32[23,4,64]{2,1,0:T(4,128)S(1)}, u32[]{:S(2)}, u32[]{:S(2)}) collective-permute-start(f32[23,4,64]{2,1,0:T(4,128)S(1)} %slice.117), channel_id=1, source_target_pairs={{0,2},{2,4},{4,6},{6,0},{1,3},{3,5},{5,7},{7,1},{8,10},{10,12},{12... | collective-permute-start | bytes 70664 | tf_op jit(solution)/shard_map/ppermute | solution.py:28
  100.6 1.4 %copy.38 = f32[22,8,16,128]{3,2,1,0:T(8,128)} copy(f32[22,8,16,128]{3,0,2,1:T(8,128)S(1)} %fusion.8) | data formatting | bytes 2883584
  102.0 2.9 %collective-permute-done.6 = f32[23,4,64]{2,1,0:T(4,128)S(1)} collective-permute-done((f32[23,4,64]{2,1,0:T(4,128)S(1)}, f32[23,4,64]{2,1,0:T(4,128)S(1)}, u32[]{:S(2)}, u32[]{:S(2)}) %collective-permute-start.6) | collective-permute-done | bytes 23584 | tf_op jit(solution)/shard_map/ppermute | solution.py:28
  105.0 0.6 slice_divide_fusion
  (18 shorter events, 0.1 us)
Async XLA Ops:
  0.6 62.4 %copy-start = (f32[22,22]{1,0:T(8,128)S(1)}, f32[22,22]{1,0:T(8,128)}, u32[]{:S(2)}) copy-start(f32[22,22]{1,0:T(8,128)} %param.11) | copy-start | bytes 5812
  4.2 7.9 %copy-start.6 = (f32[8,16,128]{2,1,0:T(8,128)S(1)}, f32[8,16,128]{2,1,0:T(8,128)}, u32[]{:S(2)}) copy-start(f32[8,16,128]{2,1,0:T(8,128)} %param.9) | copy-start | bytes 196612
  4.2 8.0 %copy-start.1 = (f32[22,8,16,128]{3,2,1,0:T(8,128)S(1)}, f32[22,8,16,128]{3,2,1,0:T(8,128)}, u32[]{:S(2)}) copy-start(f32[22,8,16,128]{3,2,1,0:T(8,128)} %param.7) | copy-start | bytes 4325380
  4.2 8.0 %copy-start.5 = (f32[8,16,128]{2,1,0:T(8,128)S(1)}, f32[8,16,128]{2,1,0:T(8,128)}, u32[]{:S(2)}) copy-start(f32[8,16,128]{2,1,0:T(8,128)} %param.8) | copy-start | bytes 196612
  6.7 8.5 %collective-permute-start.1 = (f32[23,8,16,1]{0,2,3,1:T(8,128)S(1)}, f32[23,8,16,1]{0,2,3,1:T(8,128)S(1)}, u32[]{:S(2)}, u32[]{:S(2)}) collective-permute-start(f32[23,8,16,1]{0,2,3,1:T(8,128)S(1)} %copy.25), channel_id=1, source_target_pairs={{8,0},{16,8},{24,16},{9,1},{17,9},{25,17},{10,2},{18,10},{26,18},{... | collective-permute-start | bytes 35336 | tf_op jit(solution)/shard_map/ppermute | solution.py:19
  9.1 7.6 %collective-permute-start = (f32[23,8,16,1]{0,2,3,1:T(8,128)S(1)}, f32[23,8,16,1]{0,2,3,1:T(8,128)S(1)}, u32[]{:S(2)}, u32[]{:S(2)}) collective-permute-start(f32[23,8,16,1]{0,2,3,1:T(8,128)S(1)} %copy.24), channel_id=1, source_target_pairs={{0,8},{8,16},{16,24},{1,9},{9,17},{17,25},{2,10},{10,18},{18,26},{... | collective-permute-start | bytes 35336 | tf_op jit(solution)/shard_map/ppermute | solution.py:17
  12.3 2.1 %copy-start.7 = (s32[8,16,128]{2,1,0:T(8,128)S(1)}, s32[8,16,128]{2,1,0:T(8,128)}, u32[]{:S(2)}) copy-start(s32[8,16,128]{2,1,0:T(8,128)} %param.12) | copy-start | bytes 196612
  12.4 2.7 %copy-start.10 = (s32[32]{0:T(128)S(1)}, s32[32]{0:T(128)}, u32[]{:S(2)}) copy-start(s32[32]{0:T(128)} %param.13) | copy-start | bytes 388
  21.4 14.2 %collective-permute-start.2 = (f32[23,1,16,130]{3,2,1,0:T(8,128)}, f32[23,1,16,130]{3,2,1,0:T(8,128)S(1)}, u32[]{:S(2)}, u32[]{:S(2)}) collective-permute-start(f32[23,1,16,130]{3,2,1,0:T(8,128)} %get-tuple-element.14), channel_id=1, source_target_pairs={{0,2},{2,4},{4,6},{1,3},{3,5},{5,7},{8,10},{10,12},{12,14},{9,11},... | collective-permute-start | bytes 574088 | tf_op jit(solution)/shard_map/ppermute | solution.py:17
  26.3 13.7 %collective-permute-start.3 = (f32[23,1,16,130]{3,2,1,0:T(8,128)}, f32[23,1,16,130]{3,2,1,0:T(8,128)}, u32[]{:S(2)}, u32[]{:S(2)}) collective-permute-start(f32[23,1,16,130]{3,2,1,0:T(8,128)} %get-tuple-element.15), channel_id=1, source_target_pairs={{2,0},{4,2},{6,4},{3,1},{5,3},{7,5},{10,8},{12,10},{14,12},{11,9},... | collective-permute-start | bytes 574088 | tf_op jit(solution)/shard_map/ppermute | solution.py:19
  29.7 10.4 %copy-start.2 = (f32[23,8,16,1]{3,2,1,0:T(8,128)S(1)}, f32[23,8,16,1]{3,2,1,0:T(8,128)}, u32[]{:S(2)}) copy-start(f32[23,8,16,1]{3,2,1,0:T(8,128)} %copy.26) | copy-start | bytes 35332
  42.4 8.5 %collective-permute-start.4 = (f32[23,10,1,130]{3,2,1,0:T(1,128)S(1)}, f32[23,10,1,130]{3,2,1,0:T(1,128)S(1)}, u32[]{:S(2)}, u32[]{:S(2)}) collective-permute-start(f32[23,10,1,130]{3,2,1,0:T(1,128)S(1)} %get-tuple-element.10), channel_id=1, source_target_pairs={{0,1},{2,3},{4,5},{6,7},{8,9},{10,11},{12,13},{14,15},{16,17},{18,... | collective-permute-start | bytes 358808 | tf_op jit(solution)/shard_map/ppermute | solution.py:17
  45.8 9.3 %collective-permute-start.5 = (f32[23,10,1,130]{3,2,1,0:T(1,128)S(1)}, f32[23,10,1,130]{3,2,1,0:T(1,128)S(1)}, u32[]{:S(2)}, u32[]{:S(2)}) collective-permute-start(f32[23,10,1,130]{3,2,1,0:T(1,128)S(1)} %get-tuple-element.11), channel_id=1, source_target_pairs={{1,0},{3,2},{5,4},{7,6},{9,8},{11,10},{13,12},{15,14},{17,16},{19,... | collective-permute-start | bytes 358808 | tf_op jit(solution)/shard_map/ppermute | solution.py:19
  55.2 7.8 %copy-start.3 = (f32[23,8,16,128]{3,0,2,1:T(8,128)S(1)}, f32[23,8,16,128]{3,0,2,1:T(8,128)}, u32[]{:S(2)}) copy-start(f32[23,8,16,128]{3,0,2,1:T(8,128)} %copy.29) | copy-start | bytes 4521988
  55.2 7.8 %copy-start.4 = (f32[23,8,16,1]{3,0,2,1:T(8,128)S(1)}, f32[23,8,16,1]{3,0,2,1:T(8,128)}, u32[]{:S(2)}) copy-start(f32[23,8,16,1]{3,0,2,1:T(8,128)} %copy.30) | copy-start | bytes 35332
  55.2 7.8 %copy-start.9 = (f32[22]{0:T(128)S(1)}, f32[22]{0:T(128)}, u32[]{:S(2)}) copy-start(f32[22]{0:T(128)} %param.10) | copy-start | bytes 268
  68.8 2.6 %copy-start.8 = (s32[1,8,16,128]{3,1,2,0:T(8,128)S(1)}, s32[1,8,16,128]{3,1,2,0:T(8,128)}, u32[]{:S(2)}) copy-start(s32[1,8,16,128]{3,1,2,0:T(8,128)} %copy.53) | copy-start | bytes 196612
  99.0 5.9 %collective-permute-start.6 = (f32[23,4,64]{2,1,0:T(4,128)S(1)}, f32[23,4,64]{2,1,0:T(4,128)S(1)}, u32[]{:S(2)}, u32[]{:S(2)}) collective-permute-start(f32[23,4,64]{2,1,0:T(4,128)S(1)} %slice.117), channel_id=1, source_target_pairs={{0,2},{2,4},{4,6},{6,0},{1,3},{3,5},{5,7},{7,1},{8,10},{10,12},{12... | collective-permute-start | bytes 70664 | tf_op jit(solution)/shard_map/ppermute | solution.py:28
where the time goes:
time: 106 us
  blocking collectives  23.7 us (22%)
  other arithmetic  19.4 us (18%)
  waiting for transfers between devices  18.6 us (18%)
  local copies, waits for them, and re-layouts  17.9 us (17%)
  starting transfers between devices  17 us (16%)
  matrix products  8.1 us (8%)
    psum x1, blocking collectives, on_device(): summed = lax.psum(window, ('sec', 'gy'))  23.7 us
    ppermute x3, starting transfers between devices, extended(): lax.ppermute(tail, axis, [(i, (i + 1) % count) for i in range(ends)])  11.4 us
    ppermute x3, waiting for transfers between devices, extended(): lax.ppermute(head, axis, [((i + 1) % count, i) for i in range(ends)])  8.6 us
    add x1, other arithmetic, on_device(): total + 0.5 * (local_mixing_coefficient + other[-1]) * (other[:-1] - comp...  7.78 us
    ppermute x3, waiting for transfers between devices, extended(): lax.ppermute(tail, axis, [(i, (i + 1) % count) for i in range(ends)])  7.06 us
    slice x2, other arithmetic, extended(): lax.slice_in_dim(cells, cells.shape[dim] - width, cells.shape[dim], axis=...  4.55 us
    dot_general x1, matrix products, kinetic_source_term(): jnp.einsum('kj,jxyz->kxyz', kinetics_jacobian, central_voxels, precision=...  4.27 us
    ppermute x3, starting transfers between devices, extended(): lax.ppermute(head, axis, [((i + 1) % count, i) for i in range(ends)])  4.05 us
  transfers between devices with their start and end apart: 7, of which 5 were waited for; matrix products, arithmetic and copies ran while one was open for 11% of the time, Pallas kernels for 0%

commit v1 on v0

v1 whole, which is shorter than its diff:
```python
import functools

import jax
import jax.numpy as jnp
from jax import lax
from jax.experimental import pallas as pl
from jax.experimental.pallas import tpu as pltpu
from jax.sharding import PartitionSpec as P

NB = 64
SUBLANES = 8
LANES = 128
F32 = jnp.float32
BF16 = jnp.bfloat16
VMEM = pl.BlockSpec(memory_space=pltpu.VMEM)
ANY = pl.BlockSpec(memory_space=pl.ANY)
DT = 0.05


def padded_rows(species):
    return -(-(species + 2) // SUBLANES) * SUBLANES


def lanes_of(shape):
    return lax.broadcasted_iota(jnp.int32, shape, len(shape) - 1)


def rows_of(shape):
    return lax.broadcasted_iota(jnp.int32, shape, len(shape) - 2)


def halves(block):
    high = block.astype(BF16).astype(F32)
    return jnp.concatenate([high, block - high], axis=0).astype(BF16)


def weight_column(weights_ref, rows):
    species = weights_ref.shape[1]
    shape = (rows, species)
    spread = jnp.where(rows_of(shape) == lanes_of(shape), weights_ref[...], 0.0)
    return DT * jnp.sum(spread, axis=1, keepdims=True)


def binned(values, classes):
    shape = (NB, values.shape[1])
    hits = (classes == rows_of(shape).astype(F32)).astype(F32).astype(BF16)
    return lax.dot_general(
        values, hits, (((1,), (1,)), ((), ())), preferred_element_type=F32
    )


def folded(product):
    rows = product.shape[0] // 2
    return product[:rows] + product[rows:]


def pack_kernel(planes, has_b, cells, mixing, classes, *refs):
    outs, sem = refs[:-1], refs[-1]
    rows_out, own_z = outs[0], outs[1]
    faces = list(outs[2:])
    species, row_count, depth = cells.shape
    width = row_count // planes
    for plane in range(planes):
        span = pl.ds(plane * width, width)
        for k in range(species):
            pltpu.make_async_copy(
                cells.at[k, span], rows_out.at[span, k, :], sem.at[plane]
            ).start()
    for r in range(0, row_count, SUBLANES):
        span = pl.ds(r, SUBLANES)
        rows_out[span, species, :] = mixing[span, :]
        rows_out[span, species + 1, :] = classes[span, :].astype(F32)
    shape = rows_out.shape[1:]
    lane = lanes_of(shape)
    low = jnp.zeros(shape, F32)
    high = jnp.zeros(shape, F32)
    for plane in range(planes):
        span = pl.ds(plane * width, width)
        pltpu.make_async_copy(
            cells.at[:, span], rows_out.at[pl.ds(0, species), pl.ds(0, width), :], sem.at[plane]
        ).wait()
        for r in range(plane * width, (plane + 1) * width):
            turned = pltpu.roll(rows_out[r], r, axis=1) if r else rows_out[r]
            low = jnp.where(lane == r, turned, low)
            high = jnp.where(lane == (r - 1) % depth, turned, high)
    high = pltpu.roll(high, 1, axis=1)
    own_z[0] = low
    own_z[1] = high
    for axis, both in zip(("gx", "gy", "sec"), has_b):
        even = lax.axis_index(axis) % 2 == 0
        for side in range(1 + both):
            out = faces.pop(0)
            upper = even if side == 0 else jnp.logical_not(even)
            if axis == "gx":
                first = jnp.where(upper, row_count - width, 0)
                for y in range(width):
                    out[y] = rows_out[first + y]
            elif axis == "gy":
                first = jnp.where(upper, width - 1, 0)
                for x in range(planes):
                    out[x] = rows_out[first + x * width]
            else:
                out[...] = own_z[jnp.where(upper, 1, 0)]


def inner_kernel(
    planes, cells, mixing, thermal, weights, jacobian, advanced, station_sums, coefs, square
):
    row_count, rows, depth = cells.shape
    species = jacobian.shape[0]
    width = row_count // planes
    shape = (row_count, depth)
    lane, row = lanes_of(shape), rows_of(shape)
    mix = mixing[...]
    up = 0.5 * (mix + pltpu.roll(mix, depth - 1, axis=1))
    up = jnp.where(lane == depth - 1, 0.0, up)
    coefs[0] = up
    down = pltpu.roll(up, 1, axis=1)
    coefs[1] = down
    total = up + down
    up = 0.5 * (mix + pltpu.roll(mix, row_count - 1, axis=0))
    up = jnp.where(row % width == width - 1, 0.0, up)
    coefs[2] = up
    down = pltpu.roll(up, 1, axis=0)
    coefs[3] = down
    total = total + (up + down)
    edge = jnp.zeros((width, depth), F32)
    up = jnp.concatenate([0.5 * (mix[: row_count - width] + mix[width:]), edge], axis=0)
    coefs[4] = up
    down = jnp.concatenate([edge, up[: row_count - width]], axis=0)
    coefs[5] = down
    coefs[6] = total + (up + down)
    coefs[7] = (4.0 * DT) * jnp.exp(-2.0 / thermal[...])

    square[...] = jnp.zeros_like(square)
    matrix = jacobian[...]
    matrix_high = matrix.astype(BF16).astype(F32)
    square[:species, :species] = matrix_high
    square[:species, rows : rows + species] = matrix_high
    square[rows : rows + species, :species] = matrix - matrix_high
    left = square[...].astype(BF16)

    weight = jnp.broadcast_to(weight_column(weights, rows), (rows, depth))
    ones = rows_of((rows, depth)) >= species
    station_sums[...] = jnp.zeros_like(station_sums)

    @pl.loop(0, planes)
    def _(x):
        base = x * width
        below = jnp.maximum(x - 1, 0) * width
        above = jnp.minimum(x + 1, planes - 1) * width
        made = jnp.zeros((2 * rows, NB), F32)
        for first in range(0, width, 2):
            pair = (first, first + 1)
            here = [cells[base + y] for y in pair]
            mixed = folded(
                jnp.dot(
                    left,
                    jnp.concatenate([halves(c) for c in here], axis=1),
                    preferred_element_type=F32,
                )
            )
            values, classes = [], []
            for i, y in enumerate(pair):
                r = base + y
                c = here[i]
                at = lambda n: coefs[n, pl.ds(r, 1), :]
                flux = at(0) * pltpu.roll(c, depth - 1, axis=1)
                flux += at(1) * pltpu.roll(c, 1, axis=1)
                if y < width - 1:
                    flux += at(2) * cells[r + 1]
                if y > 0:
                    flux += at(3) * cells[r - 1]
                flux += at(4) * cells[above + y]
                flux += at(5) * cells[below + y]
                flux -= at(6) * c
                new = c + weight * flux + at(7) * mixed[:, i * depth : (i + 1) * depth]
                new = jnp.where(ones, 1.0, new)
                advanced[r] = new
                values.append(halves(new))
                classes.append(cells[r, species + 1 : species + 2, :])
            made += binned(jnp.concatenate(values, axis=1), jnp.concatenate(classes, axis=1))
        station_sums[(x + 1) // 2] += folded(made)


def edge_kernel(planes, has_b, cells, own_z, sums, weights, positions, *refs):
    halos = list(refs[: 3 + sum(has_b)])
    own, carry, dx, dy, dz, station_sums = refs[3 + sum(has_b) :]
    row_count, rows, depth = cells.shape
    species = weights.shape[1]
    width = row_count // planes
    weight = jnp.broadcast_to(weight_column(weights, rows), (rows, depth))
    received = {}
    for axis, both in zip(("gx", "gy", "sec"), has_b):
        received[axis] = [halos.pop(0), halos.pop(0) if both else None]
    evens = {axis: lax.axis_index(axis) % 2 == 0 for axis in received}

    def added(c, halo):
        if halo is None:
            return weight * (0.5 * c[species : species + 1]) * (0.0 - c)
        d = 0.5 * (c[species : species + 1] + halo[species : species + 1])
        return weight * d * (halo - c)

    station_sums[...] = sums[...]
    for side in range(2):
        upper = evens["gx"] if side == 0 else jnp.logical_not(evens["gx"])
        plane = jnp.where(upper, planes - 1, 0)
        halo = received["gx"][side]
        made = jnp.zeros((2 * rows, NB), F32)
        for first in range(0, width, 2):
            values, classes = [], []
            for y in (first, first + 1):
                r = plane * width + y
                delta = added(cells[r], None if halo is None else halo[y])
                dx[side, y] = delta
                values.append(halves(delta))
                classes.append(cells[r, species + 1 : species + 2, :])
            made += binned(jnp.concatenate(values, axis=1), jnp.concatenate(classes, axis=1))
        station_sums[(plane + 1) // 2] += folded(made)
    for side in range(2):
        upper = evens["gy"] if side == 0 else jnp.logical_not(evens["gy"])
        place = jnp.where(upper, width - 1, 0)
        halo = received["gy"][side]
        for x in range(planes):
            r = place + x * width
            delta = added(cells[r], None if halo is None else halo[x])
            dy[side, x] = delta
            station_sums[(x + 1) // 2] += folded(
                binned(halves(delta), cells[r, species + 1 : species + 2, :])
            )
    stations = planes // 2 + 1
    lane = lanes_of((1, row_count))
    station = ((lane // width + 1) // 2).astype(F32)
    for side in range(2):
        upper = evens["sec"] if side == 0 else jnp.logical_not(evens["sec"])
        c = own_z[jnp.where(upper, 1, 0)]
        halo = received["sec"][side]
        delta = added(c, None if halo is None else halo[...])
        dz[side] = delta
        value = halves(delta)
        classes = c[species + 1 : species + 2]
        for j in range(stations):
            station_sums[j] += folded(binned(value, jnp.where(station == j, classes, -1.0)))
    shift = jnp.broadcast_to(positions[0:1, 0:1], (rows, NB))
    per_device = planes // 2
    for half, out in enumerate((own, carry)):
        for s in range(0, per_device, 2):
            parts = []
            for slot in (half * per_device + s, half * per_device + s + 1):
                part = jnp.zeros((rows, NB), F32)
                for j in range(stations):
                    if 0 <= slot - j < per_device:
                        part += jnp.where(shift == slot - j, station_sums[j], 0.0)
                parts.append(part)
            out[s // 2] = jnp.concatenate(parts, axis=1)


def finish_kernel(planes, advanced, dx, dy, dz, out, total, sem):
    row_count, rows, depth = advanced.shape
    species = out.shape[0]
    width = row_count // planes
    total[...] = advanced[...]
    evens = {axis: lax.axis_index(axis) % 2 == 0 for axis in ("gx", "gy", "sec")}
    for side in range(2):
        upper = evens["gx"] if side == 0 else jnp.logical_not(evens["gx"])
        first = jnp.where(upper, row_count - width, 0)
        for y in range(width):
            total[first + y] += dx[side, y]
    for side in range(2):
        upper = evens["gy"] if side == 0 else jnp.logical_not(evens["gy"])
        place = jnp.where(upper, width - 1, 0)
        for x in range(planes):
            total[place + x * width] += dy[side, x]
    shape = (rows, depth)
    lane = lanes_of(shape)
    even = jnp.broadcast_to(evens["sec"], shape)
    high = jnp.where(even, dz[0], dz[1])
    low = jnp.where(even, dz[1], dz[0])
    high = pltpu.roll(high, depth - 1, axis=1)
    for plane in range(planes):
        for r in range(plane * width, (plane + 1) * width):
            turned = depth - r if r else 0
            a = pltpu.roll(low, turned, axis=1) if r else low
            b = pltpu.roll(high, turned, axis=1) if r else high
            total[r] += jnp.where(lane == 0, a, jnp.where(lane == depth - 1, b, 0.0))
        span = pl.ds(plane * width, width)
        for k in range(species):
            pltpu.make_async_copy(
                total.at[span, k, :], out.at[k, span], sem.at[plane]
            ).start()
    for plane in range(planes):
        span = pl.ds(plane * width, width)
        pltpu.make_async_copy(
            total.at[pl.ds(0, species), pl.ds(0, width), :], out.at[:, span], sem.at[plane]
        ).wait()


def means_kernel(first, second, out):
    species, per_device, bins = out.shape
    for s in range(0, per_device, 2):
        block = first[s // 2] + second[s // 2]
        means = block / jnp.maximum(block[species + 1 : species + 2], 1.0)
        out[:, s, :] = means[:species, :bins]
        out[:, s + 1, :] = means[:species, bins:]


def struct(*shape):
    return jax.ShapeDtypeStruct(shape, F32)


def call(kernel, name, out_shape, n_in, out_specs, in_specs=None, scratch=(), flops=0, moved=0):
    return pl.pallas_call(
        kernel,
        out_shape=out_shape,
        in_specs=in_specs or [VMEM] * n_in,
        out_specs=out_specs,
        scratch_shapes=list(scratch),
        name=name,
        compiler_params=pltpu.CompilerParams(vmem_limit_bytes=32 * 1024 * 1024),
        cost_estimate=pl.CostEstimate(flops=flops, bytes_accessed=moved, transcendentals=0),
    )


def swapped(block, axis, side):
    count = lax.axis_size(axis)
    pairs = []
    for i in range(side, count - 1, 2):
        pairs += [(i, i + 1), (i + 1, i)]
    return lax.ppermute(block, axis, pairs)


def summed(block, axis):
    count = lax.axis_size(axis)
    if count & (count - 1):
        return lax.psum(block, axis)
    step = 1
    while step < count:
        block = block + lax.ppermute(block, axis, [(i, i ^ step) for i in range(count)])
        step *= 2
    return block


def on_device(
    composition_matrix,
    local_mixing_coefficient,
    thermal_field,
    component_mixing_weight,
    kinetics_jacobian,
    mixture_classes,
    streamwise_positions,
):
    species, planes, width, depth = composition_matrix.shape
    row_count = planes * width
    rows = padded_rows(species)
    cells = composition_matrix.reshape(species, row_count, depth)
    mixing = local_mixing_coefficient.reshape(row_count, depth)
    thermal = thermal_field.reshape(row_count, depth)
    classes = mixture_classes.reshape(row_count, depth)
    weights = component_mixing_weight.reshape(1, species)
    positions = streamwise_positions.reshape(1, -1)
    per_device = planes // 2
    has_b = tuple(lax.axis_size(axis) > 2 for axis in ("gx", "gy", "sec"))
    shapes = {"gx": (width, rows, depth), "gy": (planes, rows, depth), "sec": (rows, row_count)}
    sides = [
        (axis, side)
        for axis, both in zip(("gx", "gy", "sec"), has_b)
        for side in range(1 + both)
    ]
    face_shapes = [struct(*shapes[axis]) for axis, _ in sides]

    cells = pltpu.with_memory_space_constraint(cells, pltpu.HBM)
    packed = call(
        functools.partial(pack_kernel, planes, has_b),
        "faces",
        [struct(row_count, rows, depth), struct(2, rows, row_count), *face_shapes],
        3,
        [VMEM] * (2 + len(sides)),
        in_specs=[ANY, VMEM, VMEM],
        scratch=[pltpu.SemaphoreType.DMA((planes,))],
    )(cells, mixing, classes)
    rows_in, own_z, faces = packed[0], packed[1], packed[2:]
    halos = [swapped(face, axis, side) for face, (axis, side) in zip(faces, sides)]

    inner, sums = call(
        functools.partial(inner_kernel, planes),
        "inside",
        [struct(row_count, rows, depth), struct(per_device + 1, rows, NB)],
        5,
        [VMEM] * 2,
        scratch=[
            pltpu.VMEM((8, row_count, depth), F32),
            pltpu.VMEM((2 * rows, 2 * rows), F32),
        ],
        flops=10_000_000,
        moved=4_000_000,
    )(rows_in, mixing, thermal, weights, kinetics_jacobian)

    own, carry, dx, dy, dz = call(
        functools.partial(edge_kernel, planes, has_b),
        "edges",
        [
            struct(per_device // 2, rows, 2 * NB),
            struct(per_device // 2, rows, 2 * NB),
            struct(2, width, rows, depth),
            struct(2, planes, rows, depth),
            struct(2, rows, row_count),
        ],
        5 + len(halos),
        [VMEM] * 5,
        scratch=[pltpu.VMEM((per_device + 1, rows, NB), F32)],
    )(rows_in, own_z, sums, weights, positions, *halos)

    gx = lax.axis_size("gx")
    passed = lax.ppermute(carry, "gx", [(i, (i + 1) % gx) for i in range(gx)])
    window = own + passed
    window = summed(window, "sec")
    gy = lax.axis_size("gy")
    if gy == 2:
        other = lax.ppermute(window, "gy", [(0, 1), (1, 0)])
    else:
        window = summed(window, "gy")
        other = jnp.zeros_like(window)

    advanced = call(
        functools.partial(finish_kernel, planes),
        "advance",
        struct(species, row_count, depth),
        4,
        ANY,
        scratch=[
            pltpu.VMEM((row_count, rows, depth), F32),
            pltpu.SemaphoreType.DMA((planes,)),
        ],
        flops=1_000_000,
        moved=3_000_000,
    )(inner, dx, dy, dz)
    cond_means = call(means_kernel, "means", struct(species, per_device, NB), 2, VMEM)(
        window, other
    )
    return advanced.reshape(composition_matrix.shape), cond_means


def solution(mesh):
    in_specs = (
        P(None, "gx", "gy", "sec"),
        P("gx", "gy", "sec"),
        P("gx", "gy", "sec"),
        P(),
        P(),
        P("gx", "gy", "sec"),
        P(),
    )
    out_specs = (P(None, "gx", "gy", "sec"), P(None, "gx", None))
    return jax.shard_map(
        on_device, mesh=mesh, in_specs=in_specs, out_specs=out_specs, check_vma=False
    )
```

time: 106 us -> 33 us (0.31)
  blocking collectives: 23.7 us -> 0 us
  other arithmetic: 19.4 us -> 0.01 us
  local copies, waits for them, and re-layouts: 17.9 us -> 1.69 us
  waiting for transfers between devices: 18.6 us -> 5.92 us
  Pallas kernels: 0 us -> 9.67 us
  matrix products: 8.1 us -> 0 us
  starting transfers between devices: 17 us -> 14.7 us
    psum x1 -> x0, blocking collectives: 23.7 us -> none  [on_device(): summed = lax.psum(window, ('sec', 'gy'))]
    ppermute x7 -> x9, waiting for transfers between devices: 18.6 us -> 5.92 us  [the longest x2 2.97 us: summed(): lax.ppermute(block, axis, [(i, i ^ step) for i in range(count)])]
    pallas_call x0 -> x5, Pallas kernels: none -> 9.67 us  [the longest x1 4.34 us: on_device(): call(functools.partial(inner_kernel, planes), 'inside', [struct(row_count...]
    dot_general x3 -> x0, matrix products: 8.1 us -> none  [the longest x1 4.27 us: kinetic_source_term(): jnp.einsum('kj,jxyz->kxyz', kinetics_jacobian, central_voxels, precision=...]
    add x2 -> x3, other arithmetic: 7.8 us -> 0.01 us  [the longest x2 0.01 us: summed(): block + lax.ppermute(block, axis, [(i, i ^ step) for i in range(count)])]
    slice x3 -> x0, other arithmetic: 6.21 us -> none  [the longest x2 4.55 us: extended(): lax.slice_in_dim(cells, cells.shape[dim] - width, cells.shape[dim], axis=...]
    ppermute x3 -> x0, local copies, waits for them, and re-layouts: 5.95 us -> none  [the longest x2 3.51 us: extended(): lax.ppermute(head, axis, [((i + 1) % count, i) for i in range(ends)])]
    concatenate x2 -> x0, other arithmetic: 3.7 us -> none  [on_device(): jnp.concatenate([composition_matrix, local_mixing_coefficient[None]], axi...]
  transfers between devices with their start and end apart: 7 -> 9, of which waited for: 5 -> 4; matrix products, arithmetic and copies ran while one was open for 11% -> 0% of each run, Pallas kernels for 0% -> 19%
where the time goes in v1:
time: 33 us; the launch traced here: 32.7 us
  starting transfers between devices  14.7 us (45%)
  Pallas kernels  9.67 us (29%)
  waiting for transfers between devices  5.92 us (18%)
  local copies, waits for them, and re-layouts  1.69 us (5%)
  between operations  0.77 us (2%)
    ppermute x5, starting transfers between devices, swapped(): return lax.ppermute(block, axis, pairs)  5.96 us
    ppermute x1, starting transfers between devices, on_device(): passed = lax.ppermute(carry, 'gx', [(i, (i + 1) % gx) for i in range(gx)])  4.44 us
    pallas_call x1, Pallas kernels, on_device(): call(functools.partial(inner_kernel, planes), 'inside', [struct(row_count...  4.34 us
    ppermute x2, starting transfers between devices, summed(): lax.ppermute(block, axis, [(i, i ^ step) for i in range(count)])  3.73 us
    ppermute x2, waiting for transfers between devices, summed(): lax.ppermute(block, axis, [(i, i ^ step) for i in range(count)])  2.97 us
    pallas_call x1, Pallas kernels, on_device(): call(functools.partial(pack_kernel, planes, has_b), 'faces', [struct(row_...  1.95 us
    pallas_call x1, Pallas kernels, on_device(): call(functools.partial(finish_kernel, planes), 'advance', struct(species,...  1.89 us
    unnamed x12, local copies, waits for them, and re-layouts  1.69 us
  transfers between devices with their start and end apart: 9, of which 4 were waited for; matrix products, arithmetic and copies ran while one was open for 0% of the time, Pallas kernels for 19%

profile of v1, /device:TPU:0, one launch (start us, length us, event | category | flops | bytes accessed | tf_op | source)
XLA Modules:
  0.0 32.7 jit_solution(8043102489134011578)
XLA Ops:
  0.6 0.0 copy-start.4
  0.6 0.0 copy-start
  0.7 0.8 %copy-done = f32[8,16,128]{2,1,0:T(8,128)S(1)} copy-done((f32[8,16,128]{2,1,0:T(8,128)S(1)}, f32[8,16,128]{2,1,0:T(8,128)}, u32[]{:S(2)}) %copy-start) | copy-done | bytes 65560
  1.5 0.0 copy-start.1
  1.5 0.8 %copy-done.1 = s32[8,16,128]{2,1,0:T(8,128)S(1)} copy-done((s32[8,16,128]{2,1,0:T(8,128)S(1)}, s32[8,16,128]{2,1,0:T(8,128)}, u32[]{:S(2)}) %copy-start.1) | copy-done | bytes 65560
  2.3 0.0 copy-start.2
  2.3 0.0 copy-start.3
  2.3 0.0 copy-start.5
  2.3 2.0 %faces.1 = (f32[128,24,128]{2,1,0:T(8,128)S(1)}, f32[2,24,128]{2,1,0:T(8,128)S(1)}, f32[16,24,128]{2,1,0:T(8,128)S(1)}, f32[16,24,128]{2,1,0:T(8,128)S(1)}, f32[...) custom-call(f32[22,128,128]{2,1,0:T(8,128)} %bitcast.15, f32[128,128]{1,0:T(8,128)S(1)} %bitcast.7, ...), custom_call_target="tpu_custom_call" | custom-call | tf_op jit(solution)/shard_map/faces/pallas_call | solution.py:372
  4.3 3.1 %collective-permute-start = (f32[16,24,128]{2,1,0:T(8,128)S(1)}, f32[16,24,128]{2,1,0:T(8,128)S(1)}, u32[]{:S(2)}, u32[]{:S(2)}) collective-permute-start(f32[16,24,128]{2,1,0:T(8,128)S(1)} %get-tuple-element.20), channel_id=1, source_target_pairs={{0,2},{2,0},{4,6},{6,4},{1,3},{3,1},{5,7},{7,5},{8,10},{10,8},{12,... | collective-permute-start | bytes 589832 | tf_op jit(solution)/shard_map/ppermute | solution.py:329
  7.4 0.7 %collective-permute-start.1 = (f32[16,24,128]{2,1,0:T(8,128)S(1)}, f32[16,24,128]{2,1,0:T(8,128)S(1)}, u32[]{:S(2)}, u32[]{:S(2)}) collective-permute-start(f32[16,24,128]{2,1,0:T(8,128)S(1)} %get-tuple-element.21), channel_id=1, source_target_pairs={{2,4},{4,2},{3,5},{5,3},{10,12},{12,10},{11,13},{13,11},{18,20},{2... | collective-permute-start | bytes 589832 | tf_op jit(solution)/shard_map/ppermute | solution.py:329
  8.1 1.6 %collective-permute-start.2 = (f32[8,24,128]{2,1,0:T(8,128)S(1)}, f32[8,24,128]{2,1,0:T(8,128)S(1)}, u32[]{:S(2)}, u32[]{:S(2)}) collective-permute-start(f32[8,24,128]{2,1,0:T(8,128)S(1)} %get-tuple-element.22), channel_id=1, source_target_pairs={{0,1},{1,0},{2,3},{3,2},{4,5},{5,4},{6,7},{7,6},{8,9},{9,8},{10,11... | collective-permute-start | bytes 294920 | tf_op jit(solution)/shard_map/ppermute | solution.py:329
  9.6 0.0 collective-permute-start.3
  9.6 0.7 %collective-permute-start.4 = (f32[24,128]{1,0:T(8,128)S(1)}, f32[24,128]{1,0:T(8,128)S(1)}, u32[]{:S(2)}, u32[]{:S(2)}) collective-permute-start(f32[24,128]{1,0:T(8,128)S(1)} %get-tuple-element.24), channel_id=1, source_target_pairs={{8,16},{16,8},{9,17},{17,9},{10,18},{18,10},{11,19},{19,11},{12,20... | collective-permute-start | bytes 36872 | tf_op jit(solution)/shard_map/ppermute | solution.py:329
  10.3 0.0 copy-done.4
  10.3 0.0 copy-done.2
  10.3 0.0 copy-done.3
  10.3 4.3 %inside.1 = (f32[128,24,128]{2,1,0:T(8,128)S(1)}, f32[5,24,64]{2,1,0:T(8,128)S(1)}) custom-call(f32[128,24,128]{2,1,0:T(8,128)S(1)} %get-tuple-element.16.cells, f32[128,128]{1,0:T(8,128)S(1)} %bitcast.8, f32[128,128]{1,0:T(8,128)S(1)} %bitcast.10, f32[1,22]{1,0:T(1,128)S(1)} %bitcast.11, f32[22,22]{1,0:T(8,128)S(1)} %copy-done.3), custom_call_target="tpu_custom_call" | custom-call | flops 10000000 | bytes 4000000 | tf_op jit(solution)/shard_map/inside/pallas_call | solution.py:384
  14.6 0.0 collective-permute-done.3.refs_3_
  14.7 0.0 collective-permute-done.4.refs_4_
  14.7 0.0 collective-permute-done.2.refs_2_
  14.7 0.0 collective-permute-done.refs_0_
  14.7 0.0 collective-permute-done.1.refs_1_
  14.7 0.0 copy-done.5
  14.7 0.7 %edges.1 = (f32[2,24,128]{2,1,0:T(8,128)S(1)}, f32[2,24,128]{2,1,0:T(8,128)S(1)}, f32[2,16,24,128]{3,2,1,0:T(8,128)S(1)}, f32[2,8,24,128]{3,2,1,0:T(8,128)S(1)}, f32[2,24,128]{2,1,0:T(8,128)S(1)}) custom-call(f32[128,24,128]{2,1,0:T(8,128)S(1)} %get-tuple-element.16.cells, f32[2,24,128]{2,1,0:T(8,128)S(1)} %get-tuple-element.18.own_z, ...), custom_call_target="tpu_custom_call" | custom-call | tf_op jit(solution)/shard_map/edges/pallas_call | solution.py:398
  15.5 4.4 %collective-permute-start.5 = (f32[2,24,128]{2,1,0:T(8,128)S(1)}, f32[2,24,128]{2,1,0:T(8,128)S(1)}, u32[]{:S(2)}, u32[]{:S(2)}) collective-permute-start(f32[2,24,128]{2,1,0:T(8,128)S(1)} %get-tuple-element.29), channel_id=1, source_target_pairs={{0,2},{2,4},{4,6},{6,0},{1,3},{3,5},{5,7},{7,1},{8,10},{10,12},{12... | collective-permute-start | bytes 73736 | tf_op jit(solution)/shard_map/ppermute | solution.py:414
  19.9 1.5 %collective-permute-done.5 = f32[2,24,128]{2,1,0:T(8,128)S(1)} collective-permute-done((f32[2,24,128]{2,1,0:T(8,128)S(1)}, f32[2,24,128]{2,1,0:T(8,128)S(1)}, u32[]{:S(2)}, u32[]{:S(2)}) %collective-permute-start.5) | collective-permute-done | bytes 24608 | tf_op jit(solution)/shard_map/ppermute | solution.py:414
  21.4 2.0 %collective-permute-start.6 = (f32[2,24,128]{2,1,0:T(8,128)S(1)}, f32[2,24,128]{2,1,0:T(8,128)S(1)}, u32[]{:S(2)}, u32[]{:S(2)}) collective-permute-start(f32[2,24,128]{2,1,0:T(8,128)S(1)} %add.9), channel_id=1, source_target_pairs={{0,8},{8,0},{16,24},{24,16},{1,9},{9,1},{17,25},{25,17},{2,10},{10... | collective-permute-start | bytes 73736 | tf_op jit(solution)/shard_map/ppermute | solution.py:338
  23.5 0.8 %collective-permute-done.6 = f32[2,24,128]{2,1,0:T(8,128)S(1)} collective-permute-done((f32[2,24,128]{2,1,0:T(8,128)S(1)}, f32[2,24,128]{2,1,0:T(8,128)S(1)}, u32[]{:S(2)}, u32[]{:S(2)}) %collective-permute-start.6) | collective-permute-done | bytes 24608 | tf_op jit(solution)/shard_map/ppermute | solution.py:338
  24.3 1.7 %collective-permute-start.7 = (f32[2,24,128]{2,1,0:T(8,128)S(1)}, f32[2,24,128]{2,1,0:T(8,128)S(1)}, u32[]{:S(2)}, u32[]{:S(2)}) collective-permute-start(f32[2,24,128]{2,1,0:T(8,128)S(1)} %add.10), channel_id=1, source_target_pairs={{0,16},{8,24},{16,0},{24,8},{1,17},{9,25},{17,1},{25,9},{2,18},{10... | collective-permute-start | bytes 73736 | tf_op jit(solution)/shard_map/ppermute | solution.py:338
  26.0 2.1 %collective-permute-done.7 = f32[2,24,128]{2,1,0:T(8,128)S(1)} collective-permute-done((f32[2,24,128]{2,1,0:T(8,128)S(1)}, f32[2,24,128]{2,1,0:T(8,128)S(1)}, u32[]{:S(2)}, u32[]{:S(2)}) %collective-permute-start.7) | collective-permute-done | bytes 24608 | tf_op jit(solution)/shard_map/ppermute | solution.py:338
  28.2 0.5 %collective-permute-start.8 = (f32[2,24,128]{2,1,0:T(8,128)S(1)}, f32[2,24,128]{2,1,0:T(8,128)S(1)}, u32[]{:S(2)}, u32[]{:S(2)}) collective-permute-start(f32[2,24,128]{2,1,0:T(8,128)S(1)} %add.11.first), channel_id=1, source_target_pairs={{0,1},{1,0},{2,3},{3,2},{4,5},{5,4},{6,7},{7,6},{8,9},{9,8},{10,11... | collective-permute-start | bytes 73736 | tf_op jit(solution)/shard_map/ppermute | solution.py:419
  28.7 1.9 %advance.1 = f32[22,128,128]{2,1,0:T(8,128)} custom-call(f32[128,24,128]{2,1,0:T(8,128)S(1)} %get-tuple-element.17.advanced, f32[2,16,24,128]{3,2,1,0:T(8,128)S(1)} %get-tuple-element.25.dx, f32[2,8,24,128]{3,2,1,0:T(8,128)S(1)} %get-tuple-element.26.dy, f32[2,24,128]{2,1,0:T(8,128)S(1)} %get-tuple-element.27.dz), custom_call_target="tpu_custom_call" | custom-call | flops 1000000 | bytes 3000000 | tf_op jit(solution)/shard_map/advance/pallas_call | solution.py:424
  30.6 1.4 %collective-permute-done.8.second = f32[2,24,128]{2,1,0:T(8,128)S(1)} collective-permute-done((f32[2,24,128]{2,1,0:T(8,128)S(1)}, f32[2,24,128]{2,1,0:T(8,128)S(1)}, u32[]{:S(2)}, u32[]{:S(2)}) %collective-permute-start.8) | collective-permute-done | bytes 24608 | tf_op jit(solution)/shard_map/ppermute | solution.py:419
  32.0 0.7 %means.1 = f32[22,4,64]{2,1,0:T(4,128)} custom-call(f32[2,24,128]{2,1,0:T(8,128)S(1)} %add.11.first, f32[2,24,128]{2,1,0:T(8,128)S(1)} %collective-permute-done.8.second), custom_call_target="tpu_custom_call" | custom-call | tf_op jit(solution)/shard_map/means/pallas_call | solution.py:437
  (3 shorter events, 0.0 us)
Async XLA Ops:
  0.6 9.6 %copy-start.4 = (f32[22]{0:T(128)S(1)}, f32[22]{0:T(128)}, u32[]{:S(2)}) copy-start(f32[22]{0:T(128)} %param.10) | copy-start | bytes 268
  0.6 0.8 %copy-start = (f32[8,16,128]{2,1,0:T(8,128)S(1)}, f32[8,16,128]{2,1,0:T(8,128)}, u32[]{:S(2)}) copy-start(f32[8,16,128]{2,1,0:T(8,128)} %param.8) | copy-start | bytes 196612
  1.5 0.8 %copy-start.1 = (s32[8,16,128]{2,1,0:T(8,128)S(1)}, s32[8,16,128]{2,1,0:T(8,128)}, u32[]{:S(2)}) copy-start(s32[8,16,128]{2,1,0:T(8,128)} %param.12) | copy-start | bytes 196612
  2.3 8.0 %copy-start.2 = (f32[8,16,128]{2,1,0:T(8,128)S(1)}, f32[8,16,128]{2,1,0:T(8,128)}, u32[]{:S(2)}) copy-start(f32[8,16,128]{2,1,0:T(8,128)} %param.9) | copy-start | bytes 196612
  2.3 8.0 %copy-start.3 = (f32[22,22]{1,0:T(8,128)S(1)}, f32[22,22]{1,0:T(8,128)}, u32[]{:S(2)}) copy-start(f32[22,22]{1,0:T(8,128)} %jacobian.1) | copy-start | bytes 5812
  2.3 12.4 %copy-start.5 = (s32[32]{0:T(128)S(1)}, s32[32]{0:T(128)}, u32[]{:S(2)}) copy-start(s32[32]{0:T(128)} %param.13) | copy-start | bytes 388
  4.3 10.4 %collective-permute-start = (f32[16,24,128]{2,1,0:T(8,128)S(1)}, f32[16,24,128]{2,1,0:T(8,128)S(1)}, u32[]{:S(2)}, u32[]{:S(2)}) collective-permute-start(f32[16,24,128]{2,1,0:T(8,128)S(1)} %get-tuple-element.20), channel_id=1, source_target_pairs={{0,2},{2,0},{4,6},{6,4},{1,3},{3,1},{5,7},{7,5},{8,10},{10,8},{12,... | collective-permute-start | bytes 589832 | tf_op jit(solution)/shard_map/ppermute | solution.py:329
  7.4 7.3 %collective-permute-start.1 = (f32[16,24,128]{2,1,0:T(8,128)S(1)}, f32[16,24,128]{2,1,0:T(8,128)S(1)}, u32[]{:S(2)}, u32[]{:S(2)}) collective-permute-start(f32[16,24,128]{2,1,0:T(8,128)S(1)} %get-tuple-element.21), channel_id=1, source_target_pairs={{2,4},{4,2},{3,5},{5,3},{10,12},{12,10},{11,13},{13,11},{18,20},{2... | collective-permute-start | bytes 589832 | tf_op jit(solution)/shard_map/ppermute | solution.py:329
  8.1 6.6 %collective-permute-start.2 = (f32[8,24,128]{2,1,0:T(8,128)S(1)}, f32[8,24,128]{2,1,0:T(8,128)S(1)}, u32[]{:S(2)}, u32[]{:S(2)}) collective-permute-start(f32[8,24,128]{2,1,0:T(8,128)S(1)} %get-tuple-element.22), channel_id=1, source_target_pairs={{0,1},{1,0},{2,3},{3,2},{4,5},{5,4},{6,7},{7,6},{8,9},{9,8},{10,11... | collective-permute-start | bytes 294920 | tf_op jit(solution)/shard_map/ppermute | solution.py:329
  9.6 5.1 %collective-permute-start.3 = (f32[24,128]{1,0:T(8,128)S(1)}, f32[24,128]{1,0:T(8,128)S(1)}, u32[]{:S(2)}, u32[]{:S(2)}) collective-permute-start(f32[24,128]{1,0:T(8,128)S(1)} %get-tuple-element.23), channel_id=1, source_target_pairs={{0,8},{8,0},{16,24},{24,16},{1,9},{9,1},{17,25},{25,17},{2,10},{10... | collective-permute-start | bytes 36872 | tf_op jit(solution)/shard_map/ppermute | solution.py:329
  9.6 5.1 %collective-permute-start.4 = (f32[24,128]{1,0:T(8,128)S(1)}, f32[24,128]{1,0:T(8,128)S(1)}, u32[]{:S(2)}, u32[]{:S(2)}) collective-permute-start(f32[24,128]{1,0:T(8,128)S(1)} %get-tuple-element.24), channel_id=1, source_target_pairs={{8,16},{16,8},{9,17},{17,9},{10,18},{18,10},{11,19},{19,11},{12,20... | collective-permute-start | bytes 36872 | tf_op jit(solution)/shard_map/ppermute | solution.py:329
  15.5 6.0 %collective-permute-start.5 = (f32[2,24,128]{2,1,0:T(8,128)S(1)}, f32[2,24,128]{2,1,0:T(8,128)S(1)}, u32[]{:S(2)}, u32[]{:S(2)}) collective-permute-start(f32[2,24,128]{2,1,0:T(8,128)S(1)} %get-tuple-element.29), channel_id=1, source_target_pairs={{0,2},{2,4},{4,6},{6,0},{1,3},{3,5},{5,7},{7,1},{8,10},{10,12},{12... | collective-permute-start | bytes 73736 | tf_op jit(solution)/shard_map/ppermute | solution.py:414
  21.4 2.9 %collective-permute-start.6 = (f32[2,24,128]{2,1,0:T(8,128)S(1)}, f32[2,24,128]{2,1,0:T(8,128)S(1)}, u32[]{:S(2)}, u32[]{:S(2)}) collective-permute-start(f32[2,24,128]{2,1,0:T(8,128)S(1)} %add.9), channel_id=1, source_target_pairs={{0,8},{8,0},{16,24},{24,16},{1,9},{9,1},{17,25},{25,17},{2,10},{10... | collective-permute-start | bytes 73736 | tf_op jit(solution)/shard_map/ppermute | solution.py:338
  24.3 3.8 %collective-permute-start.7 = (f32[2,24,128]{2,1,0:T(8,128)S(1)}, f32[2,24,128]{2,1,0:T(8,128)S(1)}, u32[]{:S(2)}, u32[]{:S(2)}) collective-permute-start(f32[2,24,128]{2,1,0:T(8,128)S(1)} %add.10), channel_id=1, source_target_pairs={{0,16},{8,24},{16,0},{24,8},{1,17},{9,25},{17,1},{25,9},{2,18},{10... | collective-permute-start | bytes 73736 | tf_op jit(solution)/shard_map/ppermute | solution.py:338
  28.2 3.8 %collective-permute-start.8 = (f32[2,24,128]{2,1,0:T(8,128)S(1)}, f32[2,24,128]{2,1,0:T(8,128)S(1)}, u32[]{:S(2)}, u32[]{:S(2)}) collective-permute-start(f32[2,24,128]{2,1,0:T(8,128)S(1)} %add.11.first), channel_id=1, source_target_pairs={{0,1},{1,0},{2,3},{3,2},{4,5},{5,4},{6,7},{7,6},{8,9},{9,8},{10,11... | collective-permute-start | bytes 73736 | tf_op jit(solution)/shard_map/ppermute | solution.py:419

commit v2 on v1

--- a/solution.py
+++ b/solution.py
@@ -55,7 +55,7 @@
 
 
 def pack_kernel(planes, has_b, cells, mixing, classes, *refs):
-    outs, sem = refs[:-1], refs[-1]
+    outs, (bins, sem, field_sem) = refs[:-3], refs[-3:]
     rows_out, own_z = outs[0], outs[1]
     faces = list(outs[2:])
     species, row_count, depth = cells.shape
@@ -66,10 +66,17 @@
             pltpu.make_async_copy(
                 cells.at[k, span], rows_out.at[span, k, :], sem.at[plane]
             ).start()
+    field_copies = [
+        pltpu.make_async_copy(mixing, rows_out.at[:, species, :], field_sem.at[0]),
+        pltpu.make_async_copy(classes, bins, field_sem.at[1]),
+    ]
+    for copy in field_copies:
+        copy.start()
+    for copy in field_copies:
+        copy.wait()
     for r in range(0, row_count, SUBLANES):
         span = pl.ds(r, SUBLANES)
-        rows_out[span, species, :] = mixing[span, :]
-        rows_out[span, species + 1, :] = classes[span, :].astype(F32)
+        rows_out[span, species + 1, :] = bins[span, :].astype(F32)
     shape = rows_out.shape[1:]
     lane = lanes_of(shape)
     low = jnp.zeros(shape, F32)
@@ -144,11 +151,10 @@
     ones = rows_of((rows, depth)) >= species
     station_sums[...] = jnp.zeros_like(station_sums)
 
-    @pl.loop(0, planes)
-    def _(x):
+    for x in range(planes):
         base = x * width
-        below = jnp.maximum(x - 1, 0) * width
-        above = jnp.minimum(x + 1, planes - 1) * width
+        below = max(x - 1, 0) * width
+        above = min(x + 1, planes - 1) * width
         made = jnp.zeros((2 * rows, NB), F32)
         for first in range(0, width, 2):
             pair = (first, first + 1)
@@ -171,8 +177,10 @@
                     flux += at(2) * cells[r + 1]
                 if y > 0:
                     flux += at(3) * cells[r - 1]
-                flux += at(4) * cells[above + y]
-                flux += at(5) * cells[below + y]
+                if x < planes - 1:
+                    flux += at(4) * cells[above + y]
+                if x > 0:
+                    flux += at(5) * cells[below + y]
                 flux -= at(6) * c
                 new = c + weight * flux + at(7) * mixed[:, i * depth : (i + 1) * depth]
                 new = jnp.where(ones, 1.0, new)
@@ -185,7 +193,7 @@
 
 def edge_kernel(planes, has_b, cells, own_z, sums, weights, positions, *refs):
     halos = list(refs[: 3 + sum(has_b)])
-    own, carry, dx, dy, dz, station_sums = refs[3 + sum(has_b) :]
+    window, dx, dy, dz, station_sums = refs[3 + sum(has_b) :]
     row_count, rows, depth = cells.shape
     species = weights.shape[1]
     width = row_count // planes
@@ -243,16 +251,15 @@
             station_sums[j] += folded(binned(value, jnp.where(station == j, classes, -1.0)))
     shift = jnp.broadcast_to(positions[0:1, 0:1], (rows, NB))
     per_device = planes // 2
-    for half, out in enumerate((own, carry)):
-        for s in range(0, per_device, 2):
-            parts = []
-            for slot in (half * per_device + s, half * per_device + s + 1):
-                part = jnp.zeros((rows, NB), F32)
-                for j in range(stations):
-                    if 0 <= slot - j < per_device:
-                        part += jnp.where(shift == slot - j, station_sums[j], 0.0)
-                parts.append(part)
-            out[s // 2] = jnp.concatenate(parts, axis=1)
+    for s in range(0, 2 * per_device, 2):
+        parts = []
+        for slot in (s, s + 1):
+            part = jnp.zeros((rows, NB), F32)
+            for j in range(stations):
+                if 0 <= slot - j < per_device:
+                    part += jnp.where(shift == slot - j, station_sums[j], 0.0)
+            parts.append(part)
+        window[s // 2] = jnp.concatenate(parts, axis=1)
 
 
 def finish_kernel(planes, advanced, dx, dy, dz, out, total, sem):
@@ -295,10 +302,11 @@
         ).wait()
 
 
-def means_kernel(first, second, out):
+def means_kernel(own, received, out):
     species, per_device, bins = out.shape
+    even = lax.axis_index("sec") % 2 == 0
     for s in range(0, per_device, 2):
-        block = first[s // 2] + second[s // 2]
+        block = jnp.where(jnp.broadcast_to(even, own.shape[1:]), received[s // 2], own[s // 2])
         means = block / jnp.maximum(block[species + 1 : species + 2], 1.0)
         out[:, s, :] = means[:species, :bins]
         out[:, s + 1, :] = means[:species, bins:]
@@ -329,15 +337,29 @@
     return lax.ppermute(block, axis, pairs)
 
 
-def summed(block, axis):
+def on_odd(block, axis, move):
+    deep = lax.axis_size("sec")
     count = lax.axis_size(axis)
-    if count & (count - 1):
-        return lax.psum(block, axis)
+    if axis == "sec":
+        return lax.ppermute(block, axis, [(i, move(i)) for i in range(1, deep, 2)])
+    pairs = [(s * count + i, s * count + move(i)) for s in range(1, deep, 2) for i in range(count)]
+    return lax.ppermute(block, ("sec", axis), pairs)
+
+
+def summed(block):
+    deep, gx, gy = (lax.axis_size(axis) for axis in ("sec", "gx", "gy"))
+    half = block.shape[0] // 2
+    block = block + lax.ppermute(block, "sec", [(i, i + 1) for i in range(0, deep, 2)])
+    block = block[:half] + on_odd(block[half:], "gx", lambda i: (i + 1) % gx)
+    step = 2
+    while step < deep:
+        block = block + on_odd(block, "sec", lambda i: i ^ step)
+        step *= 2
     step = 1
-    while step < count:
-        block = block + lax.ppermute(block, axis, [(i, i ^ step) for i in range(count)])
+    while step < gy:
+        block = block + on_odd(block, "gy", lambda i: i ^ step)
         step *= 2
-    return block
+    return block, lax.ppermute(block, "sec", [(i + 1, i) for i in range(0, deep, 2)])
 
 
 def on_device(
@@ -368,16 +390,19 @@
     ]
     face_shapes = [struct(*shapes[axis]) for axis, _ in sides]
 
-    cells = pltpu.with_memory_space_constraint(cells, pltpu.HBM)
     packed = call(
         functools.partial(pack_kernel, planes, has_b),
         "faces",
         [struct(row_count, rows, depth), struct(2, rows, row_count), *face_shapes],
         3,
         [VMEM] * (2 + len(sides)),
-        in_specs=[ANY, VMEM, VMEM],
-        scratch=[pltpu.SemaphoreType.DMA((planes,))],
-    )(cells, mixing, classes)
+        in_specs=[ANY] * 3,
+        scratch=[
+            pltpu.VMEM((row_count, depth), jnp.int32),
+            pltpu.SemaphoreType.DMA((planes,)),
+            pltpu.SemaphoreType.DMA((2,)),
+        ],
+    )(*[pltpu.with_memory_space_constraint(x, pltpu.HBM) for x in (cells, mixing, classes)])
     rows_in, own_z, faces = packed[0], packed[1], packed[2:]
     halos = [swapped(face, axis, side) for face, (axis, side) in zip(faces, sides)]
 
@@ -395,32 +420,21 @@
         moved=4_000_000,
     )(rows_in, mixing, thermal, weights, kinetics_jacobian)
 
-    own, carry, dx, dy, dz = call(
+    window, dx, dy, dz = call(
         functools.partial(edge_kernel, planes, has_b),
         "edges",
         [
-            struct(per_device // 2, rows, 2 * NB),
-            struct(per_device // 2, rows, 2 * NB),
+            struct(per_device, rows, 2 * NB),
             struct(2, width, rows, depth),
             struct(2, planes, rows, depth),
             struct(2, rows, row_count),
         ],
         5 + len(halos),
-        [VMEM] * 5,
+        [VMEM] * 4,
         scratch=[pltpu.VMEM((per_device + 1, rows, NB), F32)],
     )(rows_in, own_z, sums, weights, positions, *halos)
 
-    gx = lax.axis_size("gx")
-    passed = lax.ppermute(carry, "gx", [(i, (i + 1) % gx) for i in range(gx)])
-    window = own + passed
-    window = summed(window, "sec")
-    gy = lax.axis_size("gy")
-    if gy == 2:
-        other = lax.ppermute(window, "gy", [(0, 1), (1, 0)])
-    else:
-        window = summed(window, "gy")
-        other = jnp.zeros_like(window)
-
+    own, received = summed(window)
     advanced = call(
         functools.partial(finish_kernel, planes),
         "advance",
@@ -435,7 +449,7 @@
         moved=3_000_000,
     )(inner, dx, dy, dz)
     cond_means = call(means_kernel, "means", struct(species, per_device, NB), 2, VMEM)(
-        window, other
+        own, received
     )
     return advanced.reshape(composition_matrix.shape), cond_means
 

time: 33 us -> 38.8 us (1.18)
  the two profiles are of different devices: /device:TPU:0 before, /device:TPU:1 now
where the time goes in v2:
time: 38.8 us; the launch traced here: 38.5 us
  starting transfers between devices  21 us (54%)
  Pallas kernels  8.77 us (23%)
  waiting for transfers between devices  7.82 us (20%)
  between operations  0.85 us (2%)
    ppermute x5, starting transfers between devices, swapped(): return lax.ppermute(block, axis, pairs)  8.39 us
    ppermute x2, starting transfers between devices, on_odd(): return lax.ppermute(block, ('sec', axis), pairs)  8.17 us
    ppermute x2, waiting for transfers between devices, on_odd(): return lax.ppermute(block, ('sec', axis), pairs)  3.32 us
    pallas_call x1, Pallas kernels, on_device(): call(functools.partial(pack_kernel, planes, has_b), 'faces', [struct(row_...  2.82 us
    ppermute x1, waiting for transfers between devices, on_odd(): return lax.ppermute(block, axis, [(i, move(i)) for i in range(1, deep, 2)])  2.64 us
    pallas_call x1, Pallas kernels, on_device(): call(functools.partial(inner_kernel, planes), 'inside', [struct(row_count...  2.54 us
    ppermute x1, starting transfers between devices, on_odd(): return lax.ppermute(block, axis, [(i, move(i)) for i in range(1, deep, 2)])  1.91 us
    pallas_call x1, Pallas kernels, on_device(): call(functools.partial(finish_kernel, planes), 'advance', struct(species,...  1.9 us
  transfers between devices with their start and end apart: 10, of which 4 were waited for; matrix products, arithmetic and copies ran while one was open for 0% of the time, Pallas kernels for 12%

profile of v2, /device:TPU:1, one launch (start us, length us, event | category | flops | bytes accessed | tf_op | source)
XLA Modules:
  0.0 38.5 jit_solution(9077938320096636767)
XLA Ops:
  0.6 0.0 copy-start
  0.6 0.0 copy-start.1
  0.7 0.0 copy-start.3
  0.7 0.0 copy-start.2
  0.7 0.0 copy-start.4
  0.7 2.8 %faces.1 = (f32[128,24,128]{2,1,0:T(8,128)S(1)}, f32[2,24,128]{2,1,0:T(8,128)S(1)}, f32[16,24,128]{2,1,0:T(8,128)S(1)}, f32[16,24,128]{2,1,0:T(8,128)S(1)}, f32[...) custom-call(f32[22,128,128]{2,1,0:T(8,128)} %bitcast.14, f32[128,128]{1,0:T(8,128)} %bitcast.7, ...), custom_call_target="tpu_custom_call" | custom-call | tf_op jit(solution)/shard_map/faces/pallas_call | solution.py:393
  3.5 2.2 %collective-permute-start = (f32[16,24,128]{2,1,0:T(8,128)S(1)}, f32[16,24,128]{2,1,0:T(8,128)S(1)}, u32[]{:S(2)}, u32[]{:S(2)}) collective-permute-start(f32[16,24,128]{2,1,0:T(8,128)S(1)} %get-tuple-element.19), channel_id=1, source_target_pairs={{0,2},{2,0},{4,6},{6,4},{1,3},{3,1},{5,7},{7,5},{8,10},{10,8},{12,... | collective-permute-start | bytes 589832 | tf_op jit(solution)/shard_map/ppermute | solution.py:337
  5.7 0.7 %collective-permute-start.1 = (f32[16,24,128]{2,1,0:T(8,128)S(1)}, f32[16,24,128]{2,1,0:T(8,128)S(1)}, u32[]{:S(2)}, u32[]{:S(2)}) collective-permute-start(f32[16,24,128]{2,1,0:T(8,128)S(1)} %get-tuple-element.20), channel_id=1, source_target_pairs={{2,4},{4,2},{3,5},{5,3},{10,12},{12,10},{11,13},{13,11},{18,20},{2... | collective-permute-start | bytes 589832 | tf_op jit(solution)/shard_map/ppermute | solution.py:337
  6.4 1.3 %collective-permute-start.2 = (f32[8,24,128]{2,1,0:T(8,128)S(1)}, f32[8,24,128]{2,1,0:T(8,128)S(1)}, u32[]{:S(2)}, u32[]{:S(2)}) collective-permute-start(f32[8,24,128]{2,1,0:T(8,128)S(1)} %get-tuple-element.21), channel_id=1, source_target_pairs={{0,1},{1,0},{2,3},{3,2},{4,5},{5,4},{6,7},{7,6},{8,9},{9,8},{10,11... | collective-permute-start | bytes 294920 | tf_op jit(solution)/shard_map/ppermute | solution.py:337
  7.6 1.2 %collective-permute-start.3 = (f32[24,128]{1,0:T(8,128)S(1)}, f32[24,128]{1,0:T(8,128)S(1)}, u32[]{:S(2)}, u32[]{:S(2)}) collective-permute-start(f32[24,128]{1,0:T(8,128)S(1)} %get-tuple-element.22), channel_id=1, source_target_pairs={{0,8},{8,0},{16,24},{24,16},{1,9},{9,1},{17,25},{25,17},{2,10},{10... | collective-permute-start | bytes 36872 | tf_op jit(solution)/shard_map/ppermute | solution.py:337
  8.9 3.0 %collective-permute-start.4 = (f32[24,128]{1,0:T(8,128)S(1)}, f32[24,128]{1,0:T(8,128)S(1)}, u32[]{:S(2)}, u32[]{:S(2)}) collective-permute-start(f32[24,128]{1,0:T(8,128)S(1)} %get-tuple-element.23), channel_id=1, source_target_pairs={{8,16},{16,8},{9,17},{17,9},{10,18},{18,10},{11,19},{19,11},{12,20... | collective-permute-start | bytes 36872 | tf_op jit(solution)/shard_map/ppermute | solution.py:337
  11.9 0.0 copy-done
  11.9 0.0 copy-done.1
  11.9 0.0 copy-done.3
  11.9 0.0 copy-done.2
  12.0 2.5 %inside.1 = (f32[128,24,128]{2,1,0:T(8,128)S(1)}, f32[5,24,64]{2,1,0:T(8,128)S(1)}) custom-call(f32[128,24,128]{2,1,0:T(8,128)S(1)} %get-tuple-element.15.cells, f32[128,128]{1,0:T(8,128)S(1)} %bitcast.8, f32[128,128]{1,0:T(8,128)S(1)} %bitcast.9, f32[1,22]{1,0:T(1,128)S(1)} %bitcast.10, f32[22,22]{1,0:T(8,128)S(1)} %copy-done.2), custom_call_target="tpu_custom_call" | custom-call | flops 10000000 | bytes 4000000 | tf_op jit(solution)/shard_map/inside/pallas_call | solution.py:409
  14.5 0.0 collective-permute-done.3.refs_3_
  14.5 0.0 collective-permute-done.4.refs_4_
  14.5 0.0 collective-permute-done.2.refs_2_
  14.6 0.0 collective-permute-done.refs_0_
  14.6 0.0 collective-permute-done.1.refs_1_
  14.6 0.0 copy-done.4
  14.6 0.7 %edges.1 = (f32[4,24,128]{2,1,0:T(8,128)S(1)}, f32[2,16,24,128]{3,2,1,0:T(8,128)S(1)}, f32[2,8,24,128]{3,2,1,0:T(8,128)S(1)}, f32[2,24,128]{2,1,0:T(8,128)S(1)}) custom-call(f32[128,24,128]{2,1,0:T(8,128)S(1)} %get-tuple-element.15.cells, f32[2,24,128]{2,1,0:T(8,128)S(1)} %get-tuple-element.17.own_z, f32[5,24,64]{2,1,0:T(8,128)S(1)} %get-tuple-element.18.sums, ...), custom_call_target="tpu_custom_call" | custom-call | tf_op jit(solution)/shard_map/edges/pallas_call | solution.py:423
  15.3 1.3 %collective-permute-start.5 = (f32[4,24,128]{2,1,0:T(8,128)S(1)}, f32[4,24,128]{2,1,0:T(8,128)S(1)}, u32[]{:S(2)}, u32[]{:S(2)}) collective-permute-start(f32[4,24,128]{2,1,0:T(8,128)S(1)} %get-tuple-element.27), channel_id=1, source_target_pairs={{0,8},{16,24},{1,9},{17,25},{2,10},{18,26},{3,11},{19,27},{4,12},{... | collective-permute-start | bytes 147464 | tf_op jit(solution)/shard_map/ppermute | solution.py:352
  16.6 1.8 %collective-permute-done.5 = f32[4,24,128]{2,1,0:T(8,128)S(1)} collective-permute-done((f32[4,24,128]{2,1,0:T(8,128)S(1)}, f32[4,24,128]{2,1,0:T(8,128)S(1)}, u32[]{:S(2)}, u32[]{:S(2)}) %collective-permute-start.5) | collective-permute-done | bytes 49184 | tf_op jit(solution)/shard_map/ppermute | solution.py:352
  18.5 6.0 %collective-permute-start.6 = (f32[2,24,128]{2,1,0:T(8,128)S(1)}, f32[2,24,128]{2,1,0:T(8,128)S(1)}, u32[]{:S(2)}, u32[]{:S(2)}) collective-permute-start(f32[2,24,128]{2,1,0:T(8,128)S(1)} %slice.9), channel_id=1, source_target_pairs={{8,10},{10,12},{12,14},{14,8},{24,26},{26,28},{28,30},{30,24},{9,1... | collective-permute-start | bytes 73736 | tf_op jit(solution)/shard_map/ppermute | solution.py:346
  24.5 0.9 %collective-permute-done.6 = f32[2,24,128]{2,1,0:T(8,128)S(1)} collective-permute-done((f32[2,24,128]{2,1,0:T(8,128)S(1)}, f32[2,24,128]{2,1,0:T(8,128)S(1)}, u32[]{:S(2)}, u32[]{:S(2)}) %collective-permute-start.6) | collective-permute-done | bytes 24608 | tf_op jit(solution)/shard_map/ppermute | solution.py:346
  25.4 1.9 %collective-permute-start.7 = (f32[2,24,128]{2,1,0:T(8,128)S(1)}, f32[2,24,128]{2,1,0:T(8,128)S(1)}, u32[]{:S(2)}, u32[]{:S(2)}) collective-permute-start(f32[2,24,128]{2,1,0:T(8,128)S(1)} %slice_add_fusion), channel_id=1, source_target_pairs={{8,24},{24,8},{9,25},{25,9},{10,26},{26,10},{11,27},{27,11},{12,28... | collective-permute-start | bytes 73736 | tf_op jit(solution)/shard_map/ppermute | solution.py:344
  27.3 2.6 %collective-permute-done.7 = f32[2,24,128]{2,1,0:T(8,128)S(1)} collective-permute-done((f32[2,24,128]{2,1,0:T(8,128)S(1)}, f32[2,24,128]{2,1,0:T(8,128)S(1)}, u32[]{:S(2)}, u32[]{:S(2)}) %collective-permute-start.7) | collective-permute-done | bytes 24608 | tf_op jit(solution)/shard_map/ppermute | solution.py:344
  30.0 2.2 %collective-permute-start.8 = (f32[2,24,128]{2,1,0:T(8,128)S(1)}, f32[2,24,128]{2,1,0:T(8,128)S(1)}, u32[]{:S(2)}, u32[]{:S(2)}) collective-permute-start(f32[2,24,128]{2,1,0:T(8,128)S(1)} %add.14), channel_id=1, source_target_pairs={{8,9},{9,8},{24,25},{25,24},{10,11},{11,10},{26,27},{27,26},{12,13... | collective-permute-start | bytes 73736 | tf_op jit(solution)/shard_map/ppermute | solution.py:346
  32.2 2.4 %collective-permute-done.8 = f32[2,24,128]{2,1,0:T(8,128)S(1)} collective-permute-done((f32[2,24,128]{2,1,0:T(8,128)S(1)}, f32[2,24,128]{2,1,0:T(8,128)S(1)}, u32[]{:S(2)}, u32[]{:S(2)}) %collective-permute-start.8) | collective-permute-done | bytes 24608 | tf_op jit(solution)/shard_map/ppermute | solution.py:346
  34.6 1.3 %collective-permute-start.9 = (f32[2,24,128]{2,1,0:T(8,128)S(1)}, f32[2,24,128]{2,1,0:T(8,128)S(1)}, u32[]{:S(2)}, u32[]{:S(2)}) collective-permute-start(f32[2,24,128]{2,1,0:T(8,128)S(1)} %add.15.own), channel_id=1, source_target_pairs={{8,0},{24,16},{9,1},{25,17},{10,2},{26,18},{11,3},{27,19},{12,4},{... | collective-permute-start | bytes 73736 | tf_op jit(solution)/shard_map/ppermute | solution.py:362
  35.9 1.9 %advance.1 = f32[22,128,128]{2,1,0:T(8,128)} custom-call(f32[128,24,128]{2,1,0:T(8,128)S(1)} %get-tuple-element.16.advanced, f32[2,16,24,128]{3,2,1,0:T(8,128)S(1)} %get-tuple-element.24.dx, f32[2,8,24,128]{3,2,1,0:T(8,128)S(1)} %get-tuple-element.25.dy, f32[2,24,128]{2,1,0:T(8,128)S(1)} %get-tuple-element.26.dz), custom_call_target="tpu_custom_call" | custom-call | flops 1000000 | bytes 3000000 | tf_op jit(solution)/shard_map/advance/pallas_call | solution.py:438
  37.8 0.0 collective-permute-done.9.received
  37.8 0.8 %means.1 = f32[22,4,64]{2,1,0:T(4,128)} custom-call(f32[2,24,128]{2,1,0:T(8,128)S(1)} %add.15.own, f32[2,24,128]{2,1,0:T(8,128)S(1)} %collective-permute-done.9.received), custom_call_target="tpu_custom_call" | custom-call | tf_op jit(solution)/shard_map/means/pallas_call | solution.py:451
  (5 shorter events, 0.0 us)
Async XLA Ops:
  0.6 11.3 %copy-start = (f32[8,16,128]{2,1,0:T(8,128)S(1)}, f32[8,16,128]{2,1,0:T(8,128)}, u32[]{:S(2)}) copy-start(f32[8,16,128]{2,1,0:T(8,128)} %param.8) | copy-start | bytes 196612
  0.6 11.3 %copy-start.1 = (f32[8,16,128]{2,1,0:T(8,128)S(1)}, f32[8,16,128]{2,1,0:T(8,128)}, u32[]{:S(2)}) copy-start(f32[8,16,128]{2,1,0:T(8,128)} %param.9) | copy-start | bytes 196612
  0.7 11.3 %copy-start.3 = (f32[22]{0:T(128)S(1)}, f32[22]{0:T(128)}, u32[]{:S(2)}) copy-start(f32[22]{0:T(128)} %param.10) | copy-start | bytes 268
  0.7 11.3 %copy-start.2 = (f32[22,22]{1,0:T(8,128)S(1)}, f32[22,22]{1,0:T(8,128)}, u32[]{:S(2)}) copy-start(f32[22,22]{1,0:T(8,128)} %jacobian.1) | copy-start | bytes 5812
  0.7 13.9 %copy-start.4 = (s32[32]{0:T(128)S(1)}, s32[32]{0:T(128)}, u32[]{:S(2)}) copy-start(s32[32]{0:T(128)} %param.13) | copy-start | bytes 388
  3.5 11.0 %collective-permute-start = (f32[16,24,128]{2,1,0:T(8,128)S(1)}, f32[16,24,128]{2,1,0:T(8,128)S(1)}, u32[]{:S(2)}, u32[]{:S(2)}) collective-permute-start(f32[16,24,128]{2,1,0:T(8,128)S(1)} %get-tuple-element.19), channel_id=1, source_target_pairs={{0,2},{2,0},{4,6},{6,4},{1,3},{3,1},{5,7},{7,5},{8,10},{10,8},{12,... | collective-permute-start | bytes 589832 | tf_op jit(solution)/shard_map/ppermute | solution.py:337
  5.7 8.9 %collective-permute-start.1 = (f32[16,24,128]{2,1,0:T(8,128)S(1)}, f32[16,24,128]{2,1,0:T(8,128)S(1)}, u32[]{:S(2)}, u32[]{:S(2)}) collective-permute-start(f32[16,24,128]{2,1,0:T(8,128)S(1)} %get-tuple-element.20), channel_id=1, source_target_pairs={{2,4},{4,2},{3,5},{5,3},{10,12},{12,10},{11,13},{13,11},{18,20},{2... | collective-permute-start | bytes 589832 | tf_op jit(solution)/shard_map/ppermute | solution.py:337
  6.4 8.2 %collective-permute-start.2 = (f32[8,24,128]{2,1,0:T(8,128)S(1)}, f32[8,24,128]{2,1,0:T(8,128)S(1)}, u32[]{:S(2)}, u32[]{:S(2)}) collective-permute-start(f32[8,24,128]{2,1,0:T(8,128)S(1)} %get-tuple-element.21), channel_id=1, source_target_pairs={{0,1},{1,0},{2,3},{3,2},{4,5},{5,4},{6,7},{7,6},{8,9},{9,8},{10,11... | collective-permute-start | bytes 294920 | tf_op jit(solution)/shard_map/ppermute | solution.py:337
  7.6 6.9 %collective-permute-start.3 = (f32[24,128]{1,0:T(8,128)S(1)}, f32[24,128]{1,0:T(8,128)S(1)}, u32[]{:S(2)}, u32[]{:S(2)}) collective-permute-start(f32[24,128]{1,0:T(8,128)S(1)} %get-tuple-element.22), channel_id=1, source_target_pairs={{0,8},{8,0},{16,24},{24,16},{1,9},{9,1},{17,25},{25,17},{2,10},{10... | collective-permute-start | bytes 36872 | tf_op jit(solution)/shard_map/ppermute | solution.py:337
  8.9 5.6 %collective-permute-start.4 = (f32[24,128]{1,0:T(8,128)S(1)}, f32[24,128]{1,0:T(8,128)S(1)}, u32[]{:S(2)}, u32[]{:S(2)}) collective-permute-start(f32[24,128]{1,0:T(8,128)S(1)} %get-tuple-element.23), channel_id=1, source_target_pairs={{8,16},{16,8},{9,17},{17,9},{10,18},{18,10},{11,19},{19,11},{12,20... | collective-permute-start | bytes 36872 | tf_op jit(solution)/shard_map/ppermute | solution.py:337
  15.3 3.1 %collective-permute-start.5 = (f32[4,24,128]{2,1,0:T(8,128)S(1)}, f32[4,24,128]{2,1,0:T(8,128)S(1)}, u32[]{:S(2)}, u32[]{:S(2)}) collective-permute-start(f32[4,24,128]{2,1,0:T(8,128)S(1)} %get-tuple-element.27), channel_id=1, source_target_pairs={{0,8},{16,24},{1,9},{17,25},{2,10},{18,26},{3,11},{19,27},{4,12},{... | collective-permute-start | bytes 147464 | tf_op jit(solution)/shard_map/ppermute | solution.py:352
  18.5 6.9 %collective-permute-start.6 = (f32[2,24,128]{2,1,0:T(8,128)S(1)}, f32[2,24,128]{2,1,0:T(8,128)S(1)}, u32[]{:S(2)}, u32[]{:S(2)}) collective-permute-start(f32[2,24,128]{2,1,0:T(8,128)S(1)} %slice.9), channel_id=1, source_target_pairs={{8,10},{10,12},{12,14},{14,8},{24,26},{26,28},{28,30},{30,24},{9,1... | collective-permute-start | bytes 73736 | tf_op jit(solution)/shard_map/ppermute | solution.py:346
  25.4 4.6 %collective-permute-start.7 = (f32[2,24,128]{2,1,0:T(8,128)S(1)}, f32[2,24,128]{2,1,0:T(8,128)S(1)}, u32[]{:S(2)}, u32[]{:S(2)}) collective-permute-start(f32[2,24,128]{2,1,0:T(8,128)S(1)} %slice_add_fusion), channel_id=1, source_target_pairs={{8,24},{24,8},{9,25},{25,9},{10,26},{26,10},{11,27},{27,11},{12,28... | collective-permute-start | bytes 73736 | tf_op jit(solution)/shard_map/ppermute | solution.py:344
  30.0 4.6 %collective-permute-start.8 = (f32[2,24,128]{2,1,0:T(8,128)S(1)}, f32[2,24,128]{2,1,0:T(8,128)S(1)}, u32[]{:S(2)}, u32[]{:S(2)}) collective-permute-start(f32[2,24,128]{2,1,0:T(8,128)S(1)} %add.14), channel_id=1, source_target_pairs={{8,9},{9,8},{24,25},{25,24},{10,11},{11,10},{26,27},{27,26},{12,13... | collective-permute-start | bytes 73736 | tf_op jit(solution)/shard_map/ppermute | solution.py:346
  34.6 3.2 %collective-permute-start.9 = (f32[2,24,128]{2,1,0:T(8,128)S(1)}, f32[2,24,128]{2,1,0:T(8,128)S(1)}, u32[]{:S(2)}, u32[]{:S(2)}) collective-permute-start(f32[2,24,128]{2,1,0:T(8,128)S(1)} %add.15.own), channel_id=1, source_target_pairs={{8,0},{24,16},{9,1},{25,17},{10,2},{26,18},{11,3},{27,19},{12,4},{... | collective-permute-start | bytes 73736 | tf_op jit(solution)/shard_map/ppermute | solution.py:362

commit v3 on v2

--- a/solution.py
+++ b/solution.py
@@ -60,18 +60,18 @@
     faces = list(outs[2:])
     species, row_count, depth = cells.shape
     width = row_count // planes
+    field_copies = [
+        pltpu.make_async_copy(mixing, rows_out.at[:, species, :], field_sem.at[0]),
+        pltpu.make_async_copy(classes, bins, field_sem.at[1]),
+    ]
+    for copy in field_copies:
+        copy.start()
     for plane in range(planes):
         span = pl.ds(plane * width, width)
         for k in range(species):
             pltpu.make_async_copy(
                 cells.at[k, span], rows_out.at[span, k, :], sem.at[plane]
             ).start()
-    field_copies = [
-        pltpu.make_async_copy(mixing, rows_out.at[:, species, :], field_sem.at[0]),
-        pltpu.make_async_copy(classes, bins, field_sem.at[1]),
-    ]
-    for copy in field_copies:
-        copy.start()
     for copy in field_copies:
         copy.wait()
     for r in range(0, row_count, SUBLANES):
@@ -203,9 +203,19 @@
         received[axis] = [halos.pop(0), halos.pop(0) if both else None]
     evens = {axis: lax.axis_index(axis) % 2 == 0 for axis in received}
 
-    def added(c, halo):
+    inside = {}
+    for axis in received:
+        place, upper = lax.axis_index(axis), jnp.logical_not(evens[axis])
+        edge = jnp.where(upper, lax.axis_size(axis) - 1, 0)
+        inside[axis] = jnp.broadcast_to(place != edge, (rows, depth))
+
+    def added(c, axis, side, part):
+        halo = received[axis][side]
         if halo is None:
             return weight * (0.5 * c[species : species + 1]) * (0.0 - c)
+        halo = halo[part]
+        if side:
+            halo = jnp.where(inside[axis], halo, 0.0)
         d = 0.5 * (c[species : species + 1] + halo[species : species + 1])
         return weight * d * (halo - c)
 
@@ -213,13 +223,12 @@
     for side in range(2):
         upper = evens["gx"] if side == 0 else jnp.logical_not(evens["gx"])
         plane = jnp.where(upper, planes - 1, 0)
-        halo = received["gx"][side]
         made = jnp.zeros((2 * rows, NB), F32)
         for first in range(0, width, 2):
             values, classes = [], []
             for y in (first, first + 1):
                 r = plane * width + y
-                delta = added(cells[r], None if halo is None else halo[y])
+                delta = added(cells[r], "gx", side, y)
                 dx[side, y] = delta
                 values.append(halves(delta))
                 classes.append(cells[r, species + 1 : species + 2, :])
@@ -228,10 +237,9 @@
     for side in range(2):
         upper = evens["gy"] if side == 0 else jnp.logical_not(evens["gy"])
         place = jnp.where(upper, width - 1, 0)
-        halo = received["gy"][side]
         for x in range(planes):
             r = place + x * width
-            delta = added(cells[r], None if halo is None else halo[x])
+            delta = added(cells[r], "gy", side, x)
             dy[side, x] = delta
             station_sums[(x + 1) // 2] += folded(
                 binned(halves(delta), cells[r, species + 1 : species + 2, :])
@@ -242,8 +250,7 @@
     for side in range(2):
         upper = evens["sec"] if side == 0 else jnp.logical_not(evens["sec"])
         c = own_z[jnp.where(upper, 1, 0)]
-        halo = received["sec"][side]
-        delta = added(c, None if halo is None else halo[...])
+        delta = added(c, "sec", side, slice(None))
         dz[side] = delta
         value = halves(delta)
         classes = c[species + 1 : species + 2]
@@ -304,9 +311,8 @@
 
 def means_kernel(own, received, out):
     species, per_device, bins = out.shape
-    even = lax.axis_index("sec") % 2 == 0
     for s in range(0, per_device, 2):
-        block = jnp.where(jnp.broadcast_to(even, own.shape[1:]), received[s // 2], own[s // 2])
+        block = own[s // 2] + received[s // 2]
         means = block / jnp.maximum(block[species + 1 : species + 2], 1.0)
         out[:, s, :] = means[:species, :bins]
         out[:, s + 1, :] = means[:species, bins:]
@@ -332,34 +338,33 @@
 def swapped(block, axis, side):
     count = lax.axis_size(axis)
     pairs = []
-    for i in range(side, count - 1, 2):
-        pairs += [(i, i + 1), (i + 1, i)]
+    for i in range(side, count, 2):
+        j = (i + 1) % count
+        pairs += [(i, j), (j, i)]
     return lax.ppermute(block, axis, pairs)
 
 
-def on_odd(block, axis, move):
+def crossed(block, axis, move):
     deep = lax.axis_size("sec")
     count = lax.axis_size(axis)
     if axis == "sec":
-        return lax.ppermute(block, axis, [(i, move(i)) for i in range(1, deep, 2)])
-    pairs = [(s * count + i, s * count + move(i)) for s in range(1, deep, 2) for i in range(count)]
+        return lax.ppermute(block, axis, [(i, move(i) ^ 1) for i in range(deep)])
+    pairs = [(s * count + i, (s ^ 1) * count + move(i)) for s in range(deep) for i in range(count)]
     return lax.ppermute(block, ("sec", axis), pairs)
 
 
 def summed(block):
     deep, gx, gy = (lax.axis_size(axis) for axis in ("sec", "gx", "gy"))
     half = block.shape[0] // 2
-    block = block + lax.ppermute(block, "sec", [(i, i + 1) for i in range(0, deep, 2)])
-    block = block[:half] + on_odd(block[half:], "gx", lambda i: (i + 1) % gx)
-    step = 2
-    while step < deep:
-        block = block + on_odd(block, "sec", lambda i: i ^ step)
-        step *= 2
-    step = 1
-    while step < gy:
-        block = block + on_odd(block, "gy", lambda i: i ^ step)
-        step *= 2
-    return block, lax.ppermute(block, "sec", [(i + 1, i) for i in range(0, deep, 2)])
+    block = block + lax.ppermute(block, "sec", [(i, i ^ 1) for i in range(deep)])
+    block = block[:half] + crossed(block[half:], "gx", lambda i: (i + 1) % gx)
+    steps = [("sec", 1 << n) for n in range(1, deep.bit_length() - 1)]
+    steps += [("gy", 1 << n) for n in range(gy.bit_length() - 1)]
+    for axis, step in steps:
+        last = crossed(block, axis, lambda i: i ^ step)
+        if (axis, step) == steps[-1]:
+            return block, last
+        block = block + last
 
 
 def on_device(

time: 38.8 us -> 32.6 us (0.84)
  the two profiles are of different devices: /device:TPU:1 before, /device:TPU:0 now
where the time goes in v3:
time: 32.6 us; the launch traced here: 32.4 us
  starting transfers between devices  11.7 us (36%)
  waiting for transfers between devices  11.2 us (34%)
  Pallas kernels  8.72 us (27%)
  between operations  0.76 us (2%)
    ppermute x5, starting transfers between devices, swapped(): return lax.ppermute(block, axis, pairs)  8.69 us
    ppermute x2, waiting for transfers between devices, crossed(): return lax.ppermute(block, ('sec', axis), pairs)  4.82 us
    ppermute x5, waiting for transfers between devices, swapped(): return lax.ppermute(block, axis, pairs)  3.22 us
    pallas_call x1, Pallas kernels, on_device(): call(functools.partial(pack_kernel, planes, has_b), 'faces', [struct(row_...  2.82 us
    pallas_call x1, Pallas kernels, on_device(): call(functools.partial(inner_kernel, planes), 'inside', [struct(row_count...  2.54 us
    ppermute x1, waiting for transfers between devices, crossed(): return lax.ppermute(block, axis, [(i, move(i) ^ 1) for i in range(deep)])  1.98 us
    pallas_call x1, Pallas kernels, on_device(): call(functools.partial(finish_kernel, planes), 'advance', struct(species,...  1.89 us
    ppermute x2, starting transfers between devices, crossed(): return lax.ppermute(block, ('sec', axis), pairs)  1.64 us
  transfers between devices with their start and end apart: 9, of which 5 were waited for; matrix products, arithmetic and copies ran while one was open for 0% of the time, Pallas kernels for 14%

profile of v3, /device:TPU:0, one launch (start us, length us, event | category | flops | bytes accessed | tf_op | source)
XLA Modules:
  0.0 32.4 jit_solution(17841274604307171747)
XLA Ops:
  0.6 0.0 copy-start
  0.6 0.0 copy-start.1
  0.7 0.0 copy-start.3
  0.7 0.0 copy-start.2
  0.7 0.0 copy-start.4
  0.7 2.8 %faces.1 = (f32[128,24,128]{2,1,0:T(8,128)S(1)}, f32[2,24,128]{2,1,0:T(8,128)S(1)}, f32[16,24,128]{2,1,0:T(8,128)S(1)}, f32[16,24,128]{2,1,0:T(8,128)S(1)}, f32[...) custom-call(f32[22,128,128]{2,1,0:T(8,128)} %bitcast.14, f32[128,128]{1,0:T(8,128)} %bitcast.7, ...), custom_call_target="tpu_custom_call" | custom-call | tf_op jit(solution)/shard_map/faces/pallas_call | solution.py:398
  3.5 3.1 %collective-permute-start = (f32[16,24,128]{2,1,0:T(8,128)S(1)}, f32[16,24,128]{2,1,0:T(8,128)S(1)}, u32[]{:S(2)}, u32[]{:S(2)}) collective-permute-start(f32[16,24,128]{2,1,0:T(8,128)S(1)} %get-tuple-element.19), channel_id=1, source_target_pairs={{0,2},{2,0},{4,6},{6,4},{1,3},{3,1},{5,7},{7,5},{8,10},{10,8},{12,... | collective-permute-start | bytes 589832 | tf_op jit(solution)/shard_map/ppermute | solution.py:344
  6.6 2.5 %collective-permute-start.1 = (f32[16,24,128]{2,1,0:T(8,128)S(1)}, f32[16,24,128]{2,1,0:T(8,128)S(1)}, u32[]{:S(2)}, u32[]{:S(2)}) collective-permute-start(f32[16,24,128]{2,1,0:T(8,128)S(1)} %get-tuple-element.20), channel_id=1, source_target_pairs={{2,4},{4,2},{6,0},{0,6},{3,5},{5,3},{7,1},{1,7},{10,12},{12,10},{1... | collective-permute-start | bytes 589832 | tf_op jit(solution)/shard_map/ppermute | solution.py:344
  9.1 1.5 %collective-permute-start.2 = (f32[8,24,128]{2,1,0:T(8,128)S(1)}, f32[8,24,128]{2,1,0:T(8,128)S(1)}, u32[]{:S(2)}, u32[]{:S(2)}) collective-permute-start(f32[8,24,128]{2,1,0:T(8,128)S(1)} %get-tuple-element.21), channel_id=1, source_target_pairs={{0,1},{1,0},{2,3},{3,2},{4,5},{5,4},{6,7},{7,6},{8,9},{9,8},{10,11... | collective-permute-start | bytes 294920 | tf_op jit(solution)/shard_map/ppermute | solution.py:344
  10.6 0.0 collective-permute-start.3
  10.6 1.6 %collective-permute-start.4 = (f32[24,128]{1,0:T(8,128)S(1)}, f32[24,128]{1,0:T(8,128)S(1)}, u32[]{:S(2)}, u32[]{:S(2)}) collective-permute-start(f32[24,128]{1,0:T(8,128)S(1)} %get-tuple-element.23), channel_id=1, source_target_pairs={{8,16},{16,8},{24,0},{0,24},{9,17},{17,9},{25,1},{1,25},{10,18},{1... | collective-permute-start | bytes 36872 | tf_op jit(solution)/shard_map/ppermute | solution.py:344
  12.2 0.0 copy-done
  12.2 0.0 copy-done.1
  12.2 0.0 copy-done.3
  12.2 0.0 copy-done.2
  12.2 2.5 %inside.1 = (f32[128,24,128]{2,1,0:T(8,128)S(1)}, f32[5,24,64]{2,1,0:T(8,128)S(1)}) custom-call(f32[128,24,128]{2,1,0:T(8,128)S(1)} %get-tuple-element.15.cells, f32[128,128]{1,0:T(8,128)S(1)} %bitcast.8, f32[128,128]{1,0:T(8,128)S(1)} %bitcast.9, f32[1,22]{1,0:T(1,128)S(1)} %bitcast.10, f32[22,22]{1,0:T(8,128)S(1)} %copy-done.2), custom_call_target="tpu_custom_call" | custom-call | flops 10000000 | bytes 4000000 | tf_op jit(solution)/shard_map/inside/pallas_call | solution.py:414
  14.8 0.0 collective-permute-done.3.refs_3_
  14.8 0.0 collective-permute-done.4.refs_4_
  14.8 0.0 collective-permute-done.2.refs_2_
  14.8 0.0 collective-permute-done.refs_0_
  14.8 3.2 %collective-permute-done.1.refs_1_ = f32[16,24,128]{2,1,0:T(8,128)S(1)} collective-permute-done((f32[16,24,128]{2,1,0:T(8,128)S(1)}, f32[16,24,128]{2,1,0:T(8,128)S(1)}, u32[]{:S(2)}, u32[]{:S(2)}) %collective-permute-start.1) | collective-permute-done | bytes 196640 | tf_op jit(solution)/shard_map/ppermute | solution.py:344
  18.0 0.0 copy-done.4
  18.0 0.7 %edges.1 = (f32[4,24,128]{2,1,0:T(8,128)S(1)}, f32[2,16,24,128]{3,2,1,0:T(8,128)S(1)}, f32[2,8,24,128]{3,2,1,0:T(8,128)S(1)}, f32[2,24,128]{2,1,0:T(8,128)S(1)}) custom-call(f32[128,24,128]{2,1,0:T(8,128)S(1)} %get-tuple-element.15.cells, f32[2,24,128]{2,1,0:T(8,128)S(1)} %get-tuple-element.17.own_z, f32[5,24,64]{2,1,0:T(8,128)S(1)} %get-tuple-element.18.sums, ...), custom_call_target="tpu_custom_call" | custom-call | tf_op jit(solution)/shard_map/edges/pallas_call | solution.py:428
  18.7 0.1 collective-permute-start.5
  18.8 1.2 %collective-permute-done.5 = f32[4,24,128]{2,1,0:T(8,128)S(1)} collective-permute-done((f32[4,24,128]{2,1,0:T(8,128)S(1)}, f32[4,24,128]{2,1,0:T(8,128)S(1)}, u32[]{:S(2)}, u32[]{:S(2)}) %collective-permute-start.5) | collective-permute-done | bytes 49184 | tf_op jit(solution)/shard_map/ppermute | solution.py:359
  20.1 0.4 %collective-permute-start.6 = (f32[2,24,128]{2,1,0:T(8,128)S(1)}, f32[2,24,128]{2,1,0:T(8,128)S(1)}, u32[]{:S(2)}, u32[]{:S(2)}) collective-permute-start(f32[2,24,128]{2,1,0:T(8,128)S(1)} %slice.9), channel_id=1, source_target_pairs={{0,10},{2,12},{4,14},{6,8},{8,2},{10,4},{12,6},{14,0},{16,26},{18,... | collective-permute-start | bytes 73736 | tf_op jit(solution)/shard_map/ppermute | solution.py:353
  20.5 4.7 %collective-permute-done.6 = f32[2,24,128]{2,1,0:T(8,128)S(1)} collective-permute-done((f32[2,24,128]{2,1,0:T(8,128)S(1)}, f32[2,24,128]{2,1,0:T(8,128)S(1)}, u32[]{:S(2)}, u32[]{:S(2)}) %collective-permute-start.6) | collective-permute-done | bytes 24608 | tf_op jit(solution)/shard_map/ppermute | solution.py:353
  25.2 1.3 %collective-permute-start.7 = (f32[2,24,128]{2,1,0:T(8,128)S(1)}, f32[2,24,128]{2,1,0:T(8,128)S(1)}, u32[]{:S(2)}, u32[]{:S(2)}) collective-permute-start(f32[2,24,128]{2,1,0:T(8,128)S(1)} %slice_add_fusion), channel_id=1, source_target_pairs={{0,24},{8,16},{16,8},{24,0},{1,25},{9,17},{17,9},{25,1},{2,26},{10... | collective-permute-start | bytes 73736 | tf_op jit(solution)/shard_map/ppermute | solution.py:351
  26.5 2.0 %collective-permute-done.7 = f32[2,24,128]{2,1,0:T(8,128)S(1)} collective-permute-done((f32[2,24,128]{2,1,0:T(8,128)S(1)}, f32[2,24,128]{2,1,0:T(8,128)S(1)}, u32[]{:S(2)}, u32[]{:S(2)}) %collective-permute-start.7) | collective-permute-done | bytes 24608 | tf_op jit(solution)/shard_map/ppermute | solution.py:351
  28.4 1.3 %collective-permute-start.8 = (f32[2,24,128]{2,1,0:T(8,128)S(1)}, f32[2,24,128]{2,1,0:T(8,128)S(1)}, u32[]{:S(2)}, u32[]{:S(2)}) collective-permute-start(f32[2,24,128]{2,1,0:T(8,128)S(1)} %add.11.own), channel_id=1, source_target_pairs={{0,9},{1,8},{8,1},{9,0},{16,25},{17,24},{24,17},{25,16},{2,11},{3,... | collective-permute-start | bytes 73736 | tf_op jit(solution)/shard_map/ppermute | solution.py:353
  29.7 1.9 %advance.1 = f32[22,128,128]{2,1,0:T(8,128)} custom-call(f32[128,24,128]{2,1,0:T(8,128)S(1)} %get-tuple-element.16.advanced, f32[2,16,24,128]{3,2,1,0:T(8,128)S(1)} %get-tuple-element.24.dx, f32[2,8,24,128]{3,2,1,0:T(8,128)S(1)} %get-tuple-element.25.dy, f32[2,24,128]{2,1,0:T(8,128)S(1)} %get-tuple-element.26.dz), custom_call_target="tpu_custom_call" | custom-call | flops 1000000 | bytes 3000000 | tf_op jit(solution)/shard_map/advance/pallas_call | solution.py:443
  31.6 0.1 collective-permute-done.8.received
  31.7 0.7 %means.1 = f32[22,4,64]{2,1,0:T(4,128)} custom-call(f32[2,24,128]{2,1,0:T(8,128)S(1)} %add.11.own, f32[2,24,128]{2,1,0:T(8,128)S(1)} %collective-permute-done.8.received), custom_call_target="tpu_custom_call" | custom-call | tf_op jit(solution)/shard_map/means/pallas_call | solution.py:456
  (4 shorter events, 0.0 us)
Async XLA Ops:
  0.6 11.6 %copy-start = (f32[8,16,128]{2,1,0:T(8,128)S(1)}, f32[8,16,128]{2,1,0:T(8,128)}, u32[]{:S(2)}) copy-start(f32[8,16,128]{2,1,0:T(8,128)} %param.8) | copy-start | bytes 196612
  0.6 11.6 %copy-start.1 = (f32[8,16,128]{2,1,0:T(8,128)S(1)}, f32[8,16,128]{2,1,0:T(8,128)}, u32[]{:S(2)}) copy-start(f32[8,16,128]{2,1,0:T(8,128)} %param.9) | copy-start | bytes 196612
  0.7 11.6 %copy-start.3 = (f32[22]{0:T(128)S(1)}, f32[22]{0:T(128)}, u32[]{:S(2)}) copy-start(f32[22]{0:T(128)} %param.10) | copy-start | bytes 268
  0.7 11.6 %copy-start.2 = (f32[22,22]{1,0:T(8,128)S(1)}, f32[22,22]{1,0:T(8,128)}, u32[]{:S(2)}) copy-start(f32[22,22]{1,0:T(8,128)} %jacobian.1) | copy-start | bytes 5812
  0.7 17.3 %copy-start.4 = (s32[32]{0:T(128)S(1)}, s32[32]{0:T(128)}, u32[]{:S(2)}) copy-start(s32[32]{0:T(128)} %param.13) | copy-start | bytes 388
  3.5 11.3 %collective-permute-start = (f32[16,24,128]{2,1,0:T(8,128)S(1)}, f32[16,24,128]{2,1,0:T(8,128)S(1)}, u32[]{:S(2)}, u32[]{:S(2)}) collective-permute-start(f32[16,24,128]{2,1,0:T(8,128)S(1)} %get-tuple-element.19), channel_id=1, source_target_pairs={{0,2},{2,0},{4,6},{6,4},{1,3},{3,1},{5,7},{7,5},{8,10},{10,8},{12,... | collective-permute-start | bytes 589832 | tf_op jit(solution)/shard_map/ppermute | solution.py:344
  6.6 11.4 %collective-permute-start.1 = (f32[16,24,128]{2,1,0:T(8,128)S(1)}, f32[16,24,128]{2,1,0:T(8,128)S(1)}, u32[]{:S(2)}, u32[]{:S(2)}) collective-permute-start(f32[16,24,128]{2,1,0:T(8,128)S(1)} %get-tuple-element.20), channel_id=1, source_target_pairs={{2,4},{4,2},{6,0},{0,6},{3,5},{5,3},{7,1},{1,7},{10,12},{12,10},{1... | collective-permute-start | bytes 589832 | tf_op jit(solution)/shard_map/ppermute | solution.py:344
  9.1 5.7 %collective-permute-start.2 = (f32[8,24,128]{2,1,0:T(8,128)S(1)}, f32[8,24,128]{2,1,0:T(8,128)S(1)}, u32[]{:S(2)}, u32[]{:S(2)}) collective-permute-start(f32[8,24,128]{2,1,0:T(8,128)S(1)} %get-tuple-element.21), channel_id=1, source_target_pairs={{0,1},{1,0},{2,3},{3,2},{4,5},{5,4},{6,7},{7,6},{8,9},{9,8},{10,11... | collective-permute-start | bytes 294920 | tf_op jit(solution)/shard_map/ppermute | solution.py:344
  10.6 4.2 %collective-permute-start.3 = (f32[24,128]{1,0:T(8,128)S(1)}, f32[24,128]{1,0:T(8,128)S(1)}, u32[]{:S(2)}, u32[]{:S(2)}) collective-permute-start(f32[24,128]{1,0:T(8,128)S(1)} %get-tuple-element.22), channel_id=1, source_target_pairs={{0,8},{8,0},{16,24},{24,16},{1,9},{9,1},{17,25},{25,17},{2,10},{10... | collective-permute-start | bytes 36872 | tf_op jit(solution)/shard_map/ppermute | solution.py:344
  10.6 4.2 %collective-permute-start.4 = (f32[24,128]{1,0:T(8,128)S(1)}, f32[24,128]{1,0:T(8,128)S(1)}, u32[]{:S(2)}, u32[]{:S(2)}) collective-permute-start(f32[24,128]{1,0:T(8,128)S(1)} %get-tuple-element.23), channel_id=1, source_target_pairs={{8,16},{16,8},{24,0},{0,24},{9,17},{17,9},{25,1},{1,25},{10,18},{1... | collective-permute-start | bytes 36872 | tf_op jit(solution)/shard_map/ppermute | solution.py:344
  18.7 1.3 %collective-permute-start.5 = (f32[4,24,128]{2,1,0:T(8,128)S(1)}, f32[4,24,128]{2,1,0:T(8,128)S(1)}, u32[]{:S(2)}, u32[]{:S(2)}) collective-permute-start(f32[4,24,128]{2,1,0:T(8,128)S(1)} %get-tuple-element.27), channel_id=1, source_target_pairs={{0,8},{8,0},{16,24},{24,16},{1,9},{9,1},{17,25},{25,17},{2,10},{10... | collective-permute-start | bytes 147464 | tf_op jit(solution)/shard_map/ppermute | solution.py:359
  20.1 5.1 %collective-permute-start.6 = (f32[2,24,128]{2,1,0:T(8,128)S(1)}, f32[2,24,128]{2,1,0:T(8,128)S(1)}, u32[]{:S(2)}, u32[]{:S(2)}) collective-permute-start(f32[2,24,128]{2,1,0:T(8,128)S(1)} %slice.9), channel_id=1, source_target_pairs={{0,10},{2,12},{4,14},{6,8},{8,2},{10,4},{12,6},{14,0},{16,26},{18,... | collective-permute-start | bytes 73736 | tf_op jit(solution)/shard_map/ppermute | solution.py:353
  25.2 3.3 %collective-permute-start.7 = (f32[2,24,128]{2,1,0:T(8,128)S(1)}, f32[2,24,128]{2,1,0:T(8,128)S(1)}, u32[]{:S(2)}, u32[]{:S(2)}) collective-permute-start(f32[2,24,128]{2,1,0:T(8,128)S(1)} %slice_add_fusion), channel_id=1, source_target_pairs={{0,24},{8,16},{16,8},{24,0},{1,25},{9,17},{17,9},{25,1},{2,26},{10... | collective-permute-start | bytes 73736 | tf_op jit(solution)/shard_map/ppermute | solution.py:351
  28.4 3.3 %collective-permute-start.8 = (f32[2,24,128]{2,1,0:T(8,128)S(1)}, f32[2,24,128]{2,1,0:T(8,128)S(1)}, u32[]{:S(2)}, u32[]{:S(2)}) collective-permute-start(f32[2,24,128]{2,1,0:T(8,128)S(1)} %add.11.own), channel_id=1, source_target_pairs={{0,9},{1,8},{8,1},{9,0},{16,25},{17,24},{24,17},{25,16},{2,11},{3,... | collective-permute-start | bytes 73736 | tf_op jit(solution)/shard_map/ppermute | solution.py:353

commit v4 on v3

--- a/solution.py
+++ b/solution.py
@@ -59,53 +59,66 @@
     rows_out, own_z = outs[0], outs[1]
     faces = list(outs[2:])
     species, row_count, depth = cells.shape
+    rows = rows_out.shape[1]
     width = row_count // planes
+    chunk = row_count // sem.shape[0]
     field_copies = [
         pltpu.make_async_copy(mixing, rows_out.at[:, species, :], field_sem.at[0]),
         pltpu.make_async_copy(classes, bins, field_sem.at[1]),
     ]
     for copy in field_copies:
         copy.start()
-    for plane in range(planes):
-        span = pl.ds(plane * width, width)
+    for n in range(sem.shape[0]):
+        span = pl.ds(n * chunk, chunk)
         for k in range(species):
             pltpu.make_async_copy(
-                cells.at[k, span], rows_out.at[span, k, :], sem.at[plane]
+                cells.at[k, span], rows_out.at[span, k, :], sem.at[n]
             ).start()
+
+    lane = lanes_of((SUBLANES, depth))
+    zero = jnp.zeros((SUBLANES, depth), F32)
+
+    def gathered(groups, span, low, high):
+        low, high = list(low), list(high)
+        for r in span:
+            at, before = lane == r, lane == (r - 1) % depth
+            for i, g in enumerate(groups):
+                block = rows_out[r, pl.ds(g, SUBLANES), :]
+                turned = pltpu.roll(block, r, axis=1) if r else block
+                low[i] = jnp.where(at, turned, low[i])
+                high[i] = jnp.where(before, turned, high[i])
+        return low, high
+
+    whole = species // SUBLANES * SUBLANES
+    first = range(0, whole, SUBLANES)
+    rest = range(whole, rows, SUBLANES)
+    low, high = [zero] * len(first), [zero] * len(first)
+    for n in range(sem.shape[0]):
+        arrived = rows_out.at[pl.ds(n * chunk, chunk), pl.ds(0, species), :]
+        pltpu.make_async_copy(arrived, arrived, sem.at[n]).wait()
+        low, high = gathered(first, range(n * chunk, (n + 1) * chunk), low, high)
     for copy in field_copies:
         copy.wait()
     for r in range(0, row_count, SUBLANES):
         span = pl.ds(r, SUBLANES)
         rows_out[span, species + 1, :] = bins[span, :].astype(F32)
-    shape = rows_out.shape[1:]
-    lane = lanes_of(shape)
-    low = jnp.zeros(shape, F32)
-    high = jnp.zeros(shape, F32)
-    for plane in range(planes):
-        span = pl.ds(plane * width, width)
-        pltpu.make_async_copy(
-            cells.at[:, span], rows_out.at[pl.ds(0, species), pl.ds(0, width), :], sem.at[plane]
-        ).wait()
-        for r in range(plane * width, (plane + 1) * width):
-            turned = pltpu.roll(rows_out[r], r, axis=1) if r else rows_out[r]
-            low = jnp.where(lane == r, turned, low)
-            high = jnp.where(lane == (r - 1) % depth, turned, high)
-    high = pltpu.roll(high, 1, axis=1)
-    own_z[0] = low
-    own_z[1] = high
+    lows, highs = gathered(rest, range(row_count), [zero] * len(rest), [zero] * len(rest))
+    for i, g in enumerate([*first, *rest]):
+        own_z[0, pl.ds(g, SUBLANES), :] = (low + lows)[i]
+        own_z[1, pl.ds(g, SUBLANES), :] = pltpu.roll((high + highs)[i], 1, axis=1)
     for axis, both in zip(("gx", "gy", "sec"), has_b):
         even = lax.axis_index(axis) % 2 == 0
         for side in range(1 + both):
             out = faces.pop(0)
             upper = even if side == 0 else jnp.logical_not(even)
             if axis == "gx":
-                first = jnp.where(upper, row_count - width, 0)
+                start = jnp.where(upper, row_count - width, 0)
                 for y in range(width):
-                    out[y] = rows_out[first + y]
+                    out[y] = rows_out[start + y]
             elif axis == "gy":
-                first = jnp.where(upper, width - 1, 0)
+                start = jnp.where(upper, width - 1, 0)
                 for x in range(planes):
-                    out[x] = rows_out[first + x * width]
+                    out[x] = rows_out[start + x * width]
             else:
                 out[...] = own_z[jnp.where(upper, 1, 0)]
 
@@ -309,10 +322,11 @@
         ).wait()
 
 
-def means_kernel(own, received, out):
+def means_kernel(*refs):
+    terms, out = refs[:-1], refs[-1]
     species, per_device, bins = out.shape
     for s in range(0, per_device, 2):
-        block = own[s // 2] + received[s // 2]
+        block = sum((term[s // 2] for term in terms[1:]), terms[0][s // 2])
         means = block / jnp.maximum(block[species + 1 : species + 2], 1.0)
         out[:, s, :] = means[:species, :bins]
         out[:, s + 1, :] = means[:species, bins:]
@@ -335,36 +349,46 @@
     )
 
 
+def joint(block, axis, source):
+    deep, count = lax.axis_size("sec"), lax.axis_size(axis)
+    pairs = []
+    for s in range(deep):
+        for i in range(count):
+            t, j = source(s, i)
+            pairs.append((t * count + j, s * count + i))
+    return lax.ppermute(block, ("sec", axis), pairs)
+
+
 def swapped(block, axis, side):
     count = lax.axis_size(axis)
-    pairs = []
-    for i in range(side, count, 2):
-        j = (i + 1) % count
-        pairs += [(i, j), (j, i)]
-    return lax.ppermute(block, axis, pairs)
-
-
-def crossed(block, axis, move):
-    deep = lax.axis_size("sec")
-    count = lax.axis_size(axis)
+    if side == 0:
+        return lax.ppermute(block, axis, [(i, i ^ 1) for i in range(count)])
     if axis == "sec":
-        return lax.ppermute(block, axis, [(i, move(i) ^ 1) for i in range(deep)])
-    pairs = [(s * count + i, (s ^ 1) * count + move(i)) for s in range(deep) for i in range(count)]
-    return lax.ppermute(block, ("sec", axis), pairs)
+        pairs = [(i, ((i + 1) ^ 1) - 1) for i in range(1, count - 1)]
+        return lax.ppermute(block, axis, [*pairs, (0, count - 1), (count - 1, 0)])
+    return joint(
+        block,
+        axis,
+        lambda s, i: (s, ((i + 1) ^ 1) - 1) if 0 < i < count - 1 else (s ^ 1, i),
+    )
 
 
 def summed(block):
     deep, gx, gy = (lax.axis_size(axis) for axis in ("sec", "gx", "gy"))
     half = block.shape[0] // 2
     block = block + lax.ppermute(block, "sec", [(i, i ^ 1) for i in range(deep)])
-    block = block[:half] + crossed(block[half:], "gx", lambda i: (i + 1) % gx)
-    steps = [("sec", 1 << n) for n in range(1, deep.bit_length() - 1)]
-    steps += [("gy", 1 << n) for n in range(gy.bit_length() - 1)]
-    for axis, step in steps:
-        last = crossed(block, axis, lambda i: i ^ step)
-        if (axis, step) == steps[-1]:
-            return block, last
-        block = block + last
+    block = block[:half] + joint(block[half:], "gx", lambda s, i: (s ^ 1, (i - 1) % gx))
+    steps = [(1 << n, 0) for n in range(1, deep.bit_length() - 1)]
+    steps += [(0, 1 << n) for n in range(gy.bit_length() - 1)]
+    terms = [block]
+    while steps:
+        (a, b), (c, d) = steps.pop(0), steps.pop(0) if steps else (0, 0)
+        block = sum(terms[1:], terms[0])
+        terms = [block]
+        for e, f in dict.fromkeys([(a, b), (c, d), (a ^ c, b ^ d)]):
+            if e or f:
+                terms.append(joint(block, "gy", lambda s, i: (s ^ 1 ^ e, i ^ f)))
+    return terms
 
 
 def on_device(
@@ -404,7 +428,7 @@
         in_specs=[ANY] * 3,
         scratch=[
             pltpu.VMEM((row_count, depth), jnp.int32),
-            pltpu.SemaphoreType.DMA((planes,)),
+            pltpu.SemaphoreType.DMA((planes // 2,)),
             pltpu.SemaphoreType.DMA((2,)),
         ],
     )(*[pltpu.with_memory_space_constraint(x, pltpu.HBM) for x in (cells, mixing, classes)])
@@ -439,7 +463,7 @@
         scratch=[pltpu.VMEM((per_device + 1, rows, NB), F32)],
     )(rows_in, own_z, sums, weights, positions, *halos)
 
-    own, received = summed(window)
+    terms = summed(window)
     advanced = call(
         functools.partial(finish_kernel, planes),
         "advance",
@@ -453,9 +477,9 @@
         flops=1_000_000,
         moved=3_000_000,
     )(inner, dx, dy, dz)
-    cond_means = call(means_kernel, "means", struct(species, per_device, NB), 2, VMEM)(
-        own, received
-    )
+    cond_means = call(
+        means_kernel, "means", struct(species, per_device, NB), len(terms), VMEM
+    )(*terms)
     return advanced.reshape(composition_matrix.shape), cond_means
 
 

time: 32.6 us -> 25.8 us (0.79)
  waiting for transfers between devices: 11.2 us -> 4.55 us
  Pallas kernels: 8.72 us -> 7.75 us
  starting transfers between devices: 11.7 us -> 12.5 us
    ppermute x8 -> x9, waiting for transfers between devices: 10 us -> 3.56 us  [the longest x5 3.52 us: joint(): return lax.ppermute(block, ('sec', axis), pairs)]
    pallas_call x1, Pallas kernels: 2.82 us -> 1.84 us  [on_device(): call(functools.partial(pack_kernel, planes, has_b), 'faces', [struct(row_...]
    ppermute x8 -> x9, starting transfers between devices: 11.6 us -> 12.2 us  [the longest x5 6.01 us: joint(): return lax.ppermute(block, ('sec', axis), pairs)]
  transfers between devices with their start and end apart: 9 -> 10, of which waited for: 5 -> 3; matrix products, arithmetic and copies ran while one was open for 0% -> 0% of each run, Pallas kernels for 14% -> 17%
where the time goes in v4:
time: 25.8 us; the launch traced here: 25.6 us
  starting transfers between devices  12.5 us (48%)
  Pallas kernels  7.75 us (30%)
  waiting for transfers between devices  4.55 us (18%)
  between operations  0.78 us (3%)
    ppermute x5, starting transfers between devices, joint(): return lax.ppermute(block, ('sec', axis), pairs)  6.01 us
    ppermute x3, starting transfers between devices, swapped(): return lax.ppermute(block, axis, [(i, i ^ 1) for i in range(count)])  4.81 us
    ppermute x5, waiting for transfers between devices, joint(): return lax.ppermute(block, ('sec', axis), pairs)  3.52 us
    pallas_call x1, Pallas kernels, on_device(): call(functools.partial(inner_kernel, planes), 'inside', [struct(row_count...  2.54 us
    pallas_call x1, Pallas kernels, on_device(): call(functools.partial(finish_kernel, planes), 'advance', struct(species,...  1.89 us
    pallas_call x1, Pallas kernels, on_device(): call(functools.partial(pack_kernel, planes, has_b), 'faces', [struct(row_...  1.84 us
    ppermute x1, starting transfers between devices, swapped(): return lax.ppermute(block, axis, [*pairs, (0, count - 1), (count - 1, 0)])  1.41 us
    ppermute x1, waiting for transfers between devices, summed(): lax.ppermute(block, 'sec', [(i, i ^ 1) for i in range(deep)])  1 us
  transfers between devices with their start and end apart: 10, of which 3 were waited for; matrix products, arithmetic and copies ran while one was open for 0% of the time, Pallas kernels for 17%

profile of v4, /device:TPU:0, one launch (start us, length us, event | category | flops | bytes accessed | tf_op | source)
XLA Modules:
  0.0 25.6 jit_solution(4272157633914368667)
XLA Ops:
  0.6 0.0 copy-start
  0.6 0.0 copy-start.1
  0.7 0.0 copy-start.3
  0.7 0.0 copy-start.2
  0.7 0.0 copy-start.4
  0.7 1.8 %faces.1 = (f32[128,24,128]{2,1,0:T(8,128)S(1)}, f32[2,24,128]{2,1,0:T(8,128)S(1)}, f32[16,24,128]{2,1,0:T(8,128)S(1)}, f32[16,24,128]{2,1,0:T(8,128)S(1)}, f32[...) custom-call(f32[22,128,128]{2,1,0:T(8,128)} %bitcast.14, f32[128,128]{1,0:T(8,128)} %bitcast.7, ...), custom_call_target="tpu_custom_call" | custom-call | tf_op jit(solution)/shard_map/faces/pallas_call | solution.py:422
  2.5 3.1 %collective-permute-start = (f32[16,24,128]{2,1,0:T(8,128)S(1)}, f32[16,24,128]{2,1,0:T(8,128)S(1)}, u32[]{:S(2)}, u32[]{:S(2)}) collective-permute-start(f32[16,24,128]{2,1,0:T(8,128)S(1)} %get-tuple-element.19), channel_id=1, source_target_pairs={{0,2},{2,0},{4,6},{6,4},{1,3},{3,1},{5,7},{7,5},{8,10},{10,8},{12,... | collective-permute-start | bytes 589832 | tf_op jit(solution)/shard_map/ppermute | solution.py:365
  5.6 0.0 collective-permute-start.1
  5.6 1.5 %collective-permute-start.2 = (f32[8,24,128]{2,1,0:T(8,128)S(1)}, f32[8,24,128]{2,1,0:T(8,128)S(1)}, u32[]{:S(2)}, u32[]{:S(2)}) collective-permute-start(f32[8,24,128]{2,1,0:T(8,128)S(1)} %get-tuple-element.21), channel_id=1, source_target_pairs={{0,1},{1,0},{2,3},{3,2},{4,5},{5,4},{6,7},{7,6},{8,9},{9,8},{10,11... | collective-permute-start | bytes 294920 | tf_op jit(solution)/shard_map/ppermute | solution.py:365
  7.1 0.2 collective-permute-start.3
  7.3 1.4 %collective-permute-start.4 = (f32[24,128]{1,0:T(8,128)S(1)}, f32[24,128]{1,0:T(8,128)S(1)}, u32[]{:S(2)}, u32[]{:S(2)}) collective-permute-start(f32[24,128]{1,0:T(8,128)S(1)} %get-tuple-element.23), channel_id=1, source_target_pairs={{8,16},{16,8},{0,24},{24,0},{9,17},{17,9},{1,25},{25,1},{10,18},{1... | collective-permute-start | bytes 36872 | tf_op jit(solution)/shard_map/ppermute | solution.py:368
  8.8 0.0 copy-done
  8.8 0.0 copy-done.1
  8.8 0.0 copy-done.3
  8.8 0.0 copy-done.2
  8.8 2.5 %inside.1 = (f32[128,24,128]{2,1,0:T(8,128)S(1)}, f32[5,24,64]{2,1,0:T(8,128)S(1)}) custom-call(f32[128,24,128]{2,1,0:T(8,128)S(1)} %get-tuple-element.15.cells, f32[128,128]{1,0:T(8,128)S(1)} %bitcast.8, f32[128,128]{1,0:T(8,128)S(1)} %bitcast.9, f32[1,22]{1,0:T(1,128)S(1)} %bitcast.10, f32[22,22]{1,0:T(8,128)S(1)} %copy-done.2), custom_call_target="tpu_custom_call" | custom-call | flops 10000000 | bytes 4000000 | tf_op jit(solution)/shard_map/inside/pallas_call | solution.py:438
  11.3 0.0 collective-permute-done.3.refs_3_
  11.3 0.0 collective-permute-done.4.refs_4_
  11.4 0.0 collective-permute-done.2.refs_2_
  11.4 0.0 collective-permute-done.refs_0_
  11.4 0.0 collective-permute-done.1.refs_1_
  11.4 0.0 copy-done.4
  11.4 0.7 %edges.1 = (f32[4,24,128]{2,1,0:T(8,128)S(1)}, f32[2,16,24,128]{3,2,1,0:T(8,128)S(1)}, f32[2,8,24,128]{3,2,1,0:T(8,128)S(1)}, f32[2,24,128]{2,1,0:T(8,128)S(1)}) custom-call(f32[128,24,128]{2,1,0:T(8,128)S(1)} %get-tuple-element.15.cells, f32[2,24,128]{2,1,0:T(8,128)S(1)} %get-tuple-element.17.own_z, f32[5,24,64]{2,1,0:T(8,128)S(1)} %get-tuple-element.18.sums, ...), custom_call_target="tpu_custom_call" | custom-call | tf_op jit(solution)/shard_map/edges/pallas_call | solution.py:452
  12.1 0.3 %collective-permute-start.5 = (f32[4,24,128]{2,1,0:T(8,128)S(1)}, f32[4,24,128]{2,1,0:T(8,128)S(1)}, u32[]{:S(2)}, u32[]{:S(2)}) collective-permute-start(f32[4,24,128]{2,1,0:T(8,128)S(1)} %get-tuple-element.27), channel_id=1, source_target_pairs={{0,8},{8,0},{16,24},{24,16},{1,9},{9,1},{17,25},{25,17},{2,10},{10... | collective-permute-start | bytes 147464 | tf_op jit(solution)/shard_map/ppermute | solution.py:379
  12.4 1.0 %collective-permute-done.5 = f32[4,24,128]{2,1,0:T(8,128)S(1)} collective-permute-done((f32[4,24,128]{2,1,0:T(8,128)S(1)}, f32[4,24,128]{2,1,0:T(8,128)S(1)}, u32[]{:S(2)}, u32[]{:S(2)}) %collective-permute-start.5) | collective-permute-done | bytes 49184 | tf_op jit(solution)/shard_map/ppermute | solution.py:379
  13.5 3.0 %collective-permute-start.6 = (f32[2,24,128]{2,1,0:T(8,128)S(1)}, f32[2,24,128]{2,1,0:T(8,128)S(1)}, u32[]{:S(2)}, u32[]{:S(2)}) collective-permute-start(f32[2,24,128]{2,1,0:T(8,128)S(1)} %slice.9), channel_id=1, source_target_pairs={{14,0},{8,2},{10,4},{12,6},{6,8},{0,10},{2,12},{4,14},{30,16},{24,... | collective-permute-start | bytes 73736 | tf_op jit(solution)/shard_map/ppermute | solution.py:359
  16.4 2.1 %collective-permute-done.6 = f32[2,24,128]{2,1,0:T(8,128)S(1)} collective-permute-done((f32[2,24,128]{2,1,0:T(8,128)S(1)}, f32[2,24,128]{2,1,0:T(8,128)S(1)}, u32[]{:S(2)}, u32[]{:S(2)}) %collective-permute-start.6) | collective-permute-done | bytes 24608 | tf_op jit(solution)/shard_map/ppermute | solution.py:359
  18.6 0.7 %collective-permute-start.7 = (f32[2,24,128]{2,1,0:T(8,128)S(1)}, f32[2,24,128]{2,1,0:T(8,128)S(1)}, u32[]{:S(2)}, u32[]{:S(2)}) collective-permute-start(f32[2,24,128]{2,1,0:T(8,128)S(1)} %slice_add_fusion.refs_0_), channel_id=1, source_target_pairs={{24,0},{25,1},{16,8},{17,9},{8,16},{9,17},{0,24},{1,25},{26,2},{27... | collective-permute-start | bytes 73736 | tf_op jit(solution)/shard_map/ppermute | solution.py:359
  19.3 1.5 %collective-permute-start.8 = (f32[2,24,128]{2,1,0:T(8,128)S(1)}, f32[2,24,128]{2,1,0:T(8,128)S(1)}, u32[]{:S(2)}, u32[]{:S(2)}) collective-permute-start(f32[2,24,128]{2,1,0:T(8,128)S(1)} %slice_add_fusion.refs_0_), channel_id=1, source_target_pairs={{9,0},{8,1},{1,8},{0,9},{25,16},{24,17},{17,24},{16,25},{11,2},{10... | collective-permute-start | bytes 73736 | tf_op jit(solution)/shard_map/ppermute | solution.py:359
  20.7 0.9 %collective-permute-start.9 = (f32[2,24,128]{2,1,0:T(8,128)S(1)}, f32[2,24,128]{2,1,0:T(8,128)S(1)}, u32[]{:S(2)}, u32[]{:S(2)}) collective-permute-start(f32[2,24,128]{2,1,0:T(8,128)S(1)} %slice_add_fusion.refs_0_), channel_id=1, source_target_pairs={{25,0},{24,1},{17,8},{16,9},{9,16},{8,17},{1,24},{0,25},{27,2},{26... | collective-permute-start | bytes 73736 | tf_op jit(solution)/shard_map/ppermute | solution.py:359
  21.6 1.9 %advance.1 = f32[22,128,128]{2,1,0:T(8,128)} custom-call(f32[128,24,128]{2,1,0:T(8,128)S(1)} %get-tuple-element.16.advanced, f32[2,16,24,128]{3,2,1,0:T(8,128)S(1)} %get-tuple-element.24.dx, f32[2,8,24,128]{3,2,1,0:T(8,128)S(1)} %get-tuple-element.25.dy, f32[2,24,128]{2,1,0:T(8,128)S(1)} %get-tuple-element.26.dz), custom_call_target="tpu_custom_call" | custom-call | flops 1000000 | bytes 3000000 | tf_op jit(solution)/shard_map/advance/pallas_call | solution.py:467
  23.5 0.0 collective-permute-done.7.refs_1_
  23.5 0.0 collective-permute-done.8.refs_2_
  23.5 1.4 %collective-permute-done.9.refs_3_ = f32[2,24,128]{2,1,0:T(8,128)S(1)} collective-permute-done((f32[2,24,128]{2,1,0:T(8,128)S(1)}, f32[2,24,128]{2,1,0:T(8,128)S(1)}, u32[]{:S(2)}, u32[]{:S(2)}) %collective-permute-start.9) | collective-permute-done | bytes 24608 | tf_op jit(solution)/shard_map/ppermute | solution.py:359
  24.9 0.7 %means.1 = f32[22,4,64]{2,1,0:T(4,128)} custom-call(f32[2,24,128]{2,1,0:T(8,128)S(1)} %slice_add_fusion.refs_0_, f32[2,24,128]{2,1,0:T(8,128)S(1)} %collective-permute-done.7.refs_1_, f32[2,24,128]{2,1,0:T(8,128)S(1)} %collective-permute-done.8.refs_2_, f32[2,24,128]{2,1,0:T(8,128)S(1)} %collective-permute-done.9.refs_3_), custom_call_target="tpu_custom_call" | custom-call | tf_op jit(solution)/shard_map/means/pallas_call | solution.py:480
  (3 shorter events, 0.0 us)
Async XLA Ops:
  0.6 8.1 %copy-start = (f32[8,16,128]{2,1,0:T(8,128)S(1)}, f32[8,16,128]{2,1,0:T(8,128)}, u32[]{:S(2)}) copy-start(f32[8,16,128]{2,1,0:T(8,128)} %param.8) | copy-start | bytes 196612
  0.6 8.1 %copy-start.1 = (f32[8,16,128]{2,1,0:T(8,128)S(1)}, f32[8,16,128]{2,1,0:T(8,128)}, u32[]{:S(2)}) copy-start(f32[8,16,128]{2,1,0:T(8,128)} %param.9) | copy-start | bytes 196612
  0.7 8.1 %copy-start.3 = (f32[22]{0:T(128)S(1)}, f32[22]{0:T(128)}, u32[]{:S(2)}) copy-start(f32[22]{0:T(128)} %param.10) | copy-start | bytes 268
  0.7 8.1 %copy-start.2 = (f32[22,22]{1,0:T(8,128)S(1)}, f32[22,22]{1,0:T(8,128)}, u32[]{:S(2)}) copy-start(f32[22,22]{1,0:T(8,128)} %jacobian.1) | copy-start | bytes 5812
  0.7 10.7 %copy-start.4 = (s32[32]{0:T(128)S(1)}, s32[32]{0:T(128)}, u32[]{:S(2)}) copy-start(s32[32]{0:T(128)} %param.13) | copy-start | bytes 388
  2.5 8.8 %collective-permute-start = (f32[16,24,128]{2,1,0:T(8,128)S(1)}, f32[16,24,128]{2,1,0:T(8,128)S(1)}, u32[]{:S(2)}, u32[]{:S(2)}) collective-permute-start(f32[16,24,128]{2,1,0:T(8,128)S(1)} %get-tuple-element.19), channel_id=1, source_target_pairs={{0,2},{2,0},{4,6},{6,4},{1,3},{3,1},{5,7},{7,5},{8,10},{10,8},{12,... | collective-permute-start | bytes 589832 | tf_op jit(solution)/shard_map/ppermute | solution.py:365
  5.6 5.8 %collective-permute-start.1 = (f32[16,24,128]{2,1,0:T(8,128)S(1)}, f32[16,24,128]{2,1,0:T(8,128)S(1)}, u32[]{:S(2)}, u32[]{:S(2)}) collective-permute-start(f32[16,24,128]{2,1,0:T(8,128)S(1)} %get-tuple-element.20), channel_id=1, source_target_pairs={{8,0},{4,2},{2,4},{14,6},{0,8},{12,10},{10,12},{6,14},{24,16},{20,... | collective-permute-start | bytes 589832 | tf_op jit(solution)/shard_map/ppermute | solution.py:359
  5.6 5.7 %collective-permute-start.2 = (f32[8,24,128]{2,1,0:T(8,128)S(1)}, f32[8,24,128]{2,1,0:T(8,128)S(1)}, u32[]{:S(2)}, u32[]{:S(2)}) collective-permute-start(f32[8,24,128]{2,1,0:T(8,128)S(1)} %get-tuple-element.21), channel_id=1, source_target_pairs={{0,1},{1,0},{2,3},{3,2},{4,5},{5,4},{6,7},{7,6},{8,9},{9,8},{10,11... | collective-permute-start | bytes 294920 | tf_op jit(solution)/shard_map/ppermute | solution.py:365
  7.1 4.2 %collective-permute-start.3 = (f32[24,128]{1,0:T(8,128)S(1)}, f32[24,128]{1,0:T(8,128)S(1)}, u32[]{:S(2)}, u32[]{:S(2)}) collective-permute-start(f32[24,128]{1,0:T(8,128)S(1)} %get-tuple-element.22), channel_id=1, source_target_pairs={{0,8},{8,0},{16,24},{24,16},{1,9},{9,1},{17,25},{25,17},{2,10},{10... | collective-permute-start | bytes 36872 | tf_op jit(solution)/shard_map/ppermute | solution.py:365
  7.3 4.0 %collective-permute-start.4 = (f32[24,128]{1,0:T(8,128)S(1)}, f32[24,128]{1,0:T(8,128)S(1)}, u32[]{:S(2)}, u32[]{:S(2)}) collective-permute-start(f32[24,128]{1,0:T(8,128)S(1)} %get-tuple-element.23), channel_id=1, source_target_pairs={{8,16},{16,8},{0,24},{24,0},{9,17},{17,9},{1,25},{25,1},{10,18},{1... | collective-permute-start | bytes 36872 | tf_op jit(solution)/shard_map/ppermute | solution.py:368
  12.1 1.3 %collective-permute-start.5 = (f32[4,24,128]{2,1,0:T(8,128)S(1)}, f32[4,24,128]{2,1,0:T(8,128)S(1)}, u32[]{:S(2)}, u32[]{:S(2)}) collective-permute-start(f32[4,24,128]{2,1,0:T(8,128)S(1)} %get-tuple-element.27), channel_id=1, source_target_pairs={{0,8},{8,0},{16,24},{24,16},{1,9},{9,1},{17,25},{25,17},{2,10},{10... | collective-permute-start | bytes 147464 | tf_op jit(solution)/shard_map/ppermute | solution.py:379
  13.5 5.1 %collective-permute-start.6 = (f32[2,24,128]{2,1,0:T(8,128)S(1)}, f32[2,24,128]{2,1,0:T(8,128)S(1)}, u32[]{:S(2)}, u32[]{:S(2)}) collective-permute-start(f32[2,24,128]{2,1,0:T(8,128)S(1)} %slice.9), channel_id=1, source_target_pairs={{14,0},{8,2},{10,4},{12,6},{6,8},{0,10},{2,12},{4,14},{30,16},{24,... | collective-permute-start | bytes 73736 | tf_op jit(solution)/shard_map/ppermute | solution.py:359
  18.6 4.9 %collective-permute-start.7 = (f32[2,24,128]{2,1,0:T(8,128)S(1)}, f32[2,24,128]{2,1,0:T(8,128)S(1)}, u32[]{:S(2)}, u32[]{:S(2)}) collective-permute-start(f32[2,24,128]{2,1,0:T(8,128)S(1)} %slice_add_fusion.refs_0_), channel_id=1, source_target_pairs={{24,0},{25,1},{16,8},{17,9},{8,16},{9,17},{0,24},{1,25},{26,2},{27... | collective-permute-start | bytes 73736 | tf_op jit(solution)/shard_map/ppermute | solution.py:359
  19.3 4.2 %collective-permute-start.8 = (f32[2,24,128]{2,1,0:T(8,128)S(1)}, f32[2,24,128]{2,1,0:T(8,128)S(1)}, u32[]{:S(2)}, u32[]{:S(2)}) collective-permute-start(f32[2,24,128]{2,1,0:T(8,128)S(1)} %slice_add_fusion.refs_0_), channel_id=1, source_target_pairs={{9,0},{8,1},{1,8},{0,9},{25,16},{24,17},{17,24},{16,25},{11,2},{10... | collective-permute-start | bytes 73736 | tf_op jit(solution)/shard_map/ppermute | solution.py:359
  20.7 4.2 %collective-permute-start.9 = (f32[2,24,128]{2,1,0:T(8,128)S(1)}, f32[2,24,128]{2,1,0:T(8,128)S(1)}, u32[]{:S(2)}, u32[]{:S(2)}) collective-permute-start(f32[2,24,128]{2,1,0:T(8,128)S(1)} %slice_add_fusion.refs_0_), channel_id=1, source_target_pairs={{25,0},{24,1},{17,8},{16,9},{9,16},{8,17},{1,24},{0,25},{27,2},{26... | collective-permute-start | bytes 73736 | tf_op jit(solution)/shard_map/ppermute | solution.py:359

commit v5 on v4

--- a/solution.py
+++ b/solution.py
@@ -54,68 +54,75 @@
     return product[:rows] + product[rows:]
 
 
-def pack_kernel(planes, has_b, cells, mixing, classes, *refs):
-    outs, (bins, sem, field_sem) = refs[:-3], refs[-3:]
-    rows_out, own_z = outs[0], outs[1]
-    faces = list(outs[2:])
+def gx_face_kernel(planes, both, cells, mixing, *refs):
+    faces, sem = refs[:-1], refs[-1]
+    species, row_count, _ = cells.shape
+    width = row_count // planes
+    even = lax.axis_index("gx") % 2 == 0
+    for side in range(1 + both):
+        upper = even if side == 0 else jnp.logical_not(even)
+        start = pl.multiple_of(jnp.where(upper, row_count - width, 0), width)
+        span = pl.ds(start, width)
+        for k in range(species):
+            pltpu.make_async_copy(
+                cells.at[k, span], faces[side].at[:, k, :], sem.at[side]
+            ).start()
+        pltpu.make_async_copy(
+            mixing.at[span], faces[side].at[:, species, :], sem.at[side]
+        ).start()
+    for side in range(1 + both):
+        arrived = faces[side].at[:, pl.ds(0, species + 1), :]
+        pltpu.make_async_copy(arrived, arrived, sem.at[side]).wait()
+
+
+def rows_kernel(planes, has_b, cells, mixing, classes, rows_out, own_z, *refs):
+    faces, (bins, sem) = list(refs[:-2]), refs[-2:]
     species, row_count, depth = cells.shape
     rows = rows_out.shape[1]
     width = row_count // planes
-    chunk = row_count // sem.shape[0]
-    field_copies = [
-        pltpu.make_async_copy(mixing, rows_out.at[:, species, :], field_sem.at[0]),
-        pltpu.make_async_copy(classes, bins, field_sem.at[1]),
+    copies = [
+        pltpu.make_async_copy(mixing, rows_out.at[:, species, :], sem.at[0]),
+        pltpu.make_async_copy(classes, bins, sem.at[1]),
     ]
-    for copy in field_copies:
+    for copy in copies:
         copy.start()
-    for n in range(sem.shape[0]):
-        span = pl.ds(n * chunk, chunk)
-        for k in range(species):
-            pltpu.make_async_copy(
-                cells.at[k, span], rows_out.at[span, k, :], sem.at[n]
-            ).start()
-
+    flat = cells.reshape(species * row_count, depth)
     lane = lanes_of((SUBLANES, depth))
-    zero = jnp.zeros((SUBLANES, depth), F32)
-
-    def gathered(groups, span, low, high):
-        low, high = list(low), list(high)
-        for r in span:
-            at, before = lane == r, lane == (r - 1) % depth
-            for i, g in enumerate(groups):
-                block = rows_out[r, pl.ds(g, SUBLANES), :]
-                turned = pltpu.roll(block, r, axis=1) if r else block
-                low[i] = jnp.where(at, turned, low[i])
-                high[i] = jnp.where(before, turned, high[i])
-        return low, high
-
-    whole = species // SUBLANES * SUBLANES
-    first = range(0, whole, SUBLANES)
-    rest = range(whole, rows, SUBLANES)
-    low, high = [zero] * len(first), [zero] * len(first)
-    for n in range(sem.shape[0]):
-        arrived = rows_out.at[pl.ds(n * chunk, chunk), pl.ds(0, species), :]
-        pltpu.make_async_copy(arrived, arrived, sem.at[n]).wait()
-        low, high = gathered(first, range(n * chunk, (n + 1) * chunk), low, high)
-    for copy in field_copies:
+    groups = range(0, rows, SUBLANES)
+    low = [jnp.zeros((SUBLANES, depth), F32)] * len(groups)
+    high = list(low)
+
+    def gather(i, r, block):
+        turned = pltpu.roll(block, r, axis=1) if r else block
+        low[i] = jnp.where(lane == r, turned, low[i])
+        high[i] = jnp.where(lane == (r - 1) % depth, turned, high[i])
+
+    for r in range(row_count):
+        for i, g in enumerate(groups):
+            count = max(0, min(SUBLANES, species - g))
+            if count:
+                block = flat[pl.ds(g * row_count + r, count, stride=row_count), :]
+                rows_out[r, pl.ds(g, count), :] = block
+            if count == SUBLANES:
+                gather(i, r, block)
+    for copy in copies:
         copy.wait()
     for r in range(0, row_count, SUBLANES):
         span = pl.ds(r, SUBLANES)
         rows_out[span, species + 1, :] = bins[span, :].astype(F32)
-    lows, highs = gathered(rest, range(row_count), [zero] * len(rest), [zero] * len(rest))
-    for i, g in enumerate([*first, *rest]):
-        own_z[0, pl.ds(g, SUBLANES), :] = (low + lows)[i]
-        own_z[1, pl.ds(g, SUBLANES), :] = pltpu.roll((high + highs)[i], 1, axis=1)
-    for axis, both in zip(("gx", "gy", "sec"), has_b):
+    for i, g in enumerate(groups):
+        if species - g < SUBLANES:
+            for r in range(row_count):
+                gather(i, r, rows_out[r, pl.ds(g, SUBLANES), :])
+    for i, g in enumerate(groups):
+        own_z[0, pl.ds(g, SUBLANES), :] = low[i]
+        own_z[1, pl.ds(g, SUBLANES), :] = pltpu.roll(high[i], 1, axis=1)
+    for axis, both in zip(("gy", "sec"), has_b):
         even = lax.axis_index(axis) % 2 == 0
         for side in range(1 + both):
             out = faces.pop(0)
             upper = even if side == 0 else jnp.logical_not(even)
-            if axis == "gx":
-                start = jnp.where(upper, row_count - width, 0)
-                for y in range(width):
-                    out[y] = rows_out[start + y]
-            elif axis == "gy":
+            if axis == "gy":
                 start = jnp.where(upper, width - 1, 0)
                 for x in range(planes):
                     out[x] = rows_out[start + x * width]
@@ -419,20 +426,35 @@
     ]
     face_shapes = [struct(*shapes[axis]) for axis, _ in sides]
 
-    packed = call(
-        functools.partial(pack_kernel, planes, has_b),
-        "faces",
-        [struct(row_count, rows, depth), struct(2, rows, row_count), *face_shapes],
+    in_hbm = [pltpu.with_memory_space_constraint(x, pltpu.HBM) for x in (cells, mixing)]
+    gx_faces = call(
+        functools.partial(gx_face_kernel, planes, has_b[0]),
+        "outer_planes",
+        [shape for shape, (axis, _) in zip(face_shapes, sides) if axis == "gx"],
+        2,
+        [VMEM] * (1 + has_b[0]),
+        in_specs=[ANY] * 2,
+        scratch=[pltpu.SemaphoreType.DMA((2,))],
+    )(*in_hbm)
+    rows_in, own_z, *faces = call(
+        functools.partial(rows_kernel, planes, has_b[1:]),
+        "rows",
+        [
+            struct(row_count, rows, depth),
+            struct(2, rows, row_count),
+            *[shape for shape, (axis, _) in zip(face_shapes, sides) if axis != "gx"],
+        ],
         3,
-        [VMEM] * (2 + len(sides)),
-        in_specs=[ANY] * 3,
+        [VMEM] * (2 + len(sides) - len(gx_faces)),
+        in_specs=[VMEM, ANY, ANY],
         scratch=[
             pltpu.VMEM((row_count, depth), jnp.int32),
-            pltpu.SemaphoreType.DMA((planes // 2,)),
             pltpu.SemaphoreType.DMA((2,)),
         ],
-    )(*[pltpu.with_memory_space_constraint(x, pltpu.HBM) for x in (cells, mixing, classes)])
-    rows_in, own_z, faces = packed[0], packed[1], packed[2:]
+        flops=4_000_000,
+        moved=3_000_000,
+    )(cells, in_hbm[1], pltpu.with_memory_space_constraint(classes, pltpu.HBM))
+    faces = [*gx_faces, *faces]
     halos = [swapped(face, axis, side) for face, (axis, side) in zip(faces, sides)]
 
     inner, sums = call(

time: 25.8 us -> 27 us (1.047)
  Pallas kernels: 7.75 us -> 8.82 us
    pallas_call x1 -> x2, Pallas kernels: 1.84 us -> 2.91 us  [the longest x1 1.88 us: on_device(): call(functools.partial(rows_kernel, planes, has_b[1:]), 'rows', [struct(r...]
  transfers between devices with their start and end apart: 10 -> 10, of which waited for: 3 -> 3; matrix products, arithmetic and copies ran while one was open for 0% -> 0% of each run, Pallas kernels for 17% -> 24%
where the time goes in v5:
time: 27 us; the launch traced here: 26.8 us
  starting transfers between devices  12.6 us (47%)
  Pallas kernels  8.82 us (33%)
  waiting for transfers between devices  4.57 us (17%)
  between operations  0.79 us (3%)
    ppermute x5, starting transfers between devices, joint(): return lax.ppermute(block, ('sec', axis), pairs)  5.99 us
    ppermute x3, starting transfers between devices, swapped(): return lax.ppermute(block, axis, [(i, i ^ 1) for i in range(count)])  4.87 us
    ppermute x5, waiting for transfers between devices, joint(): return lax.ppermute(block, ('sec', axis), pairs)  3.53 us
    pallas_call x1, Pallas kernels, on_device(): call(functools.partial(inner_kernel, planes), 'inside', [struct(row_count...  2.55 us
    pallas_call x1, Pallas kernels, on_device(): call(functools.partial(finish_kernel, planes), 'advance', struct(species,...  1.89 us
    pallas_call x1, Pallas kernels, on_device(): call(functools.partial(rows_kernel, planes, has_b[1:]), 'rows', [struct(r...  1.88 us
    ppermute x1, starting transfers between devices, swapped(): return lax.ppermute(block, axis, [*pairs, (0, count - 1), (count - 1, 0)])  1.41 us
    pallas_call x1, Pallas kernels, on_device(): call(functools.partial(gx_face_kernel, planes, has_b[0]), 'outer_planes',...  1.03 us
  transfers between devices with their start and end apart: 10, of which 3 were waited for; matrix products, arithmetic and copies ran while one was open for 0% of the time, Pallas kernels for 24%

profile of v5, /device:TPU:0, one launch (start us, length us, event | category | flops | bytes accessed | tf_op | source)
XLA Modules:
  0.0 26.8 jit_solution(8207091124835436690)
XLA Ops:
  0.6 0.0 copy-start
  0.6 0.0 copy-start.1
  0.7 0.0 copy-start.2
  0.7 0.0 copy-start.4
  0.7 0.0 copy-start.3
  0.7 1.0 %outer_planes.1 = (f32[16,24,128]{2,1,0:T(8,128)S(1)}, f32[16,24,128]{2,1,0:T(8,128)S(1)}) custom-call(f32[22,128,128]{2,1,0:T(8,128)} %bitcast.7, f32[128,128]{1,0:T(8,128)} %bitcast.9), custom_call_target="tpu_custom_call" | custom-call | tf_op jit(solution)/shard_map/outer_planes/pallas_call | solution.py:430
  1.7 3.1 %collective-permute-start = (f32[16,24,128]{2,1,0:T(8,128)S(1)}, f32[16,24,128]{2,1,0:T(8,128)S(1)}, u32[]{:S(2)}, u32[]{:S(2)}) collective-permute-start(f32[16,24,128]{2,1,0:T(8,128)S(1)} %get-tuple-element.19), channel_id=1, source_target_pairs={{0,2},{2,0},{4,6},{6,4},{1,3},{3,1},{5,7},{7,5},{8,10},{10,8},{12,... | collective-permute-start | bytes 589832 | tf_op jit(solution)/shard_map/ppermute | solution.py:372
  4.8 0.0 collective-permute-start.1
  4.8 0.0 copy-done
  4.8 0.0 copy-start.5
  4.8 1.9 %rows.1 = (f32[128,24,128]{2,1,0:T(8,128)S(1)}, f32[2,24,128]{2,1,0:T(8,128)S(1)}, f32[8,24,128]{2,1,0:T(8,128)S(1)}, f32[24,128]{1,0:T(8,128)S(1)}, f32[24,128]{1,0:T(8,128)S(1)}) custom-call(f32[22,128,128]{2,1,0:T(8,128)S(1)} %bitcast.8, f32[128,128]{1,0:T(8,128)} %bitcast.10, s32[128,128]{1,0:T(8,128)} %bitcast.17), custom_call_target="tpu_custom_call" | custom-call | flops 4000000 | bytes 3000000 | tf_op jit(solution)/shard_map/rows/pallas_call | solution.py:439
  6.7 1.6 %collective-permute-start.2 = (f32[8,24,128]{2,1,0:T(8,128)S(1)}, f32[8,24,128]{2,1,0:T(8,128)S(1)}, u32[]{:S(2)}, u32[]{:S(2)}) collective-permute-start(f32[8,24,128]{2,1,0:T(8,128)S(1)} %get-tuple-element.21), channel_id=1, source_target_pairs={{0,1},{1,0},{2,3},{3,2},{4,5},{5,4},{6,7},{7,6},{8,9},{9,8},{10,11... | collective-permute-start | bytes 294920 | tf_op jit(solution)/shard_map/ppermute | solution.py:372
  8.3 0.2 collective-permute-start.3
  8.5 1.4 %collective-permute-start.4 = (f32[24,128]{1,0:T(8,128)S(1)}, f32[24,128]{1,0:T(8,128)S(1)}, u32[]{:S(2)}, u32[]{:S(2)}) collective-permute-start(f32[24,128]{1,0:T(8,128)S(1)} %get-tuple-element.23), channel_id=1, source_target_pairs={{8,16},{16,8},{0,24},{24,0},{9,17},{17,9},{1,25},{25,1},{10,18},{1... | collective-permute-start | bytes 36872 | tf_op jit(solution)/shard_map/ppermute | solution.py:375
  9.9 0.0 copy-done.1
  9.9 0.0 copy-done.2
  9.9 0.0 copy-done.4
  9.9 0.0 copy-done.3
  9.9 2.5 %inside.1 = (f32[128,24,128]{2,1,0:T(8,128)S(1)}, f32[5,24,64]{2,1,0:T(8,128)S(1)}) custom-call(f32[128,24,128]{2,1,0:T(8,128)S(1)} %get-tuple-element.15.cells, f32[128,128]{1,0:T(8,128)S(1)} %bitcast.11, f32[128,128]{1,0:T(8,128)S(1)} %bitcast.12, f32[1,22]{1,0:T(1,128)S(1)} %bitcast.13, f32[22,22]{1,0:T(8,128)S(1)} %copy-done.3), custom_call_target="tpu_custom_call" | custom-call | flops 10000000 | bytes 4000000 | tf_op jit(solution)/shard_map/inside/pallas_call | solution.py:460
  12.5 0.0 collective-permute-done.3.refs_3_
  12.5 0.0 collective-permute-done.4.refs_4_
  12.5 0.0 collective-permute-done.2.refs_2_
  12.5 0.0 collective-permute-done.refs_0_
  12.5 0.0 collective-permute-done.1.refs_1_
  12.5 0.0 copy-done.5
  12.5 0.7 %edges.1 = (f32[4,24,128]{2,1,0:T(8,128)S(1)}, f32[2,16,24,128]{3,2,1,0:T(8,128)S(1)}, f32[2,8,24,128]{3,2,1,0:T(8,128)S(1)}, f32[2,24,128]{2,1,0:T(8,128)S(1)}) custom-call(f32[128,24,128]{2,1,0:T(8,128)S(1)} %get-tuple-element.15.cells, f32[2,24,128]{2,1,0:T(8,128)S(1)} %get-tuple-element.17.own_z, f32[5,24,64]{2,1,0:T(8,128)S(1)} %get-tuple-element.18.sums, ...), custom_call_target="tpu_custom_call" | custom-call | tf_op jit(solution)/shard_map/edges/pallas_call | solution.py:474
  13.3 0.3 %collective-permute-start.5 = (f32[4,24,128]{2,1,0:T(8,128)S(1)}, f32[4,24,128]{2,1,0:T(8,128)S(1)}, u32[]{:S(2)}, u32[]{:S(2)}) collective-permute-start(f32[4,24,128]{2,1,0:T(8,128)S(1)} %get-tuple-element.27), channel_id=1, source_target_pairs={{0,8},{8,0},{16,24},{24,16},{1,9},{9,1},{17,25},{25,17},{2,10},{10... | collective-permute-start | bytes 147464 | tf_op jit(solution)/shard_map/ppermute | solution.py:386
  13.6 1.0 %collective-permute-done.5 = f32[4,24,128]{2,1,0:T(8,128)S(1)} collective-permute-done((f32[4,24,128]{2,1,0:T(8,128)S(1)}, f32[4,24,128]{2,1,0:T(8,128)S(1)}, u32[]{:S(2)}, u32[]{:S(2)}) %collective-permute-start.5) | collective-permute-done | bytes 49184 | tf_op jit(solution)/shard_map/ppermute | solution.py:386
  14.6 3.0 %collective-permute-start.6 = (f32[2,24,128]{2,1,0:T(8,128)S(1)}, f32[2,24,128]{2,1,0:T(8,128)S(1)}, u32[]{:S(2)}, u32[]{:S(2)}) collective-permute-start(f32[2,24,128]{2,1,0:T(8,128)S(1)} %slice.9), channel_id=1, source_target_pairs={{14,0},{8,2},{10,4},{12,6},{6,8},{0,10},{2,12},{4,14},{30,16},{24,... | collective-permute-start | bytes 73736 | tf_op jit(solution)/shard_map/ppermute | solution.py:366
  17.6 2.1 %collective-permute-done.6 = f32[2,24,128]{2,1,0:T(8,128)S(1)} collective-permute-done((f32[2,24,128]{2,1,0:T(8,128)S(1)}, f32[2,24,128]{2,1,0:T(8,128)S(1)}, u32[]{:S(2)}, u32[]{:S(2)}) %collective-permute-start.6) | collective-permute-done | bytes 24608 | tf_op jit(solution)/shard_map/ppermute | solution.py:366
  19.7 0.7 %collective-permute-start.7 = (f32[2,24,128]{2,1,0:T(8,128)S(1)}, f32[2,24,128]{2,1,0:T(8,128)S(1)}, u32[]{:S(2)}, u32[]{:S(2)}) collective-permute-start(f32[2,24,128]{2,1,0:T(8,128)S(1)} %slice_add_fusion.refs_0_), channel_id=1, source_target_pairs={{24,0},{25,1},{16,8},{17,9},{8,16},{9,17},{0,24},{1,25},{26,2},{27... | collective-permute-start | bytes 73736 | tf_op jit(solution)/shard_map/ppermute | solution.py:366
  20.4 1.5 %collective-permute-start.8 = (f32[2,24,128]{2,1,0:T(8,128)S(1)}, f32[2,24,128]{2,1,0:T(8,128)S(1)}, u32[]{:S(2)}, u32[]{:S(2)}) collective-permute-start(f32[2,24,128]{2,1,0:T(8,128)S(1)} %slice_add_fusion.refs_0_), channel_id=1, source_target_pairs={{9,0},{8,1},{1,8},{0,9},{25,16},{24,17},{17,24},{16,25},{11,2},{10... | collective-permute-start | bytes 73736 | tf_op jit(solution)/shard_map/ppermute | solution.py:366
  21.9 0.9 %collective-permute-start.9 = (f32[2,24,128]{2,1,0:T(8,128)S(1)}, f32[2,24,128]{2,1,0:T(8,128)S(1)}, u32[]{:S(2)}, u32[]{:S(2)}) collective-permute-start(f32[2,24,128]{2,1,0:T(8,128)S(1)} %slice_add_fusion.refs_0_), channel_id=1, source_target_pairs={{25,0},{24,1},{17,8},{16,9},{9,16},{8,17},{1,24},{0,25},{27,2},{26... | collective-permute-start | bytes 73736 | tf_op jit(solution)/shard_map/ppermute | solution.py:366
  22.7 1.9 %advance.1 = f32[22,128,128]{2,1,0:T(8,128)} custom-call(f32[128,24,128]{2,1,0:T(8,128)S(1)} %get-tuple-element.16.advanced, f32[2,16,24,128]{3,2,1,0:T(8,128)S(1)} %get-tuple-element.24.dx, f32[2,8,24,128]{3,2,1,0:T(8,128)S(1)} %get-tuple-element.25.dy, f32[2,24,128]{2,1,0:T(8,128)S(1)} %get-tuple-element.26.dz), custom_call_target="tpu_custom_call" | custom-call | flops 1000000 | bytes 3000000 | tf_op jit(solution)/shard_map/advance/pallas_call | solution.py:489
  24.6 0.0 collective-permute-done.7.refs_1_
  24.6 0.0 collective-permute-done.8.refs_2_
  24.7 1.4 %collective-permute-done.9.refs_3_ = f32[2,24,128]{2,1,0:T(8,128)S(1)} collective-permute-done((f32[2,24,128]{2,1,0:T(8,128)S(1)}, f32[2,24,128]{2,1,0:T(8,128)S(1)}, u32[]{:S(2)}, u32[]{:S(2)}) %collective-permute-start.9) | collective-permute-done | bytes 24608 | tf_op jit(solution)/shard_map/ppermute | solution.py:366
  26.0 0.7 %means.1 = f32[22,4,64]{2,1,0:T(4,128)} custom-call(f32[2,24,128]{2,1,0:T(8,128)S(1)} %slice_add_fusion.refs_0_, f32[2,24,128]{2,1,0:T(8,128)S(1)} %collective-permute-done.7.refs_1_, f32[2,24,128]{2,1,0:T(8,128)S(1)} %collective-permute-done.8.refs_2_, f32[2,24,128]{2,1,0:T(8,128)S(1)} %collective-permute-done.9.refs_3_), custom_call_target="tpu_custom_call" | custom-call | tf_op jit(solution)/shard_map/means/pallas_call | solution.py:502
  (3 shorter events, 0.0 us)
Async XLA Ops:
  0.6 4.2 %copy-start = (f32[22,8,16,128]{3,2,1,0:T(8,128)S(1)}, f32[22,8,16,128]{3,2,1,0:T(8,128)}, u32[]{:S(2)}) copy-start(f32[22,8,16,128]{3,2,1,0:T(8,128)} %param.7) | copy-start | bytes 4325380
  0.6 9.3 %copy-start.1 = (f32[8,16,128]{2,1,0:T(8,128)S(1)}, f32[8,16,128]{2,1,0:T(8,128)}, u32[]{:S(2)}) copy-start(f32[8,16,128]{2,1,0:T(8,128)} %param.8) | copy-start | bytes 196612
  0.7 9.2 %copy-start.2 = (f32[8,16,128]{2,1,0:T(8,128)S(1)}, f32[8,16,128]{2,1,0:T(8,128)}, u32[]{:S(2)}) copy-start(f32[8,16,128]{2,1,0:T(8,128)} %param.9) | copy-start | bytes 196612
  0.7 9.2 %copy-start.4 = (f32[22]{0:T(128)S(1)}, f32[22]{0:T(128)}, u32[]{:S(2)}) copy-start(f32[22]{0:T(128)} %param.10) | copy-start | bytes 268
  0.7 9.2 %copy-start.3 = (f32[22,22]{1,0:T(8,128)S(1)}, f32[22,22]{1,0:T(8,128)}, u32[]{:S(2)}) copy-start(f32[22,22]{1,0:T(8,128)} %jacobian.1) | copy-start | bytes 5812
  1.7 10.8 %collective-permute-start = (f32[16,24,128]{2,1,0:T(8,128)S(1)}, f32[16,24,128]{2,1,0:T(8,128)S(1)}, u32[]{:S(2)}, u32[]{:S(2)}) collective-permute-start(f32[16,24,128]{2,1,0:T(8,128)S(1)} %get-tuple-element.19), channel_id=1, source_target_pairs={{0,2},{2,0},{4,6},{6,4},{1,3},{3,1},{5,7},{7,5},{8,10},{10,8},{12,... | collective-permute-start | bytes 589832 | tf_op jit(solution)/shard_map/ppermute | solution.py:372
  4.8 7.7 %collective-permute-start.1 = (f32[16,24,128]{2,1,0:T(8,128)S(1)}, f32[16,24,128]{2,1,0:T(8,128)S(1)}, u32[]{:S(2)}, u32[]{:S(2)}) collective-permute-start(f32[16,24,128]{2,1,0:T(8,128)S(1)} %get-tuple-element.20), channel_id=1, source_target_pairs={{8,0},{4,2},{2,4},{14,6},{0,8},{12,10},{10,12},{6,14},{24,16},{20,... | collective-permute-start | bytes 589832 | tf_op jit(solution)/shard_map/ppermute | solution.py:366
  4.8 7.7 %copy-start.5 = (s32[32]{0:T(128)S(1)}, s32[32]{0:T(128)}, u32[]{:S(2)}) copy-start(s32[32]{0:T(128)} %param.13) | copy-start | bytes 388
  6.7 5.8 %collective-permute-start.2 = (f32[8,24,128]{2,1,0:T(8,128)S(1)}, f32[8,24,128]{2,1,0:T(8,128)S(1)}, u32[]{:S(2)}, u32[]{:S(2)}) collective-permute-start(f32[8,24,128]{2,1,0:T(8,128)S(1)} %get-tuple-element.21), channel_id=1, source_target_pairs={{0,1},{1,0},{2,3},{3,2},{4,5},{5,4},{6,7},{7,6},{8,9},{9,8},{10,11... | collective-permute-start | bytes 294920 | tf_op jit(solution)/shard_map/ppermute | solution.py:372
  8.3 4.2 %collective-permute-start.3 = (f32[24,128]{1,0:T(8,128)S(1)}, f32[24,128]{1,0:T(8,128)S(1)}, u32[]{:S(2)}, u32[]{:S(2)}) collective-permute-start(f32[24,128]{1,0:T(8,128)S(1)} %get-tuple-element.22), channel_id=1, source_target_pairs={{0,8},{8,0},{16,24},{24,16},{1,9},{9,1},{17,25},{25,17},{2,10},{10... | collective-permute-start | bytes 36872 | tf_op jit(solution)/shard_map/ppermute | solution.py:372
  8.5 4.0 %collective-permute-start.4 = (f32[24,128]{1,0:T(8,128)S(1)}, f32[24,128]{1,0:T(8,128)S(1)}, u32[]{:S(2)}, u32[]{:S(2)}) collective-permute-start(f32[24,128]{1,0:T(8,128)S(1)} %get-tuple-element.23), channel_id=1, source_target_pairs={{8,16},{16,8},{0,24},{24,0},{9,17},{17,9},{1,25},{25,1},{10,18},{1... | collective-permute-start | bytes 36872 | tf_op jit(solution)/shard_map/ppermute | solution.py:375
  13.3 1.3 %collective-permute-start.5 = (f32[4,24,128]{2,1,0:T(8,128)S(1)}, f32[4,24,128]{2,1,0:T(8,128)S(1)}, u32[]{:S(2)}, u32[]{:S(2)}) collective-permute-start(f32[4,24,128]{2,1,0:T(8,128)S(1)} %get-tuple-element.27), channel_id=1, source_target_pairs={{0,8},{8,0},{16,24},{24,16},{1,9},{9,1},{17,25},{25,17},{2,10},{10... | collective-permute-start | bytes 147464 | tf_op jit(solution)/shard_map/ppermute | solution.py:386
  14.6 5.1 %collective-permute-start.6 = (f32[2,24,128]{2,1,0:T(8,128)S(1)}, f32[2,24,128]{2,1,0:T(8,128)S(1)}, u32[]{:S(2)}, u32[]{:S(2)}) collective-permute-start(f32[2,24,128]{2,1,0:T(8,128)S(1)} %slice.9), channel_id=1, source_target_pairs={{14,0},{8,2},{10,4},{12,6},{6,8},{0,10},{2,12},{4,14},{30,16},{24,... | collective-permute-start | bytes 73736 | tf_op jit(solution)/shard_map/ppermute | solution.py:366
  19.7 4.9 %collective-permute-start.7 = (f32[2,24,128]{2,1,0:T(8,128)S(1)}, f32[2,24,128]{2,1,0:T(8,128)S(1)}, u32[]{:S(2)}, u32[]{:S(2)}) collective-permute-start(f32[2,24,128]{2,1,0:T(8,128)S(1)} %slice_add_fusion.refs_0_), channel_id=1, source_target_pairs={{24,0},{25,1},{16,8},{17,9},{8,16},{9,17},{0,24},{1,25},{26,2},{27... | collective-permute-start | bytes 73736 | tf_op jit(solution)/shard_map/ppermute | solution.py:366
  20.4 4.2 %collective-permute-start.8 = (f32[2,24,128]{2,1,0:T(8,128)S(1)}, f32[2,24,128]{2,1,0:T(8,128)S(1)}, u32[]{:S(2)}, u32[]{:S(2)}) collective-permute-start(f32[2,24,128]{2,1,0:T(8,128)S(1)} %slice_add_fusion.refs_0_), channel_id=1, source_target_pairs={{9,0},{8,1},{1,8},{0,9},{25,16},{24,17},{17,24},{16,25},{11,2},{10... | collective-permute-start | bytes 73736 | tf_op jit(solution)/shard_map/ppermute | solution.py:366
  21.9 4.2 %collective-permute-start.9 = (f32[2,24,128]{2,1,0:T(8,128)S(1)}, f32[2,24,128]{2,1,0:T(8,128)S(1)}, u32[]{:S(2)}, u32[]{:S(2)}) collective-permute-start(f32[2,24,128]{2,1,0:T(8,128)S(1)} %slice_add_fusion.refs_0_), channel_id=1, source_target_pairs={{25,0},{24,1},{17,8},{16,9},{9,16},{8,17},{1,24},{0,25},{27,2},{26... | collective-permute-start | bytes 73736 | tf_op jit(solution)/shard_map/ppermute | solution.py:366

commit v6 on v5

--- a/solution.py
+++ b/solution.py
@@ -15,6 +15,7 @@
 VMEM = pl.BlockSpec(memory_space=pltpu.VMEM)
 ANY = pl.BlockSpec(memory_space=pl.ANY)
 DT = 0.05
+AHEAD = 2
 
 
 def padded_rows(species):
@@ -41,11 +42,16 @@
     return DT * jnp.sum(spread, axis=1, keepdims=True)
 
 
-def binned(values, classes):
-    shape = (NB, values.shape[1])
-    hits = (classes == rows_of(shape).astype(F32)).astype(F32).astype(BF16)
+def hits(classes):
+    shape = (NB, classes.shape[1])
+    bins = jnp.broadcast_to(classes.astype(BF16), shape)
+    found = bins == rows_of(shape).astype(F32).astype(BF16)
+    return jnp.where(found, jnp.ones((), BF16), jnp.zeros((), BF16))
+
+
+def binned(values, hit):
     return lax.dot_general(
-        values, hits, (((1,), (1,)), ((), ())), preferred_element_type=F32
+        values, hit, (((1,), (1,)), ((), ())), preferred_element_type=F32
     )
 
 
@@ -54,8 +60,8 @@
     return product[:rows] + product[rows:]
 
 
-def gx_face_kernel(planes, both, cells, mixing, *refs):
-    faces, sem = refs[:-1], refs[-1]
+def gx_face_kernel(planes, both, cells, mixing, classes, mixing_out, classes_out, *refs):
+    faces, sem, field_sem = refs[:-2], refs[-2], refs[-1]
     species, row_count, _ = cells.shape
     width = row_count // planes
     even = lax.axis_index("gx") % 2 == 0
@@ -70,50 +76,45 @@
         pltpu.make_async_copy(
             mixing.at[span], faces[side].at[:, species, :], sem.at[side]
         ).start()
+    field_copies = [
+        pltpu.make_async_copy(mixing, mixing_out, field_sem.at[0]),
+        pltpu.make_async_copy(classes, classes_out, field_sem.at[1]),
+    ]
+    for copy in field_copies:
+        copy.start()
     for side in range(1 + both):
         arrived = faces[side].at[:, pl.ds(0, species + 1), :]
         pltpu.make_async_copy(arrived, arrived, sem.at[side]).wait()
-
-
-def rows_kernel(planes, has_b, cells, mixing, classes, rows_out, own_z, *refs):
-    faces, (bins, sem) = list(refs[:-2]), refs[-2:]
+    for copy in field_copies:
+        copy.wait()
+
+
+def rows_kernel(planes, has_b, cells, mixing, classes, rows_out, own_z, *faces):
+    faces = list(faces)
     species, row_count, depth = cells.shape
     rows = rows_out.shape[1]
     width = row_count // planes
-    copies = [
-        pltpu.make_async_copy(mixing, rows_out.at[:, species, :], sem.at[0]),
-        pltpu.make_async_copy(classes, bins, sem.at[1]),
-    ]
-    for copy in copies:
-        copy.start()
+    for r in range(0, row_count, SUBLANES):
+        span = pl.ds(r, SUBLANES)
+        rows_out[span, species, :] = mixing[span, :]
+        rows_out[span, species + 1, :] = classes[span, :].astype(F32)
     flat = cells.reshape(species * row_count, depth)
     lane = lanes_of((SUBLANES, depth))
     groups = range(0, rows, SUBLANES)
     low = [jnp.zeros((SUBLANES, depth), F32)] * len(groups)
     high = list(low)
-
-    def gather(i, r, block):
-        turned = pltpu.roll(block, r, axis=1) if r else block
-        low[i] = jnp.where(lane == r, turned, low[i])
-        high[i] = jnp.where(lane == (r - 1) % depth, turned, high[i])
-
     for r in range(row_count):
+        at, before = lane == r, lane == (r - 1) % depth
         for i, g in enumerate(groups):
             count = max(0, min(SUBLANES, species - g))
             if count:
                 block = flat[pl.ds(g * row_count + r, count, stride=row_count), :]
                 rows_out[r, pl.ds(g, count), :] = block
-            if count == SUBLANES:
-                gather(i, r, block)
-    for copy in copies:
-        copy.wait()
-    for r in range(0, row_count, SUBLANES):
-        span = pl.ds(r, SUBLANES)
-        rows_out[span, species + 1, :] = bins[span, :].astype(F32)
-    for i, g in enumerate(groups):
-        if species - g < SUBLANES:
-            for r in range(row_count):
-                gather(i, r, rows_out[r, pl.ds(g, SUBLANES), :])
+            if count < SUBLANES:
+                block = rows_out[r, pl.ds(g, SUBLANES), :]
+            turned = pltpu.roll(block, r, axis=1) if r else block
+            low[i] = jnp.where(at, turned, low[i])
+            high[i] = jnp.where(before, turned, high[i])
     for i, g in enumerate(groups):
         own_z[0, pl.ds(g, SUBLANES), :] = low[i]
         own_z[1, pl.ds(g, SUBLANES), :] = pltpu.roll(high[i], 1, axis=1)
@@ -168,47 +169,53 @@
     left = square[...].astype(BF16)
 
     weight = jnp.broadcast_to(weight_column(weights, rows), (rows, depth))
-    ones = rows_of((rows, depth)) >= species
+    whole = species // SUBLANES * SUBLANES
+    ones = rows_of((rows - whole, depth)) >= species - whole
     station_sums[...] = jnp.zeros_like(station_sums)
 
-    for x in range(planes):
-        base = x * width
-        below = max(x - 1, 0) * width
-        above = min(x + 1, planes - 1) * width
-        made = jnp.zeros((2 * rows, NB), F32)
-        for first in range(0, width, 2):
-            pair = (first, first + 1)
-            here = [cells[base + y] for y in pair]
-            mixed = folded(
-                jnp.dot(
-                    left,
-                    jnp.concatenate([halves(c) for c in here], axis=1),
-                    preferred_element_type=F32,
-                )
-            )
-            values, classes = [], []
-            for i, y in enumerate(pair):
-                r = base + y
-                c = here[i]
-                at = lambda n: coefs[n, pl.ds(r, 1), :]
-                flux = at(0) * pltpu.roll(c, depth - 1, axis=1)
-                flux += at(1) * pltpu.roll(c, 1, axis=1)
-                if y < width - 1:
-                    flux += at(2) * cells[r + 1]
-                if y > 0:
-                    flux += at(3) * cells[r - 1]
-                if x < planes - 1:
-                    flux += at(4) * cells[above + y]
-                if x > 0:
-                    flux += at(5) * cells[below + y]
-                flux -= at(6) * c
-                new = c + weight * flux + at(7) * mixed[:, i * depth : (i + 1) * depth]
-                new = jnp.where(ones, 1.0, new)
-                advanced[r] = new
-                values.append(halves(new))
-                classes.append(cells[r, species + 1 : species + 2, :])
-            made += binned(jnp.concatenate(values, axis=1), jnp.concatenate(classes, axis=1))
-        station_sums[(x + 1) // 2] += folded(made)
+    def kinetics(pair):
+        wide = jnp.concatenate([halves(cells[r]) for r in pair], axis=1)
+        return folded(jnp.dot(left, wide, preferred_element_type=F32))
+
+    def advance(pair, mixed):
+        values, found = [], []
+        for i, r in enumerate(pair):
+            x, y = divmod(r, width)
+            c = cells[r]
+            at = lambda n: coefs[n, pl.ds(r, 1), :]
+            flux = at(0) * pltpu.roll(c, depth - 1, axis=1)
+            flux += at(1) * pltpu.roll(c, 1, axis=1)
+            if y < width - 1:
+                flux += at(2) * cells[r + 1]
+            if y > 0:
+                flux += at(3) * cells[r - 1]
+            if x < planes - 1:
+                flux += at(4) * cells[r + width]
+            if x > 0:
+                flux += at(5) * cells[r - width]
+            flux -= at(6) * c
+            new = c + weight * flux + at(7) * mixed[:, i * depth : (i + 1) * depth]
+            new = jnp.concatenate([new[:whole], jnp.where(ones, 1.0, new[whole:])], axis=0)
+            advanced[r] = new
+            values.append(halves(new))
+            found.append(hits(cells[r, species + 1 : species + 2, :]))
+        return jnp.concatenate(values, axis=1), jnp.concatenate(found, axis=1)
+
+    pairs = [(r, r + 1) for r in range(0, row_count, 2)]
+    mixed, values, made = {}, {}, 0.0
+    for t in range(len(pairs) + 2 * AHEAD):
+        if t < len(pairs):
+            mixed[t] = kinetics(pairs[t])
+        now = t - AHEAD
+        if 0 <= now < len(pairs):
+            values[now] = advance(pairs[now], mixed.pop(now))
+        last = now - AHEAD
+        if 0 <= last < len(pairs):
+            made += binned(*values.pop(last))
+            x, y = divmod(pairs[last][1], width)
+            if y == width - 1:
+                station_sums[(x + 1) // 2] += folded(made)
+                made = 0.0
 
 
 def edge_kernel(planes, has_b, cells, own_z, sums, weights, positions, *refs):
@@ -252,7 +259,7 @@
                 dx[side, y] = delta
                 values.append(halves(delta))
                 classes.append(cells[r, species + 1 : species + 2, :])
-            made += binned(jnp.concatenate(values, axis=1), jnp.concatenate(classes, axis=1))
+            made += binned(jnp.concatenate(values, axis=1), hits(jnp.concatenate(classes, axis=1)))
         station_sums[(plane + 1) // 2] += folded(made)
     for side in range(2):
         upper = evens["gy"] if side == 0 else jnp.logical_not(evens["gy"])
@@ -262,7 +269,7 @@
             delta = added(cells[r], "gy", side, x)
             dy[side, x] = delta
             station_sums[(x + 1) // 2] += folded(
-                binned(halves(delta), cells[r, species + 1 : species + 2, :])
+                binned(halves(delta), hits(cells[r, species + 1 : species + 2, :]))
             )
     stations = planes // 2 + 1
     lane = lanes_of((1, row_count))
@@ -275,7 +282,7 @@
         value = halves(delta)
         classes = c[species + 1 : species + 2]
         for j in range(stations):
-            station_sums[j] += folded(binned(value, jnp.where(station == j, classes, -1.0)))
+            station_sums[j] += folded(binned(value, hits(jnp.where(station == j, classes, -1.0))))
     shift = jnp.broadcast_to(positions[0:1, 0:1], (rows, NB))
     per_device = planes // 2
     for s in range(0, 2 * per_device, 2):
@@ -426,15 +433,19 @@
     ]
     face_shapes = [struct(*shapes[axis]) for axis, _ in sides]
 
-    in_hbm = [pltpu.with_memory_space_constraint(x, pltpu.HBM) for x in (cells, mixing)]
-    gx_faces = call(
+    in_hbm = [pltpu.with_memory_space_constraint(x, pltpu.HBM) for x in (cells, mixing, classes)]
+    mixing, classes, *gx_faces = call(
         functools.partial(gx_face_kernel, planes, has_b[0]),
         "outer_planes",
-        [shape for shape, (axis, _) in zip(face_shapes, sides) if axis == "gx"],
-        2,
-        [VMEM] * (1 + has_b[0]),
-        in_specs=[ANY] * 2,
-        scratch=[pltpu.SemaphoreType.DMA((2,))],
+        [
+            struct(row_count, depth),
+            jax.ShapeDtypeStruct((row_count, depth), jnp.int32),
+            *[shape for shape, (axis, _) in zip(face_shapes, sides) if axis == "gx"],
+        ],
+        3,
+        [VMEM] * (3 + has_b[0]),
+        in_specs=[ANY] * 3,
+        scratch=[pltpu.SemaphoreType.DMA((2,)), pltpu.SemaphoreType.DMA((2,))],
     )(*in_hbm)
     rows_in, own_z, *faces = call(
         functools.partial(rows_kernel, planes, has_b[1:]),
@@ -446,14 +457,9 @@
         ],
         3,
         [VMEM] * (2 + len(sides) - len(gx_faces)),
-        in_specs=[VMEM, ANY, ANY],
-        scratch=[
-            pltpu.VMEM((row_count, depth), jnp.int32),
-            pltpu.SemaphoreType.DMA((2,)),
-        ],
         flops=4_000_000,
         moved=3_000_000,
-    )(cells, in_hbm[1], pltpu.with_memory_space_constraint(classes, pltpu.HBM))
+    )(cells, mixing, classes)
     faces = [*gx_faces, *faces]
     halos = [swapped(face, axis, side) for face, (axis, side) in zip(faces, sides)]
 

time: 27 us -> 26.4 us (0.978)
  Pallas kernels: 8.82 us -> 8.24 us
    pallas_call x1, Pallas kernels: 1.88 us -> 1.24 us  [on_device(): call(functools.partial(rows_kernel, planes, has_b[1:]), 'rows', [struct(r...]
  transfers between devices with their start and end apart: 10 -> 10, of which waited for: 3 -> 3; matrix products, arithmetic and copies ran while one was open for 0% -> 0% of each run, Pallas kernels for 24% -> 21%
where the time goes in v6:
time: 26.4 us; the launch traced here: 26.3 us
  starting transfers between devices  12.5 us (47%)
  Pallas kernels  8.24 us (31%)
  waiting for transfers between devices  4.7 us (18%)
  between operations  0.77 us (3%)
    ppermute x5, starting transfers between devices, joint(): return lax.ppermute(block, ('sec', axis), pairs)  6.01 us
    ppermute x3, starting transfers between devices, swapped(): return lax.ppermute(block, axis, [(i, i ^ 1) for i in range(count)])  4.82 us
    ppermute x5, waiting for transfers between devices, joint(): return lax.ppermute(block, ('sec', axis), pairs)  3.68 us
    pallas_call x1, Pallas kernels, on_device(): call(functools.partial(inner_kernel, planes), 'inside', [struct(row_count...  2.41 us
    pallas_call x1, Pallas kernels, on_device(): call(functools.partial(finish_kernel, planes), 'advance', struct(species,...  1.89 us
    ppermute x1, starting transfers between devices, swapped(): return lax.ppermute(block, axis, [*pairs, (0, count - 1), (count - 1, 0)])  1.41 us
    pallas_call x1, Pallas kernels, on_device(): call(functools.partial(rows_kernel, planes, has_b[1:]), 'rows', [struct(r...  1.24 us
    pallas_call x1, Pallas kernels, on_device(): call(functools.partial(gx_face_kernel, planes, has_b[0]), 'outer_planes',...  1.23 us
  transfers between devices with their start and end apart: 10, of which 3 were waited for; matrix products, arithmetic and copies ran while one was open for 0% of the time, Pallas kernels for 21%

profile of v6, /device:TPU:0, one launch (start us, length us, event | category | flops | bytes accessed | tf_op | source)
XLA Modules:
  0.0 26.3 jit_solution(6971952511990213086)
XLA Ops:
  0.6 0.0 copy-start
  0.6 0.0 copy-start.1
  0.7 0.0 copy-start.2
  0.7 0.0 copy-start.3
  0.7 1.2 %outer_planes.1 = (f32[128,128]{1,0:T(8,128)S(1)}, s32[128,128]{1,0:T(8,128)S(1)}, f32[16,24,128]{2,1,0:T(8,128)S(1)}, f32[16,24,128]{2,1,0:T(8,128)S(1)}) custom-call(f32[22,128,128]{2,1,0:T(8,128)} %bitcast.7, f32[128,128]{1,0:T(8,128)} %bitcast.14, s32[128,128]{1,0:T(8,128)} %bitcast.15), custom_call_target="tpu_custom_call" | custom-call | tf_op jit(solution)/shard_map/outer_planes/pallas_call | solution.py:437
  1.9 3.1 %collective-permute-start = (f32[16,24,128]{2,1,0:T(8,128)S(1)}, f32[16,24,128]{2,1,0:T(8,128)S(1)}, u32[]{:S(2)}, u32[]{:S(2)}) collective-permute-start(f32[16,24,128]{2,1,0:T(8,128)S(1)} %get-tuple-element.23), channel_id=1, source_target_pairs={{0,2},{2,0},{4,6},{6,4},{1,3},{3,1},{5,7},{7,5},{8,10},{10,8},{12,... | collective-permute-start | bytes 589832 | tf_op jit(solution)/shard_map/ppermute | solution.py:379
  5.0 0.0 collective-permute-start.1
  5.0 0.0 copy-done
  5.0 0.0 copy-start.4
  5.0 1.2 %rows.1 = (f32[128,24,128]{2,1,0:T(8,128)S(1)}, f32[2,24,128]{2,1,0:T(8,128)S(1)}, f32[8,24,128]{2,1,0:T(8,128)S(1)}, f32[24,128]{1,0:T(8,128)S(1)}, f32[24,128]{1,0:T(8,128)S(1)}) custom-call(f32[22,128,128]{2,1,0:T(8,128)S(1)} %bitcast.8, f32[128,128]{1,0:T(8,128)S(1)} %get-tuple-element.17.mixing, s32[128,128]{1,0:T(8,128)S(1)} %get-tuple-element.18.classes), custom_call_target="tpu_custom_call" | custom-call | flops 4000000 | bytes 3000000 | tf_op jit(solution)/shard_map/rows/pallas_call | solution.py:450
  6.2 1.5 %collective-permute-start.2 = (f32[8,24,128]{2,1,0:T(8,128)S(1)}, f32[8,24,128]{2,1,0:T(8,128)S(1)}, u32[]{:S(2)}, u32[]{:S(2)}) collective-permute-start(f32[8,24,128]{2,1,0:T(8,128)S(1)} %get-tuple-element.25), channel_id=1, source_target_pairs={{0,1},{1,0},{2,3},{3,2},{4,5},{5,4},{6,7},{7,6},{8,9},{9,8},{10,11... | collective-permute-start | bytes 294920 | tf_op jit(solution)/shard_map/ppermute | solution.py:379
  7.8 0.2 collective-permute-start.3
  8.0 1.4 %collective-permute-start.4 = (f32[24,128]{1,0:T(8,128)S(1)}, f32[24,128]{1,0:T(8,128)S(1)}, u32[]{:S(2)}, u32[]{:S(2)}) collective-permute-start(f32[24,128]{1,0:T(8,128)S(1)} %get-tuple-element.27), channel_id=1, source_target_pairs={{8,16},{16,8},{0,24},{24,0},{9,17},{17,9},{1,25},{25,1},{10,18},{1... | collective-permute-start | bytes 36872 | tf_op jit(solution)/shard_map/ppermute | solution.py:382
  9.4 0.0 copy-done.1
  9.4 0.0 copy-done.2
  9.4 0.0 copy-done.3
  9.4 2.4 %inside.1 = (f32[128,24,128]{2,1,0:T(8,128)S(1)}, f32[5,24,64]{2,1,0:T(8,128)S(1)}) custom-call(f32[128,24,128]{2,1,0:T(8,128)S(1)} %get-tuple-element.19.cells, f32[128,128]{1,0:T(8,128)S(1)} %get-tuple-element.17.mixing, f32[128,128]{1,0:T(8,128)S(1)} %bitcast.9, f32[1,22]{1,0:T(1,128)S(1)} %bitcast.10, f32[22,22]{1,0:T(8,128)S(1)} %copy-done.2), custom_call_target="tpu_custom_call" | custom-call | flops 10000000 | bytes 4000000 | tf_op jit(solution)/shard_map/inside/pallas_call | solution.py:466
  11.8 0.0 collective-permute-done.3.refs_3_
  11.8 0.0 collective-permute-done.4.refs_4_
  11.8 0.0 collective-permute-done.2.refs_2_
  11.8 0.0 collective-permute-done.refs_0_
  11.9 0.0 collective-permute-done.1.refs_1_
  11.9 0.0 copy-done.4
  11.9 0.7 %edges.1 = (f32[4,24,128]{2,1,0:T(8,128)S(1)}, f32[2,16,24,128]{3,2,1,0:T(8,128)S(1)}, f32[2,8,24,128]{3,2,1,0:T(8,128)S(1)}, f32[2,24,128]{2,1,0:T(8,128)S(1)}) custom-call(f32[128,24,128]{2,1,0:T(8,128)S(1)} %get-tuple-element.19.cells, f32[2,24,128]{2,1,0:T(8,128)S(1)} %get-tuple-element.21.own_z, f32[5,24,64]{2,1,0:T(8,128)S(1)} %get-tuple-element.22.sums, ...), custom_call_target="tpu_custom_call" | custom-call | tf_op jit(solution)/shard_map/edges/pallas_call | solution.py:480
  12.6 0.3 %collective-permute-start.5 = (f32[4,24,128]{2,1,0:T(8,128)S(1)}, f32[4,24,128]{2,1,0:T(8,128)S(1)}, u32[]{:S(2)}, u32[]{:S(2)}) collective-permute-start(f32[4,24,128]{2,1,0:T(8,128)S(1)} %get-tuple-element.31), channel_id=1, source_target_pairs={{0,8},{8,0},{16,24},{24,16},{1,9},{9,1},{17,25},{25,17},{2,10},{10... | collective-permute-start | bytes 147464 | tf_op jit(solution)/shard_map/ppermute | solution.py:393
  12.9 1.0 %collective-permute-done.5 = f32[4,24,128]{2,1,0:T(8,128)S(1)} collective-permute-done((f32[4,24,128]{2,1,0:T(8,128)S(1)}, f32[4,24,128]{2,1,0:T(8,128)S(1)}, u32[]{:S(2)}, u32[]{:S(2)}) %collective-permute-start.5) | collective-permute-done | bytes 49184 | tf_op jit(solution)/shard_map/ppermute | solution.py:393
  13.9 3.0 %collective-permute-start.6 = (f32[2,24,128]{2,1,0:T(8,128)S(1)}, f32[2,24,128]{2,1,0:T(8,128)S(1)}, u32[]{:S(2)}, u32[]{:S(2)}) collective-permute-start(f32[2,24,128]{2,1,0:T(8,128)S(1)} %slice.9), channel_id=1, source_target_pairs={{14,0},{8,2},{10,4},{12,6},{6,8},{0,10},{2,12},{4,14},{30,16},{24,... | collective-permute-start | bytes 73736 | tf_op jit(solution)/shard_map/ppermute | solution.py:373
  16.9 2.1 %collective-permute-done.6 = f32[2,24,128]{2,1,0:T(8,128)S(1)} collective-permute-done((f32[2,24,128]{2,1,0:T(8,128)S(1)}, f32[2,24,128]{2,1,0:T(8,128)S(1)}, u32[]{:S(2)}, u32[]{:S(2)}) %collective-permute-start.6) | collective-permute-done | bytes 24608 | tf_op jit(solution)/shard_map/ppermute | solution.py:373
  19.0 0.9 %collective-permute-start.7 = (f32[2,24,128]{2,1,0:T(8,128)S(1)}, f32[2,24,128]{2,1,0:T(8,128)S(1)}, u32[]{:S(2)}, u32[]{:S(2)}) collective-permute-start(f32[2,24,128]{2,1,0:T(8,128)S(1)} %slice_add_fusion.refs_0_), channel_id=1, source_target_pairs={{24,0},{25,1},{16,8},{17,9},{8,16},{9,17},{0,24},{1,25},{26,2},{27... | collective-permute-start | bytes 73736 | tf_op jit(solution)/shard_map/ppermute | solution.py:373
  19.9 1.5 %collective-permute-start.8 = (f32[2,24,128]{2,1,0:T(8,128)S(1)}, f32[2,24,128]{2,1,0:T(8,128)S(1)}, u32[]{:S(2)}, u32[]{:S(2)}) collective-permute-start(f32[2,24,128]{2,1,0:T(8,128)S(1)} %slice_add_fusion.refs_0_), channel_id=1, source_target_pairs={{9,0},{8,1},{1,8},{0,9},{25,16},{24,17},{17,24},{16,25},{11,2},{10... | collective-permute-start | bytes 73736 | tf_op jit(solution)/shard_map/ppermute | solution.py:373
  21.4 0.7 %collective-permute-start.9 = (f32[2,24,128]{2,1,0:T(8,128)S(1)}, f32[2,24,128]{2,1,0:T(8,128)S(1)}, u32[]{:S(2)}, u32[]{:S(2)}) collective-permute-start(f32[2,24,128]{2,1,0:T(8,128)S(1)} %slice_add_fusion.refs_0_), channel_id=1, source_target_pairs={{25,0},{24,1},{17,8},{16,9},{9,16},{8,17},{1,24},{0,25},{27,2},{26... | collective-permute-start | bytes 73736 | tf_op jit(solution)/shard_map/ppermute | solution.py:373
  22.1 1.9 %advance.1 = f32[22,128,128]{2,1,0:T(8,128)} custom-call(f32[128,24,128]{2,1,0:T(8,128)S(1)} %get-tuple-element.20.advanced, f32[2,16,24,128]{3,2,1,0:T(8,128)S(1)} %get-tuple-element.28.dx, f32[2,8,24,128]{3,2,1,0:T(8,128)S(1)} %get-tuple-element.29.dy, f32[2,24,128]{2,1,0:T(8,128)S(1)} %get-tuple-element.30.dz), custom_call_target="tpu_custom_call" | custom-call | flops 1000000 | bytes 3000000 | tf_op jit(solution)/shard_map/advance/pallas_call | solution.py:495
  24.0 0.0 collective-permute-done.7.refs_1_
  24.0 0.0 collective-permute-done.8.refs_2_
  24.0 1.5 %collective-permute-done.9.refs_3_ = f32[2,24,128]{2,1,0:T(8,128)S(1)} collective-permute-done((f32[2,24,128]{2,1,0:T(8,128)S(1)}, f32[2,24,128]{2,1,0:T(8,128)S(1)}, u32[]{:S(2)}, u32[]{:S(2)}) %collective-permute-start.9) | collective-permute-done | bytes 24608 | tf_op jit(solution)/shard_map/ppermute | solution.py:373
  25.5 0.7 %means.1 = f32[22,4,64]{2,1,0:T(4,128)} custom-call(f32[2,24,128]{2,1,0:T(8,128)S(1)} %slice_add_fusion.refs_0_, f32[2,24,128]{2,1,0:T(8,128)S(1)} %collective-permute-done.7.refs_1_, f32[2,24,128]{2,1,0:T(8,128)S(1)} %collective-permute-done.8.refs_2_, f32[2,24,128]{2,1,0:T(8,128)S(1)} %collective-permute-done.9.refs_3_), custom_call_target="tpu_custom_call" | custom-call | tf_op jit(solution)/shard_map/means/pallas_call | solution.py:508
  (3 shorter events, 0.0 us)
Async XLA Ops:
  0.6 4.4 %copy-start = (f32[22,8,16,128]{3,2,1,0:T(8,128)S(1)}, f32[22,8,16,128]{3,2,1,0:T(8,128)}, u32[]{:S(2)}) copy-start(f32[22,8,16,128]{3,2,1,0:T(8,128)} %param.7) | copy-start | bytes 4325380
  0.6 8.8 %copy-start.1 = (f32[8,16,128]{2,1,0:T(8,128)S(1)}, f32[8,16,128]{2,1,0:T(8,128)}, u32[]{:S(2)}) copy-start(f32[8,16,128]{2,1,0:T(8,128)} %param.9) | copy-start | bytes 196612
  0.7 8.7 %copy-start.2 = (f32[22,22]{1,0:T(8,128)S(1)}, f32[22,22]{1,0:T(8,128)}, u32[]{:S(2)}) copy-start(f32[22,22]{1,0:T(8,128)} %jacobian.1) | copy-start | bytes 5812
  0.7 8.7 %copy-start.3 = (f32[22]{0:T(128)S(1)}, f32[22]{0:T(128)}, u32[]{:S(2)}) copy-start(f32[22]{0:T(128)} %param.10) | copy-start | bytes 268
  1.9 9.9 %collective-permute-start = (f32[16,24,128]{2,1,0:T(8,128)S(1)}, f32[16,24,128]{2,1,0:T(8,128)S(1)}, u32[]{:S(2)}, u32[]{:S(2)}) collective-permute-start(f32[16,24,128]{2,1,0:T(8,128)S(1)} %get-tuple-element.23), channel_id=1, source_target_pairs={{0,2},{2,0},{4,6},{6,4},{1,3},{3,1},{5,7},{7,5},{8,10},{10,8},{12,... | collective-permute-start | bytes 589832 | tf_op jit(solution)/shard_map/ppermute | solution.py:379
  5.0 6.9 %collective-permute-start.1 = (f32[16,24,128]{2,1,0:T(8,128)S(1)}, f32[16,24,128]{2,1,0:T(8,128)S(1)}, u32[]{:S(2)}, u32[]{:S(2)}) collective-permute-start(f32[16,24,128]{2,1,0:T(8,128)S(1)} %get-tuple-element.24), channel_id=1, source_target_pairs={{8,0},{4,2},{2,4},{14,6},{0,8},{12,10},{10,12},{6,14},{24,16},{20,... | collective-permute-start | bytes 589832 | tf_op jit(solution)/shard_map/ppermute | solution.py:373
  5.0 6.9 %copy-start.4 = (s32[32]{0:T(128)S(1)}, s32[32]{0:T(128)}, u32[]{:S(2)}) copy-start(s32[32]{0:T(128)} %param.13) | copy-start | bytes 388
  6.2 5.6 %collective-permute-start.2 = (f32[8,24,128]{2,1,0:T(8,128)S(1)}, f32[8,24,128]{2,1,0:T(8,128)S(1)}, u32[]{:S(2)}, u32[]{:S(2)}) collective-permute-start(f32[8,24,128]{2,1,0:T(8,128)S(1)} %get-tuple-element.25), channel_id=1, source_target_pairs={{0,1},{1,0},{2,3},{3,2},{4,5},{5,4},{6,7},{7,6},{8,9},{9,8},{10,11... | collective-permute-start | bytes 294920 | tf_op jit(solution)/shard_map/ppermute | solution.py:379
  7.8 4.1 %collective-permute-start.3 = (f32[24,128]{1,0:T(8,128)S(1)}, f32[24,128]{1,0:T(8,128)S(1)}, u32[]{:S(2)}, u32[]{:S(2)}) collective-permute-start(f32[24,128]{1,0:T(8,128)S(1)} %get-tuple-element.26), channel_id=1, source_target_pairs={{0,8},{8,0},{16,24},{24,16},{1,9},{9,1},{17,25},{25,17},{2,10},{10... | collective-permute-start | bytes 36872 | tf_op jit(solution)/shard_map/ppermute | solution.py:379
  8.0 3.8 %collective-permute-start.4 = (f32[24,128]{1,0:T(8,128)S(1)}, f32[24,128]{1,0:T(8,128)S(1)}, u32[]{:S(2)}, u32[]{:S(2)}) collective-permute-start(f32[24,128]{1,0:T(8,128)S(1)} %get-tuple-element.27), channel_id=1, source_target_pairs={{8,16},{16,8},{0,24},{24,0},{9,17},{17,9},{1,25},{25,1},{10,18},{1... | collective-permute-start | bytes 36872 | tf_op jit(solution)/shard_map/ppermute | solution.py:382
  12.6 1.3 %collective-permute-start.5 = (f32[4,24,128]{2,1,0:T(8,128)S(1)}, f32[4,24,128]{2,1,0:T(8,128)S(1)}, u32[]{:S(2)}, u32[]{:S(2)}) collective-permute-start(f32[4,24,128]{2,1,0:T(8,128)S(1)} %get-tuple-element.31), channel_id=1, source_target_pairs={{0,8},{8,0},{16,24},{24,16},{1,9},{9,1},{17,25},{25,17},{2,10},{10... | collective-permute-start | bytes 147464 | tf_op jit(solution)/shard_map/ppermute | solution.py:393
  13.9 5.1 %collective-permute-start.6 = (f32[2,24,128]{2,1,0:T(8,128)S(1)}, f32[2,24,128]{2,1,0:T(8,128)S(1)}, u32[]{:S(2)}, u32[]{:S(2)}) collective-permute-start(f32[2,24,128]{2,1,0:T(8,128)S(1)} %slice.9), channel_id=1, source_target_pairs={{14,0},{8,2},{10,4},{12,6},{6,8},{0,10},{2,12},{4,14},{30,16},{24,... | collective-permute-start | bytes 73736 | tf_op jit(solution)/shard_map/ppermute | solution.py:373
  19.0 4.9 %collective-permute-start.7 = (f32[2,24,128]{2,1,0:T(8,128)S(1)}, f32[2,24,128]{2,1,0:T(8,128)S(1)}, u32[]{:S(2)}, u32[]{:S(2)}) collective-permute-start(f32[2,24,128]{2,1,0:T(8,128)S(1)} %slice_add_fusion.refs_0_), channel_id=1, source_target_pairs={{24,0},{25,1},{16,8},{17,9},{8,16},{9,17},{0,24},{1,25},{26,2},{27... | collective-permute-start | bytes 73736 | tf_op jit(solution)/shard_map/ppermute | solution.py:373
  19.9 4.1 %collective-permute-start.8 = (f32[2,24,128]{2,1,0:T(8,128)S(1)}, f32[2,24,128]{2,1,0:T(8,128)S(1)}, u32[]{:S(2)}, u32[]{:S(2)}) collective-permute-start(f32[2,24,128]{2,1,0:T(8,128)S(1)} %slice_add_fusion.refs_0_), channel_id=1, source_target_pairs={{9,0},{8,1},{1,8},{0,9},{25,16},{24,17},{17,24},{16,25},{11,2},{10... | collective-permute-start | bytes 73736 | tf_op jit(solution)/shard_map/ppermute | solution.py:373
  21.4 4.2 %collective-permute-start.9 = (f32[2,24,128]{2,1,0:T(8,128)S(1)}, f32[2,24,128]{2,1,0:T(8,128)S(1)}, u32[]{:S(2)}, u32[]{:S(2)}) collective-permute-start(f32[2,24,128]{2,1,0:T(8,128)S(1)} %slice_add_fusion.refs_0_), channel_id=1, source_target_pairs={{25,0},{24,1},{17,8},{16,9},{9,16},{8,17},{1,24},{0,25},{27,2},{26... | collective-permute-start | bytes 73736 | tf_op jit(solution)/shard_map/ppermute | solution.py:373

commit v7 on v4

--- a/solution.py
+++ b/solution.py
@@ -15,6 +15,7 @@
 VMEM = pl.BlockSpec(memory_space=pltpu.VMEM)
 ANY = pl.BlockSpec(memory_space=pl.ANY)
 DT = 0.05
+AHEAD = 2
 
 
 def padded_rows(species):
@@ -41,17 +42,40 @@
     return DT * jnp.sum(spread, axis=1, keepdims=True)
 
 
-def binned(values, classes):
-    shape = (NB, values.shape[1])
-    hits = (classes == rows_of(shape).astype(F32)).astype(F32).astype(BF16)
+def hits(classes):
+    shape = (NB, classes.shape[1])
+    bins = jnp.broadcast_to(classes.astype(BF16), shape)
+    found = bins == rows_of(shape).astype(F32).astype(BF16)
+    return jnp.where(found, jnp.ones((), BF16), jnp.zeros((), BF16))
+
+
+def binned(values, hit):
     return lax.dot_general(
-        values, hits, (((1,), (1,)), ((), ())), preferred_element_type=F32
+        values, hit, (((1,), (1,)), ((), ())), preferred_element_type=F32
     )
 
 
 def folded(product):
     rows = product.shape[0] // 2
     return product[:rows] + product[rows:]
+
+
+def upper_of(axis, side):
+    even = lax.axis_index(axis) % 2 == 0
+    return even if side == 0 else jnp.logical_not(even)
+
+
+def has_neighbour(axis, side):
+    if side == 0:
+        return True
+    edge = jnp.where(upper_of(axis, 1), lax.axis_size(axis) - 1, 0)
+    return lax.axis_index(axis) != edge
+
+
+def face_rows(axis, upper, planes, width):
+    if axis == "gx":
+        return jnp.where(upper, (planes - 1) * width, 0), 1, width
+    return jnp.where(upper, width - 1, 0), width, planes
 
 
 def pack_kernel(planes, has_b, cells, mixing, classes, *refs):
@@ -107,20 +131,28 @@
         own_z[0, pl.ds(g, SUBLANES), :] = (low + lows)[i]
         own_z[1, pl.ds(g, SUBLANES), :] = pltpu.roll((high + highs)[i], 1, axis=1)
     for axis, both in zip(("gx", "gy", "sec"), has_b):
-        even = lax.axis_index(axis) % 2 == 0
         for side in range(1 + both):
             out = faces.pop(0)
-            upper = even if side == 0 else jnp.logical_not(even)
-            if axis == "gx":
-                start = jnp.where(upper, row_count - width, 0)
-                for y in range(width):
-                    out[y] = rows_out[start + y]
-            elif axis == "gy":
-                start = jnp.where(upper, width - 1, 0)
-                for x in range(planes):
-                    out[x] = rows_out[start + x * width]
-            else:
+            upper = upper_of(axis, side)
+            if axis == "sec":
                 out[...] = own_z[jnp.where(upper, 1, 0)]
+                continue
+            start, step, count = face_rows(axis, upper, planes, width)
+            for i in range(count):
+                r = start + i * step
+                out[pl.ds(i, 1), :] = rows_out[r, pl.ds(species, 1), :]
+                out[pl.ds(count + i, 1), :] = rows_out[r, pl.ds(species + 1, 1), :]
+
+
+def wide_face_kernel(planes, has_b, cells, held, *faces):
+    faces = list(faces)
+    width = cells.shape[0] // planes
+    for axis, both in zip(("gx", "gy"), has_b):
+        for side in range(1 + both):
+            out = faces.pop(0)
+            start, step, count = face_rows(axis, upper_of(axis, side), planes, width)
+            for i in range(count):
+                out[i] = cells[start + i * step]
 
 
 def inner_kernel(
@@ -161,52 +193,58 @@
     left = square[...].astype(BF16)
 
     weight = jnp.broadcast_to(weight_column(weights, rows), (rows, depth))
-    ones = rows_of((rows, depth)) >= species
+    whole = species // SUBLANES * SUBLANES
+    ones = rows_of((rows - whole, depth)) >= species - whole
     station_sums[...] = jnp.zeros_like(station_sums)
 
-    for x in range(planes):
-        base = x * width
-        below = max(x - 1, 0) * width
-        above = min(x + 1, planes - 1) * width
-        made = jnp.zeros((2 * rows, NB), F32)
-        for first in range(0, width, 2):
-            pair = (first, first + 1)
-            here = [cells[base + y] for y in pair]
-            mixed = folded(
-                jnp.dot(
-                    left,
-                    jnp.concatenate([halves(c) for c in here], axis=1),
-                    preferred_element_type=F32,
-                )
-            )
-            values, classes = [], []
-            for i, y in enumerate(pair):
-                r = base + y
-                c = here[i]
-                at = lambda n: coefs[n, pl.ds(r, 1), :]
-                flux = at(0) * pltpu.roll(c, depth - 1, axis=1)
-                flux += at(1) * pltpu.roll(c, 1, axis=1)
-                if y < width - 1:
-                    flux += at(2) * cells[r + 1]
-                if y > 0:
-                    flux += at(3) * cells[r - 1]
-                if x < planes - 1:
-                    flux += at(4) * cells[above + y]
-                if x > 0:
-                    flux += at(5) * cells[below + y]
-                flux -= at(6) * c
-                new = c + weight * flux + at(7) * mixed[:, i * depth : (i + 1) * depth]
-                new = jnp.where(ones, 1.0, new)
-                advanced[r] = new
-                values.append(halves(new))
-                classes.append(cells[r, species + 1 : species + 2, :])
-            made += binned(jnp.concatenate(values, axis=1), jnp.concatenate(classes, axis=1))
-        station_sums[(x + 1) // 2] += folded(made)
+    def kinetics(pair):
+        wide = jnp.concatenate([halves(cells[r]) for r in pair], axis=1)
+        return folded(jnp.dot(left, wide, preferred_element_type=F32))
+
+    def advance(pair, mixed):
+        values, found = [], []
+        for i, r in enumerate(pair):
+            x, y = divmod(r, width)
+            c = cells[r]
+            at = lambda n: coefs[n, pl.ds(r, 1), :]
+            flux = at(0) * pltpu.roll(c, depth - 1, axis=1)
+            flux += at(1) * pltpu.roll(c, 1, axis=1)
+            if y < width - 1:
+                flux += at(2) * cells[r + 1]
+            if y > 0:
+                flux += at(3) * cells[r - 1]
+            if x < planes - 1:
+                flux += at(4) * cells[r + width]
+            if x > 0:
+                flux += at(5) * cells[r - width]
+            flux -= at(6) * c
+            new = c + weight * flux + at(7) * mixed[:, i * depth : (i + 1) * depth]
+            new = jnp.concatenate([new[:whole], jnp.where(ones, 1.0, new[whole:])], axis=0)
+            advanced[r] = new
+            values.append(halves(new))
+            found.append(hits(cells[r, species + 1 : species + 2, :]))
+        return jnp.concatenate(values, axis=1), jnp.concatenate(found, axis=1)
+
+    pairs = [(r, r + 1) for r in range(0, row_count, 2)]
+    mixed, values, made = {}, {}, 0.0
+    for t in range(len(pairs) + 2 * AHEAD):
+        if t < len(pairs):
+            mixed[t] = kinetics(pairs[t])
+        now = t - AHEAD
+        if 0 <= now < len(pairs):
+            values[now] = advance(pairs[now], mixed.pop(now))
+        last = now - AHEAD
+        if 0 <= last < len(pairs):
+            made += binned(*values.pop(last))
+            x, y = divmod(pairs[last][1], width)
+            if y == width - 1:
+                station_sums[(x + 1) // 2] += folded(made)
+                made = 0.0
 
 
 def edge_kernel(planes, has_b, cells, own_z, sums, weights, positions, *refs):
     halos = list(refs[: 3 + sum(has_b)])
-    window, dx, dy, dz, station_sums = refs[3 + sum(has_b) :]
+    window, dz, station_sums = refs[3 + sum(has_b) :]
     row_count, rows, depth = cells.shape
     species = weights.shape[1]
     width = row_count // planes
@@ -214,61 +252,60 @@
     received = {}
     for axis, both in zip(("gx", "gy", "sec"), has_b):
         received[axis] = [halos.pop(0), halos.pop(0) if both else None]
-    evens = {axis: lax.axis_index(axis) % 2 == 0 for axis in received}
-
-    inside = {}
-    for axis in received:
-        place, upper = lax.axis_index(axis), jnp.logical_not(evens[axis])
-        edge = jnp.where(upper, lax.axis_size(axis) - 1, 0)
-        inside[axis] = jnp.broadcast_to(place != edge, (rows, depth))
-
-    def added(c, axis, side, part):
-        halo = received[axis][side]
-        if halo is None:
-            return weight * (0.5 * c[species : species + 1]) * (0.0 - c)
-        halo = halo[part]
-        if side:
-            halo = jnp.where(inside[axis], halo, 0.0)
-        d = 0.5 * (c[species : species + 1] + halo[species : species + 1])
-        return weight * d * (halo - c)
-
     station_sums[...] = sums[...]
-    for side in range(2):
-        upper = evens["gx"] if side == 0 else jnp.logical_not(evens["gx"])
-        plane = jnp.where(upper, planes - 1, 0)
-        made = jnp.zeros((2 * rows, NB), F32)
-        for first in range(0, width, 2):
-            values, classes = [], []
-            for y in (first, first + 1):
-                r = plane * width + y
-                delta = added(cells[r], "gx", side, y)
-                dx[side, y] = delta
-                values.append(halves(delta))
-                classes.append(cells[r, species + 1 : species + 2, :])
-            made += binned(jnp.concatenate(values, axis=1), jnp.concatenate(classes, axis=1))
-        station_sums[(plane + 1) // 2] += folded(made)
-    for side in range(2):
-        upper = evens["gy"] if side == 0 else jnp.logical_not(evens["gy"])
-        place = jnp.where(upper, width - 1, 0)
-        for x in range(planes):
-            r = place + x * width
-            delta = added(cells[r], "gy", side, x)
-            dy[side, x] = delta
-            station_sums[(x + 1) // 2] += folded(
-                binned(halves(delta), cells[r, species + 1 : species + 2, :])
-            )
+
+    for axis in ("gx", "gy"):
+        for side in range(2):
+            halo = received[axis][side]
+            start, step, count = face_rows(axis, upper_of(axis, side), planes, width)
+            there = jnp.zeros((2 * count, depth), F32)
+            there = there if halo is None else halo[...]
+            if side and halo is not None:
+                inside = jnp.broadcast_to(has_neighbour(axis, side), there.shape)
+                outside = jnp.where(rows_of(there.shape) < count, 0.0, -1.0)
+                there = jnp.where(inside, there, outside)
+            if halo is None:
+                there = jnp.where(rows_of(there.shape) < count, 0.0, -1.0)
+            made = jnp.zeros((2 * rows, NB), F32)
+            for first in range(0, count, 2):
+                values, found = [], []
+                for i in (first, first + 1):
+                    c = cells[start + i * step]
+                    d = 0.5 * (c[species : species + 1] + there[i : i + 1])
+                    values.append(halves(weight * d * c))
+                    found.append(
+                        hits(there[count + i : count + i + 1]) - hits(c[species + 1 : species + 2])
+                    )
+                if axis == "gx":
+                    made += binned(
+                        jnp.concatenate(values, axis=1), jnp.concatenate(found, axis=1)
+                    )
+                else:
+                    for i, value, hit in zip((first, first + 1), values, found):
+                        station_sums[(i + 1) // 2] += folded(binned(value, hit))
+            if axis == "gx":
+                plane = jnp.where(upper_of(axis, side), planes - 1, 0)
+                station_sums[(plane + 1) // 2] += folded(made)
+
     stations = planes // 2 + 1
     lane = lanes_of((1, row_count))
     station = ((lane // width + 1) // 2).astype(F32)
     for side in range(2):
-        upper = evens["sec"] if side == 0 else jnp.logical_not(evens["sec"])
-        c = own_z[jnp.where(upper, 1, 0)]
-        delta = added(c, "sec", side, slice(None))
+        c = own_z[jnp.where(upper_of("sec", side), 1, 0)]
+        halo = received["sec"][side]
+        if halo is None:
+            halo = jnp.zeros_like(c)
+        else:
+            halo = jnp.where(
+                jnp.broadcast_to(has_neighbour("sec", side), halo.shape), halo[...], 0.0
+            )
+        d = 0.5 * (c[species : species + 1] + halo[species : species + 1])
+        delta = weight * d * (halo - c)
         dz[side] = delta
         value = halves(delta)
         classes = c[species + 1 : species + 2]
         for j in range(stations):
-            station_sums[j] += folded(binned(value, jnp.where(station == j, classes, -1.0)))
+            station_sums[j] += folded(binned(value, hits(jnp.where(station == j, classes, -1.0))))
     shift = jnp.broadcast_to(positions[0:1, 0:1], (rows, NB))
     per_device = planes // 2
     for s in range(0, 2 * per_device, 2):
@@ -282,25 +319,31 @@
         window[s // 2] = jnp.concatenate(parts, axis=1)
 
 
-def finish_kernel(planes, advanced, dx, dy, dz, out, total, sem):
+def finish_kernel(planes, has_b, cells, advanced, dz, weights, *refs):
+    halos = list(refs[: 2 + sum(has_b)])
+    out, finished, total, sem = refs[2 + sum(has_b) :]
+    finished[...] = jnp.zeros_like(finished)
     row_count, rows, depth = advanced.shape
     species = out.shape[0]
     width = row_count // planes
+    weight = jnp.broadcast_to(weight_column(weights, rows), (rows, depth))
     total[...] = advanced[...]
-    evens = {axis: lax.axis_index(axis) % 2 == 0 for axis in ("gx", "gy", "sec")}
-    for side in range(2):
-        upper = evens["gx"] if side == 0 else jnp.logical_not(evens["gx"])
-        first = jnp.where(upper, row_count - width, 0)
-        for y in range(width):
-            total[first + y] += dx[side, y]
-    for side in range(2):
-        upper = evens["gy"] if side == 0 else jnp.logical_not(evens["gy"])
-        place = jnp.where(upper, width - 1, 0)
-        for x in range(planes):
-            total[place + x * width] += dy[side, x]
+    for axis, both in zip(("gx", "gy"), has_b):
+        for side in range(2):
+            halo = halos.pop(0) if side <= both else None
+            start, step, count = face_rows(axis, upper_of(axis, side), planes, width)
+            inside = jnp.broadcast_to(has_neighbour(axis, side), (rows, depth))
+            for i in range(count):
+                r = start + i * step
+                c = cells[r]
+                there = jnp.zeros_like(c) if halo is None else halo[i]
+                if side:
+                    there = jnp.where(inside, there, 0.0)
+                d = 0.5 * (c[species : species + 1] + there[species : species + 1])
+                total[r] += weight * d * (there - c)
     shape = (rows, depth)
     lane = lanes_of(shape)
-    even = jnp.broadcast_to(evens["sec"], shape)
+    even = jnp.broadcast_to(upper_of("sec", 0), shape)
     high = jnp.where(even, dz[0], dz[1])
     low = jnp.where(even, dz[1], dz[0])
     high = pltpu.roll(high, depth - 1, axis=1)
@@ -322,7 +365,7 @@
         ).wait()
 
 
-def means_kernel(*refs):
+def means_kernel(after, *refs):
     terms, out = refs[:-1], refs[-1]
     species, per_device, bins = out.shape
     for s in range(0, per_device, 2):
@@ -376,18 +419,13 @@
 def summed(block):
     deep, gx, gy = (lax.axis_size(axis) for axis in ("sec", "gx", "gy"))
     half = block.shape[0] // 2
-    block = block + lax.ppermute(block, "sec", [(i, i ^ 1) for i in range(deep)])
     block = block[:half] + joint(block[half:], "gx", lambda s, i: (s ^ 1, (i - 1) % gx))
     steps = [(1 << n, 0) for n in range(1, deep.bit_length() - 1)]
     steps += [(0, 1 << n) for n in range(gy.bit_length() - 1)]
     terms = [block]
-    while steps:
-        (a, b), (c, d) = steps.pop(0), steps.pop(0) if steps else (0, 0)
+    for e, f in steps:
         block = sum(terms[1:], terms[0])
-        terms = [block]
-        for e, f in dict.fromkeys([(a, b), (c, d), (a ^ c, b ^ d)]):
-            if e or f:
-                terms.append(joint(block, "gy", lambda s, i: (s ^ 1 ^ e, i ^ f)))
+        terms = [block, joint(block, "gy", lambda s, i: (s ^ 1 ^ e, i ^ f))]
     return terms
 
 
@@ -411,18 +449,26 @@
     positions = streamwise_positions.reshape(1, -1)
     per_device = planes // 2
     has_b = tuple(lax.axis_size(axis) > 2 for axis in ("gx", "gy", "sec"))
-    shapes = {"gx": (width, rows, depth), "gy": (planes, rows, depth), "sec": (rows, row_count)}
     sides = [
         (axis, side)
         for axis, both in zip(("gx", "gy", "sec"), has_b)
         for side in range(1 + both)
     ]
-    face_shapes = [struct(*shapes[axis]) for axis, _ in sides]
-
-    packed = call(
+    narrow = {
+        "gx": struct(2 * width, depth),
+        "gy": struct(2 * planes, depth),
+        "sec": struct(rows, row_count),
+    }
+    wide = {"gx": struct(width, rows, depth), "gy": struct(planes, rows, depth)}
+
+    rows_in, own_z, *faces = call(
         functools.partial(pack_kernel, planes, has_b),
         "faces",
-        [struct(row_count, rows, depth), struct(2, rows, row_count), *face_shapes],
+        [
+            struct(row_count, rows, depth),
+            struct(2, rows, row_count),
+            *[narrow[axis] for axis, _ in sides],
+        ],
         3,
         [VMEM] * (2 + len(sides)),
         in_specs=[ANY] * 3,
@@ -432,7 +478,6 @@
             pltpu.SemaphoreType.DMA((2,)),
         ],
     )(*[pltpu.with_memory_space_constraint(x, pltpu.HBM) for x in (cells, mixing, classes)])
-    rows_in, own_z, faces = packed[0], packed[1], packed[2:]
     halos = [swapped(face, axis, side) for face, (axis, side) in zip(faces, sides)]
 
     inner, sums = call(
@@ -449,37 +494,44 @@
         moved=4_000_000,
     )(rows_in, mixing, thermal, weights, kinetics_jacobian)
 
-    window, dx, dy, dz = call(
+    window, dz = call(
         functools.partial(edge_kernel, planes, has_b),
         "edges",
-        [
-            struct(per_device, rows, 2 * NB),
-            struct(2, width, rows, depth),
-            struct(2, planes, rows, depth),
-            struct(2, rows, row_count),
-        ],
+        [struct(per_device, rows, 2 * NB), struct(2, rows, row_count)],
         5 + len(halos),
-        [VMEM] * 4,
+        [VMEM] * 2,
         scratch=[pltpu.VMEM((per_device + 1, rows, NB), F32)],
     )(rows_in, own_z, sums, weights, positions, *halos)
 
+    deep = lax.axis_size("sec")
+    window = window + lax.ppermute(window, "sec", [(i, i ^ 1) for i in range(deep)])
     terms = summed(window)
-    advanced = call(
-        functools.partial(finish_kernel, planes),
+
+    wide_sides = [(axis, side) for axis, side in sides if axis != "sec"]
+    wide_faces = call(
+        functools.partial(wide_face_kernel, planes, has_b),
+        "wide_faces",
+        [wide[axis] for axis, _ in wide_sides],
+        2,
+        [VMEM] * len(wide_sides),
+    )(rows_in, window)
+    wide_halos = [swapped(face, axis, side) for face, (axis, side) in zip(wide_faces, wide_sides)]
+    advanced, finished = call(
+        functools.partial(finish_kernel, planes, has_b[:2]),
         "advance",
-        struct(species, row_count, depth),
-        4,
-        ANY,
+        [struct(species, row_count, depth), struct(SUBLANES, LANES)],
+        4 + len(wide_halos),
+        [ANY, VMEM],
         scratch=[
             pltpu.VMEM((row_count, rows, depth), F32),
             pltpu.SemaphoreType.DMA((planes,)),
         ],
         flops=1_000_000,
         moved=3_000_000,
-    )(inner, dx, dy, dz)
+    )(rows_in, inner, dz, weights, *wide_halos)
     cond_means = call(
-        means_kernel, "means", struct(species, per_device, NB), len(terms), VMEM
-    )(*terms)
+        means_kernel, "means", struct(species, per_device, NB), 1 + len(terms), VMEM
+    )(finished, *terms)
     return advanced.reshape(composition_matrix.shape), cond_means
 
 

time: 25.8 us -> 27.4 us (1.062)
  waiting for transfers between devices: 4.55 us -> 5.74 us
  starting transfers between devices: 12.5 us -> 13.2 us
  Pallas kernels: 7.75 us -> 7.38 us
    ppermute x3 -> x5, starting transfers between devices: 4.81 us -> 6.92 us  [swapped(): return lax.ppermute(block, axis, [(i, i ^ 1) for i in range(count)])]
    ppermute x3 -> x5, waiting for transfers between devices: 0.03 us -> 1.6 us  [swapped(): return lax.ppermute(block, axis, [(i, i ^ 1) for i in range(count)])]
    ppermute x5, starting transfers between devices: 6.01 us -> 4.94 us  [joint(): return lax.ppermute(block, ('sec', axis), pairs)]
    pallas_call x1, Pallas kernels: 2.54 us -> 2.07 us  [on_device(): call(functools.partial(inner_kernel, planes), 'inside', [struct(row_count...]
    ppermute x5, waiting for transfers between devices: 3.52 us -> 3.1 us  [joint(): return lax.ppermute(block, ('sec', axis), pairs)]
    ppermute x1, starting transfers between devices: 1.41 us -> 1.13 us  [swapped(): return lax.ppermute(block, axis, [*pairs, (0, count - 1), (count - 1, 0)])]
    pallas_call x2 -> x3, Pallas kernels: 2.64 us -> 2.72 us  [the longest x1 1.94 us: on_device(): call(functools.partial(finish_kernel, planes, has_b[:2]), 'advance', [str...]
  transfers between devices with their start and end apart: 10 -> 12, of which waited for: 3 -> 5; matrix products, arithmetic and copies ran while one was open for 0% -> 0% of each run, Pallas kernels for 17% -> 15%
where the time goes in v7:
time: 27.4 us; the launch traced here: 27.2 us
  starting transfers between devices  13.2 us (48%)
  Pallas kernels  7.38 us (27%)
  waiting for transfers between devices  5.74 us (21%)
  between operations  0.75 us (3%)
    ppermute x5, starting transfers between devices, swapped(): return lax.ppermute(block, axis, [(i, i ^ 1) for i in range(count)])  6.92 us
    ppermute x5, starting transfers between devices, joint(): return lax.ppermute(block, ('sec', axis), pairs)  4.94 us
    ppermute x5, waiting for transfers between devices, joint(): return lax.ppermute(block, ('sec', axis), pairs)  3.1 us
    pallas_call x1, Pallas kernels, on_device(): call(functools.partial(inner_kernel, planes), 'inside', [struct(row_count...  2.07 us
    pallas_call x1, Pallas kernels, on_device(): call(functools.partial(finish_kernel, planes, has_b[:2]), 'advance', [str...  1.94 us
    pallas_call x1, Pallas kernels, on_device(): call(functools.partial(pack_kernel, planes, has_b), 'faces', [struct(row_...  1.85 us
    ppermute x5, waiting for transfers between devices, swapped(): return lax.ppermute(block, axis, [(i, i ^ 1) for i in range(count)])  1.6 us
    ppermute x1, starting transfers between devices, swapped(): return lax.ppermute(block, axis, [*pairs, (0, count - 1), (count - 1, 0)])  1.13 us
  transfers between devices with their start and end apart: 12, of which 5 were waited for; matrix products, arithmetic and copies ran while one was open for 0% of the time, Pallas kernels for 15%

profile of v7, /device:TPU:0, one launch (start us, length us, event | category | flops | bytes accessed | tf_op | source)
XLA Modules:
  0.0 27.2 jit_solution(15154915307803640864)
XLA Ops:
  0.6 0.0 copy-start
  0.6 0.0 copy-start.2
  0.7 0.0 copy-start.3
  0.7 0.0 copy-start.1
  0.7 0.0 copy-start.4
  0.7 1.9 %faces.1 = (f32[128,24,128]{2,1,0:T(8,128)S(1)}, f32[2,24,128]{2,1,0:T(8,128)S(1)}, f32[32,128]{1,0:T(8,128)S(1)}, f32[32,128]{1,0:T(8,128)S(1)}, f32[16,128]{1,...) custom-call(f32[22,128,128]{2,1,0:T(8,128)} %bitcast.14, f32[128,128]{1,0:T(8,128)} %bitcast.7, ...), custom_call_target="tpu_custom_call" | custom-call | tf_op jit(solution)/shard_map/faces/pallas_call | solution.py:464
  2.5 3.1 %collective-permute-start = (f32[32,128]{1,0:T(8,128)S(1)}, f32[32,128]{1,0:T(8,128)S(1)}, u32[]{:S(2)}, u32[]{:S(2)}) collective-permute-start(f32[32,128]{1,0:T(8,128)S(1)} %get-tuple-element.22), channel_id=1, source_target_pairs={{0,2},{2,0},{4,6},{6,4},{1,3},{3,1},{5,7},{7,5},{8,10},{10,8},{12,... | collective-permute-start | bytes 49160 | tf_op jit(solution)/shard_map/ppermute | solution.py:408
  5.6 0.0 collective-permute-start.1
  5.6 0.5 %collective-permute-start.3 = (f32[24,128]{1,0:T(8,128)S(1)}, f32[24,128]{1,0:T(8,128)S(1)}, u32[]{:S(2)}, u32[]{:S(2)}) collective-permute-start(f32[24,128]{1,0:T(8,128)S(1)} %get-tuple-element.25), channel_id=1, source_target_pairs={{0,8},{8,0},{16,24},{24,16},{1,9},{9,1},{17,25},{25,17},{2,10},{10... | collective-permute-start | bytes 36872 | tf_op jit(solution)/shard_map/ppermute | solution.py:408
  6.1 1.1 %collective-permute-start.4 = (f32[24,128]{1,0:T(8,128)S(1)}, f32[24,128]{1,0:T(8,128)S(1)}, u32[]{:S(2)}, u32[]{:S(2)}) collective-permute-start(f32[24,128]{1,0:T(8,128)S(1)} %get-tuple-element.26), channel_id=1, source_target_pairs={{8,16},{16,8},{0,24},{24,0},{9,17},{17,9},{1,25},{25,1},{10,18},{1... | collective-permute-start | bytes 36872 | tf_op jit(solution)/shard_map/ppermute | solution.py:411
  7.3 1.5 %collective-permute-start.2 = (f32[16,128]{1,0:T(8,128)S(1)}, f32[16,128]{1,0:T(8,128)S(1)}, u32[]{:S(2)}, u32[]{:S(2)}) collective-permute-start(f32[16,128]{1,0:T(8,128)S(1)} %get-tuple-element.24), channel_id=1, source_target_pairs={{0,1},{1,0},{2,3},{3,2},{4,5},{5,4},{6,7},{7,6},{8,9},{9,8},{10,11... | collective-permute-start | bytes 24584 | tf_op jit(solution)/shard_map/ppermute | solution.py:408
  8.8 0.0 copy-done
  8.8 0.0 copy-done.2
  8.8 0.0 copy-done.3
  8.8 0.0 copy-done.1
  8.8 2.1 %inside.1 = (f32[128,24,128]{2,1,0:T(8,128)S(1)}, f32[5,24,64]{2,1,0:T(8,128)S(1)}) custom-call(f32[128,24,128]{2,1,0:T(8,128)S(1)} %get-tuple-element.18.cells, f32[128,128]{1,0:T(8,128)S(1)} %bitcast.8, f32[128,128]{1,0:T(8,128)S(1)} %bitcast.9, f32[1,22]{1,0:T(1,128)S(1)} %bitcast.10, f32[22,22]{1,0:T(8,128)S(1)} %copy-done.2), custom_call_target="tpu_custom_call" | custom-call | flops 10000000 | bytes 4000000 | tf_op jit(solution)/shard_map/inside/pallas_call | solution.py:483
  10.8 0.1 collective-permute-done.2.refs_2_
  10.9 0.0 collective-permute-done.3.refs_3_
  10.9 0.0 collective-permute-done.4.refs_4_
  10.9 0.0 collective-permute-done.refs_0_
  10.9 0.0 collective-permute-done.1.refs_1_
  10.9 0.0 copy-done.4
  11.0 0.7 %edges.1 = (f32[4,24,128]{2,1,0:T(8,128)S(1)}, f32[2,24,128]{2,1,0:T(8,128)S(1)}) custom-call(f32[128,24,128]{2,1,0:T(8,128)S(1)} %get-tuple-element.18.cells, f32[2,24,128]{2,1,0:T(8,128)S(1)} %get-tuple-element.20.own_z, f32[5,24,64]{2,1,0:T(8,128)S(1)} %get-tuple-element.21.sums, f32[1,22]{1,0:T(1,128)S(1)} %bitcast.11, s32[1,32]{1,0:T(1,128)S(1)} %bitcast.13, ...), custom_call_target="tpu_custom_call" | custom-call | tf_op jit(solution)/shard_map/edges/pallas_call | solution.py:497
  11.7 0.3 collective-permute-start.5
  12.0 1.0 %collective-permute-done.5 = f32[4,24,128]{2,1,0:T(8,128)S(1)} collective-permute-done((f32[4,24,128]{2,1,0:T(8,128)S(1)}, f32[4,24,128]{2,1,0:T(8,128)S(1)}, u32[]{:S(2)}, u32[]{:S(2)}) %collective-permute-start.5) | collective-permute-done | bytes 49184 | tf_op jit(solution)/shard_map/ppermute | solution.py:507
  13.0 3.0 %collective-permute-start.9 = (f32[2,24,128]{2,1,0:T(8,128)S(1)}, f32[2,24,128]{2,1,0:T(8,128)S(1)}, u32[]{:S(2)}, u32[]{:S(2)}) collective-permute-start(f32[2,24,128]{2,1,0:T(8,128)S(1)} %slice.9), channel_id=1, source_target_pairs={{14,0},{8,2},{10,4},{12,6},{6,8},{0,10},{2,12},{4,14},{30,16},{24,... | collective-permute-start | bytes 73736 | tf_op jit(solution)/shard_map/ppermute | solution.py:402
  16.0 1.6 %collective-permute-start.8 = (f32[8,24,128]{2,1,0:T(8,128)S(1)}, f32[8,24,128]{2,1,0:T(8,128)S(1)}, u32[]{:S(2)}, u32[]{:S(2)}) collective-permute-start(f32[8,24,128]{2,1,0:T(8,128)S(1)} %get-tuple-element.31), channel_id=1, source_target_pairs={{0,1},{1,0},{2,3},{3,2},{4,5},{5,4},{6,7},{7,6},{8,9},{9,8},{10,11... | collective-permute-start | bytes 294920 | tf_op jit(solution)/shard_map/ppermute | solution.py:408
  17.6 0.3 collective-permute-start.6
  17.8 0.0 collective-permute-start.7
  17.9 0.3 collective-permute-done.9
  18.1 0.4 %collective-permute-start.10 = (f32[2,24,128]{2,1,0:T(8,128)S(1)}, f32[2,24,128]{2,1,0:T(8,128)S(1)}, u32[]{:S(2)}, u32[]{:S(2)}) collective-permute-start(f32[2,24,128]{2,1,0:T(8,128)S(1)} %slice_add_fusion), channel_id=1, source_target_pairs={{24,0},{25,1},{16,8},{17,9},{8,16},{9,17},{0,24},{1,25},{26,2},{27... | collective-permute-start | bytes 73736 | tf_op jit(solution)/shard_map/ppermute | solution.py:402
  18.6 2.8 %collective-permute-done.10 = f32[2,24,128]{2,1,0:T(8,128)S(1)} collective-permute-done((f32[2,24,128]{2,1,0:T(8,128)S(1)}, f32[2,24,128]{2,1,0:T(8,128)S(1)}, u32[]{:S(2)}, u32[]{:S(2)}) %collective-permute-start.10) | collective-permute-done | bytes 24608 | tf_op jit(solution)/shard_map/ppermute | solution.py:402
  21.4 1.5 %collective-permute-start.11 = (f32[2,24,128]{2,1,0:T(8,128)S(1)}, f32[2,24,128]{2,1,0:T(8,128)S(1)}, u32[]{:S(2)}, u32[]{:S(2)}) collective-permute-start(f32[2,24,128]{2,1,0:T(8,128)S(1)} %add.11.refs_0_), channel_id=1, source_target_pairs={{9,0},{8,1},{1,8},{0,9},{25,16},{24,17},{17,24},{16,25},{11,2},{10... | collective-permute-start | bytes 73736 | tf_op jit(solution)/shard_map/ppermute | solution.py:402
  22.9 0.0 collective-permute-done.8.refs_2_
  22.9 1.5 %collective-permute-done.6.refs_0_ = f32[16,24,128]{2,1,0:T(8,128)S(1)} collective-permute-done((f32[16,24,128]{2,1,0:T(8,128)S(1)}, f32[16,24,128]{2,1,0:T(8,128)S(1)}, u32[]{:S(2)}, u32[]{:S(2)}) %collective-permute-start.6) | collective-permute-done | bytes 196640 | tf_op jit(solution)/shard_map/ppermute | solution.py:408
  24.5 0.0 collective-permute-done.7.refs_1_
  24.5 1.9 %advance.1 = (f32[22,128,128]{2,1,0:T(8,128)}, f32[8,128]{1,0:T(8,128)S(1)}) custom-call(f32[128,24,128]{2,1,0:T(8,128)S(1)} %get-tuple-element.18.cells, f32[128,24,128]{2,1,0:T(8,128)S(1)} %get-tuple-element.19.advanced, f32[2,24,128]{2,1,0:T(8,128)S(1)} %get-tuple-element.27.dz, f32[1,22]{1,0:T(1,128)S(1)} %bitcast.12, ...), custom_call_target="tpu_custom_call" | custom-call | flops 1000000 | bytes 3000000 | tf_op jit(solution)/shard_map/advance/pallas_call | solution.py:519
  26.4 0.0 collective-permute-done.11.refs_1_
  26.4 0.7 %means.1 = f32[22,4,64]{2,1,0:T(4,128)} custom-call(f32[8,128]{1,0:T(8,128)S(1)} %get-tuple-element.33.after, f32[2,24,128]{2,1,0:T(8,128)S(1)} %add.11.refs_0_, f32[2,24,128]{2,1,0:T(8,128)S(1)} %collective-permute-done.11.refs_1_), custom_call_target="tpu_custom_call" | custom-call | tf_op jit(solution)/shard_map/means/pallas_call | solution.py:532
  (5 shorter events, 0.1 us)
Async XLA Ops:
  0.6 8.1 %copy-start = (f32[8,16,128]{2,1,0:T(8,128)S(1)}, f32[8,16,128]{2,1,0:T(8,128)}, u32[]{:S(2)}) copy-start(f32[8,16,128]{2,1,0:T(8,128)} %param.8) | copy-start | bytes 196612
  0.6 8.1 %copy-start.2 = (f32[22,22]{1,0:T(8,128)S(1)}, f32[22,22]{1,0:T(8,128)}, u32[]{:S(2)}) copy-start(f32[22,22]{1,0:T(8,128)} %jacobian.1) | copy-start | bytes 5812
  0.7 8.1 %copy-start.3 = (f32[22]{0:T(128)S(1)}, f32[22]{0:T(128)}, u32[]{:S(2)}) copy-start(f32[22]{0:T(128)} %param.10) | copy-start | bytes 268
  0.7 8.1 %copy-start.1 = (f32[8,16,128]{2,1,0:T(8,128)S(1)}, f32[8,16,128]{2,1,0:T(8,128)}, u32[]{:S(2)}) copy-start(f32[8,16,128]{2,1,0:T(8,128)} %param.9) | copy-start | bytes 196612
  0.7 10.3 %copy-start.4 = (s32[32]{0:T(128)S(1)}, s32[32]{0:T(128)}, u32[]{:S(2)}) copy-start(s32[32]{0:T(128)} %param.13) | copy-start | bytes 388
  2.5 8.4 %collective-permute-start = (f32[32,128]{1,0:T(8,128)S(1)}, f32[32,128]{1,0:T(8,128)S(1)}, u32[]{:S(2)}, u32[]{:S(2)}) collective-permute-start(f32[32,128]{1,0:T(8,128)S(1)} %get-tuple-element.22), channel_id=1, source_target_pairs={{0,2},{2,0},{4,6},{6,4},{1,3},{3,1},{5,7},{7,5},{8,10},{10,8},{12,... | collective-permute-start | bytes 49160 | tf_op jit(solution)/shard_map/ppermute | solution.py:408
  5.6 5.3 %collective-permute-start.1 = (f32[32,128]{1,0:T(8,128)S(1)}, f32[32,128]{1,0:T(8,128)S(1)}, u32[]{:S(2)}, u32[]{:S(2)}) collective-permute-start(f32[32,128]{1,0:T(8,128)S(1)} %get-tuple-element.23), channel_id=1, source_target_pairs={{8,0},{4,2},{2,4},{14,6},{0,8},{12,10},{10,12},{6,14},{24,16},{20,... | collective-permute-start | bytes 49160 | tf_op jit(solution)/shard_map/ppermute | solution.py:402
  5.6 5.3 %collective-permute-start.3 = (f32[24,128]{1,0:T(8,128)S(1)}, f32[24,128]{1,0:T(8,128)S(1)}, u32[]{:S(2)}, u32[]{:S(2)}) collective-permute-start(f32[24,128]{1,0:T(8,128)S(1)} %get-tuple-element.25), channel_id=1, source_target_pairs={{0,8},{8,0},{16,24},{24,16},{1,9},{9,1},{17,25},{25,17},{2,10},{10... | collective-permute-start | bytes 36872 | tf_op jit(solution)/shard_map/ppermute | solution.py:408
  6.1 4.8 %collective-permute-start.4 = (f32[24,128]{1,0:T(8,128)S(1)}, f32[24,128]{1,0:T(8,128)S(1)}, u32[]{:S(2)}, u32[]{:S(2)}) collective-permute-start(f32[24,128]{1,0:T(8,128)S(1)} %get-tuple-element.26), channel_id=1, source_target_pairs={{8,16},{16,8},{0,24},{24,0},{9,17},{17,9},{1,25},{25,1},{10,18},{1... | collective-permute-start | bytes 36872 | tf_op jit(solution)/shard_map/ppermute | solution.py:411
  7.3 3.7 %collective-permute-start.2 = (f32[16,128]{1,0:T(8,128)S(1)}, f32[16,128]{1,0:T(8,128)S(1)}, u32[]{:S(2)}, u32[]{:S(2)}) collective-permute-start(f32[16,128]{1,0:T(8,128)S(1)} %get-tuple-element.24), channel_id=1, source_target_pairs={{0,1},{1,0},{2,3},{3,2},{4,5},{5,4},{6,7},{7,6},{8,9},{9,8},{10,11... | collective-permute-start | bytes 24584 | tf_op jit(solution)/shard_map/ppermute | solution.py:408
  11.7 1.3 %collective-permute-start.5 = (f32[4,24,128]{2,1,0:T(8,128)S(1)}, f32[4,24,128]{2,1,0:T(8,128)S(1)}, u32[]{:S(2)}, u32[]{:S(2)}) collective-permute-start(f32[4,24,128]{2,1,0:T(8,128)S(1)} %get-tuple-element.28), channel_id=1, source_target_pairs={{0,8},{8,0},{16,24},{24,16},{1,9},{9,1},{17,25},{25,17},{2,10},{10... | collective-permute-start | bytes 147464 | tf_op jit(solution)/shard_map/ppermute | solution.py:507
  13.0 5.1 %collective-permute-start.9 = (f32[2,24,128]{2,1,0:T(8,128)S(1)}, f32[2,24,128]{2,1,0:T(8,128)S(1)}, u32[]{:S(2)}, u32[]{:S(2)}) collective-permute-start(f32[2,24,128]{2,1,0:T(8,128)S(1)} %slice.9), channel_id=1, source_target_pairs={{14,0},{8,2},{10,4},{12,6},{6,8},{0,10},{2,12},{4,14},{30,16},{24,... | collective-permute-start | bytes 73736 | tf_op jit(solution)/shard_map/ppermute | solution.py:402
  16.0 6.9 %collective-permute-start.8 = (f32[8,24,128]{2,1,0:T(8,128)S(1)}, f32[8,24,128]{2,1,0:T(8,128)S(1)}, u32[]{:S(2)}, u32[]{:S(2)}) collective-permute-start(f32[8,24,128]{2,1,0:T(8,128)S(1)} %get-tuple-element.31), channel_id=1, source_target_pairs={{0,1},{1,0},{2,3},{3,2},{4,5},{5,4},{6,7},{7,6},{8,9},{9,8},{10,11... | collective-permute-start | bytes 294920 | tf_op jit(solution)/shard_map/ppermute | solution.py:408
  17.6 6.9 %collective-permute-start.6 = (f32[16,24,128]{2,1,0:T(8,128)S(1)}, f32[16,24,128]{2,1,0:T(8,128)S(1)}, u32[]{:S(2)}, u32[]{:S(2)}) collective-permute-start(f32[16,24,128]{2,1,0:T(8,128)S(1)} %get-tuple-element.29), channel_id=1, source_target_pairs={{0,2},{2,0},{4,6},{6,4},{1,3},{3,1},{5,7},{7,5},{8,10},{10,8},{12,... | collective-permute-start | bytes 589832 | tf_op jit(solution)/shard_map/ppermute | solution.py:408
  17.8 6.6 %collective-permute-start.7 = (f32[16,24,128]{2,1,0:T(8,128)S(1)}, f32[16,24,128]{2,1,0:T(8,128)S(1)}, u32[]{:S(2)}, u32[]{:S(2)}) collective-permute-start(f32[16,24,128]{2,1,0:T(8,128)S(1)} %get-tuple-element.30), channel_id=1, source_target_pairs={{8,0},{4,2},{2,4},{14,6},{0,8},{12,10},{10,12},{6,14},{24,16},{20,... | collective-permute-start | bytes 589832 | tf_op jit(solution)/shard_map/ppermute | solution.py:402
  18.1 3.3 %collective-permute-start.10 = (f32[2,24,128]{2,1,0:T(8,128)S(1)}, f32[2,24,128]{2,1,0:T(8,128)S(1)}, u32[]{:S(2)}, u32[]{:S(2)}) collective-permute-start(f32[2,24,128]{2,1,0:T(8,128)S(1)} %slice_add_fusion), channel_id=1, source_target_pairs={{24,0},{25,1},{16,8},{17,9},{8,16},{9,17},{0,24},{1,25},{26,2},{27... | collective-permute-start | bytes 73736 | tf_op jit(solution)/shard_map/ppermute | solution.py:402
  21.4 5.0 %collective-permute-start.11 = (f32[2,24,128]{2,1,0:T(8,128)S(1)}, f32[2,24,128]{2,1,0:T(8,128)S(1)}, u32[]{:S(2)}, u32[]{:S(2)}) collective-permute-start(f32[2,24,128]{2,1,0:T(8,128)S(1)} %add.11.refs_0_), channel_id=1, source_target_pairs={{9,0},{8,1},{1,8},{0,9},{25,16},{24,17},{17,24},{16,25},{11,2},{10... | collective-permute-start | bytes 73736 | tf_op jit(solution)/shard_map/ppermute | solution.py:402

commit v8 on v7

--- a/solution.py
+++ b/solution.py
@@ -135,24 +135,24 @@
             out = faces.pop(0)
             upper = upper_of(axis, side)
             if axis == "sec":
-                out[...] = own_z[jnp.where(upper, 1, 0)]
+                out[pl.ds(0, rows), :] = own_z[jnp.where(upper, 1, 0)]
                 continue
             start, step, count = face_rows(axis, upper, planes, width)
             for i in range(count):
                 r = start + i * step
-                out[pl.ds(i, 1), :] = rows_out[r, pl.ds(species, 1), :]
-                out[pl.ds(count + i, 1), :] = rows_out[r, pl.ds(species + 1, 1), :]
-
-
-def wide_face_kernel(planes, has_b, cells, held, *faces):
-    faces = list(faces)
+                if axis == "gy":
+                    out[i] = rows_out[r]
+                else:
+                    out[pl.ds(i, 1), :] = rows_out[r, pl.ds(species, 1), :]
+                    out[pl.ds(count + i, 1), :] = rows_out[r, pl.ds(species + 1, 1), :]
+
+
+def plane_kernel(planes, cells, held, *faces):
     width = cells.shape[0] // planes
-    for axis, both in zip(("gx", "gy"), has_b):
-        for side in range(1 + both):
-            out = faces.pop(0)
-            start, step, count = face_rows(axis, upper_of(axis, side), planes, width)
-            for i in range(count):
-                out[i] = cells[start + i * step]
+    for side, out in enumerate(faces):
+        start, step, count = face_rows("gx", upper_of("gx", side), planes, width)
+        for i in range(count):
+            out[i] = cells[start + i * step]
 
 
 def inner_kernel(
@@ -258,24 +258,29 @@
         for side in range(2):
             halo = received[axis][side]
             start, step, count = face_rows(axis, upper_of(axis, side), planes, width)
-            there = jnp.zeros((2 * count, depth), F32)
-            there = there if halo is None else halo[...]
-            if side and halo is not None:
-                inside = jnp.broadcast_to(has_neighbour(axis, side), there.shape)
-                outside = jnp.where(rows_of(there.shape) < count, 0.0, -1.0)
-                there = jnp.where(inside, there, outside)
-            if halo is None:
-                there = jnp.where(rows_of(there.shape) < count, 0.0, -1.0)
+            inside = jnp.broadcast_to(has_neighbour(axis, side), (1, depth))
+
+            def there(i):
+                if halo is None:
+                    return jnp.zeros((1, depth), F32), jnp.full((1, depth), -1.0, F32)
+                if axis == "gx":
+                    d, bins = halo[pl.ds(i, 1), :], halo[pl.ds(count + i, 1), :]
+                else:
+                    d = halo[i, pl.ds(species, 1), :]
+                    bins = halo[i, pl.ds(species + 1, 1), :]
+                if side:
+                    d, bins = jnp.where(inside, d, 0.0), jnp.where(inside, bins, -1.0)
+                return d, bins
+
             made = jnp.zeros((2 * rows, NB), F32)
             for first in range(0, count, 2):
                 values, found = [], []
                 for i in (first, first + 1):
                     c = cells[start + i * step]
-                    d = 0.5 * (c[species : species + 1] + there[i : i + 1])
+                    d, bins = there(i)
+                    d = 0.5 * (c[species : species + 1] + d)
                     values.append(halves(weight * d * c))
-                    found.append(
-                        hits(there[count + i : count + i + 1]) - hits(c[species + 1 : species + 2])
-                    )
+                    found.append(hits(bins) - hits(c[species + 1 : species + 2]))
                 if axis == "gx":
                     made += binned(
                         jnp.concatenate(values, axis=1), jnp.concatenate(found, axis=1)
@@ -296,9 +301,8 @@
         if halo is None:
             halo = jnp.zeros_like(c)
         else:
-            halo = jnp.where(
-                jnp.broadcast_to(has_neighbour("sec", side), halo.shape), halo[...], 0.0
-            )
+            inside = jnp.broadcast_to(has_neighbour("sec", side), c.shape)
+            halo = jnp.where(inside, halo[pl.ds(0, rows), :], 0.0)
         d = 0.5 * (c[species : species + 1] + halo[species : species + 1])
         delta = weight * d * (halo - c)
         dz[side] = delta
@@ -319,28 +323,10 @@
         window[s // 2] = jnp.concatenate(parts, axis=1)
 
 
-def finish_kernel(planes, has_b, cells, advanced, dz, weights, *refs):
-    halos = list(refs[: 2 + sum(has_b)])
-    out, finished, total, sem = refs[2 + sum(has_b) :]
-    finished[...] = jnp.zeros_like(finished)
+def interior_kernel(planes, advanced, dz, total, out, sem):
     row_count, rows, depth = advanced.shape
     species = out.shape[0]
     width = row_count // planes
-    weight = jnp.broadcast_to(weight_column(weights, rows), (rows, depth))
-    total[...] = advanced[...]
-    for axis, both in zip(("gx", "gy"), has_b):
-        for side in range(2):
-            halo = halos.pop(0) if side <= both else None
-            start, step, count = face_rows(axis, upper_of(axis, side), planes, width)
-            inside = jnp.broadcast_to(has_neighbour(axis, side), (rows, depth))
-            for i in range(count):
-                r = start + i * step
-                c = cells[r]
-                there = jnp.zeros_like(c) if halo is None else halo[i]
-                if side:
-                    there = jnp.where(inside, there, 0.0)
-                d = 0.5 * (c[species : species + 1] + there[species : species + 1])
-                total[r] += weight * d * (there - c)
     shape = (rows, depth)
     lane = lanes_of(shape)
     even = jnp.broadcast_to(upper_of("sec", 0), shape)
@@ -352,7 +338,9 @@
             turned = depth - r if r else 0
             a = pltpu.roll(low, turned, axis=1) if r else low
             b = pltpu.roll(high, turned, axis=1) if r else high
-            total[r] += jnp.where(lane == 0, a, jnp.where(lane == depth - 1, b, 0.0))
+            total[r] = advanced[r] + jnp.where(
+                lane == 0, a, jnp.where(lane == depth - 1, b, 0.0)
+            )
         span = pl.ds(plane * width, width)
         for k in range(species):
             pltpu.make_async_copy(
@@ -365,27 +353,91 @@
         ).wait()
 
 
-def means_kernel(after, *refs):
-    terms, out = refs[:-1], refs[-1]
-    species, per_device, bins = out.shape
+def last_kernel(planes, has_b, n_terms, cells, total, weights, first_out, *refs):
+    halos, terms = list(refs[: 2 + sum(has_b)]), refs[2 + sum(has_b) :][:n_terms]
+    out, means_out, changed, means, sem = refs[2 + sum(has_b) + n_terms :]
+    row_count, rows, depth = total.shape
+    species = out.shape[0]
+    width = row_count // planes
+    per_device, bins = means.shape[1:]
     for s in range(0, per_device, 2):
         block = sum((term[s // 2] for term in terms[1:]), terms[0][s // 2])
-        means = block / jnp.maximum(block[species + 1 : species + 2], 1.0)
-        out[:, s, :] = means[:species, :bins]
-        out[:, s + 1, :] = means[:species, bins:]
+        block = block / jnp.maximum(block[species + 1 : species + 2], 1.0)
+        means[:, s, :] = block[:species, :bins]
+        means[:, s + 1, :] = block[:species, bins:]
+    copies = [pltpu.make_async_copy(means, means_out, sem.at[0])]
+    copies[0].start()
+
+    weight = jnp.broadcast_to(weight_column(weights, rows), (rows, depth))
+    received = {}
+    for axis, both in zip(("gx", "gy"), has_b):
+        received[axis] = [halos.pop(0), halos.pop(0) if both else None]
+
+    def share(axis, upper, c, i):
+        first, second = received[axis]
+        is_first = jnp.broadcast_to(upper_of(axis, 0) if upper else upper_of(axis, 1), c.shape)
+        inside = jnp.broadcast_to(has_neighbour(axis, 1), c.shape)
+        other = jnp.zeros_like(c) if second is None else jnp.where(inside, second[i], 0.0)
+        there = jnp.where(is_first, first[i], other)
+        d = 0.5 * (c[species : species + 1] + there[species : species + 1])
+        return weight * d * (there - c)
+
+    n = 0
+    for x in (0, planes - 1):
+        for y in range(width):
+            r = x * width + y
+            c = cells[r]
+            new = total[r] + share("gx", x > 0, c, y)
+            if y in (0, width - 1):
+                new += share("gy", y > 0, c, x)
+            changed[n + y] = new
+        for k in range(species):
+            copies.append(
+                pltpu.make_async_copy(
+                    changed.at[pl.ds(n, width), k, :],
+                    out.at[k, pl.ds(x * width, width)],
+                    sem.at[1],
+                )
+            )
+            copies[-1].start()
+        n += width
+    planes_changed = changed.at[pl.ds(0, n), pl.ds(0, species), :]
+    cells_out = out.reshape(species, planes, width, depth)
+    start = n
+    for y in (0, width - 1):
+        for x in range(1, planes - 1):
+            r = x * width + y
+            changed[n + x - 1] = total[r] + share("gy", y > 0, cells[r], x)
+        for k in range(species):
+            copies.append(
+                pltpu.make_async_copy(
+                    changed.at[pl.ds(n, planes - 2), k, :],
+                    cells_out.at[k, pl.ds(1, planes - 2), y, :],
+                    sem.at[2],
+                )
+            )
+            copies[-1].start()
+        n += planes - 2
+    rows_changed = changed.at[pl.ds(start, n - start), pl.ds(0, species), :]
+    copies[0].wait()
+    pltpu.make_async_copy(planes_changed, planes_changed, sem.at[1]).wait()
+    pltpu.make_async_copy(rows_changed, rows_changed, sem.at[2]).wait()
 
 
 def struct(*shape):
     return jax.ShapeDtypeStruct(shape, F32)
 
 
-def call(kernel, name, out_shape, n_in, out_specs, in_specs=None, scratch=(), flops=0, moved=0):
+def call(
+    kernel, name, out_shape, n_in, out_specs, in_specs=None, scratch=(), flops=0, moved=0, aliases=None
+):
     return pl.pallas_call(
         kernel,
         out_shape=out_shape,
         in_specs=in_specs or [VMEM] * n_in,
         out_specs=out_specs,
         scratch_shapes=list(scratch),
+        input_output_aliases=aliases or {},
         name=name,
         compiler_params=pltpu.CompilerParams(vmem_limit_bytes=32 * 1024 * 1024),
         cost_estimate=pl.CostEstimate(flops=flops, bytes_accessed=moved, transcendentals=0),
@@ -423,9 +475,13 @@
     steps = [(1 << n, 0) for n in range(1, deep.bit_length() - 1)]
     steps += [(0, 1 << n) for n in range(gy.bit_length() - 1)]
     terms = [block]
-    for e, f in steps:
+    while steps:
+        (a, b), (c, d) = steps.pop(0), steps.pop(0) if steps else (0, 0)
         block = sum(terms[1:], terms[0])
-        terms = [block, joint(block, "gy", lambda s, i: (s ^ 1 ^ e, i ^ f))]
+        terms = [block]
+        for e, f in dict.fromkeys([(a, b), (c, d), (a ^ c, b ^ d)]):
+            if e or f:
+                terms.append(joint(block, "gy", lambda s, i: (s ^ 1 ^ e, i ^ f)))
     return terms
 
 
@@ -454,12 +510,14 @@
         for axis, both in zip(("gx", "gy", "sec"), has_b)
         for side in range(1 + both)
     ]
-    narrow = {
-        "gx": struct(2 * width, depth),
-        "gy": struct(2 * planes, depth),
-        "sec": struct(rows, row_count),
+    shapes = {
+        ("gx", 0): struct(2 * width, depth),
+        ("gx", 1): struct(2 * width, depth),
+        ("gy", 0): struct(planes, rows, depth),
+        ("gy", 1): struct(planes, rows, depth),
+        ("sec", 0): struct(rows, row_count),
+        ("sec", 1): struct(max(rows, 2 * width + SUBLANES), row_count),
     }
-    wide = {"gx": struct(width, rows, depth), "gy": struct(planes, rows, depth)}
 
     rows_in, own_z, *faces = call(
         functools.partial(pack_kernel, planes, has_b),
@@ -467,7 +525,7 @@
         [
             struct(row_count, rows, depth),
             struct(2, rows, row_count),
-            *[narrow[axis] for axis, _ in sides],
+            *[shapes[side] for side in sides],
         ],
         3,
         [VMEM] * (2 + len(sides)),
@@ -507,31 +565,43 @@
     window = window + lax.ppermute(window, "sec", [(i, i ^ 1) for i in range(deep)])
     terms = summed(window)
 
-    wide_sides = [(axis, side) for axis, side in sides if axis != "sec"]
-    wide_faces = call(
-        functools.partial(wide_face_kernel, planes, has_b),
-        "wide_faces",
-        [wide[axis] for axis, _ in wide_sides],
+    outer_planes = call(
+        functools.partial(plane_kernel, planes),
+        "planes",
+        [struct(width, rows, depth)] * (1 + has_b[0]),
         2,
-        [VMEM] * len(wide_sides),
+        [VMEM] * (1 + has_b[0]),
     )(rows_in, window)
-    wide_halos = [swapped(face, axis, side) for face, (axis, side) in zip(wide_faces, wide_sides)]
-    advanced, finished = call(
-        functools.partial(finish_kernel, planes, has_b[:2]),
-        "advance",
-        [struct(species, row_count, depth), struct(SUBLANES, LANES)],
-        4 + len(wide_halos),
-        [ANY, VMEM],
-        scratch=[
-            pltpu.VMEM((row_count, rows, depth), F32),
-            pltpu.SemaphoreType.DMA((planes,)),
-        ],
+    wide_halos = [swapped(face, "gx", side) for side, face in enumerate(outer_planes)]
+    wide_halos += [halo for halo, (axis, _) in zip(halos, sides) if axis == "gy"]
+
+    total, advanced = call(
+        functools.partial(interior_kernel, planes),
+        "interior",
+        [struct(row_count, rows, depth), struct(species, row_count, depth)],
+        2,
+        [VMEM, ANY],
+        scratch=[pltpu.SemaphoreType.DMA((planes,))],
         flops=1_000_000,
         moved=3_000_000,
-    )(rows_in, inner, dz, weights, *wide_halos)
-    cond_means = call(
-        means_kernel, "means", struct(species, per_device, NB), 1 + len(terms), VMEM
-    )(finished, *terms)
+    )(inner, dz)
+    ins = [rows_in, total, weights, advanced, *wide_halos, *terms]
+    specs = [VMEM] * len(ins)
+    specs[3] = ANY
+    advanced, cond_means = call(
+        functools.partial(last_kernel, planes, has_b[:2], len(terms)),
+        "last",
+        [struct(species, row_count, depth), struct(species, per_device, NB)],
+        len(ins),
+        [ANY, ANY],
+        in_specs=specs,
+        scratch=[
+            pltpu.VMEM((2 * (width + planes - 2), rows, depth), F32),
+            pltpu.VMEM((species, per_device, NB), F32),
+            pltpu.SemaphoreType.DMA((3,)),
+        ],
+        aliases={3: 0},
+    )(*ins)
     return advanced.reshape(composition_matrix.shape), cond_means
 
 

time: 27.4 us -> 24.9 us (0.909)
  waiting for transfers between devices: 5.74 us -> 2.78 us
  Pallas kernels: 7.38 us -> 7.8 us
    ppermute x5 -> x6, starting transfers between devices: 4.94 us -> 6.56 us  [joint(): return lax.ppermute(block, ('sec', axis), pairs)]
    ppermute x5 -> x4, waiting for transfers between devices: 1.6 us -> 0.02 us  [swapped(): return lax.ppermute(block, axis, [(i, i ^ 1) for i in range(count)])]
    ppermute x5 -> x4, starting transfers between devices: 6.92 us -> 5.54 us  [swapped(): return lax.ppermute(block, axis, [(i, i ^ 1) for i in range(count)])]
    ppermute x5 -> x6, waiting for transfers between devices: 3.1 us -> 1.88 us  [joint(): return lax.ppermute(block, ('sec', axis), pairs)]
    ppermute x1, starting transfers between devices: 1.13 us -> 0.68 us  [swapped(): return lax.ppermute(block, axis, [*pairs, (0, count - 1), (count - 1, 0)])]
    pallas_call x1, Pallas kernels: 2.07 us -> 2.39 us  [on_device(): call(functools.partial(inner_kernel, planes), 'inside', [struct(row_count...]
    ppermute x1, starting transfers between devices: 0.26 us -> 0.56 us  [on_device(): lax.ppermute(window, 'sec', [(i, i ^ 1) for i in range(deep)])]
  transfers between devices with their start and end apart: 12 -> 12, of which waited for: 5 -> 3; matrix products, arithmetic and copies ran while one was open for 0% -> 0% of each run, Pallas kernels for 15% -> 17%
where the time goes in v8:
time: 24.9 us; the launch traced here: 24.8 us
  starting transfers between devices  13.3 us (53%)
  Pallas kernels  7.8 us (31%)
  waiting for transfers between devices  2.78 us (11%)
  between operations  0.79 us (3%)
    ppermute x6, starting transfers between devices, joint(): return lax.ppermute(block, ('sec', axis), pairs)  6.56 us
    ppermute x4, starting transfers between devices, swapped(): return lax.ppermute(block, axis, [(i, i ^ 1) for i in range(count)])  5.54 us
    pallas_call x1, Pallas kernels, on_device(): call(functools.partial(inner_kernel, planes), 'inside', [struct(row_count...  2.39 us
    ppermute x6, waiting for transfers between devices, joint(): return lax.ppermute(block, ('sec', axis), pairs)  1.88 us
    pallas_call x1, Pallas kernels, on_device(): call(functools.partial(pack_kernel, planes, has_b), 'faces', [struct(row_...  1.84 us
    pallas_call x1, Pallas kernels, on_device(): call(functools.partial(interior_kernel, planes), 'interior', [struct(row_...  1.72 us
    pallas_call x1, Pallas kernels, on_device(): call(functools.partial(last_kernel, planes, has_b[:2], len(terms)), 'last...  1.09 us
    ppermute x1, waiting for transfers between devices, on_device(): lax.ppermute(window, 'sec', [(i, i ^ 1) for i in range(deep)])  0.88 us
  transfers between devices with their start and end apart: 12, of which 3 were waited for; matrix products, arithmetic and copies ran while one was open for 0% of the time, Pallas kernels for 17%

profile of v8, /device:TPU:0, one launch (start us, length us, event | category | flops | bytes accessed | tf_op | source)
XLA Modules:
  0.0 24.8 jit_solution(582907676252381129)
XLA Ops:
  0.6 0.0 copy-start
  0.6 0.0 copy-start.1
  0.7 0.0 copy-start.3
  0.7 0.0 copy-start.2
  0.7 0.0 copy-start.4
  0.7 1.8 %faces.1 = (f32[128,24,128]{2,1,0:T(8,128)S(1)}, f32[2,24,128]{2,1,0:T(8,128)S(1)}, f32[32,128]{1,0:T(8,128)S(1)}, f32[32,128]{1,0:T(8,128)S(1)}, f32[8,24,128]{...) custom-call(f32[22,128,128]{2,1,0:T(8,128)} %bitcast.14, f32[128,128]{1,0:T(8,128)} %bitcast.7, ...), custom_call_target="tpu_custom_call" | custom-call | tf_op jit(solution)/shard_map/faces/pallas_call | solution.py:522
  2.5 3.0 %collective-permute-start.2 = (f32[8,24,128]{2,1,0:T(8,128)S(1)}, f32[8,24,128]{2,1,0:T(8,128)S(1)}, u32[]{:S(2)}, u32[]{:S(2)}) collective-permute-start(f32[8,24,128]{2,1,0:T(8,128)S(1)} %get-tuple-element.25), channel_id=1, source_target_pairs={{0,1},{1,0},{2,3},{3,2},{4,5},{5,4},{6,7},{7,6},{8,9},{9,8},{10,11... | collective-permute-start | bytes 294920 | tf_op jit(solution)/shard_map/ppermute | solution.py:460
  5.5 0.7 %collective-permute-start.4 = (f32[40,128]{1,0:T(8,128)S(1)}, f32[40,128]{1,0:T(8,128)S(1)}, u32[]{:S(2)}, u32[]{:S(2)}) collective-permute-start(f32[40,128]{1,0:T(8,128)S(1)} %get-tuple-element.27), channel_id=1, source_target_pairs={{8,16},{16,8},{0,24},{24,0},{9,17},{17,9},{1,25},{25,1},{10,18},{1... | collective-permute-start | bytes 61448 | tf_op jit(solution)/shard_map/ppermute | solution.py:463
  6.2 1.6 %collective-permute-start = (f32[32,128]{1,0:T(8,128)S(1)}, f32[32,128]{1,0:T(8,128)S(1)}, u32[]{:S(2)}, u32[]{:S(2)}) collective-permute-start(f32[32,128]{1,0:T(8,128)S(1)} %get-tuple-element.23), channel_id=1, source_target_pairs={{0,2},{2,0},{4,6},{6,4},{1,3},{3,1},{5,7},{7,5},{8,10},{10,8},{12,... | collective-permute-start | bytes 49160 | tf_op jit(solution)/shard_map/ppermute | solution.py:460
  7.8 0.7 %collective-permute-start.1 = (f32[32,128]{1,0:T(8,128)S(1)}, f32[32,128]{1,0:T(8,128)S(1)}, u32[]{:S(2)}, u32[]{:S(2)}) collective-permute-start(f32[32,128]{1,0:T(8,128)S(1)} %get-tuple-element.24), channel_id=1, source_target_pairs={{8,0},{4,2},{2,4},{14,6},{0,8},{12,10},{10,12},{6,14},{24,16},{20,... | collective-permute-start | bytes 49160 | tf_op jit(solution)/shard_map/ppermute | solution.py:454
  8.5 0.0 collective-permute-start.3
  8.5 0.0 copy-done
  8.5 0.0 copy-done.1
  8.5 0.0 copy-done.3
  8.5 0.0 copy-done.2
  8.5 2.4 %inside.1 = (f32[128,24,128]{2,1,0:T(8,128)S(1)}, f32[5,24,64]{2,1,0:T(8,128)S(1)}) custom-call(f32[128,24,128]{2,1,0:T(8,128)S(1)} %get-tuple-element.19.cells, f32[128,128]{1,0:T(8,128)S(1)} %bitcast.8, f32[128,128]{1,0:T(8,128)S(1)} %bitcast.9, f32[1,22]{1,0:T(1,128)S(1)} %bitcast.10, f32[22,22]{1,0:T(8,128)S(1)} %copy-done.2), custom_call_target="tpu_custom_call" | custom-call | flops 10000000 | bytes 4000000 | tf_op jit(solution)/shard_map/inside/pallas_call | solution.py:541
  10.9 0.0 collective-permute-done.3.refs_3_
  10.9 0.0 collective-permute-done.refs_0_
  10.9 0.0 collective-permute-done.1.refs_1_
  10.9 0.0 collective-permute-done.4.refs_4_
  10.9 0.0 collective-permute-done.2.refs_2_
  11.0 0.0 copy-done.4
  11.0 0.7 %edges.1 = (f32[4,24,128]{2,1,0:T(8,128)S(1)}, f32[2,24,128]{2,1,0:T(8,128)S(1)}) custom-call(f32[128,24,128]{2,1,0:T(8,128)S(1)} %get-tuple-element.19.cells, f32[2,24,128]{2,1,0:T(8,128)S(1)} %get-tuple-element.21.own_z, f32[5,24,64]{2,1,0:T(8,128)S(1)} %get-tuple-element.22.sums, f32[1,22]{1,0:T(1,128)S(1)} %bitcast.11, s32[1,32]{1,0:T(1,128)S(1)} %bitcast.13, ...), custom_call_target="tpu_custom_call" | custom-call | tf_op jit(solution)/shard_map/edges/pallas_call | solution.py:555
  11.7 0.6 %collective-permute-start.5 = (f32[4,24,128]{2,1,0:T(8,128)S(1)}, f32[4,24,128]{2,1,0:T(8,128)S(1)}, u32[]{:S(2)}, u32[]{:S(2)}) collective-permute-start(f32[4,24,128]{2,1,0:T(8,128)S(1)} %get-tuple-element.31), channel_id=1, source_target_pairs={{0,8},{8,0},{16,24},{24,16},{1,9},{9,1},{17,25},{25,17},{2,10},{10... | collective-permute-start | bytes 147464 | tf_op jit(solution)/shard_map/ppermute | solution.py:565
  12.3 0.9 %collective-permute-done.5 = f32[4,24,128]{2,1,0:T(8,128)S(1)} collective-permute-done((f32[4,24,128]{2,1,0:T(8,128)S(1)}, f32[4,24,128]{2,1,0:T(8,128)S(1)}, u32[]{:S(2)}, u32[]{:S(2)}) %collective-permute-start.5) | collective-permute-done | bytes 49184 | tf_op jit(solution)/shard_map/ppermute | solution.py:565
  13.2 2.5 %collective-permute-start.8 = (f32[2,24,128]{2,1,0:T(8,128)S(1)}, f32[2,24,128]{2,1,0:T(8,128)S(1)}, u32[]{:S(2)}, u32[]{:S(2)}) collective-permute-start(f32[2,24,128]{2,1,0:T(8,128)S(1)} %slice.9), channel_id=1, source_target_pairs={{14,0},{8,2},{10,4},{12,6},{6,8},{0,10},{2,12},{4,14},{30,16},{24,... | collective-permute-start | bytes 73736 | tf_op jit(solution)/shard_map/ppermute | solution.py:454
  15.7 1.0 %collective-permute-start.6 = (f32[16,24,128]{2,1,0:T(8,128)S(1)}, f32[16,24,128]{2,1,0:T(8,128)S(1)}, u32[]{:S(2)}, u32[]{:S(2)}) collective-permute-start(f32[16,24,128]{2,1,0:T(8,128)S(1)} %get-tuple-element.32), channel_id=1, source_target_pairs={{0,2},{2,0},{4,6},{6,4},{1,3},{3,1},{5,7},{7,5},{8,10},{10,8},{12,... | collective-permute-start | bytes 589832 | tf_op jit(solution)/shard_map/ppermute | solution.py:460
  16.7 0.1 collective-permute-start.7
  16.7 1.5 %collective-permute-done.8 = f32[2,24,128]{2,1,0:T(8,128)S(1)} collective-permute-done((f32[2,24,128]{2,1,0:T(8,128)S(1)}, f32[2,24,128]{2,1,0:T(8,128)S(1)}, u32[]{:S(2)}, u32[]{:S(2)}) %collective-permute-start.8) | collective-permute-done | bytes 24608 | tf_op jit(solution)/shard_map/ppermute | solution.py:454
  18.3 0.5 %collective-permute-start.9 = (f32[2,24,128]{2,1,0:T(8,128)S(1)}, f32[2,24,128]{2,1,0:T(8,128)S(1)}, u32[]{:S(2)}, u32[]{:S(2)}) collective-permute-start(f32[2,24,128]{2,1,0:T(8,128)S(1)} %slice_add_fusion.refs_3_), channel_id=1, source_target_pairs={{24,0},{25,1},{16,8},{17,9},{8,16},{9,17},{0,24},{1,25},{26,2},{27... | collective-permute-start | bytes 73736 | tf_op jit(solution)/shard_map/ppermute | solution.py:454
  18.7 0.3 %collective-permute-start.10 = (f32[2,24,128]{2,1,0:T(8,128)S(1)}, f32[2,24,128]{2,1,0:T(8,128)S(1)}, u32[]{:S(2)}, u32[]{:S(2)}) collective-permute-start(f32[2,24,128]{2,1,0:T(8,128)S(1)} %slice_add_fusion.refs_3_), channel_id=1, source_target_pairs={{9,0},{8,1},{1,8},{0,9},{25,16},{24,17},{17,24},{16,25},{11,2},{10... | collective-permute-start | bytes 73736 | tf_op jit(solution)/shard_map/ppermute | solution.py:454
  19.1 2.5 %collective-permute-start.11 = (f32[2,24,128]{2,1,0:T(8,128)S(1)}, f32[2,24,128]{2,1,0:T(8,128)S(1)}, u32[]{:S(2)}, u32[]{:S(2)}) collective-permute-start(f32[2,24,128]{2,1,0:T(8,128)S(1)} %slice_add_fusion.refs_3_), channel_id=1, source_target_pairs={{25,0},{24,1},{17,8},{16,9},{9,16},{8,17},{1,24},{0,25},{27,2},{26... | collective-permute-start | bytes 73736 | tf_op jit(solution)/shard_map/ppermute | solution.py:454
  21.6 1.7 %interior.1 = (f32[128,24,128]{2,1,0:T(8,128)S(1)}, f32[22,128,128]{2,1,0:T(8,128)}) custom-call(f32[128,24,128]{2,1,0:T(8,128)S(1)} %get-tuple-element.20.advanced, f32[2,24,128]{2,1,0:T(8,128)S(1)} %get-tuple-element.28.dz), custom_call_target="tpu_custom_call" | custom-call | flops 1000000 | bytes 3000000 | tf_op jit(solution)/shard_map/interior/pallas_call | solution.py:578
  23.3 0.0 collective-permute-done.9.refs_4_
  23.3 0.0 collective-permute-done.10.refs_5_
  23.3 0.3 %collective-permute-done.11.refs_6_ = f32[2,24,128]{2,1,0:T(8,128)S(1)} collective-permute-done((f32[2,24,128]{2,1,0:T(8,128)S(1)}, f32[2,24,128]{2,1,0:T(8,128)S(1)}, u32[]{:S(2)}, u32[]{:S(2)}) %collective-permute-start.11) | collective-permute-done | bytes 24608 | tf_op jit(solution)/shard_map/ppermute | solution.py:454
  23.7 0.0 collective-permute-done.6.refs_0_
  23.7 0.0 collective-permute-done.7.refs_1_
  23.7 1.1 %last.1 = (f32[22,128,128]{2,1,0:T(8,128)}, f32[22,4,64]{2,1,0:T(4,128)}) custom-call(f32[128,24,128]{2,1,0:T(8,128)S(1)} %get-tuple-element.19.cells, f32[128,24,128]{2,1,0:T(8,128)S(1)} %get-tuple-element.29.total, f32[1,22]{1,0:T(1,128)S(1)} %bitcast.12, f32[22,128,128]{2,1,0:T(8,128)} %get-tuple-element.30.first_out, ...), custom_call_target="tpu_custom_call", output_to_operand_aliasing={{0}: (3, {})} | custom-call | tf_op jit(solution)/shard_map/last/pallas_call | solution.py:591
  (4 shorter events, 0.0 us)
Async XLA Ops:
  0.6 7.8 %copy-start = (f32[8,16,128]{2,1,0:T(8,128)S(1)}, f32[8,16,128]{2,1,0:T(8,128)}, u32[]{:S(2)}) copy-start(f32[8,16,128]{2,1,0:T(8,128)} %param.8) | copy-start | bytes 196612
  0.6 7.8 %copy-start.1 = (f32[8,16,128]{2,1,0:T(8,128)S(1)}, f32[8,16,128]{2,1,0:T(8,128)}, u32[]{:S(2)}) copy-start(f32[8,16,128]{2,1,0:T(8,128)} %param.9) | copy-start | bytes 196612
  0.7 7.8 %copy-start.3 = (f32[22]{0:T(128)S(1)}, f32[22]{0:T(128)}, u32[]{:S(2)}) copy-start(f32[22]{0:T(128)} %param.10) | copy-start | bytes 268
  0.7 7.8 %copy-start.2 = (f32[22,22]{1,0:T(8,128)S(1)}, f32[22,22]{1,0:T(8,128)}, u32[]{:S(2)}) copy-start(f32[22,22]{1,0:T(8,128)} %jacobian.1) | copy-start | bytes 5812
  0.7 10.3 %copy-start.4 = (s32[32]{0:T(128)S(1)}, s32[32]{0:T(128)}, u32[]{:S(2)}) copy-start(s32[32]{0:T(128)} %param.13) | copy-start | bytes 388
  2.5 8.4 %collective-permute-start.2 = (f32[8,24,128]{2,1,0:T(8,128)S(1)}, f32[8,24,128]{2,1,0:T(8,128)S(1)}, u32[]{:S(2)}, u32[]{:S(2)}) collective-permute-start(f32[8,24,128]{2,1,0:T(8,128)S(1)} %get-tuple-element.25), channel_id=1, source_target_pairs={{0,1},{1,0},{2,3},{3,2},{4,5},{5,4},{6,7},{7,6},{8,9},{9,8},{10,11... | collective-permute-start | bytes 294920 | tf_op jit(solution)/shard_map/ppermute | solution.py:460
  5.5 5.4 %collective-permute-start.4 = (f32[40,128]{1,0:T(8,128)S(1)}, f32[40,128]{1,0:T(8,128)S(1)}, u32[]{:S(2)}, u32[]{:S(2)}) collective-permute-start(f32[40,128]{1,0:T(8,128)S(1)} %get-tuple-element.27), channel_id=1, source_target_pairs={{8,16},{16,8},{0,24},{24,0},{9,17},{17,9},{1,25},{25,1},{10,18},{1... | collective-permute-start | bytes 61448 | tf_op jit(solution)/shard_map/ppermute | solution.py:463
  6.2 4.7 %collective-permute-start = (f32[32,128]{1,0:T(8,128)S(1)}, f32[32,128]{1,0:T(8,128)S(1)}, u32[]{:S(2)}, u32[]{:S(2)}) collective-permute-start(f32[32,128]{1,0:T(8,128)S(1)} %get-tuple-element.23), channel_id=1, source_target_pairs={{0,2},{2,0},{4,6},{6,4},{1,3},{3,1},{5,7},{7,5},{8,10},{10,8},{12,... | collective-permute-start | bytes 49160 | tf_op jit(solution)/shard_map/ppermute | solution.py:460
  7.8 3.1 %collective-permute-start.1 = (f32[32,128]{1,0:T(8,128)S(1)}, f32[32,128]{1,0:T(8,128)S(1)}, u32[]{:S(2)}, u32[]{:S(2)}) collective-permute-start(f32[32,128]{1,0:T(8,128)S(1)} %get-tuple-element.24), channel_id=1, source_target_pairs={{8,0},{4,2},{2,4},{14,6},{0,8},{12,10},{10,12},{6,14},{24,16},{20,... | collective-permute-start | bytes 49160 | tf_op jit(solution)/shard_map/ppermute | solution.py:454
  8.5 2.4 %collective-permute-start.3 = (f32[24,128]{1,0:T(8,128)S(1)}, f32[24,128]{1,0:T(8,128)S(1)}, u32[]{:S(2)}, u32[]{:S(2)}) collective-permute-start(f32[24,128]{1,0:T(8,128)S(1)} %get-tuple-element.26), channel_id=1, source_target_pairs={{0,8},{8,0},{16,24},{24,16},{1,9},{9,1},{17,25},{25,17},{2,10},{10... | collective-permute-start | bytes 36872 | tf_op jit(solution)/shard_map/ppermute | solution.py:460
  11.7 1.4 %collective-permute-start.5 = (f32[4,24,128]{2,1,0:T(8,128)S(1)}, f32[4,24,128]{2,1,0:T(8,128)S(1)}, u32[]{:S(2)}, u32[]{:S(2)}) collective-permute-start(f32[4,24,128]{2,1,0:T(8,128)S(1)} %get-tuple-element.31), channel_id=1, source_target_pairs={{0,8},{8,0},{16,24},{24,16},{1,9},{9,1},{17,25},{25,17},{2,10},{10... | collective-permute-start | bytes 147464 | tf_op jit(solution)/shard_map/ppermute | solution.py:565
  13.2 5.1 %collective-permute-start.8 = (f32[2,24,128]{2,1,0:T(8,128)S(1)}, f32[2,24,128]{2,1,0:T(8,128)S(1)}, u32[]{:S(2)}, u32[]{:S(2)}) collective-permute-start(f32[2,24,128]{2,1,0:T(8,128)S(1)} %slice.9), channel_id=1, source_target_pairs={{14,0},{8,2},{10,4},{12,6},{6,8},{0,10},{2,12},{4,14},{30,16},{24,... | collective-permute-start | bytes 73736 | tf_op jit(solution)/shard_map/ppermute | solution.py:454
  15.7 7.9 %collective-permute-start.6 = (f32[16,24,128]{2,1,0:T(8,128)S(1)}, f32[16,24,128]{2,1,0:T(8,128)S(1)}, u32[]{:S(2)}, u32[]{:S(2)}) collective-permute-start(f32[16,24,128]{2,1,0:T(8,128)S(1)} %get-tuple-element.32), channel_id=1, source_target_pairs={{0,2},{2,0},{4,6},{6,4},{1,3},{3,1},{5,7},{7,5},{8,10},{10,8},{12,... | collective-permute-start | bytes 589832 | tf_op jit(solution)/shard_map/ppermute | solution.py:460
  16.7 7.0 %collective-permute-start.7 = (f32[16,24,128]{2,1,0:T(8,128)S(1)}, f32[16,24,128]{2,1,0:T(8,128)S(1)}, u32[]{:S(2)}, u32[]{:S(2)}) collective-permute-start(f32[16,24,128]{2,1,0:T(8,128)S(1)} %get-tuple-element.33), channel_id=1, source_target_pairs={{8,0},{4,2},{2,4},{14,6},{0,8},{12,10},{10,12},{6,14},{24,16},{20,... | collective-permute-start | bytes 589832 | tf_op jit(solution)/shard_map/ppermute | solution.py:454
  18.3 5.0 %collective-permute-start.9 = (f32[2,24,128]{2,1,0:T(8,128)S(1)}, f32[2,24,128]{2,1,0:T(8,128)S(1)}, u32[]{:S(2)}, u32[]{:S(2)}) collective-permute-start(f32[2,24,128]{2,1,0:T(8,128)S(1)} %slice_add_fusion.refs_3_), channel_id=1, source_target_pairs={{24,0},{25,1},{16,8},{17,9},{8,16},{9,17},{0,24},{1,25},{26,2},{27... | collective-permute-start | bytes 73736 | tf_op jit(solution)/shard_map/ppermute | solution.py:454
  18.7 4.6 %collective-permute-start.10 = (f32[2,24,128]{2,1,0:T(8,128)S(1)}, f32[2,24,128]{2,1,0:T(8,128)S(1)}, u32[]{:S(2)}, u32[]{:S(2)}) collective-permute-start(f32[2,24,128]{2,1,0:T(8,128)S(1)} %slice_add_fusion.refs_3_), channel_id=1, source_target_pairs={{9,0},{8,1},{1,8},{0,9},{25,16},{24,17},{17,24},{16,25},{11,2},{10... | collective-permute-start | bytes 73736 | tf_op jit(solution)/shard_map/ppermute | solution.py:454
  19.1 4.6 %collective-permute-start.11 = (f32[2,24,128]{2,1,0:T(8,128)S(1)}, f32[2,24,128]{2,1,0:T(8,128)S(1)}, u32[]{:S(2)}, u32[]{:S(2)}) collective-permute-start(f32[2,24,128]{2,1,0:T(8,128)S(1)} %slice_add_fusion.refs_3_), channel_id=1, source_target_pairs={{25,0},{24,1},{17,8},{16,9},{9,16},{8,17},{1,24},{0,25},{27,2},{26... | collective-permute-start | bytes 73736 | tf_op jit(solution)/shard_map/ppermute | solution.py:454

commit v9 on v8

--- a/solution.py
+++ b/solution.py
@@ -244,72 +244,61 @@
 
 def edge_kernel(planes, has_b, cells, own_z, sums, weights, positions, *refs):
     halos = list(refs[: 3 + sum(has_b)])
-    window, dz, station_sums = refs[3 + sum(has_b) :]
+    window, dz = refs[3 + sum(has_b) :]
     row_count, rows, depth = cells.shape
     species = weights.shape[1]
     width = row_count // planes
+    stations = planes // 2 + 1
     weight = jnp.broadcast_to(weight_column(weights, rows), (rows, depth))
     received = {}
     for axis, both in zip(("gx", "gy", "sec"), has_b):
         received[axis] = [halos.pop(0), halos.pop(0) if both else None]
-    station_sums[...] = sums[...]
-
-    for axis in ("gx", "gy"):
-        for side in range(2):
-            halo = received[axis][side]
-            start, step, count = face_rows(axis, upper_of(axis, side), planes, width)
-            inside = jnp.broadcast_to(has_neighbour(axis, side), (1, depth))
-
-            def there(i):
-                if halo is None:
-                    return jnp.zeros((1, depth), F32), jnp.full((1, depth), -1.0, F32)
-                if axis == "gx":
-                    d, bins = halo[pl.ds(i, 1), :], halo[pl.ds(count + i, 1), :]
-                else:
-                    d = halo[i, pl.ds(species, 1), :]
-                    bins = halo[i, pl.ds(species + 1, 1), :]
-                if side:
-                    d, bins = jnp.where(inside, d, 0.0), jnp.where(inside, bins, -1.0)
-                return d, bins
-
-            made = jnp.zeros((2 * rows, NB), F32)
-            for first in range(0, count, 2):
-                values, found = [], []
-                for i in (first, first + 1):
-                    c = cells[start + i * step]
-                    d, bins = there(i)
-                    d = 0.5 * (c[species : species + 1] + d)
-                    values.append(halves(weight * d * c))
-                    found.append(hits(bins) - hits(c[species + 1 : species + 2]))
-                if axis == "gx":
-                    made += binned(
-                        jnp.concatenate(values, axis=1), jnp.concatenate(found, axis=1)
-                    )
-                else:
-                    for i, value, hit in zip((first, first + 1), values, found):
-                        station_sums[(i + 1) // 2] += folded(binned(value, hit))
-            if axis == "gx":
-                plane = jnp.where(upper_of(axis, side), planes - 1, 0)
-                station_sums[(plane + 1) // 2] += folded(made)
-
-    stations = planes // 2 + 1
-    lane = lanes_of((1, row_count))
-    station = ((lane // width + 1) // 2).astype(F32)
-    for side in range(2):
-        c = own_z[jnp.where(upper_of("sec", side), 1, 0)]
-        halo = received["sec"][side]
-        if halo is None:
-            halo = jnp.zeros_like(c)
-        else:
-            inside = jnp.broadcast_to(has_neighbour("sec", side), c.shape)
-            halo = jnp.where(inside, halo[pl.ds(0, rows), :], 0.0)
+
+    def beyond(axis, upper, part, outside):
+        first, second = (halo if halo is None else halo[part] for halo in received[axis])
+        second = jnp.full_like(first, outside) if second is None else second
+        is_first = upper_of(axis, 0) if upper else upper_of(axis, 1)
+        edge = lax.axis_size(axis) - 1 if upper else 0
+        block = jnp.where(jnp.broadcast_to(is_first, first.shape), first, second)
+        inside = jnp.broadcast_to(lax.axis_index(axis) != edge, first.shape)
+        return jnp.where(inside, block, outside)
+
+    values = [[] for _ in range(stations)]
+    found = [[] for _ in range(stations)]
+
+    def moves(x, y, d, bins):
+        c = cells[x * width + y]
+        d = 0.5 * (c[species : species + 1] + d)
+        values[(x + 1) // 2].append(halves(weight * d * c))
+        found[(x + 1) // 2].append(hits(bins) - hits(c[species + 1 : species + 2]))
+
+    for upper in (False, True):
+        d_beyond = beyond("gx", upper, pl.ds(0, width), 0.0)
+        bins_beyond = beyond("gx", upper, pl.ds(width, width), -1.0)
+        for y in range(width):
+            moves((planes - 1) * upper, y, d_beyond[y : y + 1], bins_beyond[y : y + 1])
+    for upper in (False, True):
+        for x in range(planes):
+            d = beyond("gy", upper, (x, pl.ds(species, 1)), 0.0)
+            bins = beyond("gy", upper, (x, pl.ds(species + 1, 1)), -1.0)
+            moves(x, (width - 1) * upper, d, bins)
+    station = ((lanes_of((1, row_count)) // width + 1) // 2).astype(F32)
+    for upper in (False, True):
+        c = own_z[int(upper)]
+        halo = beyond("sec", upper, pl.ds(0, rows), 0.0)
         d = 0.5 * (c[species : species + 1] + halo[species : species + 1])
         delta = weight * d * (halo - c)
-        dz[side] = delta
+        dz[int(upper)] = delta
         value = halves(delta)
-        classes = c[species + 1 : species + 2]
         for j in range(stations):
-            station_sums[j] += folded(binned(value, hits(jnp.where(station == j, classes, -1.0))))
+            values[j].append(value)
+            found[j].append(hits(jnp.where(station == j, c[species + 1 : species + 2], -1.0)))
+
+    station_sums = [
+        sums[j]
+        + folded(binned(jnp.concatenate(values[j], axis=1), jnp.concatenate(found[j], axis=1)))
+        for j in range(stations)
+    ]
     shift = jnp.broadcast_to(positions[0:1, 0:1], (rows, NB))
     per_device = planes // 2
     for s in range(0, 2 * per_device, 2):
@@ -329,10 +318,8 @@
     width = row_count // planes
     shape = (rows, depth)
     lane = lanes_of(shape)
-    even = jnp.broadcast_to(upper_of("sec", 0), shape)
-    high = jnp.where(even, dz[0], dz[1])
-    low = jnp.where(even, dz[1], dz[0])
-    high = pltpu.roll(high, depth - 1, axis=1)
+    low = dz[0]
+    high = pltpu.roll(dz[1], depth - 1, axis=1)
     for plane in range(planes):
         for r in range(plane * width, (plane + 1) * width):
             turned = depth - r if r else 0
@@ -479,7 +466,7 @@
         (a, b), (c, d) = steps.pop(0), steps.pop(0) if steps else (0, 0)
         block = sum(terms[1:], terms[0])
         terms = [block]
-        for e, f in dict.fromkeys([(a, b), (c, d), (a ^ c, b ^ d)]):
+        for e, f in dict.fromkeys([(a, b), (a ^ c, b ^ d), (c, d)]):
             if e or f:
                 terms.append(joint(block, "gy", lambda s, i: (s ^ 1 ^ e, i ^ f)))
     return terms
@@ -558,7 +545,6 @@
         [struct(per_device, rows, 2 * NB), struct(2, rows, row_count)],
         5 + len(halos),
         [VMEM] * 2,
-        scratch=[pltpu.VMEM((per_device + 1, rows, NB), F32)],
     )(rows_in, own_z, sums, weights, positions, *halos)
 
     deep = lax.axis_size("sec")

time: 24.9 us -> 24.8 us (level)
  no operation moved by 1% of the time
where the time goes in v9:
time: 24.8 us; the launch traced here: 24.6 us
  starting transfers between devices  13.3 us (54%)
  Pallas kernels  7.69 us (31%)
  waiting for transfers between devices  2.73 us (11%)
  between operations  0.78 us (3%)
    ppermute x6, starting transfers between devices, joint(): return lax.ppermute(block, ('sec', axis), pairs)  6.56 us
    ppermute x4, starting transfers between devices, swapped(): return lax.ppermute(block, axis, [(i, i ^ 1) for i in range(count)])  5.54 us
    pallas_call x1, Pallas kernels, on_device(): call(functools.partial(inner_kernel, planes), 'inside', [struct(row_count...  2.39 us
    pallas_call x1, Pallas kernels, on_device(): call(functools.partial(pack_kernel, planes, has_b), 'faces', [struct(row_...  1.84 us
    ppermute x6, waiting for transfers between devices, joint(): return lax.ppermute(block, ('sec', axis), pairs)  1.83 us
    pallas_call x1, Pallas kernels, on_device(): call(functools.partial(interior_kernel, planes), 'interior', [struct(row_...  1.72 us
    pallas_call x1, Pallas kernels, on_device(): call(functools.partial(last_kernel, planes, has_b[:2], len(terms)), 'last...  1.09 us
    ppermute x1, waiting for transfers between devices, on_device(): lax.ppermute(window, 'sec', [(i, i ^ 1) for i in range(deep)])  0.88 us
  transfers between devices with their start and end apart: 12, of which 3 were waited for; matrix products, arithmetic and copies ran while one was open for 0% of the time, Pallas kernels for 17%

profile of v9, /device:TPU:0, one launch (start us, length us, event | category | flops | bytes accessed | tf_op | source)
XLA Modules:
  0.0 24.6 jit_solution(3683063315691386242)
XLA Ops:
  0.6 0.0 copy-start
  0.6 0.0 copy-start.1
  0.7 0.0 copy-start.3
  0.7 0.0 copy-start.2
  0.7 0.0 copy-start.4
  0.7 1.8 %faces.1 = (f32[128,24,128]{2,1,0:T(8,128)S(1)}, f32[2,24,128]{2,1,0:T(8,128)S(1)}, f32[32,128]{1,0:T(8,128)S(1)}, f32[32,128]{1,0:T(8,128)S(1)}, f32[8,24,128]{...) custom-call(f32[22,128,128]{2,1,0:T(8,128)} %bitcast.14, f32[128,128]{1,0:T(8,128)} %bitcast.7, ...), custom_call_target="tpu_custom_call" | custom-call | tf_op jit(solution)/shard_map/faces/pallas_call | solution.py:509
  2.5 3.0 %collective-permute-start.2 = (f32[8,24,128]{2,1,0:T(8,128)S(1)}, f32[8,24,128]{2,1,0:T(8,128)S(1)}, u32[]{:S(2)}, u32[]{:S(2)}) collective-permute-start(f32[8,24,128]{2,1,0:T(8,128)S(1)} %get-tuple-element.25), channel_id=1, source_target_pairs={{0,1},{1,0},{2,3},{3,2},{4,5},{5,4},{6,7},{7,6},{8,9},{9,8},{10,11... | collective-permute-start | bytes 294920 | tf_op jit(solution)/shard_map/ppermute | solution.py:447
  5.5 0.7 %collective-permute-start.4 = (f32[40,128]{1,0:T(8,128)S(1)}, f32[40,128]{1,0:T(8,128)S(1)}, u32[]{:S(2)}, u32[]{:S(2)}) collective-permute-start(f32[40,128]{1,0:T(8,128)S(1)} %get-tuple-element.27), channel_id=1, source_target_pairs={{8,16},{16,8},{0,24},{24,0},{9,17},{17,9},{1,25},{25,1},{10,18},{1... | collective-permute-start | bytes 61448 | tf_op jit(solution)/shard_map/ppermute | solution.py:450
  6.2 1.6 %collective-permute-start = (f32[32,128]{1,0:T(8,128)S(1)}, f32[32,128]{1,0:T(8,128)S(1)}, u32[]{:S(2)}, u32[]{:S(2)}) collective-permute-start(f32[32,128]{1,0:T(8,128)S(1)} %get-tuple-element.23), channel_id=1, source_target_pairs={{0,2},{2,0},{4,6},{6,4},{1,3},{3,1},{5,7},{7,5},{8,10},{10,8},{12,... | collective-permute-start | bytes 49160 | tf_op jit(solution)/shard_map/ppermute | solution.py:447
  7.8 0.7 %collective-permute-start.1 = (f32[32,128]{1,0:T(8,128)S(1)}, f32[32,128]{1,0:T(8,128)S(1)}, u32[]{:S(2)}, u32[]{:S(2)}) collective-permute-start(f32[32,128]{1,0:T(8,128)S(1)} %get-tuple-element.24), channel_id=1, source_target_pairs={{8,0},{4,2},{2,4},{14,6},{0,8},{12,10},{10,12},{6,14},{24,16},{20,... | collective-permute-start | bytes 49160 | tf_op jit(solution)/shard_map/ppermute | solution.py:441
  8.5 0.0 collective-permute-start.3
  8.5 0.0 copy-done
  8.5 0.0 copy-done.1
  8.5 0.0 copy-done.3
  8.5 0.0 copy-done.2
  8.5 2.4 %inside.1 = (f32[128,24,128]{2,1,0:T(8,128)S(1)}, f32[5,24,64]{2,1,0:T(8,128)S(1)}) custom-call(f32[128,24,128]{2,1,0:T(8,128)S(1)} %get-tuple-element.19.cells, f32[128,128]{1,0:T(8,128)S(1)} %bitcast.8, f32[128,128]{1,0:T(8,128)S(1)} %bitcast.9, f32[1,22]{1,0:T(1,128)S(1)} %bitcast.10, f32[22,22]{1,0:T(8,128)S(1)} %copy-done.2), custom_call_target="tpu_custom_call" | custom-call | flops 10000000 | bytes 4000000 | tf_op jit(solution)/shard_map/inside/pallas_call | solution.py:528
  10.9 0.0 collective-permute-done.3.refs_3_
  10.9 0.0 collective-permute-done.refs_0_
  10.9 0.0 collective-permute-done.1.refs_1_
  10.9 0.0 collective-permute-done.4.refs_4_
  10.9 0.0 collective-permute-done.2.refs_2_
  11.0 0.0 copy-done.4
  11.0 0.6 %edges.1 = (f32[4,24,128]{2,1,0:T(8,128)S(1)}, f32[2,24,128]{2,1,0:T(8,128)S(1)}) custom-call(f32[128,24,128]{2,1,0:T(8,128)S(1)} %get-tuple-element.19.cells, f32[2,24,128]{2,1,0:T(8,128)S(1)} %get-tuple-element.21.own_z, f32[5,24,64]{2,1,0:T(8,128)S(1)} %get-tuple-element.22.sums, f32[1,22]{1,0:T(1,128)S(1)} %bitcast.11, s32[1,32]{1,0:T(1,128)S(1)} %bitcast.13, ...), custom_call_target="tpu_custom_call" | custom-call | tf_op jit(solution)/shard_map/edges/pallas_call | solution.py:542
  11.6 0.6 %collective-permute-start.5 = (f32[4,24,128]{2,1,0:T(8,128)S(1)}, f32[4,24,128]{2,1,0:T(8,128)S(1)}, u32[]{:S(2)}, u32[]{:S(2)}) collective-permute-start(f32[4,24,128]{2,1,0:T(8,128)S(1)} %get-tuple-element.31), channel_id=1, source_target_pairs={{0,8},{8,0},{16,24},{24,16},{1,9},{9,1},{17,25},{25,17},{2,10},{10... | collective-permute-start | bytes 147464 | tf_op jit(solution)/shard_map/ppermute | solution.py:551
  12.1 0.9 %collective-permute-done.5 = f32[4,24,128]{2,1,0:T(8,128)S(1)} collective-permute-done((f32[4,24,128]{2,1,0:T(8,128)S(1)}, f32[4,24,128]{2,1,0:T(8,128)S(1)}, u32[]{:S(2)}, u32[]{:S(2)}) %collective-permute-start.5) | collective-permute-done | bytes 49184 | tf_op jit(solution)/shard_map/ppermute | solution.py:551
  13.0 2.5 %collective-permute-start.8 = (f32[2,24,128]{2,1,0:T(8,128)S(1)}, f32[2,24,128]{2,1,0:T(8,128)S(1)}, u32[]{:S(2)}, u32[]{:S(2)}) collective-permute-start(f32[2,24,128]{2,1,0:T(8,128)S(1)} %slice.9), channel_id=1, source_target_pairs={{14,0},{8,2},{10,4},{12,6},{6,8},{0,10},{2,12},{4,14},{30,16},{24,... | collective-permute-start | bytes 73736 | tf_op jit(solution)/shard_map/ppermute | solution.py:441
  15.6 1.0 %collective-permute-start.6 = (f32[16,24,128]{2,1,0:T(8,128)S(1)}, f32[16,24,128]{2,1,0:T(8,128)S(1)}, u32[]{:S(2)}, u32[]{:S(2)}) collective-permute-start(f32[16,24,128]{2,1,0:T(8,128)S(1)} %get-tuple-element.32), channel_id=1, source_target_pairs={{0,2},{2,0},{4,6},{6,4},{1,3},{3,1},{5,7},{7,5},{8,10},{10,8},{12,... | collective-permute-start | bytes 589832 | tf_op jit(solution)/shard_map/ppermute | solution.py:447
  16.6 0.1 collective-permute-start.7
  16.6 1.5 %collective-permute-done.8 = f32[2,24,128]{2,1,0:T(8,128)S(1)} collective-permute-done((f32[2,24,128]{2,1,0:T(8,128)S(1)}, f32[2,24,128]{2,1,0:T(8,128)S(1)}, u32[]{:S(2)}, u32[]{:S(2)}) %collective-permute-start.8) | collective-permute-done | bytes 24608 | tf_op jit(solution)/shard_map/ppermute | solution.py:441
  18.2 0.5 %collective-permute-start.9 = (f32[2,24,128]{2,1,0:T(8,128)S(1)}, f32[2,24,128]{2,1,0:T(8,128)S(1)}, u32[]{:S(2)}, u32[]{:S(2)}) collective-permute-start(f32[2,24,128]{2,1,0:T(8,128)S(1)} %slice_add_fusion.refs_3_), channel_id=1, source_target_pairs={{24,0},{25,1},{16,8},{17,9},{8,16},{9,17},{0,24},{1,25},{26,2},{27... | collective-permute-start | bytes 73736 | tf_op jit(solution)/shard_map/ppermute | solution.py:441
  18.6 1.3 %collective-permute-start.10 = (f32[2,24,128]{2,1,0:T(8,128)S(1)}, f32[2,24,128]{2,1,0:T(8,128)S(1)}, u32[]{:S(2)}, u32[]{:S(2)}) collective-permute-start(f32[2,24,128]{2,1,0:T(8,128)S(1)} %slice_add_fusion.refs_3_), channel_id=1, source_target_pairs={{25,0},{24,1},{17,8},{16,9},{9,16},{8,17},{1,24},{0,25},{27,2},{26... | collective-permute-start | bytes 73736 | tf_op jit(solution)/shard_map/ppermute | solution.py:441
  19.9 1.6 %collective-permute-start.11 = (f32[2,24,128]{2,1,0:T(8,128)S(1)}, f32[2,24,128]{2,1,0:T(8,128)S(1)}, u32[]{:S(2)}, u32[]{:S(2)}) collective-permute-start(f32[2,24,128]{2,1,0:T(8,128)S(1)} %slice_add_fusion.refs_3_), channel_id=1, source_target_pairs={{9,0},{8,1},{1,8},{0,9},{25,16},{24,17},{17,24},{16,25},{11,2},{10... | collective-permute-start | bytes 73736 | tf_op jit(solution)/shard_map/ppermute | solution.py:441
  21.5 1.7 %interior.1 = (f32[128,24,128]{2,1,0:T(8,128)S(1)}, f32[22,128,128]{2,1,0:T(8,128)}) custom-call(f32[128,24,128]{2,1,0:T(8,128)S(1)} %get-tuple-element.20.advanced, f32[2,24,128]{2,1,0:T(8,128)S(1)} %get-tuple-element.28.dz), custom_call_target="tpu_custom_call" | custom-call | flops 1000000 | bytes 3000000 | tf_op jit(solution)/shard_map/interior/pallas_call | solution.py:564
  23.2 0.0 collective-permute-done.9.refs_4_
  23.2 0.0 collective-permute-done.10.refs_5_
  23.2 0.3 %collective-permute-done.11.refs_6_ = f32[2,24,128]{2,1,0:T(8,128)S(1)} collective-permute-done((f32[2,24,128]{2,1,0:T(8,128)S(1)}, f32[2,24,128]{2,1,0:T(8,128)S(1)}, u32[]{:S(2)}, u32[]{:S(2)}) %collective-permute-start.11) | collective-permute-done | bytes 24608 | tf_op jit(solution)/shard_map/ppermute | solution.py:441
  23.5 0.0 collective-permute-done.6.refs_0_
  23.5 0.0 collective-permute-done.7.refs_1_
  23.5 1.1 %last.1 = (f32[22,128,128]{2,1,0:T(8,128)}, f32[22,4,64]{2,1,0:T(4,128)}) custom-call(f32[128,24,128]{2,1,0:T(8,128)S(1)} %get-tuple-element.19.cells, f32[128,24,128]{2,1,0:T(8,128)S(1)} %get-tuple-element.29.total, f32[1,22]{1,0:T(1,128)S(1)} %bitcast.12, f32[22,128,128]{2,1,0:T(8,128)} %get-tuple-element.30.first_out, ...), custom_call_target="tpu_custom_call", output_to_operand_aliasing={{0}: (3, {})} | custom-call | tf_op jit(solution)/shard_map/last/pallas_call | solution.py:577
  (4 shorter events, 0.0 us)
Async XLA Ops:
  0.6 7.8 %copy-start = (f32[8,16,128]{2,1,0:T(8,128)S(1)}, f32[8,16,128]{2,1,0:T(8,128)}, u32[]{:S(2)}) copy-start(f32[8,16,128]{2,1,0:T(8,128)} %param.8) | copy-start | bytes 196612
  0.6 7.8 %copy-start.1 = (f32[8,16,128]{2,1,0:T(8,128)S(1)}, f32[8,16,128]{2,1,0:T(8,128)}, u32[]{:S(2)}) copy-start(f32[8,16,128]{2,1,0:T(8,128)} %param.9) | copy-start | bytes 196612
  0.7 7.8 %copy-start.3 = (f32[22]{0:T(128)S(1)}, f32[22]{0:T(128)}, u32[]{:S(2)}) copy-start(f32[22]{0:T(128)} %param.10) | copy-start | bytes 268
  0.7 7.8 %copy-start.2 = (f32[22,22]{1,0:T(8,128)S(1)}, f32[22,22]{1,0:T(8,128)}, u32[]{:S(2)}) copy-start(f32[22,22]{1,0:T(8,128)} %jacobian.1) | copy-start | bytes 5812
  0.7 10.3 %copy-start.4 = (s32[32]{0:T(128)S(1)}, s32[32]{0:T(128)}, u32[]{:S(2)}) copy-start(s32[32]{0:T(128)} %param.13) | copy-start | bytes 388
  2.5 8.4 %collective-permute-start.2 = (f32[8,24,128]{2,1,0:T(8,128)S(1)}, f32[8,24,128]{2,1,0:T(8,128)S(1)}, u32[]{:S(2)}, u32[]{:S(2)}) collective-permute-start(f32[8,24,128]{2,1,0:T(8,128)S(1)} %get-tuple-element.25), channel_id=1, source_target_pairs={{0,1},{1,0},{2,3},{3,2},{4,5},{5,4},{6,7},{7,6},{8,9},{9,8},{10,11... | collective-permute-start | bytes 294920 | tf_op jit(solution)/shard_map/ppermute | solution.py:447
  5.5 5.4 %collective-permute-start.4 = (f32[40,128]{1,0:T(8,128)S(1)}, f32[40,128]{1,0:T(8,128)S(1)}, u32[]{:S(2)}, u32[]{:S(2)}) collective-permute-start(f32[40,128]{1,0:T(8,128)S(1)} %get-tuple-element.27), channel_id=1, source_target_pairs={{8,16},{16,8},{0,24},{24,0},{9,17},{17,9},{1,25},{25,1},{10,18},{1... | collective-permute-start | bytes 61448 | tf_op jit(solution)/shard_map/ppermute | solution.py:450
  6.2 4.7 %collective-permute-start = (f32[32,128]{1,0:T(8,128)S(1)}, f32[32,128]{1,0:T(8,128)S(1)}, u32[]{:S(2)}, u32[]{:S(2)}) collective-permute-start(f32[32,128]{1,0:T(8,128)S(1)} %get-tuple-element.23), channel_id=1, source_target_pairs={{0,2},{2,0},{4,6},{6,4},{1,3},{3,1},{5,7},{7,5},{8,10},{10,8},{12,... | collective-permute-start | bytes 49160 | tf_op jit(solution)/shard_map/ppermute | solution.py:447
  7.8 3.1 %collective-permute-start.1 = (f32[32,128]{1,0:T(8,128)S(1)}, f32[32,128]{1,0:T(8,128)S(1)}, u32[]{:S(2)}, u32[]{:S(2)}) collective-permute-start(f32[32,128]{1,0:T(8,128)S(1)} %get-tuple-element.24), channel_id=1, source_target_pairs={{8,0},{4,2},{2,4},{14,6},{0,8},{12,10},{10,12},{6,14},{24,16},{20,... | collective-permute-start | bytes 49160 | tf_op jit(solution)/shard_map/ppermute | solution.py:441
  8.5 2.4 %collective-permute-start.3 = (f32[24,128]{1,0:T(8,128)S(1)}, f32[24,128]{1,0:T(8,128)S(1)}, u32[]{:S(2)}, u32[]{:S(2)}) collective-permute-start(f32[24,128]{1,0:T(8,128)S(1)} %get-tuple-element.26), channel_id=1, source_target_pairs={{0,8},{8,0},{16,24},{24,16},{1,9},{9,1},{17,25},{25,17},{2,10},{10... | collective-permute-start | bytes 36872 | tf_op jit(solution)/shard_map/ppermute | solution.py:447
  11.6 1.4 %collective-permute-start.5 = (f32[4,24,128]{2,1,0:T(8,128)S(1)}, f32[4,24,128]{2,1,0:T(8,128)S(1)}, u32[]{:S(2)}, u32[]{:S(2)}) collective-permute-start(f32[4,24,128]{2,1,0:T(8,128)S(1)} %get-tuple-element.31), channel_id=1, source_target_pairs={{0,8},{8,0},{16,24},{24,16},{1,9},{9,1},{17,25},{25,17},{2,10},{10... | collective-permute-start | bytes 147464 | tf_op jit(solution)/shard_map/ppermute | solution.py:551
  13.0 5.1 %collective-permute-start.8 = (f32[2,24,128]{2,1,0:T(8,128)S(1)}, f32[2,24,128]{2,1,0:T(8,128)S(1)}, u32[]{:S(2)}, u32[]{:S(2)}) collective-permute-start(f32[2,24,128]{2,1,0:T(8,128)S(1)} %slice.9), channel_id=1, source_target_pairs={{14,0},{8,2},{10,4},{12,6},{6,8},{0,10},{2,12},{4,14},{30,16},{24,... | collective-permute-start | bytes 73736 | tf_op jit(solution)/shard_map/ppermute | solution.py:441
  15.6 7.9 %collective-permute-start.6 = (f32[16,24,128]{2,1,0:T(8,128)S(1)}, f32[16,24,128]{2,1,0:T(8,128)S(1)}, u32[]{:S(2)}, u32[]{:S(2)}) collective-permute-start(f32[16,24,128]{2,1,0:T(8,128)S(1)} %get-tuple-element.32), channel_id=1, source_target_pairs={{0,2},{2,0},{4,6},{6,4},{1,3},{3,1},{5,7},{7,5},{8,10},{10,8},{12,... | collective-permute-start | bytes 589832 | tf_op jit(solution)/shard_map/ppermute | solution.py:447
  16.6 6.9 %collective-permute-start.7 = (f32[16,24,128]{2,1,0:T(8,128)S(1)}, f32[16,24,128]{2,1,0:T(8,128)S(1)}, u32[]{:S(2)}, u32[]{:S(2)}) collective-permute-start(f32[16,24,128]{2,1,0:T(8,128)S(1)} %get-tuple-element.33), channel_id=1, source_target_pairs={{8,0},{4,2},{2,4},{14,6},{0,8},{12,10},{10,12},{6,14},{24,16},{20,... | collective-permute-start | bytes 589832 | tf_op jit(solution)/shard_map/ppermute | solution.py:441
  18.2 5.0 %collective-permute-start.9 = (f32[2,24,128]{2,1,0:T(8,128)S(1)}, f32[2,24,128]{2,1,0:T(8,128)S(1)}, u32[]{:S(2)}, u32[]{:S(2)}) collective-permute-start(f32[2,24,128]{2,1,0:T(8,128)S(1)} %slice_add_fusion.refs_3_), channel_id=1, source_target_pairs={{24,0},{25,1},{16,8},{17,9},{8,16},{9,17},{0,24},{1,25},{26,2},{27... | collective-permute-start | bytes 73736 | tf_op jit(solution)/shard_map/ppermute | solution.py:441
  18.6 4.6 %collective-permute-start.10 = (f32[2,24,128]{2,1,0:T(8,128)S(1)}, f32[2,24,128]{2,1,0:T(8,128)S(1)}, u32[]{:S(2)}, u32[]{:S(2)}) collective-permute-start(f32[2,24,128]{2,1,0:T(8,128)S(1)} %slice_add_fusion.refs_3_), channel_id=1, source_target_pairs={{25,0},{24,1},{17,8},{16,9},{9,16},{8,17},{1,24},{0,25},{27,2},{26... | collective-permute-start | bytes 73736 | tf_op jit(solution)/shard_map/ppermute | solution.py:441
  19.9 3.6 %collective-permute-start.11 = (f32[2,24,128]{2,1,0:T(8,128)S(1)}, f32[2,24,128]{2,1,0:T(8,128)S(1)}, u32[]{:S(2)}, u32[]{:S(2)}) collective-permute-start(f32[2,24,128]{2,1,0:T(8,128)S(1)} %slice_add_fusion.refs_3_), channel_id=1, source_target_pairs={{9,0},{8,1},{1,8},{0,9},{25,16},{24,17},{17,24},{16,25},{11,2},{10... | collective-permute-start | bytes 73736 | tf_op jit(solution)/shard_map/ppermute | solution.py:441

commit v10 on v9

--- a/solution.py
+++ b/solution.py
@@ -155,11 +155,9 @@
             out[i] = cells[start + i * step]
 
 
-def inner_kernel(
-    planes, cells, mixing, thermal, weights, jacobian, advanced, station_sums, coefs, square
-):
+def inner_kernel(planes, cells, mixing, thermal, weights, diffused, sums, heated_sums, coefs):
     row_count, rows, depth = cells.shape
-    species = jacobian.shape[0]
+    species = weights.shape[1]
     width = row_count // planes
     shape = (row_count, depth)
     lane, row = lanes_of(shape), rows_of(shape)
@@ -182,28 +180,17 @@
     down = jnp.concatenate([edge, up[: row_count - width]], axis=0)
     coefs[5] = down
     coefs[6] = total + (up + down)
-    coefs[7] = (4.0 * DT) * jnp.exp(-2.0 / thermal[...])
-
-    square[...] = jnp.zeros_like(square)
-    matrix = jacobian[...]
-    matrix_high = matrix.astype(BF16).astype(F32)
-    square[:species, :species] = matrix_high
-    square[:species, rows : rows + species] = matrix_high
-    square[rows : rows + species, :species] = matrix - matrix_high
-    left = square[...].astype(BF16)
+    coefs[7] = rate(thermal)
 
     weight = jnp.broadcast_to(weight_column(weights, rows), (rows, depth))
     whole = species // SUBLANES * SUBLANES
     ones = rows_of((rows - whole, depth)) >= species - whole
-    station_sums[...] = jnp.zeros_like(station_sums)
-
-    def kinetics(pair):
-        wide = jnp.concatenate([halves(cells[r]) for r in pair], axis=1)
-        return folded(jnp.dot(left, wide, preferred_element_type=F32))
-
-    def advance(pair, mixed):
+    sums[...] = jnp.zeros_like(sums)
+    heated_sums[...] = jnp.zeros_like(heated_sums)
+
+    def advance(pair):
         values, found = [], []
-        for i, r in enumerate(pair):
+        for r in pair:
             x, y = divmod(r, width)
             c = cells[r]
             at = lambda n: coefs[n, pl.ds(r, 1), :]
@@ -218,33 +205,68 @@
             if x > 0:
                 flux += at(5) * cells[r - width]
             flux -= at(6) * c
-            new = c + weight * flux + at(7) * mixed[:, i * depth : (i + 1) * depth]
+            new = c + weight * flux
             new = jnp.concatenate([new[:whole], jnp.where(ones, 1.0, new[whole:])], axis=0)
-            advanced[r] = new
-            values.append(halves(new))
+            diffused[r] = new
+            values.append(jnp.concatenate([halves(new), halves(at(7) * c)], axis=0))
             found.append(hits(cells[r, species + 1 : species + 2, :]))
         return jnp.concatenate(values, axis=1), jnp.concatenate(found, axis=1)
 
     pairs = [(r, r + 1) for r in range(0, row_count, 2)]
-    mixed, values, made = {}, {}, 0.0
-    for t in range(len(pairs) + 2 * AHEAD):
+    values, made = {}, 0.0
+    for t in range(len(pairs) + AHEAD):
         if t < len(pairs):
-            mixed[t] = kinetics(pairs[t])
-        now = t - AHEAD
-        if 0 <= now < len(pairs):
-            values[now] = advance(pairs[now], mixed.pop(now))
-        last = now - AHEAD
-        if 0 <= last < len(pairs):
+            values[t] = advance(pairs[t])
+        last = t - AHEAD
+        if last >= 0:
             made += binned(*values.pop(last))
             x, y = divmod(pairs[last][1], width)
             if y == width - 1:
-                station_sums[(x + 1) // 2] += folded(made)
+                sums[(x + 1) // 2] += folded(made[: 2 * rows])
+                heated_sums[(x + 1) // 2] += folded(made[2 * rows :])
                 made = 0.0
 
 
-def edge_kernel(planes, has_b, cells, own_z, sums, weights, positions, *refs):
+def rate(thermal):
+    return (4.0 * DT) * jnp.exp(-2.0 / thermal[...])
+
+
+def stacked_square(jacobian, square):
+    species, rows = jacobian.shape[0], square.shape[0] // 2
+    square[...] = jnp.zeros_like(square)
+    matrix = jacobian[...]
+    matrix_high = matrix.astype(BF16).astype(F32)
+    square[:species, :species] = matrix_high
+    square[:species, rows : rows + species] = matrix_high
+    square[rows : rows + species, :species] = matrix - matrix_high
+    return square[...].astype(BF16)
+
+
+def kinetics_kernel(cells, diffused, thermal, jacobian, held, advanced, rates, square):
+    row_count, rows, depth = cells.shape
+    left = stacked_square(jacobian, square)
+    rates[...] = rate(thermal)
+    pairs = [(r, r + 1) for r in range(0, row_count, 2)]
+    mixed = {}
+    for t in range(len(pairs) + AHEAD):
+        if t < len(pairs):
+            wide = jnp.concatenate([halves(cells[r]) for r in pairs[t]], axis=1)
+            mixed[t] = folded(jnp.dot(left, wide, preferred_element_type=F32))
+        now = t - AHEAD
+        if now >= 0:
+            product = mixed.pop(now)
+            for i, r in enumerate(pairs[now]):
+                advanced[r] = (
+                    diffused[r]
+                    + rates[pl.ds(r, 1), :] * product[:, i * depth : (i + 1) * depth]
+                )
+
+
+def edge_kernel(
+    planes, has_b, cells, own_z, sums, heated_sums, weights, jacobian, positions, *refs
+):
     halos = list(refs[: 3 + sum(has_b)])
-    window, dz = refs[3 + sum(has_b) :]
+    window, dz, square = refs[3 + sum(has_b) :]
     row_count, rows, depth = cells.shape
     species = weights.shape[1]
     width = row_count // planes
@@ -294,8 +316,10 @@
             values[j].append(value)
             found[j].append(hits(jnp.where(station == j, c[species + 1 : species + 2], -1.0)))
 
+    left = stacked_square(jacobian, square)
     station_sums = [
         sums[j]
+        + folded(jnp.dot(left, halves(heated_sums[j]), preferred_element_type=F32))
         + folded(binned(jnp.concatenate(values[j], axis=1), jnp.concatenate(found[j], axis=1)))
         for j in range(stations)
     ]
@@ -525,30 +549,45 @@
     )(*[pltpu.with_memory_space_constraint(x, pltpu.HBM) for x in (cells, mixing, classes)])
     halos = [swapped(face, axis, side) for face, (axis, side) in zip(faces, sides)]
 
-    inner, sums = call(
+    diffused, sums, heated_sums = call(
         functools.partial(inner_kernel, planes),
         "inside",
-        [struct(row_count, rows, depth), struct(per_device + 1, rows, NB)],
-        5,
-        [VMEM] * 2,
-        scratch=[
-            pltpu.VMEM((8, row_count, depth), F32),
-            pltpu.VMEM((2 * rows, 2 * rows), F32),
+        [
+            struct(row_count, rows, depth),
+            struct(per_device + 1, rows, NB),
+            struct(per_device + 1, rows, NB),
         ],
+        4,
+        [VMEM] * 3,
+        scratch=[pltpu.VMEM((8, row_count, depth), F32)],
         flops=10_000_000,
         moved=4_000_000,
-    )(rows_in, mixing, thermal, weights, kinetics_jacobian)
+    )(rows_in, mixing, thermal, weights)
 
     window, dz = call(
         functools.partial(edge_kernel, planes, has_b),
         "edges",
         [struct(per_device, rows, 2 * NB), struct(2, rows, row_count)],
-        5 + len(halos),
+        7 + len(halos),
         [VMEM] * 2,
-    )(rows_in, own_z, sums, weights, positions, *halos)
+        scratch=[pltpu.VMEM((2 * rows, 2 * rows), F32)],
+    )(rows_in, own_z, sums, heated_sums, weights, kinetics_jacobian, positions, *halos)
 
     deep = lax.axis_size("sec")
     window = window + lax.ppermute(window, "sec", [(i, i ^ 1) for i in range(deep)])
+    advanced = call(
+        kinetics_kernel,
+        "kinetics",
+        struct(row_count, rows, depth),
+        5,
+        VMEM,
+        scratch=[
+            pltpu.VMEM((row_count, depth), F32),
+            pltpu.VMEM((2 * rows, 2 * rows), F32),
+        ],
+        flops=0,
+        moved=0,
+    )(rows_in, diffused, thermal, kinetics_jacobian, window)
     terms = summed(window)
 
     outer_planes = call(
@@ -557,7 +596,7 @@
         [struct(width, rows, depth)] * (1 + has_b[0]),
         2,
         [VMEM] * (1 + has_b[0]),
-    )(rows_in, window)
+    )(rows_in, advanced)
     wide_halos = [swapped(face, "gx", side) for side, face in enumerate(outer_planes)]
     wide_halos += [halo for halo, (axis, _) in zip(halos, sides) if axis == "gy"]
 
@@ -570,7 +609,7 @@
         scratch=[pltpu.SemaphoreType.DMA((planes,))],
         flops=1_000_000,
         moved=3_000_000,
-    )(inner, dz)
+    )(advanced, dz)
     ins = [rows_in, total, weights, advanced, *wide_halos, *terms]
     specs = [VMEM] * len(ins)
     specs[3] = ANY

time: 24.8 us -> 24.5 us (0.988)
  waiting for transfers between devices: 2.73 us -> 1.9 us
  Pallas kernels: 7.69 us -> 8.08 us
    ppermute x6, waiting for transfers between devices: 1.83 us -> 0.85 us  [joint(): return lax.ppermute(block, ('sec', axis), pairs)]
    pallas_call x0 -> x1, Pallas kernels: none -> 0.66 us  [on_device(): call(kinetics_kernel, 'kinetics', struct(row_count, rows, depth), 5, VMEM...]
    pallas_call x1, Pallas kernels: 2.39 us -> 2.08 us  [on_device(): call(functools.partial(inner_kernel, planes), 'inside', [struct(row_count...]
    ppermute x4, starting transfers between devices: 5.54 us -> 5.83 us  [swapped(): return lax.ppermute(block, axis, [(i, i ^ 1) for i in range(count)])]
  transfers between devices with their start and end apart: 12 -> 12, of which waited for: 3 -> 4; matrix products, arithmetic and copies ran while one was open for 0% -> 0% of each run, Pallas kernels for 17% -> 19%
where the time goes in v10:
time: 24.5 us; the launch traced here: 24.3 us
  starting transfers between devices  13.5 us (55%)
  Pallas kernels  8.08 us (33%)
  waiting for transfers between devices  1.9 us (8%)
  between operations  0.8 us (3%)
    ppermute x6, starting transfers between devices, joint(): return lax.ppermute(block, ('sec', axis), pairs)  6.43 us
    ppermute x4, starting transfers between devices, swapped(): return lax.ppermute(block, axis, [(i, i ^ 1) for i in range(count)])  5.83 us
    pallas_call x1, Pallas kernels, on_device(): call(functools.partial(inner_kernel, planes), 'inside', [struct(row_count...  2.08 us
    pallas_call x1, Pallas kernels, on_device(): call(functools.partial(pack_kernel, planes, has_b), 'faces', [struct(row_...  1.84 us
    pallas_call x1, Pallas kernels, on_device(): call(functools.partial(interior_kernel, planes), 'interior', [struct(row_...  1.72 us
    pallas_call x1, Pallas kernels, on_device(): call(functools.partial(last_kernel, planes, has_b[:2], len(terms)), 'last...  1.09 us
    ppermute x1, waiting for transfers between devices, on_device(): lax.ppermute(window, 'sec', [(i, i ^ 1) for i in range(deep)])  0.88 us
    ppermute x6, waiting for transfers between devices, joint(): return lax.ppermute(block, ('sec', axis), pairs)  0.85 us
  transfers between devices with their start and end apart: 12, of which 4 were waited for; matrix products, arithmetic and copies ran while one was open for 0% of the time, Pallas kernels for 19%

profile of v10, /device:TPU:0, one launch (start us, length us, event | category | flops | bytes accessed | tf_op | source)
XLA Modules:
  0.0 24.3 jit_solution(16300174652955373461)
XLA Ops:
  0.6 0.0 copy-start.1
  0.6 0.0 copy-start
  0.7 0.0 copy-start.3
  0.7 0.0 copy-start.2
  0.7 0.0 copy-start.4
  0.7 1.8 %faces.1 = (f32[128,24,128]{2,1,0:T(8,128)S(1)}, f32[2,24,128]{2,1,0:T(8,128)S(1)}, f32[32,128]{1,0:T(8,128)S(1)}, f32[32,128]{1,0:T(8,128)S(1)}, f32[8,24,128]{...) custom-call(f32[22,128,128]{2,1,0:T(8,128)} %bitcast.15, f32[128,128]{1,0:T(8,128)} %bitcast.9, ...), custom_call_target="tpu_custom_call" | custom-call | tf_op jit(solution)/shard_map/faces/pallas_call | solution.py:533
  2.5 3.0 %collective-permute-start.2 = (f32[8,24,128]{2,1,0:T(8,128)S(1)}, f32[8,24,128]{2,1,0:T(8,128)S(1)}, u32[]{:S(2)}, u32[]{:S(2)}) collective-permute-start(f32[8,24,128]{2,1,0:T(8,128)S(1)} %get-tuple-element.27), channel_id=1, source_target_pairs={{0,1},{1,0},{2,3},{3,2},{4,5},{5,4},{6,7},{7,6},{8,9},{9,8},{10,11... | collective-permute-start | bytes 294920 | tf_op jit(solution)/shard_map/ppermute | solution.py:471
  5.5 0.7 %collective-permute-start.4 = (f32[40,128]{1,0:T(8,128)S(1)}, f32[40,128]{1,0:T(8,128)S(1)}, u32[]{:S(2)}, u32[]{:S(2)}) collective-permute-start(f32[40,128]{1,0:T(8,128)S(1)} %get-tuple-element.29), channel_id=1, source_target_pairs={{8,16},{16,8},{0,24},{24,0},{9,17},{17,9},{1,25},{25,1},{10,18},{1... | collective-permute-start | bytes 61448 | tf_op jit(solution)/shard_map/ppermute | solution.py:474
  6.2 1.6 %collective-permute-start = (f32[32,128]{1,0:T(8,128)S(1)}, f32[32,128]{1,0:T(8,128)S(1)}, u32[]{:S(2)}, u32[]{:S(2)}) collective-permute-start(f32[32,128]{1,0:T(8,128)S(1)} %get-tuple-element.25), channel_id=1, source_target_pairs={{0,2},{2,0},{4,6},{6,4},{1,3},{3,1},{5,7},{7,5},{8,10},{10,8},{12,... | collective-permute-start | bytes 49160 | tf_op jit(solution)/shard_map/ppermute | solution.py:471
  7.8 0.7 %collective-permute-start.1 = (f32[32,128]{1,0:T(8,128)S(1)}, f32[32,128]{1,0:T(8,128)S(1)}, u32[]{:S(2)}, u32[]{:S(2)}) collective-permute-start(f32[32,128]{1,0:T(8,128)S(1)} %get-tuple-element.26), channel_id=1, source_target_pairs={{8,0},{4,2},{2,4},{14,6},{0,8},{12,10},{10,12},{6,14},{24,16},{20,... | collective-permute-start | bytes 49160 | tf_op jit(solution)/shard_map/ppermute | solution.py:465
  8.5 0.0 collective-permute-start.3
  8.5 0.0 copy-done.1
  8.5 0.0 copy-done
  8.5 0.0 copy-done.3
  8.5 2.1 %inside.1 = (f32[128,24,128]{2,1,0:T(8,128)S(1)}, f32[5,24,64]{2,1,0:T(8,128)S(1)}, f32[5,24,64]{2,1,0:T(8,128)S(1)}) custom-call(f32[128,24,128]{2,1,0:T(8,128)S(1)} %get-tuple-element.20.cells, f32[128,128]{1,0:T(8,128)S(1)} %bitcast.10, f32[128,128]{1,0:T(8,128)S(1)} %bitcast.7, f32[1,22]{1,0:T(1,128)S(1)} %bitcast.11), custom_call_target="tpu_custom_call" | custom-call | flops 10000000 | bytes 4000000 | tf_op jit(solution)/shard_map/inside/pallas_call | solution.py:552
  10.6 0.0 collective-permute-done.3.refs_3_
  10.6 0.0 collective-permute-done.refs_0_
  10.6 0.0 collective-permute-done.1.refs_1_
  10.6 0.0 collective-permute-done.4.refs_4_
  10.6 0.0 collective-permute-done.2.refs_2_
  10.6 0.0 copy-done.2
  10.6 0.0 copy-done.4
  10.6 0.6 %edges.1 = (f32[4,24,128]{2,1,0:T(8,128)S(1)}, f32[2,24,128]{2,1,0:T(8,128)S(1)}) custom-call(f32[128,24,128]{2,1,0:T(8,128)S(1)} %get-tuple-element.20.cells, f32[2,24,128]{2,1,0:T(8,128)S(1)} %get-tuple-element.22.own_z, f32[5,24,64]{2,1,0:T(8,128)S(1)} %get-tuple-element.23.sums, f32[5,24,64]{2,1,0:T(8,128)S(1)} %get-tuple-element.24.heated_sums, ...), custom_call_target="tpu_custom_call" | custom-call | tf_op jit(solution)/shard_map/edges/pallas_call | solution.py:567
  11.3 0.6 %collective-permute-start.5 = (f32[4,24,128]{2,1,0:T(8,128)S(1)}, f32[4,24,128]{2,1,0:T(8,128)S(1)}, u32[]{:S(2)}, u32[]{:S(2)}) collective-permute-start(f32[4,24,128]{2,1,0:T(8,128)S(1)} %get-tuple-element.30), channel_id=1, source_target_pairs={{0,8},{8,0},{16,24},{24,16},{1,9},{9,1},{17,25},{25,17},{2,10},{10... | collective-permute-start | bytes 147464 | tf_op jit(solution)/shard_map/ppermute | solution.py:577
  11.9 0.9 %collective-permute-done.5 = f32[4,24,128]{2,1,0:T(8,128)S(1)} collective-permute-done((f32[4,24,128]{2,1,0:T(8,128)S(1)}, f32[4,24,128]{2,1,0:T(8,128)S(1)}, u32[]{:S(2)}, u32[]{:S(2)}) %collective-permute-start.5) | collective-permute-done | bytes 49184 | tf_op jit(solution)/shard_map/ppermute | solution.py:577
  12.7 2.5 %collective-permute-start.8 = (f32[2,24,128]{2,1,0:T(8,128)S(1)}, f32[2,24,128]{2,1,0:T(8,128)S(1)}, u32[]{:S(2)}, u32[]{:S(2)}) collective-permute-start(f32[2,24,128]{2,1,0:T(8,128)S(1)} %slice.9), channel_id=1, source_target_pairs={{14,0},{8,2},{10,4},{12,6},{6,8},{0,10},{2,12},{4,14},{30,16},{24,... | collective-permute-start | bytes 73736 | tf_op jit(solution)/shard_map/ppermute | solution.py:465
  15.3 0.7 %kinetics.1.advanced.held = f32[128,24,128]{2,1,0:T(8,128)S(1)} custom-call(f32[128,24,128]{2,1,0:T(8,128)S(1)} %get-tuple-element.20.cells, f32[128,24,128]{2,1,0:T(8,128)S(1)} %get-tuple-element.21.diffused, f32[128,128]{1,0:T(8,128)S(1)} %bitcast.8, f32[22,22]{1,0:T(8,128)S(1)} %copy-done.2, f32[4,24,128]{2,1,0:T(8,128)S(1)} %add.6.held), custom_call_target="tpu_custom_call" | custom-call | tf_op jit(solution)/shard_map/kinetics/pallas_call | solution.py:578
  16.0 1.3 %collective-permute-start.6 = (f32[16,24,128]{2,1,0:T(8,128)S(1)}, f32[16,24,128]{2,1,0:T(8,128)S(1)}, u32[]{:S(2)}, u32[]{:S(2)}) collective-permute-start(f32[16,24,128]{2,1,0:T(8,128)S(1)} %get-tuple-element.34), channel_id=1, source_target_pairs={{0,2},{2,0},{4,6},{6,4},{1,3},{3,1},{5,7},{7,5},{8,10},{10,8},{12,... | collective-permute-start | bytes 589832 | tf_op jit(solution)/shard_map/ppermute | solution.py:471
  17.3 0.1 collective-permute-start.7
  17.3 0.5 %collective-permute-done.8 = f32[2,24,128]{2,1,0:T(8,128)S(1)} collective-permute-done((f32[2,24,128]{2,1,0:T(8,128)S(1)}, f32[2,24,128]{2,1,0:T(8,128)S(1)}, u32[]{:S(2)}, u32[]{:S(2)}) %collective-permute-start.8) | collective-permute-done | bytes 24608 | tf_op jit(solution)/shard_map/ppermute | solution.py:465
  17.9 0.5 %collective-permute-start.9 = (f32[2,24,128]{2,1,0:T(8,128)S(1)}, f32[2,24,128]{2,1,0:T(8,128)S(1)}, u32[]{:S(2)}, u32[]{:S(2)}) collective-permute-start(f32[2,24,128]{2,1,0:T(8,128)S(1)} %slice_add_fusion.refs_3_), channel_id=1, source_target_pairs={{24,0},{25,1},{16,8},{17,9},{8,16},{9,17},{0,24},{1,25},{26,2},{27... | collective-permute-start | bytes 73736 | tf_op jit(solution)/shard_map/ppermute | solution.py:465
  18.3 1.3 %collective-permute-start.10 = (f32[2,24,128]{2,1,0:T(8,128)S(1)}, f32[2,24,128]{2,1,0:T(8,128)S(1)}, u32[]{:S(2)}, u32[]{:S(2)}) collective-permute-start(f32[2,24,128]{2,1,0:T(8,128)S(1)} %slice_add_fusion.refs_3_), channel_id=1, source_target_pairs={{25,0},{24,1},{17,8},{16,9},{9,16},{8,17},{1,24},{0,25},{27,2},{26... | collective-permute-start | bytes 73736 | tf_op jit(solution)/shard_map/ppermute | solution.py:465
  19.6 1.4 %collective-permute-start.11 = (f32[2,24,128]{2,1,0:T(8,128)S(1)}, f32[2,24,128]{2,1,0:T(8,128)S(1)}, u32[]{:S(2)}, u32[]{:S(2)}) collective-permute-start(f32[2,24,128]{2,1,0:T(8,128)S(1)} %slice_add_fusion.refs_3_), channel_id=1, source_target_pairs={{9,0},{8,1},{1,8},{0,9},{25,16},{24,17},{17,24},{16,25},{11,2},{10... | collective-permute-start | bytes 73736 | tf_op jit(solution)/shard_map/ppermute | solution.py:465
  21.0 1.7 %interior.1 = (f32[128,24,128]{2,1,0:T(8,128)S(1)}, f32[22,128,128]{2,1,0:T(8,128)}) custom-call(f32[128,24,128]{2,1,0:T(8,128)S(1)} %kinetics.1.advanced.held, f32[2,24,128]{2,1,0:T(8,128)S(1)} %get-tuple-element.31.dz), custom_call_target="tpu_custom_call" | custom-call | flops 1000000 | bytes 3000000 | tf_op jit(solution)/shard_map/interior/pallas_call | solution.py:603
  22.8 0.0 collective-permute-done.9.refs_4_
  22.8 0.0 collective-permute-done.10.refs_5_
  22.8 0.3 %collective-permute-done.11.refs_6_ = f32[2,24,128]{2,1,0:T(8,128)S(1)} collective-permute-done((f32[2,24,128]{2,1,0:T(8,128)S(1)}, f32[2,24,128]{2,1,0:T(8,128)S(1)}, u32[]{:S(2)}, u32[]{:S(2)}) %collective-permute-start.11) | collective-permute-done | bytes 24608 | tf_op jit(solution)/shard_map/ppermute | solution.py:465
  23.1 0.2 collective-permute-done.6.refs_0_
  23.2 0.0 collective-permute-done.7.refs_1_
  23.2 1.1 %last.1 = (f32[22,128,128]{2,1,0:T(8,128)}, f32[22,4,64]{2,1,0:T(4,128)}) custom-call(f32[128,24,128]{2,1,0:T(8,128)S(1)} %get-tuple-element.20.cells, f32[128,24,128]{2,1,0:T(8,128)S(1)} %get-tuple-element.32.total, f32[1,22]{1,0:T(1,128)S(1)} %bitcast.13, f32[22,128,128]{2,1,0:T(8,128)} %get-tuple-element.33.first_out, ...), custom_call_target="tpu_custom_call", output_to_operand_aliasing={{0}: (3, {})} | custom-call | tf_op jit(solution)/shard_map/last/pallas_call | solution.py:616
  (4 shorter events, 0.1 us)
Async XLA Ops:
  0.6 7.8 %copy-start.1 = (f32[8,16,128]{2,1,0:T(8,128)S(1)}, f32[8,16,128]{2,1,0:T(8,128)}, u32[]{:S(2)}) copy-start(f32[8,16,128]{2,1,0:T(8,128)} %param.8) | copy-start | bytes 196612
  0.6 7.8 %copy-start = (f32[8,16,128]{2,1,0:T(8,128)S(1)}, f32[8,16,128]{2,1,0:T(8,128)}, u32[]{:S(2)}) copy-start(f32[8,16,128]{2,1,0:T(8,128)} %param.9) | copy-start | bytes 196612
  0.7 7.8 %copy-start.3 = (f32[22]{0:T(128)S(1)}, f32[22]{0:T(128)}, u32[]{:S(2)}) copy-start(f32[22]{0:T(128)} %param.10) | copy-start | bytes 268
  0.7 10.0 %copy-start.2 = (f32[22,22]{1,0:T(8,128)S(1)}, f32[22,22]{1,0:T(8,128)}, u32[]{:S(2)}) copy-start(f32[22,22]{1,0:T(8,128)} %jacobian.3) | copy-start | bytes 5812
  0.7 10.0 %copy-start.4 = (s32[32]{0:T(128)S(1)}, s32[32]{0:T(128)}, u32[]{:S(2)}) copy-start(s32[32]{0:T(128)} %param.13) | copy-start | bytes 388
  2.5 8.1 %collective-permute-start.2 = (f32[8,24,128]{2,1,0:T(8,128)S(1)}, f32[8,24,128]{2,1,0:T(8,128)S(1)}, u32[]{:S(2)}, u32[]{:S(2)}) collective-permute-start(f32[8,24,128]{2,1,0:T(8,128)S(1)} %get-tuple-element.27), channel_id=1, source_target_pairs={{0,1},{1,0},{2,3},{3,2},{4,5},{5,4},{6,7},{7,6},{8,9},{9,8},{10,11... | collective-permute-start | bytes 294920 | tf_op jit(solution)/shard_map/ppermute | solution.py:471
  5.5 5.1 %collective-permute-start.4 = (f32[40,128]{1,0:T(8,128)S(1)}, f32[40,128]{1,0:T(8,128)S(1)}, u32[]{:S(2)}, u32[]{:S(2)}) collective-permute-start(f32[40,128]{1,0:T(8,128)S(1)} %get-tuple-element.29), channel_id=1, source_target_pairs={{8,16},{16,8},{0,24},{24,0},{9,17},{17,9},{1,25},{25,1},{10,18},{1... | collective-permute-start | bytes 61448 | tf_op jit(solution)/shard_map/ppermute | solution.py:474
  6.2 4.4 %collective-permute-start = (f32[32,128]{1,0:T(8,128)S(1)}, f32[32,128]{1,0:T(8,128)S(1)}, u32[]{:S(2)}, u32[]{:S(2)}) collective-permute-start(f32[32,128]{1,0:T(8,128)S(1)} %get-tuple-element.25), channel_id=1, source_target_pairs={{0,2},{2,0},{4,6},{6,4},{1,3},{3,1},{5,7},{7,5},{8,10},{10,8},{12,... | collective-permute-start | bytes 49160 | tf_op jit(solution)/shard_map/ppermute | solution.py:471
  7.8 2.8 %collective-permute-start.1 = (f32[32,128]{1,0:T(8,128)S(1)}, f32[32,128]{1,0:T(8,128)S(1)}, u32[]{:S(2)}, u32[]{:S(2)}) collective-permute-start(f32[32,128]{1,0:T(8,128)S(1)} %get-tuple-element.26), channel_id=1, source_target_pairs={{8,0},{4,2},{2,4},{14,6},{0,8},{12,10},{10,12},{6,14},{24,16},{20,... | collective-permute-start | bytes 49160 | tf_op jit(solution)/shard_map/ppermute | solution.py:465
  8.5 2.1 %collective-permute-start.3 = (f32[24,128]{1,0:T(8,128)S(1)}, f32[24,128]{1,0:T(8,128)S(1)}, u32[]{:S(2)}, u32[]{:S(2)}) collective-permute-start(f32[24,128]{1,0:T(8,128)S(1)} %get-tuple-element.28), channel_id=1, source_target_pairs={{0,8},{8,0},{16,24},{24,16},{1,9},{9,1},{17,25},{25,17},{2,10},{10... | collective-permute-start | bytes 36872 | tf_op jit(solution)/shard_map/ppermute | solution.py:471
  11.3 1.4 %collective-permute-start.5 = (f32[4,24,128]{2,1,0:T(8,128)S(1)}, f32[4,24,128]{2,1,0:T(8,128)S(1)}, u32[]{:S(2)}, u32[]{:S(2)}) collective-permute-start(f32[4,24,128]{2,1,0:T(8,128)S(1)} %get-tuple-element.30), channel_id=1, source_target_pairs={{0,8},{8,0},{16,24},{24,16},{1,9},{9,1},{17,25},{25,17},{2,10},{10... | collective-permute-start | bytes 147464 | tf_op jit(solution)/shard_map/ppermute | solution.py:577
  12.7 5.1 %collective-permute-start.8 = (f32[2,24,128]{2,1,0:T(8,128)S(1)}, f32[2,24,128]{2,1,0:T(8,128)S(1)}, u32[]{:S(2)}, u32[]{:S(2)}) collective-permute-start(f32[2,24,128]{2,1,0:T(8,128)S(1)} %slice.9), channel_id=1, source_target_pairs={{14,0},{8,2},{10,4},{12,6},{6,8},{0,10},{2,12},{4,14},{30,16},{24,... | collective-permute-start | bytes 73736 | tf_op jit(solution)/shard_map/ppermute | solution.py:465
  16.0 7.2 %collective-permute-start.6 = (f32[16,24,128]{2,1,0:T(8,128)S(1)}, f32[16,24,128]{2,1,0:T(8,128)S(1)}, u32[]{:S(2)}, u32[]{:S(2)}) collective-permute-start(f32[16,24,128]{2,1,0:T(8,128)S(1)} %get-tuple-element.34), channel_id=1, source_target_pairs={{0,2},{2,0},{4,6},{6,4},{1,3},{3,1},{5,7},{7,5},{8,10},{10,8},{12,... | collective-permute-start | bytes 589832 | tf_op jit(solution)/shard_map/ppermute | solution.py:471
  17.3 6.0 %collective-permute-start.7 = (f32[16,24,128]{2,1,0:T(8,128)S(1)}, f32[16,24,128]{2,1,0:T(8,128)S(1)}, u32[]{:S(2)}, u32[]{:S(2)}) collective-permute-start(f32[16,24,128]{2,1,0:T(8,128)S(1)} %get-tuple-element.35), channel_id=1, source_target_pairs={{8,0},{4,2},{2,4},{14,6},{0,8},{12,10},{10,12},{6,14},{24,16},{20,... | collective-permute-start | bytes 589832 | tf_op jit(solution)/shard_map/ppermute | solution.py:465
  17.9 4.9 %collective-permute-start.9 = (f32[2,24,128]{2,1,0:T(8,128)S(1)}, f32[2,24,128]{2,1,0:T(8,128)S(1)}, u32[]{:S(2)}, u32[]{:S(2)}) collective-permute-start(f32[2,24,128]{2,1,0:T(8,128)S(1)} %slice_add_fusion.refs_3_), channel_id=1, source_target_pairs={{24,0},{25,1},{16,8},{17,9},{8,16},{9,17},{0,24},{1,25},{26,2},{27... | collective-permute-start | bytes 73736 | tf_op jit(solution)/shard_map/ppermute | solution.py:465
  18.3 4.4 %collective-permute-start.10 = (f32[2,24,128]{2,1,0:T(8,128)S(1)}, f32[2,24,128]{2,1,0:T(8,128)S(1)}, u32[]{:S(2)}, u32[]{:S(2)}) collective-permute-start(f32[2,24,128]{2,1,0:T(8,128)S(1)} %slice_add_fusion.refs_3_), channel_id=1, source_target_pairs={{25,0},{24,1},{17,8},{16,9},{9,16},{8,17},{1,24},{0,25},{27,2},{26... | collective-permute-start | bytes 73736 | tf_op jit(solution)/shard_map/ppermute | solution.py:465
  19.6 3.5 %collective-permute-start.11 = (f32[2,24,128]{2,1,0:T(8,128)S(1)}, f32[2,24,128]{2,1,0:T(8,128)S(1)}, u32[]{:S(2)}, u32[]{:S(2)}) collective-permute-start(f32[2,24,128]{2,1,0:T(8,128)S(1)} %slice_add_fusion.refs_3_), channel_id=1, source_target_pairs={{9,0},{8,1},{1,8},{0,9},{25,16},{24,17},{17,24},{16,25},{11,2},{10... | collective-permute-start | bytes 73736 | tf_op jit(solution)/shard_map/ppermute | solution.py:465

commit v11 on v10

--- a/solution.py
+++ b/solution.py
@@ -147,6 +147,10 @@
                     out[pl.ds(count + i, 1), :] = rows_out[r, pl.ds(species + 1, 1), :]
 
 
+def join_kernel(window, received, after, out):
+    out[...] = window[...] + received[...]
+
+
 def plane_kernel(planes, cells, held, *faces):
     width = cells.shape[0] // planes
     for side, out in enumerate(faces):
@@ -364,21 +368,11 @@
         ).wait()
 
 
-def last_kernel(planes, has_b, n_terms, cells, total, weights, first_out, *refs):
-    halos, terms = list(refs[: 2 + sum(has_b)]), refs[2 + sum(has_b) :][:n_terms]
-    out, means_out, changed, means, sem = refs[2 + sum(has_b) + n_terms :]
+def face_kernel(planes, has_b, cells, total, weights, *refs):
+    halos, changed = list(refs[:-1]), refs[-1]
     row_count, rows, depth = total.shape
-    species = out.shape[0]
+    species = weights.shape[1]
     width = row_count // planes
-    per_device, bins = means.shape[1:]
-    for s in range(0, per_device, 2):
-        block = sum((term[s // 2] for term in terms[1:]), terms[0][s // 2])
-        block = block / jnp.maximum(block[species + 1 : species + 2], 1.0)
-        means[:, s, :] = block[:species, :bins]
-        means[:, s + 1, :] = block[:species, bins:]
-    copies = [pltpu.make_async_copy(means, means_out, sem.at[0])]
-    copies[0].start()
-
     weight = jnp.broadcast_to(weight_column(weights, rows), (rows, depth))
     received = {}
     for axis, both in zip(("gx", "gy"), has_b):
@@ -401,7 +395,23 @@
             new = total[r] + share("gx", x > 0, c, y)
             if y in (0, width - 1):
                 new += share("gy", y > 0, c, x)
-            changed[n + y] = new
+            changed[n] = new
+            n += 1
+    for y in (0, width - 1):
+        for x in range(1, planes - 1):
+            r = x * width + y
+            changed[n] = total[r] + share("gy", y > 0, cells[r], x)
+            n += 1
+
+
+def last_kernel(planes, changed, first_out, *refs):
+    terms, (out, means_out, means, sem) = refs[:-4], refs[-4:]
+    species, row_count, _ = out.shape
+    width = row_count // planes
+    per_device, bins = means.shape[1:]
+    copies = []
+    n = 0
+    for x in (0, planes - 1):
         for k in range(species):
             copies.append(
                 pltpu.make_async_copy(
@@ -410,29 +420,30 @@
                     sem.at[1],
                 )
             )
-            copies[-1].start()
         n += width
-    planes_changed = changed.at[pl.ds(0, n), pl.ds(0, species), :]
-    cells_out = out.reshape(species, planes, width, depth)
-    start = n
+    cells_out = out.reshape(species, planes, width, out.shape[2])
     for y in (0, width - 1):
-        for x in range(1, planes - 1):
-            r = x * width + y
-            changed[n + x - 1] = total[r] + share("gy", y > 0, cells[r], x)
         for k in range(species):
             copies.append(
                 pltpu.make_async_copy(
                     changed.at[pl.ds(n, planes - 2), k, :],
                     cells_out.at[k, pl.ds(1, planes - 2), y, :],
-                    sem.at[2],
+                    sem.at[1],
                 )
             )
-            copies[-1].start()
         n += planes - 2
-    rows_changed = changed.at[pl.ds(start, n - start), pl.ds(0, species), :]
-    copies[0].wait()
-    pltpu.make_async_copy(planes_changed, planes_changed, sem.at[1]).wait()
-    pltpu.make_async_copy(rows_changed, rows_changed, sem.at[2]).wait()
+    for s in range(0, per_device, 2):
+        block = sum((term[s // 2] for term in terms[1:]), terms[0][s // 2])
+        block = block / jnp.maximum(block[species + 1 : species + 2], 1.0)
+        means[:, s, :] = block[:species, :bins]
+        means[:, s + 1, :] = block[:species, bins:]
+    means_copy = pltpu.make_async_copy(means, means_out, sem.at[0])
+    means_copy.start()
+    for copy in copies:
+        copy.start()
+    means_copy.wait()
+    all_changed = changed.at[pl.ds(0, n), pl.ds(0, species), :]
+    pltpu.make_async_copy(all_changed, all_changed, sem.at[1]).wait()
 
 
 def struct(*shape):
@@ -573,8 +584,6 @@
         scratch=[pltpu.VMEM((2 * rows, 2 * rows), F32)],
     )(rows_in, own_z, sums, heated_sums, weights, kinetics_jacobian, positions, *halos)
 
-    deep = lax.axis_size("sec")
-    window = window + lax.ppermute(window, "sec", [(i, i ^ 1) for i in range(deep)])
     advanced = call(
         kinetics_kernel,
         "kinetics",
@@ -588,6 +597,9 @@
         flops=0,
         moved=0,
     )(rows_in, diffused, thermal, kinetics_jacobian, window)
+    deep = lax.axis_size("sec")
+    received = lax.ppermute(window, "sec", [(i, i ^ 1) for i in range(deep)])
+    window = call(join_kernel, "join", struct(*window.shape), 3, VMEM)(window, received, advanced)
     terms = summed(window)
 
     outer_planes = call(
@@ -596,7 +608,7 @@
         [struct(width, rows, depth)] * (1 + has_b[0]),
         2,
         [VMEM] * (1 + has_b[0]),
-    )(rows_in, advanced)
+    )(rows_in, window)
     wide_halos = [swapped(face, "gx", side) for side, face in enumerate(outer_planes)]
     wide_halos += [halo for halo, (axis, _) in zip(halos, sides) if axis == "gy"]
 
@@ -610,23 +622,26 @@
         flops=1_000_000,
         moved=3_000_000,
     )(advanced, dz)
-    ins = [rows_in, total, weights, advanced, *wide_halos, *terms]
-    specs = [VMEM] * len(ins)
-    specs[3] = ANY
+    changed = call(
+        functools.partial(face_kernel, planes, has_b[:2]),
+        "rows_of_faces",
+        struct(2 * (width + planes - 2), rows, depth),
+        3 + len(wide_halos),
+        VMEM,
+    )(rows_in, total, weights, *wide_halos)
     advanced, cond_means = call(
-        functools.partial(last_kernel, planes, has_b[:2], len(terms)),
+        functools.partial(last_kernel, planes),
         "last",
         [struct(species, row_count, depth), struct(species, per_device, NB)],
-        len(ins),
+        2 + len(terms),
         [ANY, ANY],
-        in_specs=specs,
+        in_specs=[VMEM, ANY] + [VMEM] * len(terms),
         scratch=[
-            pltpu.VMEM((2 * (width + planes - 2), rows, depth), F32),
             pltpu.VMEM((species, per_device, NB), F32),
-            pltpu.SemaphoreType.DMA((3,)),
+            pltpu.SemaphoreType.DMA((2,)),
         ],
-        aliases={3: 0},
-    )(*ins)
+        aliases={1: 0},
+    )(changed, advanced, *terms)
     return advanced.reshape(composition_matrix.shape), cond_means
 
 

time: 24.5 us -> 24.3 us (level)
  waiting for transfers between devices: 1.9 us -> 1.48 us
    ppermute x1, waiting for transfers between devices: 0.88 us -> 0.21 us  [on_device(): received = lax.ppermute(window, 'sec', [(i, i ^ 1) for i in range(deep)])]
    ppermute x6, waiting for transfers between devices: 0.85 us -> 1.26 us  [joint(): return lax.ppermute(block, ('sec', axis), pairs)]
    pallas_call x1 -> x3, Pallas kernels: 1.09 us -> 1.28 us  [the longest x1 1.06 us: on_device(): call(functools.partial(last_kernel, planes), 'last', [struct(species, row...]
  transfers between devices with their start and end apart: 12 -> 12, of which waited for: 4 -> 2; matrix products, arithmetic and copies ran while one was open for 0% -> 0% of each run, Pallas kernels for 19% -> 19%
where the time goes in v11:
time: 24.3 us; the launch traced here: 24.1 us
  starting transfers between devices  13.5 us (56%)
  Pallas kernels  8.25 us (34%)
  waiting for transfers between devices  1.48 us (6%)
  between operations  0.82 us (3%)
    ppermute x6, starting transfers between devices, joint(): return lax.ppermute(block, ('sec', axis), pairs)  6.45 us
    ppermute x4, starting transfers between devices, swapped(): return lax.ppermute(block, axis, [(i, i ^ 1) for i in range(count)])  5.85 us
    pallas_call x1, Pallas kernels, on_device(): call(functools.partial(inner_kernel, planes), 'inside', [struct(row_count...  2.07 us
    pallas_call x1, Pallas kernels, on_device(): call(functools.partial(pack_kernel, planes, has_b), 'faces', [struct(row_...  1.84 us
    pallas_call x1, Pallas kernels, on_device(): call(functools.partial(interior_kernel, planes), 'interior', [struct(row_...  1.72 us
    ppermute x6, waiting for transfers between devices, joint(): return lax.ppermute(block, ('sec', axis), pairs)  1.26 us
    pallas_call x1, Pallas kernels, on_device(): call(functools.partial(last_kernel, planes), 'last', [struct(species, row...  1.06 us
    ppermute x1, starting transfers between devices, swapped(): return lax.ppermute(block, axis, [*pairs, (0, count - 1), (count - 1, 0)])  0.68 us
  transfers between devices with their start and end apart: 12, of which 2 were waited for; matrix products, arithmetic and copies ran while one was open for 0% of the time, Pallas kernels for 19%

profile of v11, /device:TPU:0, one launch (start us, length us, event | category | flops | bytes accessed | tf_op | source)
XLA Modules:
  0.0 24.1 jit_solution(12825634862670710789)
XLA Ops:
  0.6 0.0 copy-start.1
  0.6 0.0 copy-start
  0.7 0.0 copy-start.3
  0.7 0.0 copy-start.2
  0.7 0.0 copy-start.4
  0.7 1.8 %faces.1 = (f32[128,24,128]{2,1,0:T(8,128)S(1)}, f32[2,24,128]{2,1,0:T(8,128)S(1)}, f32[32,128]{1,0:T(8,128)S(1)}, f32[32,128]{1,0:T(8,128)S(1)}, f32[8,24,128]{...) custom-call(f32[22,128,128]{2,1,0:T(8,128)} %bitcast.15, f32[128,128]{1,0:T(8,128)} %bitcast.9, ...), custom_call_target="tpu_custom_call" | custom-call | tf_op jit(solution)/shard_map/faces/pallas_call | solution.py:544
  2.5 3.0 %collective-permute-start.2 = (f32[8,24,128]{2,1,0:T(8,128)S(1)}, f32[8,24,128]{2,1,0:T(8,128)S(1)}, u32[]{:S(2)}, u32[]{:S(2)}) collective-permute-start(f32[8,24,128]{2,1,0:T(8,128)S(1)} %get-tuple-element.27), channel_id=1, source_target_pairs={{0,1},{1,0},{2,3},{3,2},{4,5},{5,4},{6,7},{7,6},{8,9},{9,8},{10,11... | collective-permute-start | bytes 294920 | tf_op jit(solution)/shard_map/ppermute | solution.py:482
  5.5 0.7 %collective-permute-start.4 = (f32[40,128]{1,0:T(8,128)S(1)}, f32[40,128]{1,0:T(8,128)S(1)}, u32[]{:S(2)}, u32[]{:S(2)}) collective-permute-start(f32[40,128]{1,0:T(8,128)S(1)} %get-tuple-element.29), channel_id=1, source_target_pairs={{8,16},{16,8},{0,24},{24,0},{9,17},{17,9},{1,25},{25,1},{10,18},{1... | collective-permute-start | bytes 61448 | tf_op jit(solution)/shard_map/ppermute | solution.py:485
  6.2 1.6 %collective-permute-start = (f32[32,128]{1,0:T(8,128)S(1)}, f32[32,128]{1,0:T(8,128)S(1)}, u32[]{:S(2)}, u32[]{:S(2)}) collective-permute-start(f32[32,128]{1,0:T(8,128)S(1)} %get-tuple-element.25), channel_id=1, source_target_pairs={{0,2},{2,0},{4,6},{6,4},{1,3},{3,1},{5,7},{7,5},{8,10},{10,8},{12,... | collective-permute-start | bytes 49160 | tf_op jit(solution)/shard_map/ppermute | solution.py:482
  7.8 0.7 %collective-permute-start.1 = (f32[32,128]{1,0:T(8,128)S(1)}, f32[32,128]{1,0:T(8,128)S(1)}, u32[]{:S(2)}, u32[]{:S(2)}) collective-permute-start(f32[32,128]{1,0:T(8,128)S(1)} %get-tuple-element.26), channel_id=1, source_target_pairs={{8,0},{4,2},{2,4},{14,6},{0,8},{12,10},{10,12},{6,14},{24,16},{20,... | collective-permute-start | bytes 49160 | tf_op jit(solution)/shard_map/ppermute | solution.py:476
  8.5 0.0 collective-permute-start.3
  8.5 0.0 copy-done.1
  8.5 0.0 copy-done
  8.5 0.0 copy-done.3
  8.5 2.1 %inside.1 = (f32[128,24,128]{2,1,0:T(8,128)S(1)}, f32[5,24,64]{2,1,0:T(8,128)S(1)}, f32[5,24,64]{2,1,0:T(8,128)S(1)}) custom-call(f32[128,24,128]{2,1,0:T(8,128)S(1)} %get-tuple-element.20.cells, f32[128,128]{1,0:T(8,128)S(1)} %bitcast.10, f32[128,128]{1,0:T(8,128)S(1)} %bitcast.7, f32[1,22]{1,0:T(1,128)S(1)} %bitcast.11), custom_call_target="tpu_custom_call" | custom-call | flops 10000000 | bytes 4000000 | tf_op jit(solution)/shard_map/inside/pallas_call | solution.py:563
  10.6 0.0 collective-permute-done.3.refs_3_
  10.6 0.0 collective-permute-done.refs_0_
  10.6 0.0 collective-permute-done.1.refs_1_
  10.6 0.0 collective-permute-done.4.refs_4_
  10.6 0.0 collective-permute-done.2.refs_2_
  10.6 0.0 copy-done.2
  10.6 0.0 copy-done.4
  10.6 0.6 %edges.1 = (f32[4,24,128]{2,1,0:T(8,128)S(1)}, f32[2,24,128]{2,1,0:T(8,128)S(1)}) custom-call(f32[128,24,128]{2,1,0:T(8,128)S(1)} %get-tuple-element.20.cells, f32[2,24,128]{2,1,0:T(8,128)S(1)} %get-tuple-element.22.own_z, f32[5,24,64]{2,1,0:T(8,128)S(1)} %get-tuple-element.23.sums, f32[5,24,64]{2,1,0:T(8,128)S(1)} %get-tuple-element.24.heated_sums, ...), custom_call_target="tpu_custom_call" | custom-call | tf_op jit(solution)/shard_map/edges/pallas_call | solution.py:578
  11.3 0.6 %collective-permute-start.5 = (f32[4,24,128]{2,1,0:T(8,128)S(1)}, f32[4,24,128]{2,1,0:T(8,128)S(1)}, u32[]{:S(2)}, u32[]{:S(2)}) collective-permute-start(f32[4,24,128]{2,1,0:T(8,128)S(1)} %get-tuple-element.30.held.window), channel_id=1, source_target_pairs={{0,8},{8,0},{16,24},{24,16},{1,9},{9,1},{17,25},{25,17},{2,10},{10... | collective-permute-start | bytes 147464 | tf_op jit(solution)/shard_map/ppermute | solution.py:601
  11.8 0.7 %kinetics.1.advanced.after = f32[128,24,128]{2,1,0:T(8,128)S(1)} custom-call(f32[128,24,128]{2,1,0:T(8,128)S(1)} %get-tuple-element.20.cells, f32[128,24,128]{2,1,0:T(8,128)S(1)} %get-tuple-element.21.diffused, f32[128,128]{1,0:T(8,128)S(1)} %bitcast.8, f32[22,22]{1,0:T(8,128)S(1)} %copy-done.2, f32[4,24,128]{2,1,0:T(8,128)S(1)} %get-tuple-element.30.held.window), custom_call_target="tpu_custom_call" | custom-call | tf_op jit(solution)/shard_map/kinetics/pallas_call | solution.py:587
  12.5 0.2 collective-permute-done.5.received
  12.7 2.5 %collective-permute-start.8 = (f32[2,24,128]{2,1,0:T(8,128)S(1)}, f32[2,24,128]{2,1,0:T(8,128)S(1)}, u32[]{:S(2)}, u32[]{:S(2)}) collective-permute-start(f32[2,24,128]{2,1,0:T(8,128)S(1)} %slice.9), channel_id=1, source_target_pairs={{14,0},{8,2},{10,4},{12,6},{6,8},{0,10},{2,12},{4,14},{30,16},{24,... | collective-permute-start | bytes 73736 | tf_op jit(solution)/shard_map/ppermute | solution.py:476
  15.3 1.3 %collective-permute-start.6 = (f32[16,24,128]{2,1,0:T(8,128)S(1)}, f32[16,24,128]{2,1,0:T(8,128)S(1)}, u32[]{:S(2)}, u32[]{:S(2)}) collective-permute-start(f32[16,24,128]{2,1,0:T(8,128)S(1)} %get-tuple-element.33), channel_id=1, source_target_pairs={{0,2},{2,0},{4,6},{6,4},{1,3},{3,1},{5,7},{7,5},{8,10},{10,8},{12,... | collective-permute-start | bytes 589832 | tf_op jit(solution)/shard_map/ppermute | solution.py:482
  16.6 0.1 collective-permute-start.7
  16.6 1.2 %collective-permute-done.8 = f32[2,24,128]{2,1,0:T(8,128)S(1)} collective-permute-done((f32[2,24,128]{2,1,0:T(8,128)S(1)}, f32[2,24,128]{2,1,0:T(8,128)S(1)}, u32[]{:S(2)}, u32[]{:S(2)}) %collective-permute-start.8) | collective-permute-done | bytes 24608 | tf_op jit(solution)/shard_map/ppermute | solution.py:476
  17.9 0.5 %collective-permute-start.9 = (f32[2,24,128]{2,1,0:T(8,128)S(1)}, f32[2,24,128]{2,1,0:T(8,128)S(1)}, u32[]{:S(2)}, u32[]{:S(2)}) collective-permute-start(f32[2,24,128]{2,1,0:T(8,128)S(1)} %slice_add_fusion.refs_0_), channel_id=1, source_target_pairs={{24,0},{25,1},{16,8},{17,9},{8,16},{9,17},{0,24},{1,25},{26,2},{27... | collective-permute-start | bytes 73736 | tf_op jit(solution)/shard_map/ppermute | solution.py:476
  18.3 1.3 %collective-permute-start.10 = (f32[2,24,128]{2,1,0:T(8,128)S(1)}, f32[2,24,128]{2,1,0:T(8,128)S(1)}, u32[]{:S(2)}, u32[]{:S(2)}) collective-permute-start(f32[2,24,128]{2,1,0:T(8,128)S(1)} %slice_add_fusion.refs_0_), channel_id=1, source_target_pairs={{25,0},{24,1},{17,8},{16,9},{9,16},{8,17},{1,24},{0,25},{27,2},{26... | collective-permute-start | bytes 73736 | tf_op jit(solution)/shard_map/ppermute | solution.py:476
  19.6 1.4 %collective-permute-start.11 = (f32[2,24,128]{2,1,0:T(8,128)S(1)}, f32[2,24,128]{2,1,0:T(8,128)S(1)}, u32[]{:S(2)}, u32[]{:S(2)}) collective-permute-start(f32[2,24,128]{2,1,0:T(8,128)S(1)} %slice_add_fusion.refs_0_), channel_id=1, source_target_pairs={{9,0},{8,1},{1,8},{0,9},{25,16},{24,17},{17,24},{16,25},{11,2},{10... | collective-permute-start | bytes 73736 | tf_op jit(solution)/shard_map/ppermute | solution.py:476
  21.0 1.7 %interior.1 = (f32[128,24,128]{2,1,0:T(8,128)S(1)}, f32[22,128,128]{2,1,0:T(8,128)}) custom-call(f32[128,24,128]{2,1,0:T(8,128)S(1)} %kinetics.1.advanced.after, f32[2,24,128]{2,1,0:T(8,128)S(1)} %get-tuple-element.31.dz), custom_call_target="tpu_custom_call" | custom-call | flops 1000000 | bytes 3000000 | tf_op jit(solution)/shard_map/interior/pallas_call | solution.py:615
  22.8 0.0 collective-permute-done.6.refs_0_
  22.8 0.0 collective-permute-done.7.refs_1_
  22.8 0.2 rows_of_faces.1.changed
  23.0 0.0 collective-permute-done.9.refs_1_
  23.0 0.0 collective-permute-done.10.refs_2_
  23.0 0.0 collective-permute-done.11.refs_3_
  23.1 1.1 %last.1 = (f32[22,128,128]{2,1,0:T(8,128)}, f32[22,4,64]{2,1,0:T(4,128)}) custom-call(f32[44,24,128]{2,1,0:T(8,128)S(1)} %rows_of_faces.1.changed, f32[22,128,128]{2,1,0:T(8,128)} %get-tuple-element.35.first_out, f32[2,24,128]{2,1,0:T(8,128)S(1)} %slice_add_fusion.refs_0_, ...), custom_call_target="tpu_custom_call", output_to_operand_aliasing={{0}: (1, {})} | custom-call | tf_op jit(solution)/shard_map/last/pallas_call | solution.py:632
  (4 shorter events, 0.0 us)
Async XLA Ops:
  0.6 7.8 %copy-start.1 = (f32[8,16,128]{2,1,0:T(8,128)S(1)}, f32[8,16,128]{2,1,0:T(8,128)}, u32[]{:S(2)}) copy-start(f32[8,16,128]{2,1,0:T(8,128)} %param.8) | copy-start | bytes 196612
  0.6 7.8 %copy-start = (f32[8,16,128]{2,1,0:T(8,128)S(1)}, f32[8,16,128]{2,1,0:T(8,128)}, u32[]{:S(2)}) copy-start(f32[8,16,128]{2,1,0:T(8,128)} %param.9) | copy-start | bytes 196612
  0.7 7.8 %copy-start.3 = (f32[22]{0:T(128)S(1)}, f32[22]{0:T(128)}, u32[]{:S(2)}) copy-start(f32[22]{0:T(128)} %param.10) | copy-start | bytes 268
  0.7 10.0 %copy-start.2 = (f32[22,22]{1,0:T(8,128)S(1)}, f32[22,22]{1,0:T(8,128)}, u32[]{:S(2)}) copy-start(f32[22,22]{1,0:T(8,128)} %jacobian.3) | copy-start | bytes 5812
  0.7 10.0 %copy-start.4 = (s32[32]{0:T(128)S(1)}, s32[32]{0:T(128)}, u32[]{:S(2)}) copy-start(s32[32]{0:T(128)} %param.13) | copy-start | bytes 388
  2.5 8.1 %collective-permute-start.2 = (f32[8,24,128]{2,1,0:T(8,128)S(1)}, f32[8,24,128]{2,1,0:T(8,128)S(1)}, u32[]{:S(2)}, u32[]{:S(2)}) collective-permute-start(f32[8,24,128]{2,1,0:T(8,128)S(1)} %get-tuple-element.27), channel_id=1, source_target_pairs={{0,1},{1,0},{2,3},{3,2},{4,5},{5,4},{6,7},{7,6},{8,9},{9,8},{10,11... | collective-permute-start | bytes 294920 | tf_op jit(solution)/shard_map/ppermute | solution.py:482
  5.5 5.1 %collective-permute-start.4 = (f32[40,128]{1,0:T(8,128)S(1)}, f32[40,128]{1,0:T(8,128)S(1)}, u32[]{:S(2)}, u32[]{:S(2)}) collective-permute-start(f32[40,128]{1,0:T(8,128)S(1)} %get-tuple-element.29), channel_id=1, source_target_pairs={{8,16},{16,8},{0,24},{24,0},{9,17},{17,9},{1,25},{25,1},{10,18},{1... | collective-permute-start | bytes 61448 | tf_op jit(solution)/shard_map/ppermute | solution.py:485
  6.2 4.4 %collective-permute-start = (f32[32,128]{1,0:T(8,128)S(1)}, f32[32,128]{1,0:T(8,128)S(1)}, u32[]{:S(2)}, u32[]{:S(2)}) collective-permute-start(f32[32,128]{1,0:T(8,128)S(1)} %get-tuple-element.25), channel_id=1, source_target_pairs={{0,2},{2,0},{4,6},{6,4},{1,3},{3,1},{5,7},{7,5},{8,10},{10,8},{12,... | collective-permute-start | bytes 49160 | tf_op jit(solution)/shard_map/ppermute | solution.py:482
  7.8 2.8 %collective-permute-start.1 = (f32[32,128]{1,0:T(8,128)S(1)}, f32[32,128]{1,0:T(8,128)S(1)}, u32[]{:S(2)}, u32[]{:S(2)}) collective-permute-start(f32[32,128]{1,0:T(8,128)S(1)} %get-tuple-element.26), channel_id=1, source_target_pairs={{8,0},{4,2},{2,4},{14,6},{0,8},{12,10},{10,12},{6,14},{24,16},{20,... | collective-permute-start | bytes 49160 | tf_op jit(solution)/shard_map/ppermute | solution.py:476
  8.5 2.1 %collective-permute-start.3 = (f32[24,128]{1,0:T(8,128)S(1)}, f32[24,128]{1,0:T(8,128)S(1)}, u32[]{:S(2)}, u32[]{:S(2)}) collective-permute-start(f32[24,128]{1,0:T(8,128)S(1)} %get-tuple-element.28), channel_id=1, source_target_pairs={{0,8},{8,0},{16,24},{24,16},{1,9},{9,1},{17,25},{25,17},{2,10},{10... | collective-permute-start | bytes 36872 | tf_op jit(solution)/shard_map/ppermute | solution.py:482
  11.3 1.4 %collective-permute-start.5 = (f32[4,24,128]{2,1,0:T(8,128)S(1)}, f32[4,24,128]{2,1,0:T(8,128)S(1)}, u32[]{:S(2)}, u32[]{:S(2)}) collective-permute-start(f32[4,24,128]{2,1,0:T(8,128)S(1)} %get-tuple-element.30.held.window), channel_id=1, source_target_pairs={{0,8},{8,0},{16,24},{24,16},{1,9},{9,1},{17,25},{25,17},{2,10},{10... | collective-permute-start | bytes 147464 | tf_op jit(solution)/shard_map/ppermute | solution.py:601
  12.7 5.1 %collective-permute-start.8 = (f32[2,24,128]{2,1,0:T(8,128)S(1)}, f32[2,24,128]{2,1,0:T(8,128)S(1)}, u32[]{:S(2)}, u32[]{:S(2)}) collective-permute-start(f32[2,24,128]{2,1,0:T(8,128)S(1)} %slice.9), channel_id=1, source_target_pairs={{14,0},{8,2},{10,4},{12,6},{6,8},{0,10},{2,12},{4,14},{30,16},{24,... | collective-permute-start | bytes 73736 | tf_op jit(solution)/shard_map/ppermute | solution.py:476
  15.3 7.4 %collective-permute-start.6 = (f32[16,24,128]{2,1,0:T(8,128)S(1)}, f32[16,24,128]{2,1,0:T(8,128)S(1)}, u32[]{:S(2)}, u32[]{:S(2)}) collective-permute-start(f32[16,24,128]{2,1,0:T(8,128)S(1)} %get-tuple-element.33), channel_id=1, source_target_pairs={{0,2},{2,0},{4,6},{6,4},{1,3},{3,1},{5,7},{7,5},{8,10},{10,8},{12,... | collective-permute-start | bytes 589832 | tf_op jit(solution)/shard_map/ppermute | solution.py:482
  16.6 6.2 %collective-permute-start.7 = (f32[16,24,128]{2,1,0:T(8,128)S(1)}, f32[16,24,128]{2,1,0:T(8,128)S(1)}, u32[]{:S(2)}, u32[]{:S(2)}) collective-permute-start(f32[16,24,128]{2,1,0:T(8,128)S(1)} %get-tuple-element.34), channel_id=1, source_target_pairs={{8,0},{4,2},{2,4},{14,6},{0,8},{12,10},{10,12},{6,14},{24,16},{20,... | collective-permute-start | bytes 589832 | tf_op jit(solution)/shard_map/ppermute | solution.py:476
  17.9 5.1 %collective-permute-start.9 = (f32[2,24,128]{2,1,0:T(8,128)S(1)}, f32[2,24,128]{2,1,0:T(8,128)S(1)}, u32[]{:S(2)}, u32[]{:S(2)}) collective-permute-start(f32[2,24,128]{2,1,0:T(8,128)S(1)} %slice_add_fusion.refs_0_), channel_id=1, source_target_pairs={{24,0},{25,1},{16,8},{17,9},{8,16},{9,17},{0,24},{1,25},{26,2},{27... | collective-permute-start | bytes 73736 | tf_op jit(solution)/shard_map/ppermute | solution.py:476
  18.3 4.7 %collective-permute-start.10 = (f32[2,24,128]{2,1,0:T(8,128)S(1)}, f32[2,24,128]{2,1,0:T(8,128)S(1)}, u32[]{:S(2)}, u32[]{:S(2)}) collective-permute-start(f32[2,24,128]{2,1,0:T(8,128)S(1)} %slice_add_fusion.refs_0_), channel_id=1, source_target_pairs={{25,0},{24,1},{17,8},{16,9},{9,16},{8,17},{1,24},{0,25},{27,2},{26... | collective-permute-start | bytes 73736 | tf_op jit(solution)/shard_map/ppermute | solution.py:476
  19.6 3.5 %collective-permute-start.11 = (f32[2,24,128]{2,1,0:T(8,128)S(1)}, f32[2,24,128]{2,1,0:T(8,128)S(1)}, u32[]{:S(2)}, u32[]{:S(2)}) collective-permute-start(f32[2,24,128]{2,1,0:T(8,128)S(1)} %slice_add_fusion.refs_0_), channel_id=1, source_target_pairs={{9,0},{8,1},{1,8},{0,9},{25,16},{24,17},{17,24},{16,25},{11,2},{10... | collective-permute-start | bytes 73736 | tf_op jit(solution)/shard_map/ppermute | solution.py:476

commit v12 on v11

--- a/solution.py
+++ b/solution.py
@@ -159,7 +159,7 @@
             out[i] = cells[start + i * step]
 
 
-def inner_kernel(planes, cells, mixing, thermal, weights, diffused, sums, heated_sums, coefs):
+def inner_kernel(planes, cells, mixing, thermal, weights, diffused, sums, heated_sums, coefs, between):
     row_count, rows, depth = cells.shape
     species = weights.shape[1]
     width = row_count // planes
@@ -169,28 +169,19 @@
     up = 0.5 * (mix + pltpu.roll(mix, depth - 1, axis=1))
     up = jnp.where(lane == depth - 1, 0.0, up)
     coefs[0] = up
-    down = pltpu.roll(up, 1, axis=1)
-    coefs[1] = down
-    total = up + down
     up = 0.5 * (mix + pltpu.roll(mix, row_count - 1, axis=0))
-    up = jnp.where(row % width == width - 1, 0.0, up)
-    coefs[2] = up
-    down = pltpu.roll(up, 1, axis=0)
-    coefs[3] = down
-    total = total + (up + down)
+    coefs[1] = jnp.where(row % width == width - 1, 0.0, up)
     edge = jnp.zeros((width, depth), F32)
-    up = jnp.concatenate([0.5 * (mix[: row_count - width] + mix[width:]), edge], axis=0)
-    coefs[4] = up
-    down = jnp.concatenate([edge, up[: row_count - width]], axis=0)
-    coefs[5] = down
-    coefs[6] = total + (up + down)
-    coefs[7] = rate(thermal)
+    coefs[2] = jnp.concatenate([0.5 * (mix[: row_count - width] + mix[width:]), edge], axis=0)
+    coefs[3] = rate(thermal)
 
     weight = jnp.broadcast_to(weight_column(weights, rows), (rows, depth))
     whole = species // SUBLANES * SUBLANES
     ones = rows_of((rows - whole, depth)) >= species - whole
     sums[...] = jnp.zeros_like(sums)
     heated_sums[...] = jnp.zeros_like(heated_sums)
+
+    across = []
 
     def advance(pair):
         values, found = [], []
@@ -198,21 +189,23 @@
             x, y = divmod(r, width)
             c = cells[r]
             at = lambda n: coefs[n, pl.ds(r, 1), :]
-            flux = at(0) * pltpu.roll(c, depth - 1, axis=1)
-            flux += at(1) * pltpu.roll(c, 1, axis=1)
+            along = at(0) * (pltpu.roll(c, depth - 1, axis=1) - c)
+            flux = along - pltpu.roll(along, 1, axis=1)
+            if y > 0:
+                flux -= across.pop()
             if y < width - 1:
-                flux += at(2) * cells[r + 1]
-            if y > 0:
-                flux += at(3) * cells[r - 1]
+                across.append(at(1) * (cells[r + 1] - c))
+                flux += across[0]
+            if x > 0:
+                flux -= between[y]
             if x < planes - 1:
-                flux += at(4) * cells[r + width]
-            if x > 0:
-                flux += at(5) * cells[r - width]
-            flux -= at(6) * c
+                upward = at(2) * (cells[r + width] - c)
+                between[y] = upward
+                flux += upward
             new = c + weight * flux
             new = jnp.concatenate([new[:whole], jnp.where(ones, 1.0, new[whole:])], axis=0)
             diffused[r] = new
-            values.append(jnp.concatenate([halves(new), halves(at(7) * c)], axis=0))
+            values.append(jnp.concatenate([halves(new), halves(at(3) * c)], axis=0))
             found.append(hits(cells[r, species + 1 : species + 2, :]))
         return jnp.concatenate(values, axis=1), jnp.concatenate(found, axis=1)
 
@@ -340,68 +333,57 @@
         window[s // 2] = jnp.concatenate(parts, axis=1)
 
 
-def interior_kernel(planes, advanced, dz, total, out, sem):
+def neighbour_share(received, weight, axis, upper, c, i):
+    first, second = received
+    species_row = slice(weight[1], weight[1] + 1)
+    is_first = jnp.broadcast_to(upper_of(axis, 0) if upper else upper_of(axis, 1), c.shape)
+    inside = jnp.broadcast_to(has_neighbour(axis, 1), c.shape)
+    other = jnp.zeros_like(c) if second is None else jnp.where(inside, second[i], 0.0)
+    there = jnp.where(is_first, first[i], other)
+    d = 0.5 * (c[species_row] + there[species_row])
+    return weight[0] * d * (there - c)
+
+
+def interior_kernel(planes, cells, advanced, dz, weights, *refs):
+    received, (total, out, sem) = [*refs[:-3], None][:2], refs[-3:]
     row_count, rows, depth = advanced.shape
     species = out.shape[0]
     width = row_count // planes
+    weight = (jnp.broadcast_to(weight_column(weights, rows), (rows, depth)), species)
     shape = (rows, depth)
     lane = lanes_of(shape)
     low = dz[0]
     high = pltpu.roll(dz[1], depth - 1, axis=1)
-    for plane in range(planes):
-        for r in range(plane * width, (plane + 1) * width):
-            turned = depth - r if r else 0
-            a = pltpu.roll(low, turned, axis=1) if r else low
-            b = pltpu.roll(high, turned, axis=1) if r else high
-            total[r] = advanced[r] + jnp.where(
-                lane == 0, a, jnp.where(lane == depth - 1, b, 0.0)
-            )
-        span = pl.ds(plane * width, width)
+    mixed = [jnp.where(lane % 2 == parity, low, high) for parity in range(2)]
+    ends = jnp.logical_or(lane == 0, lane == depth - 1)
+    chunk = row_count // sem.shape[0]
+    spans = [pl.ds(start, chunk) for start in range(0, row_count, chunk)]
+    for n, span in enumerate(spans):
+        for r in range(n * chunk, (n + 1) * chunk):
+            turned = pltpu.roll(mixed[r % 2], depth - r, axis=1) if r else mixed[0]
+            new = advanced[r] + jnp.where(ends, turned, 0.0)
+            x, y = divmod(r, width)
+            if y in (0, width - 1):
+                new += neighbour_share(received, weight, "gy", y > 0, cells[r], x)
+            total[r] = new
         for k in range(species):
-            pltpu.make_async_copy(
-                total.at[span, k, :], out.at[k, span], sem.at[plane]
-            ).start()
-    for plane in range(planes):
-        span = pl.ds(plane * width, width)
-        pltpu.make_async_copy(
-            total.at[pl.ds(0, species), pl.ds(0, width), :], out.at[:, span], sem.at[plane]
-        ).wait()
-
-
-def face_kernel(planes, has_b, cells, total, weights, *refs):
-    halos, changed = list(refs[:-1]), refs[-1]
+            pltpu.make_async_copy(total.at[span, k, :], out.at[k, span], sem.at[n]).start()
+    for n, span in enumerate(spans):
+        written = total.at[span, pl.ds(0, species), :]
+        pltpu.make_async_copy(written, written, sem.at[n]).wait()
+
+
+def face_kernel(planes, cells, total, weights, *refs):
+    received, changed = [*refs[:-1], None][:2], refs[-1]
     row_count, rows, depth = total.shape
     species = weights.shape[1]
     width = row_count // planes
-    weight = jnp.broadcast_to(weight_column(weights, rows), (rows, depth))
-    received = {}
-    for axis, both in zip(("gx", "gy"), has_b):
-        received[axis] = [halos.pop(0), halos.pop(0) if both else None]
-
-    def share(axis, upper, c, i):
-        first, second = received[axis]
-        is_first = jnp.broadcast_to(upper_of(axis, 0) if upper else upper_of(axis, 1), c.shape)
-        inside = jnp.broadcast_to(has_neighbour(axis, 1), c.shape)
-        other = jnp.zeros_like(c) if second is None else jnp.where(inside, second[i], 0.0)
-        there = jnp.where(is_first, first[i], other)
-        d = 0.5 * (c[species : species + 1] + there[species : species + 1])
-        return weight * d * (there - c)
-
-    n = 0
-    for x in (0, planes - 1):
+    weight = (jnp.broadcast_to(weight_column(weights, rows), (rows, depth)), species)
+    for n, x in enumerate((0, planes - 1)):
         for y in range(width):
             r = x * width + y
-            c = cells[r]
-            new = total[r] + share("gx", x > 0, c, y)
-            if y in (0, width - 1):
-                new += share("gy", y > 0, c, x)
-            changed[n] = new
-            n += 1
-    for y in (0, width - 1):
-        for x in range(1, planes - 1):
-            r = x * width + y
-            changed[n] = total[r] + share("gy", y > 0, cells[r], x)
-            n += 1
+            new = total[r] + neighbour_share(received, weight, "gx", x > 0, cells[r], y)
+            changed[n, :, y, :] = new[:species]
 
 
 def last_kernel(planes, changed, first_out, *refs):
@@ -409,41 +391,19 @@
     species, row_count, _ = out.shape
     width = row_count // planes
     per_device, bins = means.shape[1:]
-    copies = []
-    n = 0
-    for x in (0, planes - 1):
-        for k in range(species):
-            copies.append(
-                pltpu.make_async_copy(
-                    changed.at[pl.ds(n, width), k, :],
-                    out.at[k, pl.ds(x * width, width)],
-                    sem.at[1],
-                )
-            )
-        n += width
-    cells_out = out.reshape(species, planes, width, out.shape[2])
-    for y in (0, width - 1):
-        for k in range(species):
-            copies.append(
-                pltpu.make_async_copy(
-                    changed.at[pl.ds(n, planes - 2), k, :],
-                    cells_out.at[k, pl.ds(1, planes - 2), y, :],
-                    sem.at[1],
-                )
-            )
-        n += planes - 2
     for s in range(0, per_device, 2):
         block = sum((term[s // 2] for term in terms[1:]), terms[0][s // 2])
         block = block / jnp.maximum(block[species + 1 : species + 2], 1.0)
         means[:, s, :] = block[:species, :bins]
         means[:, s + 1, :] = block[:species, bins:]
-    means_copy = pltpu.make_async_copy(means, means_out, sem.at[0])
-    means_copy.start()
+    copies = [pltpu.make_async_copy(means, means_out, sem.at[0])]
+    for n, x in enumerate((0, planes - 1)):
+        rows_out = out.at[:, pl.ds(x * width, width)]
+        copies.append(pltpu.make_async_copy(changed.at[n], rows_out, sem.at[1 + n]))
     for copy in copies:
         copy.start()
-    means_copy.wait()
-    all_changed = changed.at[pl.ds(0, n), pl.ds(0, species), :]
-    pltpu.make_async_copy(all_changed, all_changed, sem.at[1]).wait()
+    for copy in copies:
+        copy.wait()
 
 
 def struct(*shape):
@@ -570,7 +530,10 @@
         ],
         4,
         [VMEM] * 3,
-        scratch=[pltpu.VMEM((8, row_count, depth), F32)],
+        scratch=[
+            pltpu.VMEM((4, row_count, depth), F32),
+            pltpu.VMEM((width, rows, depth), F32),
+        ],
         flops=10_000_000,
         moved=4_000_000,
     )(rows_in, mixing, thermal, weights)
@@ -610,22 +573,22 @@
         [VMEM] * (1 + has_b[0]),
     )(rows_in, window)
     wide_halos = [swapped(face, "gx", side) for side, face in enumerate(outer_planes)]
-    wide_halos += [halo for halo, (axis, _) in zip(halos, sides) if axis == "gy"]
+    gy_halos = [halo for halo, (axis, _) in zip(halos, sides) if axis == "gy"]
 
     total, advanced = call(
         functools.partial(interior_kernel, planes),
         "interior",
         [struct(row_count, rows, depth), struct(species, row_count, depth)],
-        2,
+        4 + len(gy_halos),
         [VMEM, ANY],
-        scratch=[pltpu.SemaphoreType.DMA((planes,))],
+        scratch=[pltpu.SemaphoreType.DMA((planes // 2,))],
         flops=1_000_000,
         moved=3_000_000,
-    )(advanced, dz)
+    )(rows_in, advanced, dz, weights, *gy_halos)
     changed = call(
-        functools.partial(face_kernel, planes, has_b[:2]),
-        "rows_of_faces",
-        struct(2 * (width + planes - 2), rows, depth),
+        functools.partial(face_kernel, planes),
+        "outer_rows",
+        struct(2, species, width, depth),
         3 + len(wide_halos),
         VMEM,
     )(rows_in, total, weights, *wide_halos)
@@ -638,7 +601,7 @@
         in_specs=[VMEM, ANY] + [VMEM] * len(terms),
         scratch=[
             pltpu.VMEM((species, per_device, NB), F32),
-            pltpu.SemaphoreType.DMA((2,)),
+            pltpu.SemaphoreType.DMA((3,)),
         ],
         aliases={1: 0},
     )(changed, advanced, *terms)

time: 24.3 us -> 24.1 us (level)
  Pallas kernels: 8.25 us -> 7.8 us
    pallas_call x1, Pallas kernels: 1.72 us -> 1.35 us  [on_device(): call(functools.partial(interior_kernel, planes), 'interior', [struct(row_...]
  transfers between devices with their start and end apart: 12 -> 12, of which waited for: 2 -> 4; matrix products, arithmetic and copies ran while one was open for 0% -> 0% of each run, Pallas kernels for 19% -> 18%
where the time goes in v12:
time: 24.1 us; the launch traced here: 23.9 us
  starting transfers between devices  13.6 us (56%)
  Pallas kernels  7.8 us (32%)
  waiting for transfers between devices  1.67 us (7%)
  between operations  0.81 us (3%)
    ppermute x6, starting transfers between devices, joint(): return lax.ppermute(block, ('sec', axis), pairs)  6.44 us
    ppermute x4, starting transfers between devices, swapped(): return lax.ppermute(block, axis, [(i, i ^ 1) for i in range(count)])  5.92 us
    pallas_call x1, Pallas kernels, on_device(): call(functools.partial(inner_kernel, planes), 'inside', [struct(row_count...  2.01 us
    pallas_call x1, Pallas kernels, on_device(): call(functools.partial(pack_kernel, planes, has_b), 'faces', [struct(row_...  1.84 us
    pallas_call x1, Pallas kernels, on_device(): call(functools.partial(interior_kernel, planes), 'interior', [struct(row_...  1.35 us
    ppermute x6, waiting for transfers between devices, joint(): return lax.ppermute(block, ('sec', axis), pairs)  1.21 us
    pallas_call x1, Pallas kernels, on_device(): call(functools.partial(last_kernel, planes), 'last', [struct(species, row...  0.9 us
    ppermute x1, starting transfers between devices, swapped(): return lax.ppermute(block, axis, [*pairs, (0, count - 1), (count - 1, 0)])  0.68 us
  transfers between devices with their start and end apart: 12, of which 4 were waited for; matrix products, arithmetic and copies ran while one was open for 0% of the time, Pallas kernels for 18%

profile of v12, /device:TPU:0, one launch (start us, length us, event | category | flops | bytes accessed | tf_op | source)
XLA Modules:
  0.0 23.9 jit_solution(10060893006089707214)
XLA Ops:
  0.6 0.0 copy-start.1
  0.6 0.0 copy-start
  0.7 0.0 copy-start.3
  0.7 0.0 copy-start.2
  0.7 0.0 copy-start.4
  0.7 1.8 %faces.1 = (f32[128,24,128]{2,1,0:T(8,128)S(1)}, f32[2,24,128]{2,1,0:T(8,128)S(1)}, f32[32,128]{1,0:T(8,128)S(1)}, f32[32,128]{1,0:T(8,128)S(1)}, f32[8,24,128]{...) custom-call(f32[22,128,128]{2,1,0:T(8,128)} %bitcast.16, f32[128,128]{1,0:T(8,128)} %bitcast.9, ...), custom_call_target="tpu_custom_call" | custom-call | tf_op jit(solution)/shard_map/faces/pallas_call | solution.py:504
  2.5 3.0 %collective-permute-start.2 = (f32[8,24,128]{2,1,0:T(8,128)S(1)}, f32[8,24,128]{2,1,0:T(8,128)S(1)}, u32[]{:S(2)}, u32[]{:S(2)}) collective-permute-start(f32[8,24,128]{2,1,0:T(8,128)S(1)} %get-tuple-element.27), channel_id=1, source_target_pairs={{0,1},{1,0},{2,3},{3,2},{4,5},{5,4},{6,7},{7,6},{8,9},{9,8},{10,11... | collective-permute-start | bytes 294920 | tf_op jit(solution)/shard_map/ppermute | solution.py:442
  5.5 0.7 %collective-permute-start.4 = (f32[40,128]{1,0:T(8,128)S(1)}, f32[40,128]{1,0:T(8,128)S(1)}, u32[]{:S(2)}, u32[]{:S(2)}) collective-permute-start(f32[40,128]{1,0:T(8,128)S(1)} %get-tuple-element.29), channel_id=1, source_target_pairs={{8,16},{16,8},{0,24},{24,0},{9,17},{17,9},{1,25},{25,1},{10,18},{1... | collective-permute-start | bytes 61448 | tf_op jit(solution)/shard_map/ppermute | solution.py:445
  6.2 1.6 %collective-permute-start = (f32[32,128]{1,0:T(8,128)S(1)}, f32[32,128]{1,0:T(8,128)S(1)}, u32[]{:S(2)}, u32[]{:S(2)}) collective-permute-start(f32[32,128]{1,0:T(8,128)S(1)} %get-tuple-element.25), channel_id=1, source_target_pairs={{0,2},{2,0},{4,6},{6,4},{1,3},{3,1},{5,7},{7,5},{8,10},{10,8},{12,... | collective-permute-start | bytes 49160 | tf_op jit(solution)/shard_map/ppermute | solution.py:442
  7.8 0.7 %collective-permute-start.1 = (f32[32,128]{1,0:T(8,128)S(1)}, f32[32,128]{1,0:T(8,128)S(1)}, u32[]{:S(2)}, u32[]{:S(2)}) collective-permute-start(f32[32,128]{1,0:T(8,128)S(1)} %get-tuple-element.26), channel_id=1, source_target_pairs={{8,0},{4,2},{2,4},{14,6},{0,8},{12,10},{10,12},{6,14},{24,16},{20,... | collective-permute-start | bytes 49160 | tf_op jit(solution)/shard_map/ppermute | solution.py:436
  8.5 0.0 collective-permute-start.3
  8.5 0.0 copy-done.1
  8.5 0.0 copy-done
  8.5 0.0 copy-done.3
  8.5 2.0 %inside.1 = (f32[128,24,128]{2,1,0:T(8,128)S(1)}, f32[5,24,64]{2,1,0:T(8,128)S(1)}, f32[5,24,64]{2,1,0:T(8,128)S(1)}) custom-call(f32[128,24,128]{2,1,0:T(8,128)S(1)} %get-tuple-element.20.cells, f32[128,128]{1,0:T(8,128)S(1)} %bitcast.10, f32[128,128]{1,0:T(8,128)S(1)} %bitcast.7, f32[1,22]{1,0:T(1,128)S(1)} %bitcast.11), custom_call_target="tpu_custom_call" | custom-call | flops 10000000 | bytes 4000000 | tf_op jit(solution)/shard_map/inside/pallas_call | solution.py:523
  10.5 0.0 collective-permute-done.3.refs_3_
  10.5 0.0 collective-permute-done.refs_0_
  10.5 0.0 collective-permute-done.1.refs_1_
  10.5 0.0 collective-permute-done.4.refs_4_
  10.6 0.0 collective-permute-done.2.refs_2_.refs_0_
  10.6 0.0 copy-done.2
  10.6 0.0 copy-done.4
  10.6 0.6 %edges.1 = (f32[4,24,128]{2,1,0:T(8,128)S(1)}, f32[2,24,128]{2,1,0:T(8,128)S(1)}) custom-call(f32[128,24,128]{2,1,0:T(8,128)S(1)} %get-tuple-element.20.cells, f32[2,24,128]{2,1,0:T(8,128)S(1)} %get-tuple-element.22.own_z, f32[5,24,64]{2,1,0:T(8,128)S(1)} %get-tuple-element.23.sums, f32[5,24,64]{2,1,0:T(8,128)S(1)} %get-tuple-element.24.heated_sums, ...), custom_call_target="tpu_custom_call" | custom-call | tf_op jit(solution)/shard_map/edges/pallas_call | solution.py:541
  11.2 0.6 %collective-permute-start.5 = (f32[4,24,128]{2,1,0:T(8,128)S(1)}, f32[4,24,128]{2,1,0:T(8,128)S(1)}, u32[]{:S(2)}, u32[]{:S(2)}) collective-permute-start(f32[4,24,128]{2,1,0:T(8,128)S(1)} %get-tuple-element.30.held.window), channel_id=1, source_target_pairs={{0,8},{8,0},{16,24},{24,16},{1,9},{9,1},{17,25},{25,17},{2,10},{10... | collective-permute-start | bytes 147464 | tf_op jit(solution)/shard_map/ppermute | solution.py:564
  11.8 0.6 %kinetics.1.advanced.after = f32[128,24,128]{2,1,0:T(8,128)S(1)} custom-call(f32[128,24,128]{2,1,0:T(8,128)S(1)} %get-tuple-element.20.cells, f32[128,24,128]{2,1,0:T(8,128)S(1)} %get-tuple-element.21.diffused, f32[128,128]{1,0:T(8,128)S(1)} %bitcast.8, f32[22,22]{1,0:T(8,128)S(1)} %copy-done.2, f32[4,24,128]{2,1,0:T(8,128)S(1)} %get-tuple-element.30.held.window), custom_call_target="tpu_custom_call" | custom-call | tf_op jit(solution)/shard_map/kinetics/pallas_call | solution.py:550
  12.4 0.2 collective-permute-done.5.received
  12.7 2.5 %collective-permute-start.8 = (f32[2,24,128]{2,1,0:T(8,128)S(1)}, f32[2,24,128]{2,1,0:T(8,128)S(1)}, u32[]{:S(2)}, u32[]{:S(2)}) collective-permute-start(f32[2,24,128]{2,1,0:T(8,128)S(1)} %slice.9), channel_id=1, source_target_pairs={{14,0},{8,2},{10,4},{12,6},{6,8},{0,10},{2,12},{4,14},{30,16},{24,... | collective-permute-start | bytes 73736 | tf_op jit(solution)/shard_map/ppermute | solution.py:436
  15.2 1.3 %collective-permute-start.6 = (f32[16,24,128]{2,1,0:T(8,128)S(1)}, f32[16,24,128]{2,1,0:T(8,128)S(1)}, u32[]{:S(2)}, u32[]{:S(2)}) collective-permute-start(f32[16,24,128]{2,1,0:T(8,128)S(1)} %get-tuple-element.33), channel_id=1, source_target_pairs={{0,2},{2,0},{4,6},{6,4},{1,3},{3,1},{5,7},{7,5},{8,10},{10,8},{12,... | collective-permute-start | bytes 589832 | tf_op jit(solution)/shard_map/ppermute | solution.py:442
  16.6 0.1 collective-permute-start.7
  16.6 1.1 %collective-permute-done.8 = f32[2,24,128]{2,1,0:T(8,128)S(1)} collective-permute-done((f32[2,24,128]{2,1,0:T(8,128)S(1)}, f32[2,24,128]{2,1,0:T(8,128)S(1)}, u32[]{:S(2)}, u32[]{:S(2)}) %collective-permute-start.8) | collective-permute-done | bytes 24608 | tf_op jit(solution)/shard_map/ppermute | solution.py:436
  17.8 0.5 %collective-permute-start.9 = (f32[2,24,128]{2,1,0:T(8,128)S(1)}, f32[2,24,128]{2,1,0:T(8,128)S(1)}, u32[]{:S(2)}, u32[]{:S(2)}) collective-permute-start(f32[2,24,128]{2,1,0:T(8,128)S(1)} %slice_add_fusion.refs_0_), channel_id=1, source_target_pairs={{24,0},{25,1},{16,8},{17,9},{8,16},{9,17},{0,24},{1,25},{26,2},{27... | collective-permute-start | bytes 73736 | tf_op jit(solution)/shard_map/ppermute | solution.py:436
  18.2 1.3 %collective-permute-start.10 = (f32[2,24,128]{2,1,0:T(8,128)S(1)}, f32[2,24,128]{2,1,0:T(8,128)S(1)}, u32[]{:S(2)}, u32[]{:S(2)}) collective-permute-start(f32[2,24,128]{2,1,0:T(8,128)S(1)} %slice_add_fusion.refs_0_), channel_id=1, source_target_pairs={{25,0},{24,1},{17,8},{16,9},{9,16},{8,17},{1,24},{0,25},{27,2},{26... | collective-permute-start | bytes 73736 | tf_op jit(solution)/shard_map/ppermute | solution.py:436
  19.5 1.4 %collective-permute-start.11 = (f32[2,24,128]{2,1,0:T(8,128)S(1)}, f32[2,24,128]{2,1,0:T(8,128)S(1)}, u32[]{:S(2)}, u32[]{:S(2)}) collective-permute-start(f32[2,24,128]{2,1,0:T(8,128)S(1)} %slice_add_fusion.refs_0_), channel_id=1, source_target_pairs={{9,0},{8,1},{1,8},{0,9},{25,16},{24,17},{17,24},{16,25},{11,2},{10... | collective-permute-start | bytes 73736 | tf_op jit(solution)/shard_map/ppermute | solution.py:436
  21.0 1.4 %interior.1 = (f32[128,24,128]{2,1,0:T(8,128)S(1)}, f32[22,128,128]{2,1,0:T(8,128)}) custom-call(f32[128,24,128]{2,1,0:T(8,128)S(1)} %get-tuple-element.20.cells, f32[128,24,128]{2,1,0:T(8,128)S(1)} %kinetics.1.advanced.after, f32[2,24,128]{2,1,0:T(8,128)S(1)} %get-tuple-element.31.dz, f32[1,22]{1,0:T(1,128)S(1)} %bitcast.13, ...), custom_call_target="tpu_custom_call" | custom-call | flops 1000000 | bytes 3000000 | tf_op jit(solution)/shard_map/interior/pallas_call | solution.py:578
  22.3 0.2 collective-permute-done.6.refs_0_
  22.5 0.0 collective-permute-done.7.refs_1_
  22.5 0.4 %outer_rows.1.changed = f32[2,22,16,128]{3,2,1,0:T(8,128)S(1)} custom-call(f32[128,24,128]{2,1,0:T(8,128)S(1)} %get-tuple-element.20.cells, f32[128,24,128]{2,1,0:T(8,128)S(1)} %get-tuple-element.32.total, f32[1,22]{1,0:T(1,128)S(1)} %bitcast.14, f32[16,24,128]{2,1,0:T(8,128)S(1)} %collective-permute-done.6.refs_0_, ...), custom_call_target="tpu_custom_call" | custom-call | tf_op jit(solution)/shard_map/outer_rows/pallas_call | solution.py:588
  22.9 0.0 collective-permute-done.9.refs_1_
  22.9 0.0 collective-permute-done.10.refs_2_
  22.9 0.1 collective-permute-done.11.refs_3_
  23.0 0.9 %last.1 = (f32[22,128,128]{2,1,0:T(8,128)}, f32[22,4,64]{2,1,0:T(4,128)}) custom-call(f32[2,22,16,128]{3,2,1,0:T(8,128)S(1)} %outer_rows.1.changed, f32[22,128,128]{2,1,0:T(8,128)} %get-tuple-element.35.first_out, f32[2,24,128]{2,1,0:T(8,128)S(1)} %slice_add_fusion.refs_0_, ...), custom_call_target="tpu_custom_call", output_to_operand_aliasing={{0}: (1, {})} | custom-call | tf_op jit(solution)/shard_map/last/pallas_call | solution.py:595
  (4 shorter events, 0.0 us)
Async XLA Ops:
  0.6 7.8 %copy-start.1 = (f32[8,16,128]{2,1,0:T(8,128)S(1)}, f32[8,16,128]{2,1,0:T(8,128)}, u32[]{:S(2)}) copy-start(f32[8,16,128]{2,1,0:T(8,128)} %param.8) | copy-start | bytes 196612
  0.6 7.8 %copy-start = (f32[8,16,128]{2,1,0:T(8,128)S(1)}, f32[8,16,128]{2,1,0:T(8,128)}, u32[]{:S(2)}) copy-start(f32[8,16,128]{2,1,0:T(8,128)} %param.9) | copy-start | bytes 196612
  0.7 7.8 %copy-start.3 = (f32[22]{0:T(128)S(1)}, f32[22]{0:T(128)}, u32[]{:S(2)}) copy-start(f32[22]{0:T(128)} %param.10) | copy-start | bytes 268
  0.7 9.9 %copy-start.2 = (f32[22,22]{1,0:T(8,128)S(1)}, f32[22,22]{1,0:T(8,128)}, u32[]{:S(2)}) copy-start(f32[22,22]{1,0:T(8,128)} %jacobian.3) | copy-start | bytes 5812
  0.7 9.9 %copy-start.4 = (s32[32]{0:T(128)S(1)}, s32[32]{0:T(128)}, u32[]{:S(2)}) copy-start(s32[32]{0:T(128)} %param.13) | copy-start | bytes 388
  2.5 8.0 %collective-permute-start.2 = (f32[8,24,128]{2,1,0:T(8,128)S(1)}, f32[8,24,128]{2,1,0:T(8,128)S(1)}, u32[]{:S(2)}, u32[]{:S(2)}) collective-permute-start(f32[8,24,128]{2,1,0:T(8,128)S(1)} %get-tuple-element.27), channel_id=1, source_target_pairs={{0,1},{1,0},{2,3},{3,2},{4,5},{5,4},{6,7},{7,6},{8,9},{9,8},{10,11... | collective-permute-start | bytes 294920 | tf_op jit(solution)/shard_map/ppermute | solution.py:442
  5.5 5.0 %collective-permute-start.4 = (f32[40,128]{1,0:T(8,128)S(1)}, f32[40,128]{1,0:T(8,128)S(1)}, u32[]{:S(2)}, u32[]{:S(2)}) collective-permute-start(f32[40,128]{1,0:T(8,128)S(1)} %get-tuple-element.29), channel_id=1, source_target_pairs={{8,16},{16,8},{0,24},{24,0},{9,17},{17,9},{1,25},{25,1},{10,18},{1... | collective-permute-start | bytes 61448 | tf_op jit(solution)/shard_map/ppermute | solution.py:445
  6.2 4.3 %collective-permute-start = (f32[32,128]{1,0:T(8,128)S(1)}, f32[32,128]{1,0:T(8,128)S(1)}, u32[]{:S(2)}, u32[]{:S(2)}) collective-permute-start(f32[32,128]{1,0:T(8,128)S(1)} %get-tuple-element.25), channel_id=1, source_target_pairs={{0,2},{2,0},{4,6},{6,4},{1,3},{3,1},{5,7},{7,5},{8,10},{10,8},{12,... | collective-permute-start | bytes 49160 | tf_op jit(solution)/shard_map/ppermute | solution.py:442
  7.8 2.7 %collective-permute-start.1 = (f32[32,128]{1,0:T(8,128)S(1)}, f32[32,128]{1,0:T(8,128)S(1)}, u32[]{:S(2)}, u32[]{:S(2)}) collective-permute-start(f32[32,128]{1,0:T(8,128)S(1)} %get-tuple-element.26), channel_id=1, source_target_pairs={{8,0},{4,2},{2,4},{14,6},{0,8},{12,10},{10,12},{6,14},{24,16},{20,... | collective-permute-start | bytes 49160 | tf_op jit(solution)/shard_map/ppermute | solution.py:436
  8.5 2.0 %collective-permute-start.3 = (f32[24,128]{1,0:T(8,128)S(1)}, f32[24,128]{1,0:T(8,128)S(1)}, u32[]{:S(2)}, u32[]{:S(2)}) collective-permute-start(f32[24,128]{1,0:T(8,128)S(1)} %get-tuple-element.28), channel_id=1, source_target_pairs={{0,8},{8,0},{16,24},{24,16},{1,9},{9,1},{17,25},{25,17},{2,10},{10... | collective-permute-start | bytes 36872 | tf_op jit(solution)/shard_map/ppermute | solution.py:442
  11.2 1.4 %collective-permute-start.5 = (f32[4,24,128]{2,1,0:T(8,128)S(1)}, f32[4,24,128]{2,1,0:T(8,128)S(1)}, u32[]{:S(2)}, u32[]{:S(2)}) collective-permute-start(f32[4,24,128]{2,1,0:T(8,128)S(1)} %get-tuple-element.30.held.window), channel_id=1, source_target_pairs={{0,8},{8,0},{16,24},{24,16},{1,9},{9,1},{17,25},{25,17},{2,10},{10... | collective-permute-start | bytes 147464 | tf_op jit(solution)/shard_map/ppermute | solution.py:564
  12.7 5.1 %collective-permute-start.8 = (f32[2,24,128]{2,1,0:T(8,128)S(1)}, f32[2,24,128]{2,1,0:T(8,128)S(1)}, u32[]{:S(2)}, u32[]{:S(2)}) collective-permute-start(f32[2,24,128]{2,1,0:T(8,128)S(1)} %slice.9), channel_id=1, source_target_pairs={{14,0},{8,2},{10,4},{12,6},{6,8},{0,10},{2,12},{4,14},{30,16},{24,... | collective-permute-start | bytes 73736 | tf_op jit(solution)/shard_map/ppermute | solution.py:436
  15.2 7.3 %collective-permute-start.6 = (f32[16,24,128]{2,1,0:T(8,128)S(1)}, f32[16,24,128]{2,1,0:T(8,128)S(1)}, u32[]{:S(2)}, u32[]{:S(2)}) collective-permute-start(f32[16,24,128]{2,1,0:T(8,128)S(1)} %get-tuple-element.33), channel_id=1, source_target_pairs={{0,2},{2,0},{4,6},{6,4},{1,3},{3,1},{5,7},{7,5},{8,10},{10,8},{12,... | collective-permute-start | bytes 589832 | tf_op jit(solution)/shard_map/ppermute | solution.py:442
  16.6 6.0 %collective-permute-start.7 = (f32[16,24,128]{2,1,0:T(8,128)S(1)}, f32[16,24,128]{2,1,0:T(8,128)S(1)}, u32[]{:S(2)}, u32[]{:S(2)}) collective-permute-start(f32[16,24,128]{2,1,0:T(8,128)S(1)} %get-tuple-element.34), channel_id=1, source_target_pairs={{8,0},{4,2},{2,4},{14,6},{0,8},{12,10},{10,12},{6,14},{24,16},{20,... | collective-permute-start | bytes 589832 | tf_op jit(solution)/shard_map/ppermute | solution.py:436
  17.8 5.1 %collective-permute-start.9 = (f32[2,24,128]{2,1,0:T(8,128)S(1)}, f32[2,24,128]{2,1,0:T(8,128)S(1)}, u32[]{:S(2)}, u32[]{:S(2)}) collective-permute-start(f32[2,24,128]{2,1,0:T(8,128)S(1)} %slice_add_fusion.refs_0_), channel_id=1, source_target_pairs={{24,0},{25,1},{16,8},{17,9},{8,16},{9,17},{0,24},{1,25},{26,2},{27... | collective-permute-start | bytes 73736 | tf_op jit(solution)/shard_map/ppermute | solution.py:436
  18.2 4.7 %collective-permute-start.10 = (f32[2,24,128]{2,1,0:T(8,128)S(1)}, f32[2,24,128]{2,1,0:T(8,128)S(1)}, u32[]{:S(2)}, u32[]{:S(2)}) collective-permute-start(f32[2,24,128]{2,1,0:T(8,128)S(1)} %slice_add_fusion.refs_0_), channel_id=1, source_target_pairs={{25,0},{24,1},{17,8},{16,9},{9,16},{8,17},{1,24},{0,25},{27,2},{26... | collective-permute-start | bytes 73736 | tf_op jit(solution)/shard_map/ppermute | solution.py:436
  19.5 3.5 %collective-permute-start.11 = (f32[2,24,128]{2,1,0:T(8,128)S(1)}, f32[2,24,128]{2,1,0:T(8,128)S(1)}, u32[]{:S(2)}, u32[]{:S(2)}) collective-permute-start(f32[2,24,128]{2,1,0:T(8,128)S(1)} %slice_add_fusion.refs_0_), channel_id=1, source_target_pairs={{9,0},{8,1},{1,8},{0,9},{25,16},{24,17},{17,24},{16,25},{11,2},{10... | collective-permute-start | bytes 73736 | tf_op jit(solution)/shard_map/ppermute | solution.py:436

commit v13 on v12

--- a/solution.py
+++ b/solution.py
@@ -147,10 +147,6 @@
                     out[pl.ds(count + i, 1), :] = rows_out[r, pl.ds(species + 1, 1), :]
 
 
-def join_kernel(window, received, after, out):
-    out[...] = window[...] + received[...]
-
-
 def plane_kernel(planes, cells, held, *faces):
     width = cells.shape[0] // planes
     for side, out in enumerate(faces):
@@ -454,6 +450,7 @@
     deep, gx, gy = (lax.axis_size(axis) for axis in ("sec", "gx", "gy"))
     half = block.shape[0] // 2
     block = block[:half] + joint(block[half:], "gx", lambda s, i: (s ^ 1, (i - 1) % gx))
+    block = block + lax.ppermute(block, "sec", [(i, i ^ 1) for i in range(deep)])
     steps = [(1 << n, 0) for n in range(1, deep.bit_length() - 1)]
     steps += [(0, 1 << n) for n in range(gy.bit_length() - 1)]
     terms = [block]
@@ -560,9 +557,6 @@
         flops=0,
         moved=0,
     )(rows_in, diffused, thermal, kinetics_jacobian, window)
-    deep = lax.axis_size("sec")
-    received = lax.ppermute(window, "sec", [(i, i ^ 1) for i in range(deep)])
-    window = call(join_kernel, "join", struct(*window.shape), 3, VMEM)(window, received, advanced)
     terms = summed(window)
 
     outer_planes = call(
@@ -571,7 +565,7 @@
         [struct(width, rows, depth)] * (1 + has_b[0]),
         2,
         [VMEM] * (1 + has_b[0]),
-    )(rows_in, window)
+    )(rows_in, advanced)
     wide_halos = [swapped(face, "gx", side) for side, face in enumerate(outer_planes)]
     gy_halos = [halo for halo, (axis, _) in zip(halos, sides) if axis == "gy"]
 

time: 24.1 us -> 24 us (level)
    ppermute x6, starting transfers between devices: 6.44 us -> 7.18 us  [joint(): return lax.ppermute(block, ('sec', axis), pairs)]
    ppermute x6, waiting for transfers between devices: 1.21 us -> 0.56 us  [joint(): return lax.ppermute(block, ('sec', axis), pairs)]
    ppermute x1, waiting for transfers between devices: 0.24 us -> 0.85 us  [summed(): lax.ppermute(block, 'sec', [(i, i ^ 1) for i in range(deep)])]
    ppermute x4, starting transfers between devices: 5.92 us -> 5.34 us  [swapped(): return lax.ppermute(block, axis, [(i, i ^ 1) for i in range(count)])]
  transfers between devices with their start and end apart: 12 -> 12, of which waited for: 4 -> 3; matrix products, arithmetic and copies ran while one was open for 0% -> 0% of each run, Pallas kernels for 18% -> 19%
where the time goes in v13:
time: 24 us; the launch traced here: 23.8 us
  starting transfers between devices  13.7 us (57%)
  Pallas kernels  7.79 us (32%)
  waiting for transfers between devices  1.43 us (6%)
  between operations  0.83 us (3%)
    ppermute x6, starting transfers between devices, joint(): return lax.ppermute(block, ('sec', axis), pairs)  7.18 us
    ppermute x4, starting transfers between devices, swapped(): return lax.ppermute(block, axis, [(i, i ^ 1) for i in range(count)])  5.34 us
    pallas_call x1, Pallas kernels, on_device(): call(functools.partial(inner_kernel, planes), 'inside', [struct(row_count...  2.01 us
    pallas_call x1, Pallas kernels, on_device(): call(functools.partial(pack_kernel, planes, has_b), 'faces', [struct(row_...  1.84 us
    pallas_call x1, Pallas kernels, on_device(): call(functools.partial(interior_kernel, planes), 'interior', [struct(row_...  1.35 us
    pallas_call x1, Pallas kernels, on_device(): call(functools.partial(last_kernel, planes), 'last', [struct(species, row...  0.9 us
    ppermute x1, waiting for transfers between devices, summed(): lax.ppermute(block, 'sec', [(i, i ^ 1) for i in range(deep)])  0.85 us
    ppermute x1, starting transfers between devices, swapped(): return lax.ppermute(block, axis, [*pairs, (0, count - 1), (count - 1, 0)])  0.68 us
  transfers between devices with their start and end apart: 12, of which 3 were waited for; matrix products, arithmetic and copies ran while one was open for 0% of the time, Pallas kernels for 19%

profile of v13, /device:TPU:0, one launch (start us, length us, event | category | flops | bytes accessed | tf_op | source)
XLA Modules:
  0.0 23.8 jit_solution(17143708630657807724)
XLA Ops:
  0.6 0.0 copy-start.1
  0.6 0.0 copy-start
  0.7 0.0 copy-start.3
  0.7 0.0 copy-start.2
  0.7 0.0 copy-start.4
  0.7 1.8 %faces.1 = (f32[128,24,128]{2,1,0:T(8,128)S(1)}, f32[2,24,128]{2,1,0:T(8,128)S(1)}, f32[32,128]{1,0:T(8,128)S(1)}, f32[32,128]{1,0:T(8,128)S(1)}, f32[8,24,128]{...) custom-call(f32[22,128,128]{2,1,0:T(8,128)} %bitcast.16, f32[128,128]{1,0:T(8,128)} %bitcast.9, ...), custom_call_target="tpu_custom_call" | custom-call | tf_op jit(solution)/shard_map/faces/pallas_call | solution.py:501
  2.5 3.0 %collective-permute-start.2 = (f32[8,24,128]{2,1,0:T(8,128)S(1)}, f32[8,24,128]{2,1,0:T(8,128)S(1)}, u32[]{:S(2)}, u32[]{:S(2)}) collective-permute-start(f32[8,24,128]{2,1,0:T(8,128)S(1)} %get-tuple-element.27), channel_id=1, source_target_pairs={{0,1},{1,0},{2,3},{3,2},{4,5},{5,4},{6,7},{7,6},{8,9},{9,8},{10,11... | collective-permute-start | bytes 294920 | tf_op jit(solution)/shard_map/ppermute | solution.py:438
  5.5 0.7 %collective-permute-start.4 = (f32[40,128]{1,0:T(8,128)S(1)}, f32[40,128]{1,0:T(8,128)S(1)}, u32[]{:S(2)}, u32[]{:S(2)}) collective-permute-start(f32[40,128]{1,0:T(8,128)S(1)} %get-tuple-element.29), channel_id=1, source_target_pairs={{8,16},{16,8},{0,24},{24,0},{9,17},{17,9},{1,25},{25,1},{10,18},{1... | collective-permute-start | bytes 61448 | tf_op jit(solution)/shard_map/ppermute | solution.py:441
  6.2 1.6 %collective-permute-start = (f32[32,128]{1,0:T(8,128)S(1)}, f32[32,128]{1,0:T(8,128)S(1)}, u32[]{:S(2)}, u32[]{:S(2)}) collective-permute-start(f32[32,128]{1,0:T(8,128)S(1)} %get-tuple-element.25), channel_id=1, source_target_pairs={{0,2},{2,0},{4,6},{6,4},{1,3},{3,1},{5,7},{7,5},{8,10},{10,8},{12,... | collective-permute-start | bytes 49160 | tf_op jit(solution)/shard_map/ppermute | solution.py:438
  7.8 0.7 %collective-permute-start.1 = (f32[32,128]{1,0:T(8,128)S(1)}, f32[32,128]{1,0:T(8,128)S(1)}, u32[]{:S(2)}, u32[]{:S(2)}) collective-permute-start(f32[32,128]{1,0:T(8,128)S(1)} %get-tuple-element.26), channel_id=1, source_target_pairs={{8,0},{4,2},{2,4},{14,6},{0,8},{12,10},{10,12},{6,14},{24,16},{20,... | collective-permute-start | bytes 49160 | tf_op jit(solution)/shard_map/ppermute | solution.py:432
  8.5 0.0 collective-permute-start.3
  8.5 0.0 copy-done.1
  8.5 0.0 copy-done
  8.5 0.0 copy-done.3
  8.5 2.0 %inside.1 = (f32[128,24,128]{2,1,0:T(8,128)S(1)}, f32[5,24,64]{2,1,0:T(8,128)S(1)}, f32[5,24,64]{2,1,0:T(8,128)S(1)}) custom-call(f32[128,24,128]{2,1,0:T(8,128)S(1)} %get-tuple-element.20.cells, f32[128,128]{1,0:T(8,128)S(1)} %bitcast.10, f32[128,128]{1,0:T(8,128)S(1)} %bitcast.7, f32[1,22]{1,0:T(1,128)S(1)} %bitcast.11), custom_call_target="tpu_custom_call" | custom-call | flops 10000000 | bytes 4000000 | tf_op jit(solution)/shard_map/inside/pallas_call | solution.py:520
  10.5 0.0 collective-permute-done.3.refs_3_
  10.5 0.0 collective-permute-done.refs_0_
  10.5 0.0 collective-permute-done.1.refs_1_
  10.5 0.0 collective-permute-done.4.refs_4_
  10.6 0.0 collective-permute-done.2.refs_2_.refs_0_
  10.6 0.0 copy-done.2
  10.6 0.0 copy-done.4
  10.6 0.6 %edges.1 = (f32[4,24,128]{2,1,0:T(8,128)S(1)}, f32[2,24,128]{2,1,0:T(8,128)S(1)}) custom-call(f32[128,24,128]{2,1,0:T(8,128)S(1)} %get-tuple-element.20.cells, f32[2,24,128]{2,1,0:T(8,128)S(1)} %get-tuple-element.22.own_z, f32[5,24,64]{2,1,0:T(8,128)S(1)} %get-tuple-element.23.sums, f32[5,24,64]{2,1,0:T(8,128)S(1)} %get-tuple-element.24.heated_sums, ...), custom_call_target="tpu_custom_call" | custom-call | tf_op jit(solution)/shard_map/edges/pallas_call | solution.py:538
  11.2 2.6 %collective-permute-start.7 = (f32[2,24,128]{2,1,0:T(8,128)S(1)}, f32[2,24,128]{2,1,0:T(8,128)S(1)}, u32[]{:S(2)}, u32[]{:S(2)}) collective-permute-start(f32[2,24,128]{2,1,0:T(8,128)S(1)} %slice.7), channel_id=1, source_target_pairs={{14,0},{8,2},{10,4},{12,6},{6,8},{0,10},{2,12},{4,14},{30,16},{24,... | collective-permute-start | bytes 73736 | tf_op jit(solution)/shard_map/ppermute | solution.py:432
  13.9 0.6 %kinetics.1.advanced.held = f32[128,24,128]{2,1,0:T(8,128)S(1)} custom-call(f32[128,24,128]{2,1,0:T(8,128)S(1)} %get-tuple-element.20.cells, f32[128,24,128]{2,1,0:T(8,128)S(1)} %get-tuple-element.21.diffused, f32[128,128]{1,0:T(8,128)S(1)} %bitcast.8, f32[22,22]{1,0:T(8,128)S(1)} %copy-done.2, f32[4,24,128]{2,1,0:T(8,128)S(1)} %get-tuple-element.30.held), custom_call_target="tpu_custom_call" | custom-call | tf_op jit(solution)/shard_map/kinetics/pallas_call | solution.py:547
  14.6 0.8 %collective-permute-start.5 = (f32[16,24,128]{2,1,0:T(8,128)S(1)}, f32[16,24,128]{2,1,0:T(8,128)S(1)}, u32[]{:S(2)}, u32[]{:S(2)}) collective-permute-start(f32[16,24,128]{2,1,0:T(8,128)S(1)} %get-tuple-element.33), channel_id=1, source_target_pairs={{0,2},{2,0},{4,6},{6,4},{1,3},{3,1},{5,7},{7,5},{8,10},{10,8},{12,... | collective-permute-start | bytes 589832 | tf_op jit(solution)/shard_map/ppermute | solution.py:438
  15.3 0.7 %collective-permute-start.6 = (f32[16,24,128]{2,1,0:T(8,128)S(1)}, f32[16,24,128]{2,1,0:T(8,128)S(1)}, u32[]{:S(2)}, u32[]{:S(2)}) collective-permute-start(f32[16,24,128]{2,1,0:T(8,128)S(1)} %get-tuple-element.34), channel_id=1, source_target_pairs={{8,0},{4,2},{2,4},{14,6},{0,8},{12,10},{10,12},{6,14},{24,16},{20,... | collective-permute-start | bytes 589832 | tf_op jit(solution)/shard_map/ppermute | solution.py:432
  16.0 0.3 %collective-permute-done.7 = f32[2,24,128]{2,1,0:T(8,128)S(1)} collective-permute-done((f32[2,24,128]{2,1,0:T(8,128)S(1)}, f32[2,24,128]{2,1,0:T(8,128)S(1)}, u32[]{:S(2)}, u32[]{:S(2)}) %collective-permute-start.7) | collective-permute-done | bytes 24608 | tf_op jit(solution)/shard_map/ppermute | solution.py:432
  16.3 0.5 %collective-permute-start.8 = (f32[2,24,128]{2,1,0:T(8,128)S(1)}, f32[2,24,128]{2,1,0:T(8,128)S(1)}, u32[]{:S(2)}, u32[]{:S(2)}) collective-permute-start(f32[2,24,128]{2,1,0:T(8,128)S(1)} %slice_add_fusion), channel_id=1, source_target_pairs={{0,8},{8,0},{16,24},{24,16},{1,9},{9,1},{17,25},{25,17},{2,10},{10... | collective-permute-start | bytes 73736 | tf_op jit(solution)/shard_map/ppermute | solution.py:453
  16.8 0.8 %collective-permute-done.8 = f32[2,24,128]{2,1,0:T(8,128)S(1)} collective-permute-done((f32[2,24,128]{2,1,0:T(8,128)S(1)}, f32[2,24,128]{2,1,0:T(8,128)S(1)}, u32[]{:S(2)}, u32[]{:S(2)}) %collective-permute-start.8) | collective-permute-done | bytes 24608 | tf_op jit(solution)/shard_map/ppermute | solution.py:453
  17.7 0.5 %collective-permute-start.9 = (f32[2,24,128]{2,1,0:T(8,128)S(1)}, f32[2,24,128]{2,1,0:T(8,128)S(1)}, u32[]{:S(2)}, u32[]{:S(2)}) collective-permute-start(f32[2,24,128]{2,1,0:T(8,128)S(1)} %add.7.refs_0_), channel_id=1, source_target_pairs={{24,0},{25,1},{16,8},{17,9},{8,16},{9,17},{0,24},{1,25},{26,2},{27... | collective-permute-start | bytes 73736 | tf_op jit(solution)/shard_map/ppermute | solution.py:432
  18.1 1.3 %collective-permute-start.10 = (f32[2,24,128]{2,1,0:T(8,128)S(1)}, f32[2,24,128]{2,1,0:T(8,128)S(1)}, u32[]{:S(2)}, u32[]{:S(2)}) collective-permute-start(f32[2,24,128]{2,1,0:T(8,128)S(1)} %add.7.refs_0_), channel_id=1, source_target_pairs={{25,0},{24,1},{17,8},{16,9},{9,16},{8,17},{1,24},{0,25},{27,2},{26... | collective-permute-start | bytes 73736 | tf_op jit(solution)/shard_map/ppermute | solution.py:432
  19.4 1.4 %collective-permute-start.11 = (f32[2,24,128]{2,1,0:T(8,128)S(1)}, f32[2,24,128]{2,1,0:T(8,128)S(1)}, u32[]{:S(2)}, u32[]{:S(2)}) collective-permute-start(f32[2,24,128]{2,1,0:T(8,128)S(1)} %add.7.refs_0_), channel_id=1, source_target_pairs={{9,0},{8,1},{1,8},{0,9},{25,16},{24,17},{17,24},{16,25},{11,2},{10... | collective-permute-start | bytes 73736 | tf_op jit(solution)/shard_map/ppermute | solution.py:432
  20.8 1.4 %interior.1 = (f32[128,24,128]{2,1,0:T(8,128)S(1)}, f32[22,128,128]{2,1,0:T(8,128)}) custom-call(f32[128,24,128]{2,1,0:T(8,128)S(1)} %get-tuple-element.20.cells, f32[128,24,128]{2,1,0:T(8,128)S(1)} %kinetics.1.advanced.held, f32[2,24,128]{2,1,0:T(8,128)S(1)} %get-tuple-element.31.dz, f32[1,22]{1,0:T(1,128)S(1)} %bitcast.13, ...), custom_call_target="tpu_custom_call" | custom-call | flops 1000000 | bytes 3000000 | tf_op jit(solution)/shard_map/interior/pallas_call | solution.py:572
  22.2 0.0 collective-permute-done.5.refs_0_
  22.2 0.0 collective-permute-done.6.refs_1_
  22.2 0.4 %outer_rows.1.changed = f32[2,22,16,128]{3,2,1,0:T(8,128)S(1)} custom-call(f32[128,24,128]{2,1,0:T(8,128)S(1)} %get-tuple-element.20.cells, f32[128,24,128]{2,1,0:T(8,128)S(1)} %get-tuple-element.32.total, f32[1,22]{1,0:T(1,128)S(1)} %bitcast.14, f32[16,24,128]{2,1,0:T(8,128)S(1)} %collective-permute-done.5.refs_0_, ...), custom_call_target="tpu_custom_call" | custom-call | tf_op jit(solution)/shard_map/outer_rows/pallas_call | solution.py:582
  22.6 0.0 collective-permute-done.9.refs_1_
  22.6 0.0 collective-permute-done.10.refs_2_
  22.6 0.3 %collective-permute-done.11.refs_3_ = f32[2,24,128]{2,1,0:T(8,128)S(1)} collective-permute-done((f32[2,24,128]{2,1,0:T(8,128)S(1)}, f32[2,24,128]{2,1,0:T(8,128)S(1)}, u32[]{:S(2)}, u32[]{:S(2)}) %collective-permute-start.11) | collective-permute-done | bytes 24608 | tf_op jit(solution)/shard_map/ppermute | solution.py:432
  22.9 0.9 %last.1 = (f32[22,128,128]{2,1,0:T(8,128)}, f32[22,4,64]{2,1,0:T(4,128)}) custom-call(f32[2,22,16,128]{3,2,1,0:T(8,128)S(1)} %outer_rows.1.changed, f32[22,128,128]{2,1,0:T(8,128)} %get-tuple-element.35.first_out, f32[2,24,128]{2,1,0:T(8,128)S(1)} %add.7.refs_0_, f32[2,24,128]{2,1,0:T(8,128)S(1)} %collective-permute-done.9.refs_1_, ...), custom_call_target="tpu_custom_call", output_to_operand_aliasing={{0}: (1, {})} | custom-call | tf_op jit(solution)/shard_map/last/pallas_call | solution.py:589
  (4 shorter events, 0.1 us)
Async XLA Ops:
  0.6 7.8 %copy-start.1 = (f32[8,16,128]{2,1,0:T(8,128)S(1)}, f32[8,16,128]{2,1,0:T(8,128)}, u32[]{:S(2)}) copy-start(f32[8,16,128]{2,1,0:T(8,128)} %param.8) | copy-start | bytes 196612
  0.6 7.8 %copy-start = (f32[8,16,128]{2,1,0:T(8,128)S(1)}, f32[8,16,128]{2,1,0:T(8,128)}, u32[]{:S(2)}) copy-start(f32[8,16,128]{2,1,0:T(8,128)} %param.9) | copy-start | bytes 196612
  0.7 7.8 %copy-start.3 = (f32[22]{0:T(128)S(1)}, f32[22]{0:T(128)}, u32[]{:S(2)}) copy-start(f32[22]{0:T(128)} %param.10) | copy-start | bytes 268
  0.7 9.9 %copy-start.2 = (f32[22,22]{1,0:T(8,128)S(1)}, f32[22,22]{1,0:T(8,128)}, u32[]{:S(2)}) copy-start(f32[22,22]{1,0:T(8,128)} %jacobian.3) | copy-start | bytes 5812
  0.7 9.9 %copy-start.4 = (s32[32]{0:T(128)S(1)}, s32[32]{0:T(128)}, u32[]{:S(2)}) copy-start(s32[32]{0:T(128)} %param.13) | copy-start | bytes 388
  2.5 8.0 %collective-permute-start.2 = (f32[8,24,128]{2,1,0:T(8,128)S(1)}, f32[8,24,128]{2,1,0:T(8,128)S(1)}, u32[]{:S(2)}, u32[]{:S(2)}) collective-permute-start(f32[8,24,128]{2,1,0:T(8,128)S(1)} %get-tuple-element.27), channel_id=1, source_target_pairs={{0,1},{1,0},{2,3},{3,2},{4,5},{5,4},{6,7},{7,6},{8,9},{9,8},{10,11... | collective-permute-start | bytes 294920 | tf_op jit(solution)/shard_map/ppermute | solution.py:438
  5.5 5.0 %collective-permute-start.4 = (f32[40,128]{1,0:T(8,128)S(1)}, f32[40,128]{1,0:T(8,128)S(1)}, u32[]{:S(2)}, u32[]{:S(2)}) collective-permute-start(f32[40,128]{1,0:T(8,128)S(1)} %get-tuple-element.29), channel_id=1, source_target_pairs={{8,16},{16,8},{0,24},{24,0},{9,17},{17,9},{1,25},{25,1},{10,18},{1... | collective-permute-start | bytes 61448 | tf_op jit(solution)/shard_map/ppermute | solution.py:441
  6.2 4.3 %collective-permute-start = (f32[32,128]{1,0:T(8,128)S(1)}, f32[32,128]{1,0:T(8,128)S(1)}, u32[]{:S(2)}, u32[]{:S(2)}) collective-permute-start(f32[32,128]{1,0:T(8,128)S(1)} %get-tuple-element.25), channel_id=1, source_target_pairs={{0,2},{2,0},{4,6},{6,4},{1,3},{3,1},{5,7},{7,5},{8,10},{10,8},{12,... | collective-permute-start | bytes 49160 | tf_op jit(solution)/shard_map/ppermute | solution.py:438
  7.8 2.7 %collective-permute-start.1 = (f32[32,128]{1,0:T(8,128)S(1)}, f32[32,128]{1,0:T(8,128)S(1)}, u32[]{:S(2)}, u32[]{:S(2)}) collective-permute-start(f32[32,128]{1,0:T(8,128)S(1)} %get-tuple-element.26), channel_id=1, source_target_pairs={{8,0},{4,2},{2,4},{14,6},{0,8},{12,10},{10,12},{6,14},{24,16},{20,... | collective-permute-start | bytes 49160 | tf_op jit(solution)/shard_map/ppermute | solution.py:432
  8.5 2.0 %collective-permute-start.3 = (f32[24,128]{1,0:T(8,128)S(1)}, f32[24,128]{1,0:T(8,128)S(1)}, u32[]{:S(2)}, u32[]{:S(2)}) collective-permute-start(f32[24,128]{1,0:T(8,128)S(1)} %get-tuple-element.28), channel_id=1, source_target_pairs={{0,8},{8,0},{16,24},{24,16},{1,9},{9,1},{17,25},{25,17},{2,10},{10... | collective-permute-start | bytes 36872 | tf_op jit(solution)/shard_map/ppermute | solution.py:438
  11.2 5.1 %collective-permute-start.7 = (f32[2,24,128]{2,1,0:T(8,128)S(1)}, f32[2,24,128]{2,1,0:T(8,128)S(1)}, u32[]{:S(2)}, u32[]{:S(2)}) collective-permute-start(f32[2,24,128]{2,1,0:T(8,128)S(1)} %slice.7), channel_id=1, source_target_pairs={{14,0},{8,2},{10,4},{12,6},{6,8},{0,10},{2,12},{4,14},{30,16},{24,... | collective-permute-start | bytes 73736 | tf_op jit(solution)/shard_map/ppermute | solution.py:432
  14.6 7.7 %collective-permute-start.5 = (f32[16,24,128]{2,1,0:T(8,128)S(1)}, f32[16,24,128]{2,1,0:T(8,128)S(1)}, u32[]{:S(2)}, u32[]{:S(2)}) collective-permute-start(f32[16,24,128]{2,1,0:T(8,128)S(1)} %get-tuple-element.33), channel_id=1, source_target_pairs={{0,2},{2,0},{4,6},{6,4},{1,3},{3,1},{5,7},{7,5},{8,10},{10,8},{12,... | collective-permute-start | bytes 589832 | tf_op jit(solution)/shard_map/ppermute | solution.py:438
  15.3 6.9 %collective-permute-start.6 = (f32[16,24,128]{2,1,0:T(8,128)S(1)}, f32[16,24,128]{2,1,0:T(8,128)S(1)}, u32[]{:S(2)}, u32[]{:S(2)}) collective-permute-start(f32[16,24,128]{2,1,0:T(8,128)S(1)} %get-tuple-element.34), channel_id=1, source_target_pairs={{8,0},{4,2},{2,4},{14,6},{0,8},{12,10},{10,12},{6,14},{24,16},{20,... | collective-permute-start | bytes 589832 | tf_op jit(solution)/shard_map/ppermute | solution.py:432
  16.3 1.3 %collective-permute-start.8 = (f32[2,24,128]{2,1,0:T(8,128)S(1)}, f32[2,24,128]{2,1,0:T(8,128)S(1)}, u32[]{:S(2)}, u32[]{:S(2)}) collective-permute-start(f32[2,24,128]{2,1,0:T(8,128)S(1)} %slice_add_fusion), channel_id=1, source_target_pairs={{0,8},{8,0},{16,24},{24,16},{1,9},{9,1},{17,25},{25,17},{2,10},{10... | collective-permute-start | bytes 73736 | tf_op jit(solution)/shard_map/ppermute | solution.py:453
  17.7 4.9 %collective-permute-start.9 = (f32[2,24,128]{2,1,0:T(8,128)S(1)}, f32[2,24,128]{2,1,0:T(8,128)S(1)}, u32[]{:S(2)}, u32[]{:S(2)}) collective-permute-start(f32[2,24,128]{2,1,0:T(8,128)S(1)} %add.7.refs_0_), channel_id=1, source_target_pairs={{24,0},{25,1},{16,8},{17,9},{8,16},{9,17},{0,24},{1,25},{26,2},{27... | collective-permute-start | bytes 73736 | tf_op jit(solution)/shard_map/ppermute | solution.py:432
  18.1 4.5 %collective-permute-start.10 = (f32[2,24,128]{2,1,0:T(8,128)S(1)}, f32[2,24,128]{2,1,0:T(8,128)S(1)}, u32[]{:S(2)}, u32[]{:S(2)}) collective-permute-start(f32[2,24,128]{2,1,0:T(8,128)S(1)} %add.7.refs_0_), channel_id=1, source_target_pairs={{25,0},{24,1},{17,8},{16,9},{9,16},{8,17},{1,24},{0,25},{27,2},{26... | collective-permute-start | bytes 73736 | tf_op jit(solution)/shard_map/ppermute | solution.py:432
  19.4 3.5 %collective-permute-start.11 = (f32[2,24,128]{2,1,0:T(8,128)S(1)}, f32[2,24,128]{2,1,0:T(8,128)S(1)}, u32[]{:S(2)}, u32[]{:S(2)}) collective-permute-start(f32[2,24,128]{2,1,0:T(8,128)S(1)} %add.7.refs_0_), channel_id=1, source_target_pairs={{9,0},{8,1},{1,8},{0,9},{25,16},{24,17},{17,24},{16,25},{11,2},{10... | collective-permute-start | bytes 73736 | tf_op jit(solution)/shard_map/ppermute | solution.py:432

commit v14 on v13

--- a/solution.py
+++ b/solution.py
@@ -387,17 +387,18 @@
     species, row_count, _ = out.shape
     width = row_count // planes
     per_device, bins = means.shape[1:]
+    copies = []
+    for n, x in enumerate((0, planes - 1)):
+        rows_out = out.at[:, pl.ds(x * width, width)]
+        copies.append(pltpu.make_async_copy(changed.at[n], rows_out, sem.at[1 + n]))
+        copies[n].start()
     for s in range(0, per_device, 2):
         block = sum((term[s // 2] for term in terms[1:]), terms[0][s // 2])
         block = block / jnp.maximum(block[species + 1 : species + 2], 1.0)
         means[:, s, :] = block[:species, :bins]
         means[:, s + 1, :] = block[:species, bins:]
-    copies = [pltpu.make_async_copy(means, means_out, sem.at[0])]
-    for n, x in enumerate((0, planes - 1)):
-        rows_out = out.at[:, pl.ds(x * width, width)]
-        copies.append(pltpu.make_async_copy(changed.at[n], rows_out, sem.at[1 + n]))
-    for copy in copies:
-        copy.start()
+    copies.append(pltpu.make_async_copy(means, means_out, sem.at[0]))
+    copies[-1].start()
     for copy in copies:
         copy.wait()
 

time: 24 us -> 23.8 us (level)
  no operation moved by 1% of the time
where the time goes in v14:
time: 23.8 us; the launch traced here: 23.7 us
  starting transfers between devices  13.7 us (58%)
  Pallas kernels  7.66 us (32%)
  waiting for transfers between devices  1.43 us (6%)
  between operations  0.83 us (3%)
    ppermute x6, starting transfers between devices, joint(): return lax.ppermute(block, ('sec', axis), pairs)  7.18 us
    ppermute x4, starting transfers between devices, swapped(): return lax.ppermute(block, axis, [(i, i ^ 1) for i in range(count)])  5.34 us
    pallas_call x1, Pallas kernels, on_device(): call(functools.partial(inner_kernel, planes), 'inside', [struct(row_count...  2.01 us
    pallas_call x1, Pallas kernels, on_device(): call(functools.partial(pack_kernel, planes, has_b), 'faces', [struct(row_...  1.84 us
    pallas_call x1, Pallas kernels, on_device(): call(functools.partial(interior_kernel, planes), 'interior', [struct(row_...  1.35 us
    ppermute x1, waiting for transfers between devices, summed(): lax.ppermute(block, 'sec', [(i, i ^ 1) for i in range(deep)])  0.85 us
    pallas_call x1, Pallas kernels, on_device(): call(functools.partial(last_kernel, planes), 'last', [struct(species, row...  0.78 us
    ppermute x1, starting transfers between devices, swapped(): return lax.ppermute(block, axis, [*pairs, (0, count - 1), (count - 1, 0)])  0.68 us
  transfers between devices with their start and end apart: 12, of which 3 were waited for; matrix products, arithmetic and copies ran while one was open for 0% of the time, Pallas kernels for 19%

profile of v14, /device:TPU:0, one launch (start us, length us, event | category | flops | bytes accessed | tf_op | source)
XLA Modules:
  0.0 23.7 jit_solution(12379442685723383252)
XLA Ops:
  0.6 0.0 copy-start.1
  0.6 0.0 copy-start
  0.7 0.0 copy-start.3
  0.7 0.0 copy-start.2
  0.7 0.0 copy-start.4
  0.7 1.8 %faces.1 = (f32[128,24,128]{2,1,0:T(8,128)S(1)}, f32[2,24,128]{2,1,0:T(8,128)S(1)}, f32[32,128]{1,0:T(8,128)S(1)}, f32[32,128]{1,0:T(8,128)S(1)}, f32[8,24,128]{...) custom-call(f32[22,128,128]{2,1,0:T(8,128)} %bitcast.16, f32[128,128]{1,0:T(8,128)} %bitcast.9, ...), custom_call_target="tpu_custom_call" | custom-call | tf_op jit(solution)/shard_map/faces/pallas_call | solution.py:502
  2.5 3.0 %collective-permute-start.2 = (f32[8,24,128]{2,1,0:T(8,128)S(1)}, f32[8,24,128]{2,1,0:T(8,128)S(1)}, u32[]{:S(2)}, u32[]{:S(2)}) collective-permute-start(f32[8,24,128]{2,1,0:T(8,128)S(1)} %get-tuple-element.27), channel_id=1, source_target_pairs={{0,1},{1,0},{2,3},{3,2},{4,5},{5,4},{6,7},{7,6},{8,9},{9,8},{10,11... | collective-permute-start | bytes 294920 | tf_op jit(solution)/shard_map/ppermute | solution.py:439
  5.5 0.7 %collective-permute-start.4 = (f32[40,128]{1,0:T(8,128)S(1)}, f32[40,128]{1,0:T(8,128)S(1)}, u32[]{:S(2)}, u32[]{:S(2)}) collective-permute-start(f32[40,128]{1,0:T(8,128)S(1)} %get-tuple-element.29), channel_id=1, source_target_pairs={{8,16},{16,8},{0,24},{24,0},{9,17},{17,9},{1,25},{25,1},{10,18},{1... | collective-permute-start | bytes 61448 | tf_op jit(solution)/shard_map/ppermute | solution.py:442
  6.2 1.6 %collective-permute-start = (f32[32,128]{1,0:T(8,128)S(1)}, f32[32,128]{1,0:T(8,128)S(1)}, u32[]{:S(2)}, u32[]{:S(2)}) collective-permute-start(f32[32,128]{1,0:T(8,128)S(1)} %get-tuple-element.25), channel_id=1, source_target_pairs={{0,2},{2,0},{4,6},{6,4},{1,3},{3,1},{5,7},{7,5},{8,10},{10,8},{12,... | collective-permute-start | bytes 49160 | tf_op jit(solution)/shard_map/ppermute | solution.py:439
  7.8 0.7 %collective-permute-start.1 = (f32[32,128]{1,0:T(8,128)S(1)}, f32[32,128]{1,0:T(8,128)S(1)}, u32[]{:S(2)}, u32[]{:S(2)}) collective-permute-start(f32[32,128]{1,0:T(8,128)S(1)} %get-tuple-element.26), channel_id=1, source_target_pairs={{8,0},{4,2},{2,4},{14,6},{0,8},{12,10},{10,12},{6,14},{24,16},{20,... | collective-permute-start | bytes 49160 | tf_op jit(solution)/shard_map/ppermute | solution.py:433
  8.5 0.0 collective-permute-start.3
  8.5 0.0 copy-done.1
  8.5 0.0 copy-done
  8.5 0.0 copy-done.3
  8.5 2.0 %inside.1 = (f32[128,24,128]{2,1,0:T(8,128)S(1)}, f32[5,24,64]{2,1,0:T(8,128)S(1)}, f32[5,24,64]{2,1,0:T(8,128)S(1)}) custom-call(f32[128,24,128]{2,1,0:T(8,128)S(1)} %get-tuple-element.20.cells, f32[128,128]{1,0:T(8,128)S(1)} %bitcast.10, f32[128,128]{1,0:T(8,128)S(1)} %bitcast.7, f32[1,22]{1,0:T(1,128)S(1)} %bitcast.11), custom_call_target="tpu_custom_call" | custom-call | flops 10000000 | bytes 4000000 | tf_op jit(solution)/shard_map/inside/pallas_call | solution.py:521
  10.5 0.0 collective-permute-done.3.refs_3_
  10.5 0.0 collective-permute-done.refs_0_
  10.5 0.0 collective-permute-done.1.refs_1_
  10.5 0.0 collective-permute-done.4.refs_4_
  10.6 0.0 collective-permute-done.2.refs_2_.refs_0_
  10.6 0.0 copy-done.2
  10.6 0.0 copy-done.4
  10.6 0.6 %edges.1 = (f32[4,24,128]{2,1,0:T(8,128)S(1)}, f32[2,24,128]{2,1,0:T(8,128)S(1)}) custom-call(f32[128,24,128]{2,1,0:T(8,128)S(1)} %get-tuple-element.20.cells, f32[2,24,128]{2,1,0:T(8,128)S(1)} %get-tuple-element.22.own_z, f32[5,24,64]{2,1,0:T(8,128)S(1)} %get-tuple-element.23.sums, f32[5,24,64]{2,1,0:T(8,128)S(1)} %get-tuple-element.24.heated_sums, ...), custom_call_target="tpu_custom_call" | custom-call | tf_op jit(solution)/shard_map/edges/pallas_call | solution.py:539
  11.2 2.6 %collective-permute-start.7 = (f32[2,24,128]{2,1,0:T(8,128)S(1)}, f32[2,24,128]{2,1,0:T(8,128)S(1)}, u32[]{:S(2)}, u32[]{:S(2)}) collective-permute-start(f32[2,24,128]{2,1,0:T(8,128)S(1)} %slice.7), channel_id=1, source_target_pairs={{14,0},{8,2},{10,4},{12,6},{6,8},{0,10},{2,12},{4,14},{30,16},{24,... | collective-permute-start | bytes 73736 | tf_op jit(solution)/shard_map/ppermute | solution.py:433
  13.9 0.6 %kinetics.1.advanced.held = f32[128,24,128]{2,1,0:T(8,128)S(1)} custom-call(f32[128,24,128]{2,1,0:T(8,128)S(1)} %get-tuple-element.20.cells, f32[128,24,128]{2,1,0:T(8,128)S(1)} %get-tuple-element.21.diffused, f32[128,128]{1,0:T(8,128)S(1)} %bitcast.8, f32[22,22]{1,0:T(8,128)S(1)} %copy-done.2, f32[4,24,128]{2,1,0:T(8,128)S(1)} %get-tuple-element.30.held), custom_call_target="tpu_custom_call" | custom-call | tf_op jit(solution)/shard_map/kinetics/pallas_call | solution.py:548
  14.6 0.8 %collective-permute-start.5 = (f32[16,24,128]{2,1,0:T(8,128)S(1)}, f32[16,24,128]{2,1,0:T(8,128)S(1)}, u32[]{:S(2)}, u32[]{:S(2)}) collective-permute-start(f32[16,24,128]{2,1,0:T(8,128)S(1)} %get-tuple-element.33), channel_id=1, source_target_pairs={{0,2},{2,0},{4,6},{6,4},{1,3},{3,1},{5,7},{7,5},{8,10},{10,8},{12,... | collective-permute-start | bytes 589832 | tf_op jit(solution)/shard_map/ppermute | solution.py:439
  15.3 0.7 %collective-permute-start.6 = (f32[16,24,128]{2,1,0:T(8,128)S(1)}, f32[16,24,128]{2,1,0:T(8,128)S(1)}, u32[]{:S(2)}, u32[]{:S(2)}) collective-permute-start(f32[16,24,128]{2,1,0:T(8,128)S(1)} %get-tuple-element.34), channel_id=1, source_target_pairs={{8,0},{4,2},{2,4},{14,6},{0,8},{12,10},{10,12},{6,14},{24,16},{20,... | collective-permute-start | bytes 589832 | tf_op jit(solution)/shard_map/ppermute | solution.py:433
  16.0 0.3 %collective-permute-done.7 = f32[2,24,128]{2,1,0:T(8,128)S(1)} collective-permute-done((f32[2,24,128]{2,1,0:T(8,128)S(1)}, f32[2,24,128]{2,1,0:T(8,128)S(1)}, u32[]{:S(2)}, u32[]{:S(2)}) %collective-permute-start.7) | collective-permute-done | bytes 24608 | tf_op jit(solution)/shard_map/ppermute | solution.py:433
  16.3 0.5 %collective-permute-start.8 = (f32[2,24,128]{2,1,0:T(8,128)S(1)}, f32[2,24,128]{2,1,0:T(8,128)S(1)}, u32[]{:S(2)}, u32[]{:S(2)}) collective-permute-start(f32[2,24,128]{2,1,0:T(8,128)S(1)} %slice_add_fusion), channel_id=1, source_target_pairs={{0,8},{8,0},{16,24},{24,16},{1,9},{9,1},{17,25},{25,17},{2,10},{10... | collective-permute-start | bytes 73736 | tf_op jit(solution)/shard_map/ppermute | solution.py:454
  16.8 0.8 %collective-permute-done.8 = f32[2,24,128]{2,1,0:T(8,128)S(1)} collective-permute-done((f32[2,24,128]{2,1,0:T(8,128)S(1)}, f32[2,24,128]{2,1,0:T(8,128)S(1)}, u32[]{:S(2)}, u32[]{:S(2)}) %collective-permute-start.8) | collective-permute-done | bytes 24608 | tf_op jit(solution)/shard_map/ppermute | solution.py:454
  17.7 0.5 %collective-permute-start.9 = (f32[2,24,128]{2,1,0:T(8,128)S(1)}, f32[2,24,128]{2,1,0:T(8,128)S(1)}, u32[]{:S(2)}, u32[]{:S(2)}) collective-permute-start(f32[2,24,128]{2,1,0:T(8,128)S(1)} %add.7.refs_0_), channel_id=1, source_target_pairs={{24,0},{25,1},{16,8},{17,9},{8,16},{9,17},{0,24},{1,25},{26,2},{27... | collective-permute-start | bytes 73736 | tf_op jit(solution)/shard_map/ppermute | solution.py:433
  18.1 1.3 %collective-permute-start.10 = (f32[2,24,128]{2,1,0:T(8,128)S(1)}, f32[2,24,128]{2,1,0:T(8,128)S(1)}, u32[]{:S(2)}, u32[]{:S(2)}) collective-permute-start(f32[2,24,128]{2,1,0:T(8,128)S(1)} %add.7.refs_0_), channel_id=1, source_target_pairs={{25,0},{24,1},{17,8},{16,9},{9,16},{8,17},{1,24},{0,25},{27,2},{26... | collective-permute-start | bytes 73736 | tf_op jit(solution)/shard_map/ppermute | solution.py:433
  19.4 1.4 %collective-permute-start.11 = (f32[2,24,128]{2,1,0:T(8,128)S(1)}, f32[2,24,128]{2,1,0:T(8,128)S(1)}, u32[]{:S(2)}, u32[]{:S(2)}) collective-permute-start(f32[2,24,128]{2,1,0:T(8,128)S(1)} %add.7.refs_0_), channel_id=1, source_target_pairs={{9,0},{8,1},{1,8},{0,9},{25,16},{24,17},{17,24},{16,25},{11,2},{10... | collective-permute-start | bytes 73736 | tf_op jit(solution)/shard_map/ppermute | solution.py:433
  20.8 1.4 %interior.1 = (f32[128,24,128]{2,1,0:T(8,128)S(1)}, f32[22,128,128]{2,1,0:T(8,128)}) custom-call(f32[128,24,128]{2,1,0:T(8,128)S(1)} %get-tuple-element.20.cells, f32[128,24,128]{2,1,0:T(8,128)S(1)} %kinetics.1.advanced.held, f32[2,24,128]{2,1,0:T(8,128)S(1)} %get-tuple-element.31.dz, f32[1,22]{1,0:T(1,128)S(1)} %bitcast.13, ...), custom_call_target="tpu_custom_call" | custom-call | flops 1000000 | bytes 3000000 | tf_op jit(solution)/shard_map/interior/pallas_call | solution.py:573
  22.2 0.0 collective-permute-done.5.refs_0_
  22.2 0.0 collective-permute-done.6.refs_1_
  22.2 0.4 %outer_rows.1.changed = f32[2,22,16,128]{3,2,1,0:T(8,128)S(1)} custom-call(f32[128,24,128]{2,1,0:T(8,128)S(1)} %get-tuple-element.20.cells, f32[128,24,128]{2,1,0:T(8,128)S(1)} %get-tuple-element.32.total, f32[1,22]{1,0:T(1,128)S(1)} %bitcast.14, f32[16,24,128]{2,1,0:T(8,128)S(1)} %collective-permute-done.5.refs_0_, ...), custom_call_target="tpu_custom_call" | custom-call | tf_op jit(solution)/shard_map/outer_rows/pallas_call | solution.py:583
  22.6 0.0 collective-permute-done.9.refs_1_
  22.6 0.0 collective-permute-done.10.refs_2_
  22.6 0.3 %collective-permute-done.11.refs_3_ = f32[2,24,128]{2,1,0:T(8,128)S(1)} collective-permute-done((f32[2,24,128]{2,1,0:T(8,128)S(1)}, f32[2,24,128]{2,1,0:T(8,128)S(1)}, u32[]{:S(2)}, u32[]{:S(2)}) %collective-permute-start.11) | collective-permute-done | bytes 24608 | tf_op jit(solution)/shard_map/ppermute | solution.py:433
  22.9 0.8 %last.1 = (f32[22,128,128]{2,1,0:T(8,128)}, f32[22,4,64]{2,1,0:T(4,128)}) custom-call(f32[2,22,16,128]{3,2,1,0:T(8,128)S(1)} %outer_rows.1.changed, f32[22,128,128]{2,1,0:T(8,128)} %get-tuple-element.35.first_out, f32[2,24,128]{2,1,0:T(8,128)S(1)} %add.7.refs_0_, f32[2,24,128]{2,1,0:T(8,128)S(1)} %collective-permute-done.9.refs_1_, ...), custom_call_target="tpu_custom_call", output_to_operand_aliasing={{0}: (1, {})} | custom-call | tf_op jit(solution)/shard_map/last/pallas_call | solution.py:590
  (4 shorter events, 0.1 us)
Async XLA Ops:
  0.6 7.8 %copy-start.1 = (f32[8,16,128]{2,1,0:T(8,128)S(1)}, f32[8,16,128]{2,1,0:T(8,128)}, u32[]{:S(2)}) copy-start(f32[8,16,128]{2,1,0:T(8,128)} %param.8) | copy-start | bytes 196612
  0.6 7.8 %copy-start = (f32[8,16,128]{2,1,0:T(8,128)S(1)}, f32[8,16,128]{2,1,0:T(8,128)}, u32[]{:S(2)}) copy-start(f32[8,16,128]{2,1,0:T(8,128)} %param.9) | copy-start | bytes 196612
  0.7 7.8 %copy-start.3 = (f32[22]{0:T(128)S(1)}, f32[22]{0:T(128)}, u32[]{:S(2)}) copy-start(f32[22]{0:T(128)} %param.10) | copy-start | bytes 268
  0.7 9.9 %copy-start.2 = (f32[22,22]{1,0:T(8,128)S(1)}, f32[22,22]{1,0:T(8,128)}, u32[]{:S(2)}) copy-start(f32[22,22]{1,0:T(8,128)} %jacobian.3) | copy-start | bytes 5812
  0.7 9.9 %copy-start.4 = (s32[32]{0:T(128)S(1)}, s32[32]{0:T(128)}, u32[]{:S(2)}) copy-start(s32[32]{0:T(128)} %param.13) | copy-start | bytes 388
  2.5 8.0 %collective-permute-start.2 = (f32[8,24,128]{2,1,0:T(8,128)S(1)}, f32[8,24,128]{2,1,0:T(8,128)S(1)}, u32[]{:S(2)}, u32[]{:S(2)}) collective-permute-start(f32[8,24,128]{2,1,0:T(8,128)S(1)} %get-tuple-element.27), channel_id=1, source_target_pairs={{0,1},{1,0},{2,3},{3,2},{4,5},{5,4},{6,7},{7,6},{8,9},{9,8},{10,11... | collective-permute-start | bytes 294920 | tf_op jit(solution)/shard_map/ppermute | solution.py:439
  5.5 5.0 %collective-permute-start.4 = (f32[40,128]{1,0:T(8,128)S(1)}, f32[40,128]{1,0:T(8,128)S(1)}, u32[]{:S(2)}, u32[]{:S(2)}) collective-permute-start(f32[40,128]{1,0:T(8,128)S(1)} %get-tuple-element.29), channel_id=1, source_target_pairs={{8,16},{16,8},{0,24},{24,0},{9,17},{17,9},{1,25},{25,1},{10,18},{1... | collective-permute-start | bytes 61448 | tf_op jit(solution)/shard_map/ppermute | solution.py:442
  6.2 4.3 %collective-permute-start = (f32[32,128]{1,0:T(8,128)S(1)}, f32[32,128]{1,0:T(8,128)S(1)}, u32[]{:S(2)}, u32[]{:S(2)}) collective-permute-start(f32[32,128]{1,0:T(8,128)S(1)} %get-tuple-element.25), channel_id=1, source_target_pairs={{0,2},{2,0},{4,6},{6,4},{1,3},{3,1},{5,7},{7,5},{8,10},{10,8},{12,... | collective-permute-start | bytes 49160 | tf_op jit(solution)/shard_map/ppermute | solution.py:439
  7.8 2.7 %collective-permute-start.1 = (f32[32,128]{1,0:T(8,128)S(1)}, f32[32,128]{1,0:T(8,128)S(1)}, u32[]{:S(2)}, u32[]{:S(2)}) collective-permute-start(f32[32,128]{1,0:T(8,128)S(1)} %get-tuple-element.26), channel_id=1, source_target_pairs={{8,0},{4,2},{2,4},{14,6},{0,8},{12,10},{10,12},{6,14},{24,16},{20,... | collective-permute-start | bytes 49160 | tf_op jit(solution)/shard_map/ppermute | solution.py:433
  8.5 2.0 %collective-permute-start.3 = (f32[24,128]{1,0:T(8,128)S(1)}, f32[24,128]{1,0:T(8,128)S(1)}, u32[]{:S(2)}, u32[]{:S(2)}) collective-permute-start(f32[24,128]{1,0:T(8,128)S(1)} %get-tuple-element.28), channel_id=1, source_target_pairs={{0,8},{8,0},{16,24},{24,16},{1,9},{9,1},{17,25},{25,17},{2,10},{10... | collective-permute-start | bytes 36872 | tf_op jit(solution)/shard_map/ppermute | solution.py:439
  11.2 5.1 %collective-permute-start.7 = (f32[2,24,128]{2,1,0:T(8,128)S(1)}, f32[2,24,128]{2,1,0:T(8,128)S(1)}, u32[]{:S(2)}, u32[]{:S(2)}) collective-permute-start(f32[2,24,128]{2,1,0:T(8,128)S(1)} %slice.7), channel_id=1, source_target_pairs={{14,0},{8,2},{10,4},{12,6},{6,8},{0,10},{2,12},{4,14},{30,16},{24,... | collective-permute-start | bytes 73736 | tf_op jit(solution)/shard_map/ppermute | solution.py:433
  14.6 7.7 %collective-permute-start.5 = (f32[16,24,128]{2,1,0:T(8,128)S(1)}, f32[16,24,128]{2,1,0:T(8,128)S(1)}, u32[]{:S(2)}, u32[]{:S(2)}) collective-permute-start(f32[16,24,128]{2,1,0:T(8,128)S(1)} %get-tuple-element.33), channel_id=1, source_target_pairs={{0,2},{2,0},{4,6},{6,4},{1,3},{3,1},{5,7},{7,5},{8,10},{10,8},{12,... | collective-permute-start | bytes 589832 | tf_op jit(solution)/shard_map/ppermute | solution.py:439
  15.3 6.9 %collective-permute-start.6 = (f32[16,24,128]{2,1,0:T(8,128)S(1)}, f32[16,24,128]{2,1,0:T(8,128)S(1)}, u32[]{:S(2)}, u32[]{:S(2)}) collective-permute-start(f32[16,24,128]{2,1,0:T(8,128)S(1)} %get-tuple-element.34), channel_id=1, source_target_pairs={{8,0},{4,2},{2,4},{14,6},{0,8},{12,10},{10,12},{6,14},{24,16},{20,... | collective-permute-start | bytes 589832 | tf_op jit(solution)/shard_map/ppermute | solution.py:433
  16.3 1.3 %collective-permute-start.8 = (f32[2,24,128]{2,1,0:T(8,128)S(1)}, f32[2,24,128]{2,1,0:T(8,128)S(1)}, u32[]{:S(2)}, u32[]{:S(2)}) collective-permute-start(f32[2,24,128]{2,1,0:T(8,128)S(1)} %slice_add_fusion), channel_id=1, source_target_pairs={{0,8},{8,0},{16,24},{24,16},{1,9},{9,1},{17,25},{25,17},{2,10},{10... | collective-permute-start | bytes 73736 | tf_op jit(solution)/shard_map/ppermute | solution.py:454
  17.7 4.9 %collective-permute-start.9 = (f32[2,24,128]{2,1,0:T(8,128)S(1)}, f32[2,24,128]{2,1,0:T(8,128)S(1)}, u32[]{:S(2)}, u32[]{:S(2)}) collective-permute-start(f32[2,24,128]{2,1,0:T(8,128)S(1)} %add.7.refs_0_), channel_id=1, source_target_pairs={{24,0},{25,1},{16,8},{17,9},{8,16},{9,17},{0,24},{1,25},{26,2},{27... | collective-permute-start | bytes 73736 | tf_op jit(solution)/shard_map/ppermute | solution.py:433
  18.1 4.5 %collective-permute-start.10 = (f32[2,24,128]{2,1,0:T(8,128)S(1)}, f32[2,24,128]{2,1,0:T(8,128)S(1)}, u32[]{:S(2)}, u32[]{:S(2)}) collective-permute-start(f32[2,24,128]{2,1,0:T(8,128)S(1)} %add.7.refs_0_), channel_id=1, source_target_pairs={{25,0},{24,1},{17,8},{16,9},{9,16},{8,17},{1,24},{0,25},{27,2},{26... | collective-permute-start | bytes 73736 | tf_op jit(solution)/shard_map/ppermute | solution.py:433
  19.4 3.5 %collective-permute-start.11 = (f32[2,24,128]{2,1,0:T(8,128)S(1)}, f32[2,24,128]{2,1,0:T(8,128)S(1)}, u32[]{:S(2)}, u32[]{:S(2)}) collective-permute-start(f32[2,24,128]{2,1,0:T(8,128)S(1)} %add.7.refs_0_), channel_id=1, source_target_pairs={{9,0},{8,1},{1,8},{0,9},{25,16},{24,17},{17,24},{16,25},{11,2},{10... | collective-permute-start | bytes 73736 | tf_op jit(solution)/shard_map/ppermute | solution.py:433

commit v15 on v14

--- a/solution.py
+++ b/solution.py
@@ -305,9 +305,10 @@
         delta = weight * d * (halo - c)
         dz[int(upper)] = delta
         value = halves(delta)
+        hit = hits(c[species + 1 : species + 2])
         for j in range(stations):
             values[j].append(value)
-            found[j].append(hits(jnp.where(station == j, c[species + 1 : species + 2], -1.0)))
+            found[j].append(hit * (station == j).astype(F32).astype(BF16))
 
     left = stacked_square(jacobian, square)
     station_sums = [

time: 23.8 us -> 23.9 us (level)
  no operation moved by 1% of the time
where the time goes in v15:
time: 23.9 us; the launch traced here: 23.7 us
  starting transfers between devices  13.7 us (57%)
  Pallas kernels  7.68 us (32%)
  waiting for transfers between devices  1.46 us (6%)
  between operations  0.83 us (3%)
    ppermute x6, starting transfers between devices, joint(): return lax.ppermute(block, ('sec', axis), pairs)  7.18 us
    ppermute x4, starting transfers between devices, swapped(): return lax.ppermute(block, axis, [(i, i ^ 1) for i in range(count)])  5.32 us
    pallas_call x1, Pallas kernels, on_device(): call(functools.partial(inner_kernel, planes), 'inside', [struct(row_count...  2.01 us
    pallas_call x1, Pallas kernels, on_device(): call(functools.partial(pack_kernel, planes, has_b), 'faces', [struct(row_...  1.84 us
    pallas_call x1, Pallas kernels, on_device(): call(functools.partial(interior_kernel, planes), 'interior', [struct(row_...  1.35 us
    ppermute x1, waiting for transfers between devices, summed(): lax.ppermute(block, 'sec', [(i, i ^ 1) for i in range(deep)])  0.85 us
    pallas_call x1, Pallas kernels, on_device(): call(functools.partial(last_kernel, planes), 'last', [struct(species, row...  0.78 us
    ppermute x1, starting transfers between devices, swapped(): return lax.ppermute(block, axis, [*pairs, (0, count - 1), (count - 1, 0)])  0.68 us
  transfers between devices with their start and end apart: 12, of which 3 were waited for; matrix products, arithmetic and copies ran while one was open for 0% of the time, Pallas kernels for 19%

profile of v15, /device:TPU:0, one launch (start us, length us, event | category | flops | bytes accessed | tf_op | source)
XLA Modules:
  0.0 23.7 jit_solution(11862695781302105953)
XLA Ops:
  0.6 0.0 copy-start.1
  0.6 0.0 copy-start
  0.7 0.0 copy-start.3
  0.7 0.0 copy-start.2
  0.7 0.0 copy-start.4
  0.7 1.8 %faces.1 = (f32[128,24,128]{2,1,0:T(8,128)S(1)}, f32[2,24,128]{2,1,0:T(8,128)S(1)}, f32[32,128]{1,0:T(8,128)S(1)}, f32[32,128]{1,0:T(8,128)S(1)}, f32[8,24,128]{...) custom-call(f32[22,128,128]{2,1,0:T(8,128)} %bitcast.16, f32[128,128]{1,0:T(8,128)} %bitcast.9, ...), custom_call_target="tpu_custom_call" | custom-call | tf_op jit(solution)/shard_map/faces/pallas_call | solution.py:503
  2.5 3.0 %collective-permute-start.2 = (f32[8,24,128]{2,1,0:T(8,128)S(1)}, f32[8,24,128]{2,1,0:T(8,128)S(1)}, u32[]{:S(2)}, u32[]{:S(2)}) collective-permute-start(f32[8,24,128]{2,1,0:T(8,128)S(1)} %get-tuple-element.27), channel_id=1, source_target_pairs={{0,1},{1,0},{2,3},{3,2},{4,5},{5,4},{6,7},{7,6},{8,9},{9,8},{10,11... | collective-permute-start | bytes 294920 | tf_op jit(solution)/shard_map/ppermute | solution.py:440
  5.5 0.7 %collective-permute-start.4 = (f32[40,128]{1,0:T(8,128)S(1)}, f32[40,128]{1,0:T(8,128)S(1)}, u32[]{:S(2)}, u32[]{:S(2)}) collective-permute-start(f32[40,128]{1,0:T(8,128)S(1)} %get-tuple-element.29), channel_id=1, source_target_pairs={{8,16},{16,8},{0,24},{24,0},{9,17},{17,9},{1,25},{25,1},{10,18},{1... | collective-permute-start | bytes 61448 | tf_op jit(solution)/shard_map/ppermute | solution.py:443
  6.2 1.6 %collective-permute-start = (f32[32,128]{1,0:T(8,128)S(1)}, f32[32,128]{1,0:T(8,128)S(1)}, u32[]{:S(2)}, u32[]{:S(2)}) collective-permute-start(f32[32,128]{1,0:T(8,128)S(1)} %get-tuple-element.25), channel_id=1, source_target_pairs={{0,2},{2,0},{4,6},{6,4},{1,3},{3,1},{5,7},{7,5},{8,10},{10,8},{12,... | collective-permute-start | bytes 49160 | tf_op jit(solution)/shard_map/ppermute | solution.py:440
  7.8 0.7 %collective-permute-start.1 = (f32[32,128]{1,0:T(8,128)S(1)}, f32[32,128]{1,0:T(8,128)S(1)}, u32[]{:S(2)}, u32[]{:S(2)}) collective-permute-start(f32[32,128]{1,0:T(8,128)S(1)} %get-tuple-element.26), channel_id=1, source_target_pairs={{8,0},{4,2},{2,4},{14,6},{0,8},{12,10},{10,12},{6,14},{24,16},{20,... | collective-permute-start | bytes 49160 | tf_op jit(solution)/shard_map/ppermute | solution.py:434
  8.5 0.0 collective-permute-start.3
  8.5 0.0 copy-done.1
  8.5 0.0 copy-done
  8.5 0.0 copy-done.3
  8.5 2.0 %inside.1 = (f32[128,24,128]{2,1,0:T(8,128)S(1)}, f32[5,24,64]{2,1,0:T(8,128)S(1)}, f32[5,24,64]{2,1,0:T(8,128)S(1)}) custom-call(f32[128,24,128]{2,1,0:T(8,128)S(1)} %get-tuple-element.20.cells, f32[128,128]{1,0:T(8,128)S(1)} %bitcast.10, f32[128,128]{1,0:T(8,128)S(1)} %bitcast.7, f32[1,22]{1,0:T(1,128)S(1)} %bitcast.11), custom_call_target="tpu_custom_call" | custom-call | flops 10000000 | bytes 4000000 | tf_op jit(solution)/shard_map/inside/pallas_call | solution.py:522
  10.5 0.0 collective-permute-done.3.refs_3_
  10.5 0.0 collective-permute-done.refs_0_
  10.5 0.0 collective-permute-done.1.refs_1_
  10.5 0.0 collective-permute-done.4.refs_4_
  10.6 0.0 collective-permute-done.2.refs_2_.refs_0_
  10.6 0.0 copy-done.2
  10.6 0.0 copy-done.4
  10.6 0.6 %edges.1 = (f32[4,24,128]{2,1,0:T(8,128)S(1)}, f32[2,24,128]{2,1,0:T(8,128)S(1)}) custom-call(f32[128,24,128]{2,1,0:T(8,128)S(1)} %get-tuple-element.20.cells, f32[2,24,128]{2,1,0:T(8,128)S(1)} %get-tuple-element.22.own_z, f32[5,24,64]{2,1,0:T(8,128)S(1)} %get-tuple-element.23.sums, f32[5,24,64]{2,1,0:T(8,128)S(1)} %get-tuple-element.24.heated_sums, ...), custom_call_target="tpu_custom_call" | custom-call | tf_op jit(solution)/shard_map/edges/pallas_call | solution.py:540
  11.2 2.6 %collective-permute-start.7 = (f32[2,24,128]{2,1,0:T(8,128)S(1)}, f32[2,24,128]{2,1,0:T(8,128)S(1)}, u32[]{:S(2)}, u32[]{:S(2)}) collective-permute-start(f32[2,24,128]{2,1,0:T(8,128)S(1)} %slice.7), channel_id=1, source_target_pairs={{14,0},{8,2},{10,4},{12,6},{6,8},{0,10},{2,12},{4,14},{30,16},{24,... | collective-permute-start | bytes 73736 | tf_op jit(solution)/shard_map/ppermute | solution.py:434
  13.9 0.6 %kinetics.1.advanced.held = f32[128,24,128]{2,1,0:T(8,128)S(1)} custom-call(f32[128,24,128]{2,1,0:T(8,128)S(1)} %get-tuple-element.20.cells, f32[128,24,128]{2,1,0:T(8,128)S(1)} %get-tuple-element.21.diffused, f32[128,128]{1,0:T(8,128)S(1)} %bitcast.8, f32[22,22]{1,0:T(8,128)S(1)} %copy-done.2, f32[4,24,128]{2,1,0:T(8,128)S(1)} %get-tuple-element.30.held), custom_call_target="tpu_custom_call" | custom-call | tf_op jit(solution)/shard_map/kinetics/pallas_call | solution.py:549
  14.6 0.7 %collective-permute-start.5 = (f32[16,24,128]{2,1,0:T(8,128)S(1)}, f32[16,24,128]{2,1,0:T(8,128)S(1)}, u32[]{:S(2)}, u32[]{:S(2)}) collective-permute-start(f32[16,24,128]{2,1,0:T(8,128)S(1)} %get-tuple-element.33), channel_id=1, source_target_pairs={{0,2},{2,0},{4,6},{6,4},{1,3},{3,1},{5,7},{7,5},{8,10},{10,8},{12,... | collective-permute-start | bytes 589832 | tf_op jit(solution)/shard_map/ppermute | solution.py:440
  15.3 0.7 %collective-permute-start.6 = (f32[16,24,128]{2,1,0:T(8,128)S(1)}, f32[16,24,128]{2,1,0:T(8,128)S(1)}, u32[]{:S(2)}, u32[]{:S(2)}) collective-permute-start(f32[16,24,128]{2,1,0:T(8,128)S(1)} %get-tuple-element.34), channel_id=1, source_target_pairs={{8,0},{4,2},{2,4},{14,6},{0,8},{12,10},{10,12},{6,14},{24,16},{20,... | collective-permute-start | bytes 589832 | tf_op jit(solution)/shard_map/ppermute | solution.py:434
  16.0 0.3 %collective-permute-done.7 = f32[2,24,128]{2,1,0:T(8,128)S(1)} collective-permute-done((f32[2,24,128]{2,1,0:T(8,128)S(1)}, f32[2,24,128]{2,1,0:T(8,128)S(1)}, u32[]{:S(2)}, u32[]{:S(2)}) %collective-permute-start.7) | collective-permute-done | bytes 24608 | tf_op jit(solution)/shard_map/ppermute | solution.py:434
  16.3 0.5 %collective-permute-start.8 = (f32[2,24,128]{2,1,0:T(8,128)S(1)}, f32[2,24,128]{2,1,0:T(8,128)S(1)}, u32[]{:S(2)}, u32[]{:S(2)}) collective-permute-start(f32[2,24,128]{2,1,0:T(8,128)S(1)} %slice_add_fusion), channel_id=1, source_target_pairs={{0,8},{8,0},{16,24},{24,16},{1,9},{9,1},{17,25},{25,17},{2,10},{10... | collective-permute-start | bytes 73736 | tf_op jit(solution)/shard_map/ppermute | solution.py:455
  16.8 0.8 %collective-permute-done.8 = f32[2,24,128]{2,1,0:T(8,128)S(1)} collective-permute-done((f32[2,24,128]{2,1,0:T(8,128)S(1)}, f32[2,24,128]{2,1,0:T(8,128)S(1)}, u32[]{:S(2)}, u32[]{:S(2)}) %collective-permute-start.8) | collective-permute-done | bytes 24608 | tf_op jit(solution)/shard_map/ppermute | solution.py:455
  17.7 0.4 %collective-permute-start.9 = (f32[2,24,128]{2,1,0:T(8,128)S(1)}, f32[2,24,128]{2,1,0:T(8,128)S(1)}, u32[]{:S(2)}, u32[]{:S(2)}) collective-permute-start(f32[2,24,128]{2,1,0:T(8,128)S(1)} %add.7.refs_0_), channel_id=1, source_target_pairs={{24,0},{25,1},{16,8},{17,9},{8,16},{9,17},{0,24},{1,25},{26,2},{27... | collective-permute-start | bytes 73736 | tf_op jit(solution)/shard_map/ppermute | solution.py:434
  18.1 1.3 %collective-permute-start.10 = (f32[2,24,128]{2,1,0:T(8,128)S(1)}, f32[2,24,128]{2,1,0:T(8,128)S(1)}, u32[]{:S(2)}, u32[]{:S(2)}) collective-permute-start(f32[2,24,128]{2,1,0:T(8,128)S(1)} %add.7.refs_0_), channel_id=1, source_target_pairs={{25,0},{24,1},{17,8},{16,9},{9,16},{8,17},{1,24},{0,25},{27,2},{26... | collective-permute-start | bytes 73736 | tf_op jit(solution)/shard_map/ppermute | solution.py:434
  19.4 1.4 %collective-permute-start.11 = (f32[2,24,128]{2,1,0:T(8,128)S(1)}, f32[2,24,128]{2,1,0:T(8,128)S(1)}, u32[]{:S(2)}, u32[]{:S(2)}) collective-permute-start(f32[2,24,128]{2,1,0:T(8,128)S(1)} %add.7.refs_0_), channel_id=1, source_target_pairs={{9,0},{8,1},{1,8},{0,9},{25,16},{24,17},{17,24},{16,25},{11,2},{10... | collective-permute-start | bytes 73736 | tf_op jit(solution)/shard_map/ppermute | solution.py:434
  20.9 1.4 %interior.1 = (f32[128,24,128]{2,1,0:T(8,128)S(1)}, f32[22,128,128]{2,1,0:T(8,128)}) custom-call(f32[128,24,128]{2,1,0:T(8,128)S(1)} %get-tuple-element.20.cells, f32[128,24,128]{2,1,0:T(8,128)S(1)} %kinetics.1.advanced.held, f32[2,24,128]{2,1,0:T(8,128)S(1)} %get-tuple-element.31.dz, f32[1,22]{1,0:T(1,128)S(1)} %bitcast.13, ...), custom_call_target="tpu_custom_call" | custom-call | flops 1000000 | bytes 3000000 | tf_op jit(solution)/shard_map/interior/pallas_call | solution.py:574
  22.2 0.0 collective-permute-done.5.refs_0_
  22.2 0.0 collective-permute-done.6.refs_1_
  22.2 0.4 %outer_rows.1.changed = f32[2,22,16,128]{3,2,1,0:T(8,128)S(1)} custom-call(f32[128,24,128]{2,1,0:T(8,128)S(1)} %get-tuple-element.20.cells, f32[128,24,128]{2,1,0:T(8,128)S(1)} %get-tuple-element.32.total, f32[1,22]{1,0:T(1,128)S(1)} %bitcast.14, f32[16,24,128]{2,1,0:T(8,128)S(1)} %collective-permute-done.5.refs_0_, ...), custom_call_target="tpu_custom_call" | custom-call | tf_op jit(solution)/shard_map/outer_rows/pallas_call | solution.py:584
  22.6 0.0 collective-permute-done.9.refs_1_
  22.6 0.0 collective-permute-done.10.refs_2_
  22.6 0.3 %collective-permute-done.11.refs_3_ = f32[2,24,128]{2,1,0:T(8,128)S(1)} collective-permute-done((f32[2,24,128]{2,1,0:T(8,128)S(1)}, f32[2,24,128]{2,1,0:T(8,128)S(1)}, u32[]{:S(2)}, u32[]{:S(2)}) %collective-permute-start.11) | collective-permute-done | bytes 24608 | tf_op jit(solution)/shard_map/ppermute | solution.py:434
  22.9 0.8 %last.1 = (f32[22,128,128]{2,1,0:T(8,128)}, f32[22,4,64]{2,1,0:T(4,128)}) custom-call(f32[2,22,16,128]{3,2,1,0:T(8,128)S(1)} %outer_rows.1.changed, f32[22,128,128]{2,1,0:T(8,128)} %get-tuple-element.35.first_out, f32[2,24,128]{2,1,0:T(8,128)S(1)} %add.7.refs_0_, f32[2,24,128]{2,1,0:T(8,128)S(1)} %collective-permute-done.9.refs_1_, ...), custom_call_target="tpu_custom_call", output_to_operand_aliasing={{0}: (1, {})} | custom-call | tf_op jit(solution)/shard_map/last/pallas_call | solution.py:591
  (4 shorter events, 0.1 us)
Async XLA Ops:
  0.6 7.8 %copy-start.1 = (f32[8,16,128]{2,1,0:T(8,128)S(1)}, f32[8,16,128]{2,1,0:T(8,128)}, u32[]{:S(2)}) copy-start(f32[8,16,128]{2,1,0:T(8,128)} %param.8) | copy-start | bytes 196612
  0.6 7.8 %copy-start = (f32[8,16,128]{2,1,0:T(8,128)S(1)}, f32[8,16,128]{2,1,0:T(8,128)}, u32[]{:S(2)}) copy-start(f32[8,16,128]{2,1,0:T(8,128)} %param.9) | copy-start | bytes 196612
  0.7 7.8 %copy-start.3 = (f32[22]{0:T(128)S(1)}, f32[22]{0:T(128)}, u32[]{:S(2)}) copy-start(f32[22]{0:T(128)} %param.10) | copy-start | bytes 268
  0.7 9.9 %copy-start.2 = (f32[22,22]{1,0:T(8,128)S(1)}, f32[22,22]{1,0:T(8,128)}, u32[]{:S(2)}) copy-start(f32[22,22]{1,0:T(8,128)} %jacobian.3) | copy-start | bytes 5812
  0.7 9.9 %copy-start.4 = (s32[32]{0:T(128)S(1)}, s32[32]{0:T(128)}, u32[]{:S(2)}) copy-start(s32[32]{0:T(128)} %param.13) | copy-start | bytes 388
  2.5 8.0 %collective-permute-start.2 = (f32[8,24,128]{2,1,0:T(8,128)S(1)}, f32[8,24,128]{2,1,0:T(8,128)S(1)}, u32[]{:S(2)}, u32[]{:S(2)}) collective-permute-start(f32[8,24,128]{2,1,0:T(8,128)S(1)} %get-tuple-element.27), channel_id=1, source_target_pairs={{0,1},{1,0},{2,3},{3,2},{4,5},{5,4},{6,7},{7,6},{8,9},{9,8},{10,11... | collective-permute-start | bytes 294920 | tf_op jit(solution)/shard_map/ppermute | solution.py:440
  5.5 5.0 %collective-permute-start.4 = (f32[40,128]{1,0:T(8,128)S(1)}, f32[40,128]{1,0:T(8,128)S(1)}, u32[]{:S(2)}, u32[]{:S(2)}) collective-permute-start(f32[40,128]{1,0:T(8,128)S(1)} %get-tuple-element.29), channel_id=1, source_target_pairs={{8,16},{16,8},{0,24},{24,0},{9,17},{17,9},{1,25},{25,1},{10,18},{1... | collective-permute-start | bytes 61448 | tf_op jit(solution)/shard_map/ppermute | solution.py:443
  6.2 4.3 %collective-permute-start = (f32[32,128]{1,0:T(8,128)S(1)}, f32[32,128]{1,0:T(8,128)S(1)}, u32[]{:S(2)}, u32[]{:S(2)}) collective-permute-start(f32[32,128]{1,0:T(8,128)S(1)} %get-tuple-element.25), channel_id=1, source_target_pairs={{0,2},{2,0},{4,6},{6,4},{1,3},{3,1},{5,7},{7,5},{8,10},{10,8},{12,... | collective-permute-start | bytes 49160 | tf_op jit(solution)/shard_map/ppermute | solution.py:440
  7.8 2.7 %collective-permute-start.1 = (f32[32,128]{1,0:T(8,128)S(1)}, f32[32,128]{1,0:T(8,128)S(1)}, u32[]{:S(2)}, u32[]{:S(2)}) collective-permute-start(f32[32,128]{1,0:T(8,128)S(1)} %get-tuple-element.26), channel_id=1, source_target_pairs={{8,0},{4,2},{2,4},{14,6},{0,8},{12,10},{10,12},{6,14},{24,16},{20,... | collective-permute-start | bytes 49160 | tf_op jit(solution)/shard_map/ppermute | solution.py:434
  8.5 2.0 %collective-permute-start.3 = (f32[24,128]{1,0:T(8,128)S(1)}, f32[24,128]{1,0:T(8,128)S(1)}, u32[]{:S(2)}, u32[]{:S(2)}) collective-permute-start(f32[24,128]{1,0:T(8,128)S(1)} %get-tuple-element.28), channel_id=1, source_target_pairs={{0,8},{8,0},{16,24},{24,16},{1,9},{9,1},{17,25},{25,17},{2,10},{10... | collective-permute-start | bytes 36872 | tf_op jit(solution)/shard_map/ppermute | solution.py:440
  11.2 5.1 %collective-permute-start.7 = (f32[2,24,128]{2,1,0:T(8,128)S(1)}, f32[2,24,128]{2,1,0:T(8,128)S(1)}, u32[]{:S(2)}, u32[]{:S(2)}) collective-permute-start(f32[2,24,128]{2,1,0:T(8,128)S(1)} %slice.7), channel_id=1, source_target_pairs={{14,0},{8,2},{10,4},{12,6},{6,8},{0,10},{2,12},{4,14},{30,16},{24,... | collective-permute-start | bytes 73736 | tf_op jit(solution)/shard_map/ppermute | solution.py:434
  14.6 7.7 %collective-permute-start.5 = (f32[16,24,128]{2,1,0:T(8,128)S(1)}, f32[16,24,128]{2,1,0:T(8,128)S(1)}, u32[]{:S(2)}, u32[]{:S(2)}) collective-permute-start(f32[16,24,128]{2,1,0:T(8,128)S(1)} %get-tuple-element.33), channel_id=1, source_target_pairs={{0,2},{2,0},{4,6},{6,4},{1,3},{3,1},{5,7},{7,5},{8,10},{10,8},{12,... | collective-permute-start | bytes 589832 | tf_op jit(solution)/shard_map/ppermute | solution.py:440
  15.3 6.9 %collective-permute-start.6 = (f32[16,24,128]{2,1,0:T(8,128)S(1)}, f32[16,24,128]{2,1,0:T(8,128)S(1)}, u32[]{:S(2)}, u32[]{:S(2)}) collective-permute-start(f32[16,24,128]{2,1,0:T(8,128)S(1)} %get-tuple-element.34), channel_id=1, source_target_pairs={{8,0},{4,2},{2,4},{14,6},{0,8},{12,10},{10,12},{6,14},{24,16},{20,... | collective-permute-start | bytes 589832 | tf_op jit(solution)/shard_map/ppermute | solution.py:434
  16.3 1.3 %collective-permute-start.8 = (f32[2,24,128]{2,1,0:T(8,128)S(1)}, f32[2,24,128]{2,1,0:T(8,128)S(1)}, u32[]{:S(2)}, u32[]{:S(2)}) collective-permute-start(f32[2,24,128]{2,1,0:T(8,128)S(1)} %slice_add_fusion), channel_id=1, source_target_pairs={{0,8},{8,0},{16,24},{24,16},{1,9},{9,1},{17,25},{25,17},{2,10},{10... | collective-permute-start | bytes 73736 | tf_op jit(solution)/shard_map/ppermute | solution.py:455
  17.7 4.9 %collective-permute-start.9 = (f32[2,24,128]{2,1,0:T(8,128)S(1)}, f32[2,24,128]{2,1,0:T(8,128)S(1)}, u32[]{:S(2)}, u32[]{:S(2)}) collective-permute-start(f32[2,24,128]{2,1,0:T(8,128)S(1)} %add.7.refs_0_), channel_id=1, source_target_pairs={{24,0},{25,1},{16,8},{17,9},{8,16},{9,17},{0,24},{1,25},{26,2},{27... | collective-permute-start | bytes 73736 | tf_op jit(solution)/shard_map/ppermute | solution.py:434
  18.1 4.5 %collective-permute-start.10 = (f32[2,24,128]{2,1,0:T(8,128)S(1)}, f32[2,24,128]{2,1,0:T(8,128)S(1)}, u32[]{:S(2)}, u32[]{:S(2)}) collective-permute-start(f32[2,24,128]{2,1,0:T(8,128)S(1)} %add.7.refs_0_), channel_id=1, source_target_pairs={{25,0},{24,1},{17,8},{16,9},{9,16},{8,17},{1,24},{0,25},{27,2},{26... | collective-permute-start | bytes 73736 | tf_op jit(solution)/shard_map/ppermute | solution.py:434
  19.4 3.5 %collective-permute-start.11 = (f32[2,24,128]{2,1,0:T(8,128)S(1)}, f32[2,24,128]{2,1,0:T(8,128)S(1)}, u32[]{:S(2)}, u32[]{:S(2)}) collective-permute-start(f32[2,24,128]{2,1,0:T(8,128)S(1)} %add.7.refs_0_), channel_id=1, source_target_pairs={{9,0},{8,1},{1,8},{0,9},{25,16},{24,17},{17,24},{16,25},{11,2},{10... | collective-permute-start | bytes 73736 | tf_op jit(solution)/shard_map/ppermute | solution.py:434
